TPU v7x, 256 devices: a whole 4x4x8 slice. The times are simulated.
256 devices in a mesh: tm: 4 (over x), sx: 16 (over z, core), sy: 4 (over y).
Axes of the slice: x: 4, y: 4, z: 8, core: 2. Of those that a mesh axis runs over, the one named last changes fastest.
Arguments:
- initial_state: float32 [4, 256, 64, 128], P(None, 'sx', 'sy'), may hold values from -6 to 6
- start_old: float32 [4, 4, 256, 64, 128], P('tm', None, 'sx', 'sy'), may hold values from -6 to 6
- end_old: float32 [4, 4, 256, 64, 128], P('tm', None, 'sx', 'sy'), may hold values from -6 to 6
- coarse_old: float32 [4, 4, 128, 32, 64], P('tm', None, 'sx', 'sy'), may hold values from -6 to 6
Outputs:
- new_start: float32 [4, 4, 256, 64, 128], P('tm', None, 'sx', 'sy')
- fine_end: float32 [4, 4, 256, 64, 128], P('tm', None, 'sx', 'sy')
- coarse_end: float32 [4, 4, 128, 32, 64], P('tm', None, 'sx', 'sy')
All inputs are finite; a program needn't handle non-finite values.
Results may differ from a plain program's by a relative error of at most 0.0001.
Values sent between devices are 32-bit elements; how exact they have to be, the bound alone decides.
No kernel may reach another device: no remote copies, remote signals or barrier semaphores. Data moves between devices by JAX's collectives and lax.ppermute only.
A program may use at most 128 MiB of HBM per device.

v0:
```python
import jax
import jax.numpy as jnp
from jax import lax
from jax.sharding import PartitionSpec as P

LEVELS = 5
SWEEPS = 3


OMEGA = 2.0 / 3.0
STEP = 0.5


def padded_2(cells, sides, width):
    for axis, dim in sides:
        count = lax.axis_size(axis)
        head = lax.slice_in_dim(cells, 0, width, axis=dim)
        tail = lax.slice_in_dim(cells, cells.shape[dim] - width, cells.shape[dim], axis=dim)
        cells = jnp.concatenate(
            [
                lax.ppermute(tail, axis, [(i, (i + 1) % count) for i in range(count)]),
                cells,
                lax.ppermute(head, axis, [((i + 1) % count, i) for i in range(count)]),
            ],
            axis=dim,
        )
    return cells


def passed_along(value, axis, steps):
    count = lax.axis_size(axis)
    leading, last = (max(0, -steps), min(count, count - steps))
    return lax.ppermute(value, axis, [(source, source + steps) for source in range(leading, last)])


def plus_x(padded):
    return padded[..., 2:, 1:-1, :]


def minus_x(padded):
    return padded[..., :-2, 1:-1, :]


def plus_y(padded):
    return padded[..., 1:-1, 2:, :]


def minus_y(padded):
    return padded[..., 1:-1, :-2, :]


def centre(padded):
    return padded[..., 1:-1, 1:-1, :]


def plus_z(field):
    return jnp.roll(field, -1, -1)


def minus_z(field):
    return jnp.roll(field, 1, -1)


def neighbours(padded):
    middle = centre(padded)
    return (
        plus_x(padded)
        + minus_x(padded)
        + plus_y(padded)
        + minus_y(padded)
        + plus_z(middle)
        + minus_z(middle)
    )


def relax_once(padded, source, spacing_sq):
    middle = centre(padded)
    return middle + OMEGA * ((neighbours(padded) - spacing_sq * source) / 6.0 - middle)


def first_relax(source, spacing_sq):
    return OMEGA * ((0.0 - spacing_sq * source) / 6.0)


def defect(padded, source, spacing_sq):
    return source - (neighbours(padded) - 6.0 * centre(padded)) / spacing_sq


def restrict(field):
    lead = field.shape[:-3]
    size_x, size_y, size_z = field.shape[-3:]
    blocks = field.reshape(lead + (size_x // 2, 2, size_y // 2, 2, size_z // 2, 2))
    return blocks.mean(axis=(-5, -3, -1))


def prolong(field):
    return jnp.repeat(jnp.repeat(jnp.repeat(field, 2, -3), 2, -2), 2, -1)


def explicit_rate(padded, per_cell):
    middle = centre(padded)
    grad_x = (plus_x(padded) - minus_x(padded)) * 0.5
    grad_y = (plus_y(padded) - minus_y(padded)) * 0.5
    grad_z = (plus_z(middle) - minus_z(middle)) * 0.5
    carried = -(middle[0] * grad_x + middle[1] * grad_y + middle[2] * grad_z) * per_cell
    lifted = jnp.concatenate([carried[:2], carried[2:3] + middle[3:4], carried[3:]], axis=0)
    return STEP * lifted


def divergence(pad_u, pad_v, middle_w, per_cell):
    total = (plus_x(pad_u) - minus_x(pad_u)) * 0.5 + (plus_y(pad_v) - minus_y(pad_v)) * 0.5
    total = total + (plus_z(middle_w) - minus_z(middle_w)) * 0.5
    return total * per_cell


def correct(combined, padded, per_cell):
    middle = centre(padded)
    grad_x = (plus_x(padded) - minus_x(padded)) * 0.5 * per_cell
    grad_y = (plus_y(padded) - minus_y(padded)) * 0.5 * per_cell
    grad_z = (plus_z(middle) - minus_z(middle)) * 0.5 * per_cell
    return jnp.stack(
        [combined[0] - grad_x, combined[1] - grad_y, combined[2] - grad_z, combined[3]]
    )


def coarsest(source, spacing_sq):
    estimate = first_relax(source, spacing_sq)
    for counter in range(SWEEPS - 1):
        padded = padded_2(estimate, (("sx", 0), ("sy", 1)), 1)
        estimate = relax_once(padded, source, spacing_sq)
    return estimate


def vcycle(source, level):
    spacing_sq = 4.0**level
    if level == LEVELS - 1:
        return coarsest(source, spacing_sq)
    estimate = first_relax(source, spacing_sq)
    padded = padded_2(estimate, (("sx", 0), ("sy", 1)), 1)
    coarser = vcycle(restrict(defect(padded, source, spacing_sq)), level + 1)
    estimate = estimate + prolong(coarser)
    padded = padded_2(estimate, (("sx", 0), ("sy", 1)), 1)
    return relax_once(padded, source, spacing_sq)


def source_of(combined, level):
    rim_state = padded_2(combined[:2], (("sx", 1), ("sy", 2)), 1)
    return divergence(rim_state[0], rim_state[1], combined[2], 0.5**level)


def project(combined, source, level):
    pressure = vcycle(source, level)
    padded = padded_2(pressure, (("sx", 0), ("sy", 1)), 1)
    return correct(combined, padded, 0.5**level)


def coarse_step(state):
    padded = padded_2(state, (("sx", 1), ("sy", 2)), 1)
    combined = state + explicit_rate(padded, 0.5)
    source = source_of(combined, 1)
    return project(combined, source, 1)


def shards(initial_state, start_old, end_old, coarse_old):
    begin_state = start_old[0]
    end_state = end_old[0]
    stacked = jnp.concatenate([begin_state, end_state], axis=0)
    padded = padded_2(stacked, (("sx", 1), ("sy", 2)), 1)
    combined = begin_state + 0.5 * (explicit_rate(padded[:4], 1.0) + explicit_rate(padded[4:], 1.0))
    source = source_of(combined, 0)
    fine_end = project(combined, source, 0)
    jump_fine = fine_end - prolong(coarse_old[0])
    jump_in = passed_along(jump_fine, "tm", 1)
    opening = restrict(initial_state)
    position = lax.axis_index("tm")
    leading = position == 0
    lowered = restrict(jump_in)

    def one_round(counter, carry):
        current, previous, arrived = carry
        coarse_out = coarse_step(current)
        arrived = passed_along(coarse_out, "tm", 1)
        current = jnp.where(leading, opening, arrived + lowered)
        return (current, coarse_out, arrived)

    initial = (
        jnp.where(leading, opening, lowered),
        jnp.zeros_like(opening),
        jnp.zeros_like(opening),
    )
    current, coarse_out, arrived = lax.fori_loop(0, lax.axis_size("tm"), one_round, initial)
    new_start = jnp.where(leading, initial_state, jump_in + prolong(arrived))
    return (new_start[None], fine_end[None], coarse_out[None])


def solution(mesh):
    in_specs = (
        P(None, "sx", "sy", None),
        P("tm", None, "sx", "sy", None),
        P("tm", None, "sx", "sy", None),
        P("tm", None, "sx", "sy", None),
    )
    out_specs = (
        P("tm", None, "sx", "sy", None),
        P("tm", None, "sx", "sy", None),
        P("tm", None, "sx", "sy", None),
    )
    return jax.shard_map(shards, mesh=mesh, in_specs=in_specs, out_specs=out_specs, check_vma=False)
```

profile of v0, /device:TPU:1, one launch (start us, length us, event | category | flops | bytes accessed | tf_op | source)
XLA Modules:
  0.0 734.9 jit_solution(8755976310470966199)
XLA Ops:
  31.5 3.3 collective-permute-start.50
  40.2 4.4 collective-permute-start.53
  54.1 9.7 %reshape.414 = f32[8,2,8,2,64,2]{5,4,3,2,1,0:T(8,128)} reshape(f32[16,16,128]{2,1,0:T(8,128)S(1)} %fusion.121) | data formatting | bytes 262144 | tf_op jit(solution)/shard_map/reshape | solution.py:92
  63.8 4.1 reduce_sum.109
  67.9 5.1 collective-permute-start.57
  79.5 4.3 collective-permute-start.61
  89.1 4.3 collective-permute-start.65
  98.6 4.3 collective-permute-start.69
  109.5 4.5 collective-permute-start.73
  120.4 4.2 collective-permute-start.77
  130.0 4.3 collective-permute-start.81
  140.1 4.3 collective-permute-start.85
  150.7 4.5 collective-permute-start.89
  160.6 4.3 collective-permute-start.93
  174.1 8.8 %copy.691 = f32[4,16,16,128]{0,3,2,1:T(8,128)} copy(f32[4,16,16,128]{3,2,1,0:T(8,128)S(1)} %copy-done.4) | data formatting | bytes 1048576 | tf_op args[0]
  185.8 13.1 %reduce_sum.115 = f32[4,8,8,64]{0,3,2,1:T(8,128)} reduce(f32[4,8,2,8,2,64,2]{0,6,5,4,3,2,1:T(2,128)} %bitcast.184, f32[]{:T(128)} %constant.250.clone.1), dimensions={2,4,6}, to_apply=%region_5.6 | reduce | flops 114688 | bytes 589828 | tf_op jit(solution)/shard_map/reduce_sum | solution.py:93
  198.9 8.8 %copy.692 = f32[4,16,16,128]{0,3,2,1:T(8,128)} copy(f32[4,16,16,128]{3,2,1,0:T(8,128)S(1)} %collective-permute-done.97) | data formatting | bytes 1048576 | tf_op jit(solution)/shard_map/ppermute | solution.py:33
  207.7 13.1 %reduce_sum.116 = f32[4,8,8,64]{0,3,2,1:T(8,128)} reduce(f32[4,8,2,8,2,64,2]{0,6,5,4,3,2,1:T(2,128)} %bitcast.185, f32[]{:T(128)} %constant.250.clone.1), dimensions={2,4,6}, to_apply=%region_6.7 | reduce | flops 114688 | bytes 589828 | tf_op jit(solution)/shard_map/reduce_sum | solution.py:93
  220.7 5.2 broadcast_multiply_fusion.2
  231.2 487.5 %while.19 = (s32[]{:T(128)}, f32[4,8,8,64]{3,2,1,0:T(8,128)S(1)}, f32[4,8,8,64]{3,2,1,0:T(8,128)}, f32[4,8,8,64]{3,2,1,0:T(8,128)}, pred[]{:T(512)}, /*index=5*/...) while((s32[]{:T(128)}, f32[4,8,8,64]{3,2,1,0:T(8,128)S(1)}, ...), condition=%wide.region_12.13_spmd, body=%wide.region_7.12_spmd.sunk | while | flops 820178 | bytes 4723658 | solution.py:191
  231.4 3.3 collective-permute-start
  242.2 3.6 collective-permute-start.4
  255.0 5.1 collective-permute-start.8
  266.3 4.3 collective-permute-start.12
  276.1 4.0 collective-permute-start.16
  285.7 4.1 collective-permute-start.20
  296.4 4.5 collective-permute-start.24
  307.2 4.3 collective-permute-start.28
  317.0 4.1 collective-permute-start.32
  326.7 4.1 collective-permute-start.36
  336.4 3.3 collective-permute-start.40
  362.2 4.6 collective-permute-start.4
  376.1 5.1 collective-permute-start.8
  387.5 4.3 collective-permute-start.12
  397.2 4.0 collective-permute-start.16
  406.8 4.1 collective-permute-start.20
  417.5 4.5 collective-permute-start.24
  428.4 4.3 collective-permute-start.28
  438.1 4.1 collective-permute-start.32
  447.8 4.1 collective-permute-start.36
  457.5 3.3 collective-permute-start.40
  467.7 4.1 collective-permute-start.44
  484.3 4.6 collective-permute-start.4
  498.2 5.1 collective-permute-start.8
  509.6 4.3 collective-permute-start.12
  519.3 4.0 collective-permute-start.16
  528.9 4.1 collective-permute-start.20
  539.6 4.5 collective-permute-start.24
  550.5 4.3 collective-permute-start.28
  560.2 4.1 collective-permute-start.32
  569.9 4.1 collective-permute-start.36
  589.8 4.1 collective-permute-start.44
  606.4 4.6 collective-permute-start.4
  620.3 5.1 collective-permute-start.8
  631.7 4.3 collective-permute-start.12
  641.5 4.0 collective-permute-start.16
  651.0 4.1 collective-permute-start.20
  661.7 4.5 collective-permute-start.24
  672.6 4.3 collective-permute-start.28
  682.3 4.1 collective-permute-start.32
  692.0 4.1 collective-permute-start.36
  711.9 4.1 collective-permute-start.44
  725.9 5.0 select_bitcast_fusion
  731.0 3.7 copy.700
  (995 shorter events, 430.6 us)
Async XLA Ops:
  1.5 11.2 %collective-permute-start.45 = (f32[8,1,16,128]{3,2,1,0:T(8,128)S(1)}, f32[8,1,16,128]{3,2,1,0:T(8,128)S(1)}, u32[]{:S(2)}, u32[]{:S(2)}) collective-permute-start(f32[8,1,16,128]{3,2,1,0:T(8,128)S(1)} %get-tuple-element.348), channel_id=1, source_target_pairs={{4,0},{8,4},{12,8},{16,12},{20,16},{24,20},{28,24},{32,28},{36,32}... | collective-permute-start | bytes 196616 | tf_op jit(solution)/shard_map/ppermute | solution.py:23
  4.8 7.9 %collective-permute-start.46 = (f32[8,1,16,128]{3,2,1,0:T(8,128)S(1)}, f32[8,1,16,128]{3,2,1,0:T(8,128)S(1)}, u32[]{:S(2)}, u32[]{:S(2)}) collective-permute-start(f32[8,1,16,128]{3,2,1,0:T(8,128)S(1)} %get-tuple-element.347), channel_id=1, source_target_pairs={{0,4},{4,8},{8,12},{12,16},{16,20},{20,24},{24,28},{28,32},{32,36}... | collective-permute-start | bytes 196616 | tf_op jit(solution)/shard_map/ppermute | solution.py:21
  13.4 12.5 %collective-permute-start.47 = (f32[8,18,1,128]{3,0,2,1:T(8,128)}, f32[8,18,1,128]{3,0,2,1:T(8,128)}, u32[]{:S(2)}, u32[]{:S(2)}) collective-permute-start(f32[8,18,1,128]{3,0,2,1:T(8,128)} %copy.703), channel_id=1, source_target_pairs={{1,0},{2,1},{3,2},{0,3},{5,4},{6,5},{7,6},{4,7},{9,8},{10,9},{11,1... | collective-permute-start | bytes 221192 | tf_op jit(solution)/shard_map/ppermute | solution.py:23
  16.6 10.3 %collective-permute-start.48 = (f32[8,18,1,128]{3,0,2,1:T(8,128)}, f32[8,18,1,128]{3,0,2,1:T(8,128)}, u32[]{:S(2)}, u32[]{:S(2)}) collective-permute-start(f32[8,18,1,128]{3,0,2,1:T(8,128)} %copy.704), channel_id=1, source_target_pairs={{0,1},{1,2},{2,3},{3,0},{4,5},{5,6},{6,7},{7,4},{8,9},{9,10},{10,1... | collective-permute-start | bytes 221192 | tf_op jit(solution)/shard_map/ppermute | solution.py:21
  30.7 4.7 collective-permute-start.49
  40.2 5.2 collective-permute-start.53
  67.9 5.9 collective-permute-start.57
  79.5 5.1 collective-permute-start.61
  89.1 5.1 collective-permute-start.65
  98.6 5.1 collective-permute-start.69
  109.5 5.3 collective-permute-start.73
  120.4 5.0 collective-permute-start.77
  130.0 5.1 collective-permute-start.81
  140.1 5.1 collective-permute-start.85
  150.7 5.4 collective-permute-start.89
  160.6 5.1 collective-permute-start.93
  171.0 28.0 %collective-permute-start.97 = (f32[4,16,16,128]{3,2,1,0:T(8,128)S(1)}, f32[4,16,16,128]{3,2,1,0:T(8,128)S(1)}, u32[]{:S(2)}, u32[]{:S(2)}) collective-permute-start(f32[4,16,16,128]{3,2,1,0:T(8,128)S(1)} %get-tuple-element.352), channel_id=1, source_target_pairs={{0,64},{64,128},{128,192},{1,65},{65,129},{129,193},{2,66},{66,130... | collective-permute-start | bytes 1572872 | tf_op jit(solution)/shard_map/ppermute | solution.py:33
  231.4 5.3 collective-permute-start
  255.0 5.9 collective-permute-start.8
  266.3 5.1 collective-permute-start.12
  276.1 4.8 collective-permute-start.16
  285.7 4.9 collective-permute-start.20
  296.4 5.3 collective-permute-start.24
  307.2 5.1 collective-permute-start.28
  317.0 5.0 collective-permute-start.32
  326.7 5.0 collective-permute-start.36
  336.4 5.2 collective-permute-start.40
  346.6 5.0 collective-permute-start.44
  352.3 5.3 collective-permute-start
  362.2 5.4 collective-permute-start.4
  376.1 5.9 collective-permute-start.8
  387.5 5.1 collective-permute-start.12
  397.2 4.8 collective-permute-start.16
  406.8 4.9 collective-permute-start.20
  417.5 5.3 collective-permute-start.24
  428.4 5.1 collective-permute-start.28
  438.1 5.0 collective-permute-start.32
  447.8 5.0 collective-permute-start.36
  457.5 5.2 collective-permute-start.40
  467.7 6.0 collective-permute-start.44
  474.4 5.3 collective-permute-start
  484.3 5.4 collective-permute-start.4
  498.2 5.9 collective-permute-start.8
  509.6 5.1 collective-permute-start.12
  519.3 4.8 collective-permute-start.16
  528.9 4.9 collective-permute-start.20
  539.6 5.3 collective-permute-start.24
  550.5 5.1 collective-permute-start.28
  560.2 5.0 collective-permute-start.32
  569.9 5.0 collective-permute-start.36
  579.6 5.2 collective-permute-start.40
  589.8 6.0 collective-permute-start.44
  596.5 5.3 collective-permute-start
  606.4 5.4 collective-permute-start.4
  620.3 5.9 collective-permute-start.8
  631.7 5.1 collective-permute-start.12
  641.5 4.8 collective-permute-start.16
  651.0 4.9 collective-permute-start.20
  661.7 5.3 collective-permute-start.24
  672.6 5.1 collective-permute-start.28
  682.3 5.0 collective-permute-start.32
  692.0 5.0 collective-permute-start.36
  701.7 5.2 collective-permute-start.40
  711.9 6.0 collective-permute-start.44
  (187 other events, 584.1 us)
where the time goes:
time: 748 us; the launch traced here: 735 us
  starting transfers between devices  420 us (56%)
  waiting for transfers between devices  150 us (20%)
  local copies, waits for them, and re-layouts  92.8 us (12%)
  other arithmetic  68.3 us (9%)
    ppermute x114, starting transfers between devices, padded_2(): lax.ppermute(head, axis, [((i + 1) % count, i) for i in range(count)])  323 us
    ppermute x114, waiting for transfers between devices, padded_2(): lax.ppermute(tail, axis, [(i, (i + 1) % count) for i in range(count)])  90.8 us
    ppermute x114, starting transfers between devices, padded_2(): lax.ppermute(tail, axis, [(i, (i + 1) % count) for i in range(count)])  78.9 us
    ppermute x114, waiting for transfers between devices, padded_2(): lax.ppermute(head, axis, [((i + 1) % count, i) for i in range(count)])  51.9 us
    reduce_sum x23, other arithmetic, restrict(): return blocks.mean(axis=(-5, -3, -1))  32.6 us
    unnamed x25, local copies, waits for them, and re-layouts  18.5 us
    ppermute x5, starting transfers between devices, passed_along(): lax.ppermute(value, axis, [(source, source + steps) for source in range(l...  18.5 us
    reshape x11, local copies, waits for them, and re-layouts, restrict(): field.reshape(lead + (size_x // 2, 2, size_y // 2, 2, size_z // 2, 2))  15.6 us
  transfers between devices with their start and end apart: 233, of which 195 were waited for; matrix products, arithmetic and copies ran while one was open for 8% of the time, Pallas kernels for 0%

commit v1 on v0

v1 whole, which is shorter than its diff:
```python
import jax
import jax.numpy as jnp
from jax import lax
from jax.experimental import pallas as pl
from jax.experimental.pallas import tpu as pltpu
from jax.sharding import PartitionSpec as P

F32 = jnp.float32
HIGH = lax.Precision.HIGHEST


def call(body, outs, args, scratch=(), smem=0, limit=24):
    vmem = pl.BlockSpec(memory_space=pltpu.VMEM)
    scalar = pl.BlockSpec(memory_space=pltpu.SMEM)
    single = not isinstance(outs, list)
    shapes = [outs] if single else outs
    got = pl.pallas_call(
        body,
        out_shape=[jax.ShapeDtypeStruct(s, F32) for s in shapes],
        in_specs=[scalar] * smem + [vmem] * (len(args) - smem),
        out_specs=[vmem] * len(shapes),
        scratch_shapes=[pltpu.VMEM(s, F32) for s in scratch],
        compiler_params=pltpu.CompilerParams(vmem_limit_bytes=limit * 2**20),
        name=body.__name__,
    )(*args)
    return got[0] if single else got


def shifted(value, amount, axis):
    return pltpu.roll(value, amount % value.shape[axis], axis)


def nxt(value, step, axis):
    return shifted(value, -step, axis)


def prv(value, step, axis):
    return shifted(value, step, axis)


def index_along(shape, axis):
    return lax.broadcasted_iota(jnp.int32, shape, axis)


def pair_sum(value, step, axis):
    upper = (index_along(value.shape, axis) // step) % 2 == 1
    return value + jnp.where(upper, prv(value, step, axis), nxt(value, step, axis))


def ring_sum(value, step_y, step_z):
    return (
        nxt(value, step_y, 0)
        + prv(value, step_y, 0)
        + nxt(value, step_z, 1)
        + prv(value, step_z, 1)
    )


def restricted_defect(before, first, second, after, step_y, step_z):
    both = first + second
    total = both * (1.0 / 3.0) + (before + both + after + ring_sum(both, step_y, step_z)) * (1.0 / 9.0)
    return pair_sum(pair_sum(total, step_y, 0), step_z, 1) * 0.125


def smoothed(before, here, after, source, spacing_sq, step_y, step_z):
    around = before + after + ring_sum(here, step_y, step_z)
    return here * (1.0 / 3.0) + (around - spacing_sq * source) * (1.0 / 9.0)


def deep_pressure(r3, step_y, step_z):
    r4 = [
        restricted_defect(r3[2 * w], r3[2 * w + 1], r3[2 * w + 2], r3[2 * w + 3], step_y, step_z)
        for w in range(7)
    ]
    low_y, low_z = 2 * step_y, 2 * step_z
    p4 = [r * (-256.0 / 9.0) for r in r4]
    for sweep in range(2):
        inner = range(1 + sweep, 6 - sweep)
        fresh = {w: smoothed(p4[w - 1], p4[w], p4[w + 1], r4[w], 256.0, low_y, low_z) for w in inner}
        p4 = [fresh.get(w) for w in range(7)]
    e3 = {q: r3[q] * (-64.0 / 9.0) + p4[(q - 7) // 2 + 3] for q in range(5, 11)}
    return [
        smoothed(e3[q - 1], e3[q], e3[q + 1], r3[q], 64.0, step_y, step_z) for q in range(6, 10)
    ]


def advected(ref, base, i, comp):
    here = ref[base + comp, i]
    grad_x = ref[base + comp, i + 1] - ref[base + comp, i - 1]
    grad_y = nxt(here, 1, 0) - prv(here, 1, 0)
    grad_z = nxt(here, 1, 1) - prv(here, 1, 1)
    return ref[base, i] * grad_x + ref[base + 1, i] * grad_y + ref[base + 2, i] * grad_z


def z_pick(high):
    k = index_along((128, 128), 0)
    j = index_along((128, 128), 1)
    return jnp.where(k // 2 == j - 64 * high, 1.0, 0.0).astype(F32)


def z_spread(high):
    k = index_along((128, 128), 0)
    j = index_along((128, 128), 1)
    return jnp.where(k == j // 2 + 64 * high, 1.0, 0.0).astype(F32)


def dot(a, b):
    return lax.dot_general(a, b, (((1,), (0,)), ((), ())), precision=HIGH, preferred_element_type=F32)


def restricted_packed(fine, rows, half):
    for comp in range(4):
        for big in range(8):
            rows[comp, big] = fine[comp, 2 * big] + fine[comp, 2 * big + 1]
    for comp in range(4):
        for big in range(8):
            half[comp, big] = rows[comp, big, pl.ds(0, 8, 2), :] + rows[comp, big, pl.ds(1, 8, 2), :]
    low, high = z_pick(0), z_pick(1)
    return [
        0.125
        * (
            dot(half[2 * h].reshape(64, 128), low)
            + dot(half[2 * h + 1].reshape(64, 128), high)
        )
        for h in range(2)
    ]


def opening_body(initial, out, rows, half):
    packed = restricted_packed(initial, rows, half)
    for h in range(2):
        out[h] = packed[h].reshape(8, 8, 128)


def fine_source_body(begin, end, left, right, low, high, comb_out, r0_out, state, comb):
    for f in range(8):
        own = begin if f < 4 else end
        c = f % 4
        state[f, 0:2, 4:20] = left[f]
        state[f, 2:18, 4:20] = own[c]
        state[f, 18:20, 4:20] = right[f]
        state[f, :, 2:4] = low[f]
        state[f, :, 20:22] = high[f]

    def one(i, carry):
        for c in range(4):
            total = state[c, i] - 0.125 * (advected(state, 0, i, c) + advected(state, 4, i, c))
            if c == 2:
                total = total + 0.25 * (state[3, i] + state[7, i])
            comb[c, i - 1] = total
        return carry

    lax.fori_loop(1, 19, one, 0)

    def two(x, carry):
        v = comb[1, x + 1]
        w = comb[2, x + 1]
        div = comb[0, x + 2] - comb[0, x] + nxt(v, 1, 0) - prv(v, 1, 0) + nxt(w, 1, 1) - prv(w, 1, 1)
        r0_out[x] = (0.5 * div)[4:20]
        for c in range(4):
            comb_out[c, x] = comb[c, x + 1, 4:20, :]
        return carry

    lax.fori_loop(0, 16, two, 0)


def fine_down_body(own, left, right, low, high, r0, r1, r2p):
    r0[0:5, 8:24] = left[...]
    r0[5:21, 8:24] = own[...]
    r0[21:26, 8:24] = right[...]
    r0[:, 0:8] = low[...]
    r0[:, 24:32] = high[...]

    def one(k, carry):
        a = 2 * k + 1
        r1[k] = restricted_defect(r0[a - 1], r0[a], r0[a + 1], r0[a + 2], 1, 1)
        return carry

    lax.fori_loop(0, 12, one, 0)
    row = index_along((32, 128), 0)
    lane = index_along((32, 128), 1)
    mine = (row >= 8) & (row < 24) & (row % 4 == 0) & (lane % 4 == row // 4 - 2)
    for m in range(4):
        k = 2 * m + 2
        r2 = restricted_defect(r1[k - 1], r1[k], r1[k + 1], r1[k + 2], 2, 2)
        r2p[m : m + 1, :] = jnp.sum(jnp.where(mine, r2, 0.0), axis=0, keepdims=True)


def fine_up_body(where, gathered, r1, r0, comb, old, fine, rj, r2, e2, p2, e1, p1, e0, p0, rows, half):
    sx, sy = where[0], where[1]
    for d in range(9):
        for b in range(4):
            peer = ((sx + d + 12) % 16) * 4 + (sy + b + 3) % 4
            block = gathered[peer]
            for n in range(4):
                r2[4 * d + n, 4 * b : 4 * b + 4, :] = jnp.broadcast_to(block[n : n + 1], (4, 128))
    lane = index_along((16, 128), 1)
    row = index_along((16, 128), 0)
    mine = lane % 4 == row % 4

    def unpack(n, carry):
        r2[n] = pair_sum(pair_sum(jnp.where(mine, r2[n], 0.0), 1, 1), 2, 1)
        return carry

    lax.fori_loop(1, 35, unpack, 0)
    r3 = [
        restricted_defect(r2[2 * q + 1], r2[2 * q + 2], r2[2 * q + 3], r2[2 * q + 4], 1, 4)
        for q in range(16)
    ]
    p3 = deep_pressure(r3, 2, 8)
    for i in range(8):
        e2[i] = r2[14 + i] * (-16.0 / 9.0) + p3[i // 2]
    for i in range(6):
        value = smoothed(e2[i], e2[i + 1], e2[i + 2], r2[15 + i], 16.0, 1, 4)
        for y2 in range(8):
            p2[i, 4 * y2 : 4 * y2 + 4, :] = jnp.broadcast_to(value[y2 + 2 : y2 + 3], (4, 128))

    def lift(k, carry):
        e1[k] = r1[k] * (-4.0 / 9.0) + p2[k // 2]
        return carry

    lax.fori_loop(0, 12, lift, 0)

    def relax1(k, carry):
        p1[k] = smoothed(e1[k], e1[k + 1], e1[k + 2], r1[k + 1], 4.0, 2, 2)
        return carry

    lax.fori_loop(0, 10, relax1, 0)

    def lift0(j, carry):
        e0[j] = r0[j + 3] * (-1.0 / 9.0) + p1[j // 2]
        return carry

    lax.fori_loop(0, 20, lift0, 0)

    def relax0(j, carry):
        p0[j] = smoothed(e0[j], e0[j + 1], e0[j + 2], r0[j + 4], 1.0, 1, 1)
        return carry

    lax.fori_loop(0, 18, relax0, 0)

    def slope(x, carry):
        here = p0[x + 1]
        fine[0, x] = comb[0, x] - 0.5 * (p0[x + 2] - p0[x])[8:24]
        fine[1, x] = comb[1, x] - 0.5 * (nxt(here, 1, 0) - prv(here, 1, 0))[8:24]
        fine[2, x] = comb[2, x] - 0.5 * (nxt(here, 1, 1) - prv(here, 1, 1))[8:24]
        fine[3, x] = comb[3, x]
        return carry

    lax.fori_loop(0, 16, slope, 0)
    packed = restricted_packed(fine, rows, half)
    for h in range(2):
        rj[h] = packed[h].reshape(8, 8, 128) - old[h]


def coarse_down_body(left, own, right, comb_out, r1_out, r2_out, r3p, state, comb, r1):
    lane = index_along((32, 128), 1)
    row = index_along((32, 128), 0)
    for side, ref in enumerate((left, own, right)):

        def unpack(x, carry, side=side, ref=ref):
            for h in range(2):
                pair = ref[h, x]
                other = shifted(pair, 64, 1)
                state[2 * h, 8 * side + x] = jnp.where(lane < 64, pair, other)
                state[2 * h + 1, 8 * side + x] = jnp.where(lane < 64, other, pair)
            return carry

        lax.fori_loop(0, 8, unpack, 0)

    def one(i, carry):
        for c in range(3):
            total = state[c, i] - 0.125 * advected(state, 0, i, c)
            if c == 2:
                total = total + 0.5 * state[3, i]
            comb[c, i - 2] = total
        return carry

    lax.fori_loop(2, 22, one, 0)

    def own_b(x, carry):
        comb_out[3, x] = state[3, x + 8] - 0.125 * advected(state, 0, x + 8, 3)
        for c in range(3):
            comb_out[c, x] = comb[c, x + 6]
        return carry

    lax.fori_loop(0, 8, own_b, 0)

    def two(k, carry):
        v = comb[1, k + 1]
        w = comb[2, k + 1]
        div = comb[0, k + 2] - comb[0, k] + nxt(v, 1, 0) - prv(v, 1, 0) + nxt(w, 1, 1) - prv(w, 1, 1)
        r1[k] = 0.25 * div
        return carry

    lax.fori_loop(0, 18, two, 0)

    def three(m, carry):
        a = 2 * m + 1
        r2_out[m] = restricted_defect(r1[a - 1], r1[a], r1[a + 1], r1[a + 2], 1, 1)
        return carry

    lax.fori_loop(0, 8, three, 0)
    r1_out[...] = r1[3:15]
    mine = (row % 4 == 0) & (lane % 4 + 4 * (lane // 64) == row // 4)
    for x3 in range(2):
        m = 2 * x3 + 2
        r3 = restricted_defect(r2_out[m - 1], r2_out[m], r2_out[m + 1], r2_out[m + 2], 2, 2)
        r3p[x3 : x3 + 1, :] = jnp.sum(jnp.where(mine, r3, 0.0), axis=0, keepdims=True)


def coarse_up_core(where, gathered, comb, r1, r2, p3, p2, e2, e1, p1, emit):
    sx = where[0]
    lane = index_along((8, 128), 1)
    row = index_along((8, 128), 0)
    mine = lane % 4 + 4 * (lane // 64) == row
    r3 = []
    for q in range(16):
        x3 = q - 7
        block = gathered[(sx + x3 // 2 + 16) % 16]
        value = jnp.where(mine, jnp.broadcast_to(block[x3 % 2 : x3 % 2 + 1], (8, 128)), 0.0)
        value = value + shifted(value, 64, 1)
        r3.append(pair_sum(pair_sum(value, 1, 1), 2, 1))
    for i, value in enumerate(deep_pressure(r3, 1, 4)):
        for y3 in range(8):
            p3[i, 4 * y3 : 4 * y3 + 4, :] = jnp.broadcast_to(value[y3 : y3 + 1], (4, 128))

    def lift2(m, carry):
        e2[m] = r2[m] * (-16.0 / 9.0) + p3[m // 2]
        return carry

    lax.fori_loop(0, 8, lift2, 0)

    def relax2(m, carry):
        p2[m] = smoothed(e2[m], e2[m + 1], e2[m + 2], r2[m + 1], 16.0, 2, 2)
        return carry

    lax.fori_loop(0, 6, relax2, 0)

    def lift1(k, carry):
        e1[k] = r1[k] * (-4.0 / 9.0) + p2[k // 2]
        return carry

    lax.fori_loop(0, 12, lift1, 0)

    def relax1(k, carry):
        p1[k] = smoothed(e1[k], e1[k + 1], e1[k + 2], r1[k + 1], 4.0, 1, 1)
        return carry

    lax.fori_loop(0, 10, relax1, 0)
    lane = index_along((32, 128), 1)

    def slope(x, carry):
        here = p1[x + 1]
        u = comb[0, x] - 0.25 * (p1[x + 2] - p1[x])
        v = comb[1, x] - 0.25 * (nxt(here, 1, 0) - prv(here, 1, 0))
        w = comb[2, x] - 0.25 * (nxt(here, 1, 1) - prv(here, 1, 1))
        emit(x, jnp.where(lane < 64, u, v), jnp.where(lane < 64, w, comb[3, x]))
        return carry

    lax.fori_loop(0, 8, slope, 0)


def coarse_up_body(where, gathered, comb, r1, r2, ended, *scratch):
    def emit(x, uv, wb):
        ended[0, x] = uv
        ended[1, x] = wb

    coarse_up_core(where, gathered, comb, r1, r2, *scratch, emit)


def coarse_up_next_body(where, gathered, comb, r1, r2, jump, ended, following, *scratch):
    def emit(x, uv, wb):
        ended[0, x] = uv
        ended[1, x] = wb
        following[0, x] = uv + jump[0, x]
        following[1, x] = wb + jump[1, x]

    coarse_up_core(where, gathered, comb, r1, r2, *scratch, emit)


UP_SCRATCH = [(4, 32, 128), (6, 32, 128), (8, 32, 128), (12, 32, 128), (10, 32, 128)]


def rows_of(where, step):
    return pl.ds(pl.multiple_of(8 * ((where[1] + 4 - step) % 4), 8), 8)


def join_body(where, a0, a1, a2, a3, out):
    for step, ref in enumerate((a0, a1, a2, a3)):
        rows = rows_of(where, step)
        for h in range(2):
            for x in range(8):
                out[h, x, rows, :] = ref[h, x]


def join_jumps_body(where, a0, a1, a2, a3, ended, first, second, third):
    for step, ref in enumerate((a0, a1, a2, a3)):
        rows = rows_of(where, step)
        for h in range(2):
            for x in range(8):
                first[h, x, rows, :] = ref[0, h, x] + ended[h, x, rows, :]
                second[h, x, rows, :] = ref[1, h, x]
                third[h, x, rows, :] = ref[2, h, x]


def new_start_body(where, fine, initial, c1, c2, c3, out, rows, half, tall):
    t = where[2]

    @pl.when(t == 0)
    def _():
        out[...] = initial[...]

    @pl.when(t > 0)
    def _():
        packed = restricted_packed(fine, rows, half)
        mine = rows_of(where, 0)
        for h in range(2):
            state = jnp.where(
                t == 1, c1[h, :, mine, :], jnp.where(t == 2, c2[h, :, mine, :], c3[h, :, mine, :])
            )
            change = state.reshape(64, 128) - packed[h]
            for side in range(2):
                comp = 2 * h + side
                wide = dot(change, z_spread(side)).reshape(8, 8, 128)
                for x in range(8):
                    tall[comp, x, pl.ds(0, 8, 2), :] = wide[x]
                    tall[comp, x, pl.ds(1, 8, 2), :] = wide[x]
        for comp in range(4):
            for x in range(16):
                out[comp, x] = fine[comp, x] + tall[comp, x // 2]


def coarse_end_body(where, e0, e1, e2, e3, out):
    t = where[2]
    mine = rows_of(where, 0)
    for h in range(2):
        low = jnp.where(t == 0, e0[h, :, mine, :], e1[h, :, mine, :])
        high = jnp.where(t == 2, e2[h, :, mine, :], e3[h, :, mine, :])
        value = jnp.where(t < 2, low, high)
        out[2 * h] = value[:, :, :64]
        out[2 * h + 1] = shifted(value, 64, 2)[:, :, :64]


def moved(value, axis, step):
    count = lax.axis_size(axis)
    return lax.ppermute(value, axis, [(i, (i + step) % count) for i in range(count)])


def both_sides(low_face, high_face, axis):
    return moved(high_face, axis, 1), moved(low_face, axis, -1)


def around(value, axis):
    return [moved(value, axis, step) for step in range(1, 4)]


def shards(initial_state, start_old, end_old, coarse_old):
    begin, end, old = start_old[0], end_old[0], coarse_old[0]
    sx, sy, t = lax.axis_index("sx"), lax.axis_index("sy"), lax.axis_index("tm")
    where = jnp.stack([sx, sy, t]).astype(jnp.int32)

    opening = call(opening_body, (2, 8, 8, 128), [initial_state], [(4, 8, 16, 128), (4, 8, 8, 128)])
    old_packed = jnp.stack(
        [jnp.concatenate([old[0], old[1]], axis=-1), jnp.concatenate([old[2], old[3]], axis=-1)]
    )

    def face(cut):
        return jnp.concatenate([begin[cut], end[cut]], axis=0)

    every = slice(None)
    left, right = both_sides(
        face((every, slice(0, 2))), face((every, slice(14, 16))), "sx"
    )

    def y_face(cut):
        inner = face((every, every, cut))
        return jnp.concatenate([left[:, :, cut], inner, right[:, :, cut]], axis=1)

    low, high = both_sides(y_face(slice(0, 2)), y_face(slice(14, 16)), "sy")
    comb, r0 = call(
        fine_source_body,
        [(4, 16, 16, 128), (16, 16, 128)],
        [begin, end, left, right, low, high],
        [(8, 20, 24, 128), (4, 18, 24, 128)],
    )

    c0 = call(join_body, (2, 8, 32, 128), [where, opening] + around(opening, "sy"), smem=1)

    def coarse_down(state):
        lo, hi = both_sides(state, state, "sx")
        return call(
            coarse_down_body,
            [(4, 8, 32, 128), (12, 32, 128), (8, 32, 128), (2, 128)],
            [lo, state, hi],
            [(4, 24, 32, 128), (3, 20, 32, 128), (18, 32, 128)],
        )

    comb0, first0, second0, third0 = coarse_down(c0)

    left, right = both_sides(r0[:5], r0[11:], "sx")

    def source_face(cut):
        return jnp.concatenate([left[:, cut], r0[:, cut], right[:, cut]], axis=0)

    low, high = both_sides(source_face(slice(0, 8)), source_face(slice(8, 16)), "sy")
    r0_wide, r1, r2p = call(
        fine_down_body,
        [(26, 32, 128), (12, 32, 128), (4, 128)],
        [r0, left, right, low, high],
    )

    message = jnp.concatenate([r2p, third0, jnp.zeros((2, 128), F32)], axis=0)
    gathered = lax.all_to_all(jnp.broadcast_to(message[None], (64, 8, 128)), ("sx", "sy"), 0, 0)
    fine_end, rj = call(
        fine_up_body,
        [(4, 16, 16, 128), (2, 8, 8, 128)],
        [where, gathered, r1, r0_wide, comb, old_packed],
        [
            (36, 16, 128),
            (8, 16, 128),
            (6, 32, 128),
            (12, 32, 128),
            (10, 32, 128),
            (20, 32, 128),
            (18, 32, 128),
            (4, 8, 16, 128),
            (4, 8, 8, 128),
        ],
        smem=1,
    )
    ended0 = call(
        coarse_up_body,
        (2, 8, 32, 128),
        [where, gathered[::4, 4:6], comb0, first0, second0],
        UP_SCRATCH,
        smem=1,
    )

    turned = [rj] + around(rj, "tm")

    def slice_of(s):
        back = (t - s) % 4
        return jnp.where(
            back < 2,
            jnp.where(back == 0, turned[0], turned[1]),
            jnp.where(back == 2, turned[2], turned[3]),
        )

    jumps = jnp.stack([slice_of(s) for s in range(3)])
    c1, jump1, jump2 = call(
        join_jumps_body,
        [(2, 8, 32, 128)] * 3,
        [where, jumps] + around(jumps, "sy") + [ended0],
        smem=1,
    )
    fine_before = moved(fine_end, "tm", 1)

    def coarse_step(state, jump):
        combined, level1, level2, message = coarse_down(state)
        got = lax.all_to_all(jnp.broadcast_to(message[None], (16, 2, 128)), "sx", 0, 0)
        args = [where, got, combined, level1, level2]
        if jump is None:
            return call(coarse_up_body, (2, 8, 32, 128), args, UP_SCRATCH, smem=1)
        return call(
            coarse_up_next_body, [(2, 8, 32, 128)] * 2, args + [jump], UP_SCRATCH, smem=1
        )

    ended1, c2 = coarse_step(c1, jump1)
    ended2, c3 = coarse_step(c2, jump2)
    new_start = call(
        new_start_body,
        (4, 16, 16, 128),
        [where, fine_before, initial_state, c1, c2, c3],
        [(4, 8, 16, 128), (4, 8, 8, 128), (4, 8, 16, 128)],
        smem=1,
    )
    ended3 = coarse_step(c3, None)
    coarse_end = call(coarse_end_body, (4, 8, 8, 64), [where, ended0, ended1, ended2, ended3], smem=1)
    return (new_start[None], fine_end[None], coarse_end[None])


def solution(mesh):
    in_specs = (
        P(None, "sx", "sy", None),
        P("tm", None, "sx", "sy", None),
        P("tm", None, "sx", "sy", None),
        P("tm", None, "sx", "sy", None),
    )
    out_specs = (
        P("tm", None, "sx", "sy", None),
        P("tm", None, "sx", "sy", None),
        P("tm", None, "sx", "sy", None),
    )
    return jax.shard_map(shards, mesh=mesh, in_specs=in_specs, out_specs=out_specs, check_vma=False)
```

time: 748 us -> 194 us (0.26); the launches traced: 735 us -> 194 us
  starting transfers between devices: 420 us -> 47.3 us
  waiting for transfers between devices: 150 us -> 52.2 us
  local copies, waits for them, and re-layouts: 92.8 us -> 2.67 us
  other arithmetic: 68.3 us -> 0.47 us
  Pallas kernels: 0 us -> 63.4 us
  blocking collectives: 0 us -> 27.1 us
    ppermute x233 -> x26, starting transfers between devices: 420 us -> 31.9 us  [moved(): lax.ppermute(value, axis, [(i, (i + step) % count) for i in range(count)])]
    ppermute x233 -> x26, waiting for transfers between devices: 150 us -> 34.1 us  [moved(): lax.ppermute(value, axis, [(i, (i + step) % count) for i in range(count)])]
    pallas_call x0 -> x16, Pallas kernels: none -> 63.4 us  [call(): pl.pallas_call(body, out_shape=[jax.ShapeDtypeStruct(s, F32) for s in sha...]
    reduce_sum x23 -> x0, other arithmetic: 32.6 us -> none  [restrict(): return blocks.mean(axis=(-5, -3, -1))]
    all_to_all x0 -> x2, blocking collectives: none -> 27.1 us  [coarse_step(): lax.all_to_all(jnp.broadcast_to(message[None], (16, 2, 128)), 'sx', 0, 0)]
    reshape x36 -> x0, local copies, waits for them, and re-layouts: 24.6 us -> none  [the longest x11 15.6 us: restrict(): field.reshape(lead + (size_x // 2, 2, size_y // 2, 2, size_z // 2, 2))]
    slice x187 -> x9, local copies, waits for them, and re-layouts: 20.5 us -> 1.21 us  [the longest x2 1.15 us: face(): return jnp.concatenate([begin[cut], end[cut]], axis=0)]
    unnamed x25 -> x8, local copies, waits for them, and re-layouts: 18.5 us -> 0.02 us
  transfers between devices with their start and end apart: 233 -> 28, of which waited for: 195 -> 17; matrix products, arithmetic and copies ran while one was open for 8% -> 1% of each run, Pallas kernels for 0% -> 18%
where the time goes in v1:
time: 194 us
  Pallas kernels  63.4 us (33%)
  waiting for transfers between devices  52.2 us (27%)
  starting transfers between devices  47.3 us (24%)
  blocking collectives  27.1 us (14%)
  local copies, waits for them, and re-layouts  2.67 us (1%)
    pallas_call x16, Pallas kernels, call(): pl.pallas_call(body, out_shape=[jax.ShapeDtypeStruct(s, F32) for s in sha...  63.4 us
    ppermute x26, waiting for transfers between devices, moved(): lax.ppermute(value, axis, [(i, (i + step) % count) for i in range(count)])  34.1 us
    ppermute x26, starting transfers between devices, moved(): lax.ppermute(value, axis, [(i, (i + step) % count) for i in range(count)])  31.9 us
    all_to_all x2, blocking collectives, coarse_step(): lax.all_to_all(jnp.broadcast_to(message[None], (16, 2, 128)), 'sx', 0, 0)  27.1 us
    all_to_all x1, waiting for transfers between devices, shards(): lax.all_to_all(jnp.broadcast_to(message[None], (64, 8, 128)), ('sx', 'sy'...  12.2 us
    all_to_all x1, starting transfers between devices, shards(): lax.all_to_all(jnp.broadcast_to(message[None], (64, 8, 128)), ('sx', 'sy'...  9.78 us
    all_to_all x1, waiting for transfers between devices, coarse_step(): lax.all_to_all(jnp.broadcast_to(message[None], (16, 2, 128)), 'sx', 0, 0)  5.95 us
    all_to_all x1, starting transfers between devices, coarse_step(): lax.all_to_all(jnp.broadcast_to(message[None], (16, 2, 128)), 'sx', 0, 0)  5.6 us
  transfers between devices with their start and end apart: 28, of which 17 were waited for; matrix products, arithmetic and copies ran while one was open for 1% of the time, Pallas kernels for 18%

profile of v1, /device:TPU:1, one launch (start us, length us, event | category | flops | bytes accessed | tf_op | source)
XLA Modules:
  0.0 194.0 jit_solution(14156390877821865006)
XLA Ops:
  0.7 1.0 fusion.2
  1.7 3.0 %collective-permute-start = (f32[8,2,16,128]{3,2,1,0:T(8,128)S(1)}, f32[8,2,16,128]{3,2,1,0:T(8,128)S(1)}, u32[]{:S(2)}, u32[]{:S(2)}) collective-permute-start(f32[8,2,16,128]{3,2,1,0:T(8,128)S(1)} %pad_maximum_fusion.3), channel_id=1, source_target_pairs={{0,4},{4,8},{8,12},{12,16},{16,20},{20,24},{24,28},{28,32},{32,36}... | collective-permute-start | bytes 393224 | tf_op jit(solution)/shard_map/ppermute | solution.py:447
  4.8 0.2 collective-permute-start.1
  5.0 0.1 fusion
  5.1 1.6 collective-permute-done.left
  6.7 2.7 %collective-permute-done.1.right = f32[8,2,16,128]{3,2,1,0:T(8,128)S(1)} collective-permute-done((f32[8,2,16,128]{3,2,1,0:T(8,128)S(1)}, f32[8,2,16,128]{3,2,1,0:T(8,128)S(1)}, u32[]{:S(2)}, u32[]{:S(2)}) %collective-permute-start.1) | collective-permute-done | bytes 131104 | tf_op jit(solution)/shard_map/ppermute | solution.py:447
  9.6 1.4 collective-permute-start.2
  11.0 1.5 collective-permute-start.3
  12.6 0.3 opening_body.1.a0
  12.9 1.5 collective-permute-start.10
  14.5 0.3 collective-permute-start.9
  14.8 0.7 collective-permute-start.8
  15.6 1.0 collective-permute-done.10.a3
  16.5 2.8 %collective-permute-done.9.a2 = f32[2,8,8,128]{3,2,1,0:T(8,128)S(1)} collective-permute-done((f32[2,8,8,128]{3,2,1,0:T(8,128)S(1)}, f32[2,8,8,128]{3,2,1,0:T(8,128)S(1)}, u32[]{:S(2)}, u32[]{:S(2)}) %collective-permute-start.9) | collective-permute-done | bytes 65568 | tf_op jit(solution)/shard_map/ppermute | solution.py:447
  19.3 0.5 collective-permute-done.8.a1
  19.8 0.6 join_body.1.own
  20.4 3.7 %collective-permute-start.12 = (f32[2,8,32,128]{3,2,1,0:T(8,128)S(1)}, f32[2,8,32,128]{3,2,1,0:T(8,128)S(1)}, u32[]{:S(2)}, u32[]{:S(2)}) collective-permute-start(f32[2,8,32,128]{3,2,1,0:T(8,128)S(1)} %join_body.1.own), channel_id=1, source_target_pairs={{0,60},{4,0},{8,4},{12,8},{16,12},{20,16},{24,20},{28,24},{32,28},... | collective-permute-start | bytes 786440 | tf_op jit(solution)/shard_map/ppermute | solution.py:447
  24.1 3.7 %fine_source_body.1 = (f32[4,16,16,128]{3,2,1,0:T(8,128)S(1)}, f32[16,16,128]{2,1,0:T(8,128)S(1)}) custom-call(f32[4,16,16,128]{3,2,1,0:T(8,128)S(1)} %bitcast.28, f32[4,16,16,128]{3,2,1,0:T(8,128)S(1)} %bitcast.31, f32[8,2,16,128]{3,2,1,0:T(8,128)S(1)} %collective-permute-done.left, f32[8,2,16,128]{3,2,1,0:T(8,128)S(1)} %collective-permute-done.1.right, ...), custom_call_target="tpu_custom_call" | custom-call | tf_op jit(solution)/shard_map/fine_source_body/pallas_call | solution.py:17
  27.8 2.5 %collective-permute-start.5 = (f32[5,16,128]{2,1,0:T(8,128)S(1)}, f32[5,16,128]{2,1,0:T(8,128)S(1)}, u32[]{:S(2)}, u32[]{:S(2)}) collective-permute-start(f32[5,16,128]{2,1,0:T(8,128)S(1)} %get-tuple-element.80), channel_id=1, source_target_pairs={{0,60},{4,0},{8,4},{12,8},{16,12},{20,16},{24,20},{28,24},{32,28},... | collective-permute-start | bytes 122888 | tf_op jit(solution)/shard_map/ppermute | solution.py:447
  30.3 1.2 collective-permute-done.5.right
  31.5 2.4 %collective-permute-done.4.left = f32[5,16,128]{2,1,0:T(8,128)S(1)} collective-permute-done((f32[5,16,128]{2,1,0:T(8,128)S(1)}, f32[5,16,128]{2,1,0:T(8,128)S(1)}, u32[]{:S(2)}, u32[]{:S(2)}) %collective-permute-start.4) | collective-permute-done | bytes 40992 | tf_op jit(solution)/shard_map/ppermute | solution.py:447
  33.9 0.8 collective-permute-start.6
  34.7 2.1 %collective-permute-start.7 = (f32[26,8,128]{2,1,0:T(8,128)S(1)}, f32[26,8,128]{2,1,0:T(8,128)S(1)}, u32[]{:S(2)}, u32[]{:S(2)}) collective-permute-start(f32[26,8,128]{2,1,0:T(8,128)S(1)} %pad_maximum_fusion.6), channel_id=1, source_target_pairs={{0,3},{1,0},{2,1},{3,2},{4,7},{5,4},{6,5},{7,6},{8,11},{9,8},{10,9... | collective-permute-start | bytes 319496 | tf_op jit(solution)/shard_map/ppermute | solution.py:447
  36.9 7.3 %coarse_down_body.4 = (f32[4,8,32,128]{3,2,1,0:T(8,128)S(1)}, f32[12,32,128]{2,1,0:T(8,128)S(1)}, f32[8,32,128]{2,1,0:T(8,128)S(1)}, f32[2,128]{1,0:T(2,128)S(1)}) custom-call(f32[2,8,32,128]{3,2,1,0:T(8,128)S(1)} %collective-permute-done.11.left, f32[2,8,32,128]{3,2,1,0:T(8,128)S(1)} %join_body.1.own, f32[2,8,32,128]{3,2,1,0:T(8,128)S(1)} %collective-permute-done.12.right), custom_call_target="tpu_custom_call" | custom-call | tf_op jit(solution)/shard_map/coarse_down_body/pallas_call | solution.py:17
  44.2 2.2 %fine_down_body.1 = (f32[26,32,128]{2,1,0:T(8,128)S(1)}, f32[12,32,128]{2,1,0:T(8,128)S(1)}, f32[4,128]{1,0:T(4,128)S(1)}) custom-call(f32[16,16,128]{2,1,0:T(8,128)S(1)} %get-tuple-element.33.own, f32[5,16,128]{2,1,0:T(8,128)S(1)} %collective-permute-done.4.left, f32[5,16,128]{2,1,0:T(8,128)S(1)} %collective-permute-done.5.right, ...), custom_call_target="tpu_custom_call" | custom-call | tf_op jit(solution)/shard_map/fine_down_body/pallas_call | solution.py:17
  46.4 0.7 broadcast_in_dim.17
  47.2 9.8 %all-to-all-start = ((f32[64,8,128]{2,1,0:T(8,128)}), f32[64,8,128]{2,1,0:T(8,128)S(1)}, u32[]{:S(2)}, u32[]{:S(2)}) async-start(f32[64,8,128]{2,1,0:T(8,128)} %broadcast_in_dim.17), calls=%async_computation | async-start | bytes 524288 | tf_op jit(solution)/shard_map/all_to_all | solution.py:514
  57.1 12.2 %all-to-all-done.gathered = f32[64,8,128]{2,1,0:T(8,128)S(1)} async-done(((f32[64,8,128]{2,1,0:T(8,128)}), f32[64,8,128]{2,1,0:T(8,128)S(1)}, u32[]{:S(2)}, u32[]{:S(2)}) %all-to-all-start) | async-done | bytes 262176 | tf_op jit(solution)/shard_map/all_to_all | solution.py:514
  69.2 10.9 %fine_up_body.1 = (f32[4,16,16,128]{3,2,1,0:T(8,128)}, f32[2,8,8,128]{3,2,1,0:T(8,128)S(1)}) custom-call(s32[3]{0:T(128)S(1)} %pad_add_fusion.where, f32[64,8,128]{2,1,0:T(8,128)S(1)} %all-to-all-done.gathered, f32[12,32,128]{2,1,0:T(8,128)S(1)} %get-tuple-element.36.r1, f32[26,32,128]{2,1,0:T(8,128)S(1)} %get-tuple-element.37.r0, ...), custom_call_target="tpu_custom_call" | custom-call | tf_op jit(solution)/shard_map/fine_up_body/pallas_call | solution.py:17
  80.1 2.5 %collective-permute-start.16 = (f32[2,8,8,128]{3,2,1,0:T(8,128)S(1)}, f32[2,8,8,128]{3,2,1,0:T(8,128)S(1)}, u32[]{:S(2)}, u32[]{:S(2)}) collective-permute-start(f32[2,8,8,128]{3,2,1,0:T(8,128)S(1)} %get-tuple-element.40), channel_id=1, source_target_pairs={{0,192},{64,0},{128,64},{192,128},{1,193},{65,1},{129,65},{193,129... | collective-permute-start | bytes 196616 | tf_op jit(solution)/shard_map/ppermute | solution.py:447
  82.6 0.5 collective-permute-start.15
  83.1 0.6 collective-permute-start.14
  83.7 0.2 collective-permute-done.16
  84.0 3.3 %collective-permute-done.15 = f32[2,8,8,128]{3,2,1,0:T(8,128)S(1)} collective-permute-done((f32[2,8,8,128]{3,2,1,0:T(8,128)S(1)}, f32[2,8,8,128]{3,2,1,0:T(8,128)S(1)}, u32[]{:S(2)}, u32[]{:S(2)}) %collective-permute-start.15) | collective-permute-done | bytes 65568 | tf_op jit(solution)/shard_map/ppermute | solution.py:447
  87.3 0.7 collective-permute-done.14
  88.0 1.5 collective-permute-start.19
  89.5 0.8 collective-permute-start.18
  90.3 0.3 collective-permute-start.17
  90.5 3.3 %coarse_up_body.2.ended.e0 = f32[2,8,32,128]{3,2,1,0:T(8,128)S(1)} custom-call(s32[3]{0:T(128)S(1)} %pad_add_fusion.where, f32[16,2,128]{2,1,0:T(2,128)S(1)} %slice.103.gathered, f32[4,8,32,128]{3,2,1,0:T(8,128)S(1)} %get-tuple-element.41.comb, f32[12,32,128]{2,1,0:T(8,128)S(1)} %get-tuple-element.42.r1, f32[8,32,128]{2,1,0:T(8,128)S(1)} %get-tuple-element.43.r2), custom_call_target="tpu_custom_call" | custom-call | tf_op jit(solution)/shard_map/coarse_up_body/pallas_call | solution.py:17
  93.9 1.7 collective-permute-done.18.a2
  95.6 3.2 %collective-permute-done.17.a1 = f32[3,2,8,8,128]{4,3,2,1,0:T(8,128)S(1)} collective-permute-done((f32[3,2,8,8,128]{4,3,2,1,0:T(8,128)S(1)}, f32[3,2,8,8,128]{4,3,2,1,0:T(8,128)S(1)}, u32[]{:S(2)}, u32[]{:S(2)}) %collective-permute-start.17) | collective-permute-done | bytes 196640 | tf_op jit(solution)/shard_map/ppermute | solution.py:447
  98.8 0.6 join_jumps_body.1
  99.4 3.7 %collective-permute-start.21 = (f32[2,8,32,128]{3,2,1,0:T(8,128)S(1)}, f32[2,8,32,128]{3,2,1,0:T(8,128)S(1)}, u32[]{:S(2)}, u32[]{:S(2)}) collective-permute-start(f32[2,8,32,128]{3,2,1,0:T(8,128)S(1)} %get-tuple-element.44.own.c1), channel_id=1, source_target_pairs={{0,60},{4,0},{8,4},{12,8},{16,12},{20,16},{24,20},{28,24},{32,28},... | collective-permute-start | bytes 786440 | tf_op jit(solution)/shard_map/ppermute | solution.py:447
  103.2 0.7 collective-permute-start.20
  103.9 4.0 %collective-permute-done.21.right = f32[2,8,32,128]{3,2,1,0:T(8,128)S(1)} collective-permute-done((f32[2,8,32,128]{3,2,1,0:T(8,128)S(1)}, f32[2,8,32,128]{3,2,1,0:T(8,128)S(1)}, u32[]{:S(2)}, u32[]{:S(2)}) %collective-permute-start.21) | collective-permute-done | bytes 262176 | tf_op jit(solution)/shard_map/ppermute | solution.py:447
  107.9 7.3 %coarse_down_body.5 = (f32[4,8,32,128]{3,2,1,0:T(8,128)S(1)}, f32[12,32,128]{2,1,0:T(8,128)S(1)}, f32[8,32,128]{2,1,0:T(8,128)S(1)}, f32[2,128]{1,0:T(2,128)S(1)}) custom-call(f32[2,8,32,128]{3,2,1,0:T(8,128)S(1)} %collective-permute-done.20.left, f32[2,8,32,128]{3,2,1,0:T(8,128)S(1)} %get-tuple-element.44.own.c1, ...), custom_call_target="tpu_custom_call" | custom-call | tf_op jit(solution)/shard_map/coarse_down_body/pallas_call | solution.py:17
  115.2 14.4 %all_to_all.20.gathered = f32[16,2,128]{2,1,0:T(2,128)S(1)} all-to-all(f32[16,2,128]{2,1,0:T(2,128)S(1)} %broadcast_in_dim.18), channel_id=1, replica_groups=mesh['tm'=4,'sx'=16,'sy'=4] {'sx'}, dimensions={0} | all-to-all | bytes 32768 | tf_op jit(solution)/shard_map/all_to_all | solution.py:561
  129.6 3.3 %coarse_up_next_body.2 = (f32[2,8,32,128]{3,2,1,0:T(8,128)S(1)}, f32[2,8,32,128]{3,2,1,0:T(8,128)S(1)}) custom-call(s32[3]{0:T(128)S(1)} %pad_add_fusion.where, f32[16,2,128]{2,1,0:T(2,128)S(1)} %all_to_all.20.gathered, f32[4,8,32,128]{3,2,1,0:T(8,128)S(1)} %get-tuple-element.46.comb, f32[12,32,128]{2,1,0:T(8,128)S(1)} %get-tuple-element.47.r1, ...), custom_call_target="tpu_custom_call" | custom-call | tf_op jit(solution)/shard_map/coarse_up_next_body/pallas_call | solution.py:17
  133.0 0.4 collective-permute-start.23
  133.4 1.4 collective-permute-start.22
  134.7 4.3 %collective-permute-done.23.right = f32[2,8,32,128]{3,2,1,0:T(8,128)S(1)} collective-permute-done((f32[2,8,32,128]{3,2,1,0:T(8,128)S(1)}, f32[2,8,32,128]{3,2,1,0:T(8,128)S(1)}, u32[]{:S(2)}, u32[]{:S(2)}) %collective-permute-start.23) | collective-permute-done | bytes 262176 | tf_op jit(solution)/shard_map/ppermute | solution.py:447
  139.1 7.3 %coarse_down_body.6 = (f32[4,8,32,128]{3,2,1,0:T(8,128)S(1)}, f32[12,32,128]{2,1,0:T(8,128)S(1)}, f32[8,32,128]{2,1,0:T(8,128)S(1)}, f32[2,128]{1,0:T(2,128)S(1)}) custom-call(f32[2,8,32,128]{3,2,1,0:T(8,128)S(1)} %collective-permute-done.22.left, f32[2,8,32,128]{3,2,1,0:T(8,128)S(1)} %get-tuple-element.50.own.c2, ...), custom_call_target="tpu_custom_call" | custom-call | tf_op jit(solution)/shard_map/coarse_down_body/pallas_call | solution.py:17
  146.3 12.7 %all_to_all.21.gathered = f32[16,2,128]{2,1,0:T(2,128)S(1)} all-to-all(f32[16,2,128]{2,1,0:T(2,128)S(1)} %broadcast_in_dim.19), channel_id=1, replica_groups=mesh['tm'=4,'sx'=16,'sy'=4] {'sx'}, dimensions={0} | all-to-all | bytes 32768 | tf_op jit(solution)/shard_map/all_to_all | solution.py:561
  159.1 3.3 %coarse_up_next_body.3 = (f32[2,8,32,128]{3,2,1,0:T(8,128)S(1)}, f32[2,8,32,128]{3,2,1,0:T(8,128)S(1)}) custom-call(s32[3]{0:T(128)S(1)} %pad_add_fusion.where, f32[16,2,128]{2,1,0:T(2,128)S(1)} %all_to_all.21.gathered, f32[4,8,32,128]{3,2,1,0:T(8,128)S(1)} %get-tuple-element.52.comb, f32[12,32,128]{2,1,0:T(8,128)S(1)} %get-tuple-element.53.r1, ...), custom_call_target="tpu_custom_call" | custom-call | tf_op jit(solution)/shard_map/coarse_up_next_body/pallas_call | solution.py:17
  162.4 0.4 collective-permute-start.25
  162.8 1.4 collective-permute-start.24
  164.2 4.3 %collective-permute-done.25.right = f32[2,8,32,128]{3,2,1,0:T(8,128)S(1)} collective-permute-done((f32[2,8,32,128]{3,2,1,0:T(8,128)S(1)}, f32[2,8,32,128]{3,2,1,0:T(8,128)S(1)}, u32[]{:S(2)}, u32[]{:S(2)}) %collective-permute-start.25) | collective-permute-done | bytes 262176 | tf_op jit(solution)/shard_map/ppermute | solution.py:447
  168.5 7.3 %coarse_down_body.7 = (f32[4,8,32,128]{3,2,1,0:T(8,128)S(1)}, f32[12,32,128]{2,1,0:T(8,128)S(1)}, f32[8,32,128]{2,1,0:T(8,128)S(1)}, f32[2,128]{1,0:T(2,128)S(1)}) custom-call(f32[2,8,32,128]{3,2,1,0:T(8,128)S(1)} %collective-permute-done.24.left, f32[2,8,32,128]{3,2,1,0:T(8,128)S(1)} %get-tuple-element.56.c3.own, ...), custom_call_target="tpu_custom_call" | custom-call | tf_op jit(solution)/shard_map/coarse_down_body/pallas_call | solution.py:17
  175.8 0.6 broadcast_in_dim.42
  176.4 5.6 %all-to-all-start.3 = ((f32[16,2,128]{2,1,0:T(2,128)}), f32[16,2,128]{2,1,0:T(2,128)S(1)}, u32[]{:S(2)}, u32[]{:S(2)}) async-start(f32[16,2,128]{2,1,0:T(2,128)} %broadcast_in_dim.42), calls=%async_computation.3 | async-start | bytes 32768 | tf_op jit(solution)/shard_map/all_to_all | solution.py:561
  182.0 1.4 new_start_body.1
  183.4 5.9 %all-to-all-done.3.gathered = f32[16,2,128]{2,1,0:T(2,128)S(1)} async-done(((f32[16,2,128]{2,1,0:T(2,128)}), f32[16,2,128]{2,1,0:T(2,128)S(1)}, u32[]{:S(2)}, u32[]{:S(2)}) %all-to-all-start.3) | async-done | bytes 16416 | tf_op jit(solution)/shard_map/all_to_all | solution.py:561
  189.3 3.3 %coarse_up_body.3.e3 = f32[2,8,32,128]{3,2,1,0:T(8,128)S(1)} custom-call(s32[3]{0:T(128)S(1)} %pad_add_fusion.where, f32[16,2,128]{2,1,0:T(2,128)S(1)} %all-to-all-done.3.gathered, f32[4,8,32,128]{3,2,1,0:T(8,128)S(1)} %get-tuple-element.60.comb, f32[12,32,128]{2,1,0:T(8,128)S(1)} %get-tuple-element.61.r1, f32[8,32,128]{2,1,0:T(8,128)S(1)} %get-tuple-element.62.r2), custom_call_target="tpu_custom_call" | custom-call | tf_op jit(solution)/shard_map/coarse_up_body/pallas_call | solution.py:17
  192.6 1.3 coarse_end_body.1
  (46 shorter events, 0.7 us)
Async XLA Ops:
  0.6 4.4 %copy-start.1 = (f32[1,4,16,16,128]{4,3,2,1,0:T(8,128)S(1)}, f32[1,4,16,16,128]{4,3,2,1,0:T(8,128)}, u32[]{:S(2)}) copy-start(f32[1,4,16,16,128]{4,3,2,1,0:T(8,128)} %param.5) | copy-start | bytes 1572868
  0.6 4.4 %copy-start.2 = (f32[1,4,16,16,128]{4,3,2,1,0:T(8,128)S(1)}, f32[1,4,16,16,128]{4,3,2,1,0:T(8,128)}, u32[]{:S(2)}) copy-start(f32[1,4,16,16,128]{4,3,2,1,0:T(8,128)} %param.6) | copy-start | bytes 1572868
  1.7 5.0 %collective-permute-start = (f32[8,2,16,128]{3,2,1,0:T(8,128)S(1)}, f32[8,2,16,128]{3,2,1,0:T(8,128)S(1)}, u32[]{:S(2)}, u32[]{:S(2)}) collective-permute-start(f32[8,2,16,128]{3,2,1,0:T(8,128)S(1)} %pad_maximum_fusion.3), channel_id=1, source_target_pairs={{0,4},{4,8},{8,12},{12,16},{16,20},{20,24},{24,28},{28,32},{32,36}... | collective-permute-start | bytes 393224 | tf_op jit(solution)/shard_map/ppermute | solution.py:447
  4.8 4.7 %collective-permute-start.1 = (f32[8,2,16,128]{3,2,1,0:T(8,128)S(1)}, f32[8,2,16,128]{3,2,1,0:T(8,128)S(1)}, u32[]{:S(2)}, u32[]{:S(2)}) collective-permute-start(f32[8,2,16,128]{3,2,1,0:T(8,128)S(1)} %pad_maximum_fusion.4), channel_id=1, source_target_pairs={{0,60},{4,0},{8,4},{12,8},{16,12},{20,16},{24,20},{28,24},{32,28},... | collective-permute-start | bytes 393224 | tf_op jit(solution)/shard_map/ppermute | solution.py:447
  5.1 7.4 %copy-start = (f32[4,16,16,128]{3,2,1,0:T(8,128)S(1)}, f32[4,16,16,128]{3,2,1,0:T(8,128)}, u32[]{:S(2)}) copy-start(f32[4,16,16,128]{3,2,1,0:T(8,128)} %initial.3) | copy-start | bytes 1572868
  9.6 14.5 %collective-permute-start.2 = (f32[8,20,2,128]{3,2,1,0:T(2,128)S(1)}, f32[8,20,2,128]{3,2,1,0:T(2,128)S(1)}, u32[]{:S(2)}, u32[]{:S(2)}) collective-permute-start(f32[8,20,2,128]{3,2,1,0:T(2,128)S(1)} %pad_maximum_fusion.1), channel_id=1, source_target_pairs={{0,1},{1,2},{2,3},{3,0},{4,5},{5,6},{6,7},{7,4},{8,9},{9,10},{10,1... | collective-permute-start | bytes 491528 | tf_op jit(solution)/shard_map/ppermute | solution.py:447
  11.0 13.1 %collective-permute-start.3 = (f32[8,20,2,128]{3,2,1,0:T(2,128)S(1)}, f32[8,20,2,128]{3,2,1,0:T(2,128)S(1)}, u32[]{:S(2)}, u32[]{:S(2)}) collective-permute-start(f32[8,20,2,128]{3,2,1,0:T(2,128)S(1)} %pad_maximum_fusion.2), channel_id=1, source_target_pairs={{0,3},{1,0},{2,1},{3,2},{4,7},{5,4},{6,5},{7,6},{8,11},{9,8},{10,9... | collective-permute-start | bytes 491528 | tf_op jit(solution)/shard_map/ppermute | solution.py:447
  12.9 3.6 %collective-permute-start.10 = (f32[2,8,8,128]{3,2,1,0:T(8,128)S(1)}, f32[2,8,8,128]{3,2,1,0:T(8,128)S(1)}, u32[]{:S(2)}, u32[]{:S(2)}) collective-permute-start(f32[2,8,8,128]{3,2,1,0:T(8,128)S(1)} %opening_body.1.a0), channel_id=1, source_target_pairs={{0,3},{1,0},{2,1},{3,2},{4,7},{5,4},{6,5},{7,6},{8,11},{9,8},{10,9... | collective-permute-start | bytes 196616 | tf_op jit(solution)/shard_map/ppermute | solution.py:447
  14.5 4.8 %collective-permute-start.9 = (f32[2,8,8,128]{3,2,1,0:T(8,128)S(1)}, f32[2,8,8,128]{3,2,1,0:T(8,128)S(1)}, u32[]{:S(2)}, u32[]{:S(2)}) collective-permute-start(f32[2,8,8,128]{3,2,1,0:T(8,128)S(1)} %opening_body.1.a0), channel_id=1, source_target_pairs={{0,2},{1,3},{2,0},{3,1},{4,6},{5,7},{6,4},{7,5},{8,10},{9,11},{10,... | collective-permute-start | bytes 196616 | tf_op jit(solution)/shard_map/ppermute | solution.py:447
  14.8 5.0 %collective-permute-start.8 = (f32[2,8,8,128]{3,2,1,0:T(8,128)S(1)}, f32[2,8,8,128]{3,2,1,0:T(8,128)S(1)}, u32[]{:S(2)}, u32[]{:S(2)}) collective-permute-start(f32[2,8,8,128]{3,2,1,0:T(8,128)S(1)} %opening_body.1.a0), channel_id=1, source_target_pairs={{0,1},{1,2},{2,3},{3,0},{4,5},{5,6},{6,7},{7,4},{8,9},{9,10},{10,1... | collective-permute-start | bytes 196616 | tf_op jit(solution)/shard_map/ppermute | solution.py:447
  20.4 16.5 %collective-permute-start.12 = (f32[2,8,32,128]{3,2,1,0:T(8,128)S(1)}, f32[2,8,32,128]{3,2,1,0:T(8,128)S(1)}, u32[]{:S(2)}, u32[]{:S(2)}) collective-permute-start(f32[2,8,32,128]{3,2,1,0:T(8,128)S(1)} %join_body.1.own), channel_id=1, source_target_pairs={{0,60},{4,0},{8,4},{12,8},{16,12},{20,16},{24,20},{28,24},{32,28},... | collective-permute-start | bytes 786440 | tf_op jit(solution)/shard_map/ppermute | solution.py:447
  24.1 12.8 %collective-permute-start.11 = (f32[2,8,32,128]{3,2,1,0:T(8,128)S(1)}, f32[2,8,32,128]{3,2,1,0:T(8,128)S(1)}, u32[]{:S(2)}, u32[]{:S(2)}) collective-permute-start(f32[2,8,32,128]{3,2,1,0:T(8,128)S(1)} %join_body.1.own), channel_id=1, source_target_pairs={{0,4},{4,8},{8,12},{12,16},{16,20},{20,24},{24,28},{28,32},{32,36}... | collective-permute-start | bytes 786440 | tf_op jit(solution)/shard_map/ppermute | solution.py:447
  27.8 3.7 %collective-permute-start.5 = (f32[5,16,128]{2,1,0:T(8,128)S(1)}, f32[5,16,128]{2,1,0:T(8,128)S(1)}, u32[]{:S(2)}, u32[]{:S(2)}) collective-permute-start(f32[5,16,128]{2,1,0:T(8,128)S(1)} %get-tuple-element.80), channel_id=1, source_target_pairs={{0,60},{4,0},{8,4},{12,8},{16,12},{20,16},{24,20},{28,24},{32,28},... | collective-permute-start | bytes 122888 | tf_op jit(solution)/shard_map/ppermute | solution.py:447
  30.3 3.7 %collective-permute-start.4 = (f32[5,16,128]{2,1,0:T(8,128)S(1)}, f32[5,16,128]{2,1,0:T(8,128)S(1)}, u32[]{:S(2)}, u32[]{:S(2)}) collective-permute-start(f32[5,16,128]{2,1,0:T(8,128)S(1)} %get-tuple-element.81), channel_id=1, source_target_pairs={{0,4},{4,8},{8,12},{12,16},{16,20},{20,24},{24,28},{28,32},{32,36}... | collective-permute-start | bytes 122888 | tf_op jit(solution)/shard_map/ppermute | solution.py:447
  33.9 10.2 %collective-permute-start.6 = (f32[26,8,128]{2,1,0:T(8,128)S(1)}, f32[26,8,128]{2,1,0:T(8,128)S(1)}, u32[]{:S(2)}, u32[]{:S(2)}) collective-permute-start(f32[26,8,128]{2,1,0:T(8,128)S(1)} %pad_maximum_fusion.5), channel_id=1, source_target_pairs={{0,1},{1,2},{2,3},{3,0},{4,5},{5,6},{6,7},{7,4},{8,9},{9,10},{10,1... | collective-permute-start | bytes 319496 | tf_op jit(solution)/shard_map/ppermute | solution.py:447
  34.7 9.4 %collective-permute-start.7 = (f32[26,8,128]{2,1,0:T(8,128)S(1)}, f32[26,8,128]{2,1,0:T(8,128)S(1)}, u32[]{:S(2)}, u32[]{:S(2)}) collective-permute-start(f32[26,8,128]{2,1,0:T(8,128)S(1)} %pad_maximum_fusion.6), channel_id=1, source_target_pairs={{0,3},{1,0},{2,1},{3,2},{4,7},{5,4},{6,5},{7,6},{8,11},{9,8},{10,9... | collective-permute-start | bytes 319496 | tf_op jit(solution)/shard_map/ppermute | solution.py:447
  47.2 9.8 %copy-start.3 = (f32[1,4,8,8,64]{4,3,2,1,0:T(8,128)S(1)}, f32[1,4,8,8,64]{4,3,2,1,0:T(8,128)}, u32[]{:S(2)}) copy-start(f32[1,4,8,8,64]{4,3,2,1,0:T(8,128)} %param.7) | copy-start | bytes 196612
  47.2 22.1 %all-to-all-start = ((f32[64,8,128]{2,1,0:T(8,128)}), f32[64,8,128]{2,1,0:T(8,128)S(1)}, u32[]{:S(2)}, u32[]{:S(2)}) async-start(f32[64,8,128]{2,1,0:T(8,128)} %broadcast_in_dim.17), calls=%async_computation | async-start | bytes 524288 | tf_op jit(solution)/shard_map/all_to_all | solution.py:514
  80.1 3.8 %collective-permute-start.16 = (f32[2,8,8,128]{3,2,1,0:T(8,128)S(1)}, f32[2,8,8,128]{3,2,1,0:T(8,128)S(1)}, u32[]{:S(2)}, u32[]{:S(2)}) collective-permute-start(f32[2,8,8,128]{3,2,1,0:T(8,128)S(1)} %get-tuple-element.40), channel_id=1, source_target_pairs={{0,192},{64,0},{128,64},{192,128},{1,193},{65,1},{129,65},{193,129... | collective-permute-start | bytes 196616 | tf_op jit(solution)/shard_map/ppermute | solution.py:447
  82.6 4.7 %collective-permute-start.15 = (f32[2,8,8,128]{3,2,1,0:T(8,128)S(1)}, f32[2,8,8,128]{3,2,1,0:T(8,128)S(1)}, u32[]{:S(2)}, u32[]{:S(2)}) collective-permute-start(f32[2,8,8,128]{3,2,1,0:T(8,128)S(1)} %get-tuple-element.40), channel_id=1, source_target_pairs={{0,128},{64,192},{128,0},{192,64},{1,129},{65,193},{129,1},{193,65... | collective-permute-start | bytes 196616 | tf_op jit(solution)/shard_map/ppermute | solution.py:447
  83.1 4.8 %collective-permute-start.14 = (f32[2,8,8,128]{3,2,1,0:T(8,128)S(1)}, f32[2,8,8,128]{3,2,1,0:T(8,128)S(1)}, u32[]{:S(2)}, u32[]{:S(2)}) collective-permute-start(f32[2,8,8,128]{3,2,1,0:T(8,128)S(1)} %get-tuple-element.40), channel_id=1, source_target_pairs={{0,64},{64,128},{128,192},{192,0},{1,65},{65,129},{129,193},{193,1... | collective-permute-start | bytes 196616 | tf_op jit(solution)/shard_map/ppermute | solution.py:447
  88.0 5.9 %collective-permute-start.19 = (f32[3,2,8,8,128]{4,3,2,1,0:T(8,128)S(1)}, f32[3,2,8,8,128]{4,3,2,1,0:T(8,128)S(1)}, u32[]{:S(2)}, u32[]{:S(2)}) collective-permute-start(f32[3,2,8,8,128]{4,3,2,1,0:T(8,128)S(1)} %pad_maximum_fusion.a0), channel_id=1, source_target_pairs={{0,3},{1,0},{2,1},{3,2},{4,7},{5,4},{6,5},{7,6},{8,11},{9,8},{10,9... | collective-permute-start | bytes 589832 | tf_op jit(solution)/shard_map/ppermute | solution.py:447
  89.5 6.1 %collective-permute-start.18 = (f32[3,2,8,8,128]{4,3,2,1,0:T(8,128)S(1)}, f32[3,2,8,8,128]{4,3,2,1,0:T(8,128)S(1)}, u32[]{:S(2)}, u32[]{:S(2)}) collective-permute-start(f32[3,2,8,8,128]{4,3,2,1,0:T(8,128)S(1)} %pad_maximum_fusion.a0), channel_id=1, source_target_pairs={{0,2},{1,3},{2,0},{3,1},{4,6},{5,7},{6,4},{7,5},{8,10},{9,11},{10,... | collective-permute-start | bytes 589832 | tf_op jit(solution)/shard_map/ppermute | solution.py:447
  90.3 8.5 %collective-permute-start.17 = (f32[3,2,8,8,128]{4,3,2,1,0:T(8,128)S(1)}, f32[3,2,8,8,128]{4,3,2,1,0:T(8,128)S(1)}, u32[]{:S(2)}, u32[]{:S(2)}) collective-permute-start(f32[3,2,8,8,128]{4,3,2,1,0:T(8,128)S(1)} %pad_maximum_fusion.a0), channel_id=1, source_target_pairs={{0,1},{1,2},{2,3},{3,0},{4,5},{5,6},{6,7},{7,4},{8,9},{9,10},{10,1... | collective-permute-start | bytes 589832 | tf_op jit(solution)/shard_map/ppermute | solution.py:447
  99.4 8.5 %collective-permute-start.21 = (f32[2,8,32,128]{3,2,1,0:T(8,128)S(1)}, f32[2,8,32,128]{3,2,1,0:T(8,128)S(1)}, u32[]{:S(2)}, u32[]{:S(2)}) collective-permute-start(f32[2,8,32,128]{3,2,1,0:T(8,128)S(1)} %get-tuple-element.44.own.c1), channel_id=1, source_target_pairs={{0,60},{4,0},{8,4},{12,8},{16,12},{20,16},{24,20},{28,24},{32,28},... | collective-permute-start | bytes 786440 | tf_op jit(solution)/shard_map/ppermute | solution.py:447
  103.2 4.8 %collective-permute-start.20 = (f32[2,8,32,128]{3,2,1,0:T(8,128)S(1)}, f32[2,8,32,128]{3,2,1,0:T(8,128)S(1)}, u32[]{:S(2)}, u32[]{:S(2)}) collective-permute-start(f32[2,8,32,128]{3,2,1,0:T(8,128)S(1)} %get-tuple-element.44.own.c1), channel_id=1, source_target_pairs={{0,4},{4,8},{8,12},{12,16},{16,20},{20,24},{24,28},{28,32},{32,36}... | collective-permute-start | bytes 786440 | tf_op jit(solution)/shard_map/ppermute | solution.py:447
  133.0 6.1 %collective-permute-start.23 = (f32[2,8,32,128]{3,2,1,0:T(8,128)S(1)}, f32[2,8,32,128]{3,2,1,0:T(8,128)S(1)}, u32[]{:S(2)}, u32[]{:S(2)}) collective-permute-start(f32[2,8,32,128]{3,2,1,0:T(8,128)S(1)} %get-tuple-element.50.own.c2), channel_id=1, source_target_pairs={{0,60},{4,0},{8,4},{12,8},{16,12},{20,16},{24,20},{28,24},{32,28},... | collective-permute-start | bytes 786440 | tf_op jit(solution)/shard_map/ppermute | solution.py:447
  133.4 5.7 %collective-permute-start.22 = (f32[2,8,32,128]{3,2,1,0:T(8,128)S(1)}, f32[2,8,32,128]{3,2,1,0:T(8,128)S(1)}, u32[]{:S(2)}, u32[]{:S(2)}) collective-permute-start(f32[2,8,32,128]{3,2,1,0:T(8,128)S(1)} %get-tuple-element.50.own.c2), channel_id=1, source_target_pairs={{0,4},{4,8},{8,12},{12,16},{16,20},{20,24},{24,28},{28,32},{32,36}... | collective-permute-start | bytes 786440 | tf_op jit(solution)/shard_map/ppermute | solution.py:447
  134.7 47.3 %collective-permute-start.13 = (f32[4,16,16,128]{3,2,1,0:T(8,128)}, f32[4,16,16,128]{3,2,1,0:T(8,128)S(1)}, u32[]{:S(2)}, u32[]{:S(2)}) collective-permute-start(f32[4,16,16,128]{3,2,1,0:T(8,128)} %get-tuple-element.39), channel_id=1, source_target_pairs={{0,64},{64,128},{128,192},{192,0},{1,65},{65,129},{129,193},{193,1... | collective-permute-start | bytes 1572872 | tf_op jit(solution)/shard_map/ppermute | solution.py:447
  162.4 6.1 %collective-permute-start.25 = (f32[2,8,32,128]{3,2,1,0:T(8,128)S(1)}, f32[2,8,32,128]{3,2,1,0:T(8,128)S(1)}, u32[]{:S(2)}, u32[]{:S(2)}) collective-permute-start(f32[2,8,32,128]{3,2,1,0:T(8,128)S(1)} %get-tuple-element.56.c3.own), channel_id=1, source_target_pairs={{0,60},{4,0},{8,4},{12,8},{16,12},{20,16},{24,20},{28,24},{32,28},... | collective-permute-start | bytes 786440 | tf_op jit(solution)/shard_map/ppermute | solution.py:447
  162.8 5.7 %collective-permute-start.24 = (f32[2,8,32,128]{3,2,1,0:T(8,128)S(1)}, f32[2,8,32,128]{3,2,1,0:T(8,128)S(1)}, u32[]{:S(2)}, u32[]{:S(2)}) collective-permute-start(f32[2,8,32,128]{3,2,1,0:T(8,128)S(1)} %get-tuple-element.56.c3.own), channel_id=1, source_target_pairs={{0,4},{4,8},{8,12},{12,16},{16,20},{20,24},{24,28},{28,32},{32,36}... | collective-permute-start | bytes 786440 | tf_op jit(solution)/shard_map/ppermute | solution.py:447
  176.4 12.9 %all-to-all-start.3 = ((f32[16,2,128]{2,1,0:T(2,128)}), f32[16,2,128]{2,1,0:T(2,128)S(1)}, u32[]{:S(2)}, u32[]{:S(2)}) async-start(f32[16,2,128]{2,1,0:T(2,128)} %broadcast_in_dim.42), calls=%async_computation.3 | async-start | bytes 32768 | tf_op jit(solution)/shard_map/all_to_all | solution.py:561

commit v2 on v1

v2 whole, which is shorter than its diff:
```python
import jax
import jax.numpy as jnp
from jax import lax
from jax.experimental import pallas as pl
from jax.experimental.pallas import tpu as pltpu
from jax.sharding import PartitionSpec as P

F32 = jnp.float32
HIGH = lax.Precision.HIGHEST


def call(body, outs, args, scratch=(), smem=0, limit=24):
    vmem = pl.BlockSpec(memory_space=pltpu.VMEM)
    scalar = pl.BlockSpec(memory_space=pltpu.SMEM)
    single = not isinstance(outs, list)
    shapes = [outs] if single else outs
    got = pl.pallas_call(
        body,
        out_shape=[jax.ShapeDtypeStruct(s, F32) for s in shapes],
        in_specs=[scalar] * smem + [vmem] * (len(args) - smem),
        out_specs=[vmem] * len(shapes),
        scratch_shapes=[pltpu.VMEM(s, F32) for s in scratch],
        compiler_params=pltpu.CompilerParams(vmem_limit_bytes=limit * 2**20),
        name=body.__name__,
    )(*args)
    return got[0] if single else got


def shifted(value, amount, axis):
    return pltpu.roll(value, amount % value.shape[axis], axis)


def nxt(value, step, axis):
    return shifted(value, -step, axis)


def prv(value, step, axis):
    return shifted(value, step, axis)


def index_along(shape, axis):
    return lax.broadcasted_iota(jnp.int32, shape, axis)


def pair_sum(value, step, axis):
    upper = (index_along(value.shape, axis) // step) % 2 == 1
    return value + jnp.where(upper, prv(value, step, axis), nxt(value, step, axis))


def ring_sum(value, step_y, step_z):
    return (
        nxt(value, step_y, 0)
        + prv(value, step_y, 0)
        + nxt(value, step_z, 1)
        + prv(value, step_z, 1)
    )


def restricted_defect(before, first, second, after, step_y, step_z):
    both = first + second
    total = both * (1.0 / 3.0) + (before + both + after + ring_sum(both, step_y, step_z)) * (1.0 / 9.0)
    return pair_sum(pair_sum(total, step_y, 0), step_z, 1) * 0.125


def smoothed(before, here, after, source, spacing_sq, step_y, step_z):
    around = before + after + ring_sum(here, step_y, step_z)
    return here * (1.0 / 3.0) + (around - spacing_sq * source) * (1.0 / 9.0)


def deep_pressure(r3, step_y, step_z):
    r4 = [
        restricted_defect(r3[2 * w], r3[2 * w + 1], r3[2 * w + 2], r3[2 * w + 3], step_y, step_z)
        for w in range(7)
    ]
    low_y, low_z = 2 * step_y, 2 * step_z
    p4 = [r * (-256.0 / 9.0) for r in r4]
    for sweep in range(2):
        inner = range(1 + sweep, 6 - sweep)
        fresh = {w: smoothed(p4[w - 1], p4[w], p4[w + 1], r4[w], 256.0, low_y, low_z) for w in inner}
        p4 = [fresh.get(w) for w in range(7)]
    e3 = {q: r3[q] * (-64.0 / 9.0) + p4[(q - 7) // 2 + 3] for q in range(5, 11)}
    return [
        smoothed(e3[q - 1], e3[q], e3[q + 1], r3[q], 64.0, step_y, step_z) for q in range(6, 10)
    ]


def advected(ref, base, i, comp):
    here = ref[base + comp, i]
    grad_x = ref[base + comp, i + 1] - ref[base + comp, i - 1]
    grad_y = nxt(here, 1, 0) - prv(here, 1, 0)
    grad_z = nxt(here, 1, 1) - prv(here, 1, 1)
    return ref[base, i] * grad_x + ref[base + 1, i] * grad_y + ref[base + 2, i] * grad_z


def z_pick(high):
    k = index_along((128, 128), 0)
    j = index_along((128, 128), 1)
    return jnp.where(k // 2 == j - 64 * high, 1.0, 0.0).astype(F32)


def z_spread(high):
    k = index_along((128, 128), 0)
    j = index_along((128, 128), 1)
    return jnp.where(k == j // 2 + 64 * high, 1.0, 0.0).astype(F32)


def dot(a, b):
    return lax.dot_general(a, b, (((1,), (0,)), ((), ())), precision=HIGH, preferred_element_type=F32)


def restricted_packed(fine, rows, half):
    for comp in range(4):
        for big in range(8):
            rows[comp, big] = fine[comp, 2 * big] + fine[comp, 2 * big + 1]
    for comp in range(4):
        for big in range(8):
            half[comp, big] = rows[comp, big, pl.ds(0, 8, 2), :] + rows[comp, big, pl.ds(1, 8, 2), :]
    low, high = z_pick(0), z_pick(1)
    return [
        0.125
        * (
            dot(half[2 * h].reshape(64, 128), low)
            + dot(half[2 * h + 1].reshape(64, 128), high)
        )
        for h in range(2)
    ]


def opening_body(initial, out, rows, half):
    packed = restricted_packed(initial, rows, half)
    for h in range(2):
        out[h] = packed[h].reshape(8, 8, 128)


def level2_pressure(r2, e2, step_z):
    r3 = [
        restricted_defect(r2[2 * q + 1], r2[2 * q + 2], r2[2 * q + 3], r2[2 * q + 4], 1, step_z)
        for q in range(16)
    ]
    p3 = deep_pressure(r3, 2, 2 * step_z)
    for i in range(8):
        e2[i] = r2[14 + i] * (-16.0 / 9.0) + p3[i // 2]
    return [
        smoothed(e2[i], e2[i + 1], e2[i + 2], r2[15 + i], 16.0, 1, step_z) for i in range(6)
    ]


def bit_lane(value, lane, step, bit):
    same = (lane // step) % 2 == bit
    return jnp.where(same, value, nxt(value, step, 1) if bit else prv(value, step, 1))


def fine_source_body(begin, end, left, right, low, high, comb_out, r0_out, state, comb):
    for f in range(8):
        own = begin if f < 4 else end
        c = f % 4
        state[f, 0:2, 4:20] = left[f]
        state[f, 2:18, 4:20] = own[c]
        state[f, 18:20, 4:20] = right[f]
        state[f, :, 2:4] = low[20 * f : 20 * f + 20]
        state[f, :, 20:22] = high[20 * f : 20 * f + 20]
    for i in range(1, 19):
        for c in range(4):
            total = state[c, i] - 0.125 * (advected(state, 0, i, c) + advected(state, 4, i, c))
            if c == 2:
                total = total + 0.25 * (state[3, i] + state[7, i])
            comb[c, i - 1] = total
    for x in range(16):
        v = comb[1, x + 1]
        w = comb[2, x + 1]
        div = comb[0, x + 2] - comb[0, x] + nxt(v, 1, 0) - prv(v, 1, 0) + nxt(w, 1, 1) - prv(w, 1, 1)
        r0_out[x] = (0.5 * div)[4:20]
        for c in range(4):
            comb_out[c, x] = comb[c, x + 1, 4:20, :]


def fine_down_body(own, below, across, above, coarse, to_left, to_right, r0_out, r0, r1, r2):
    r0[:, 0:16] = below[...]
    r0[:, 16:32] = own[...]
    r0[:, 32:48] = above[...]
    r0[:, 48:64] = across[...]
    r0_out[...] = r0[:, 8:40]
    zero = jnp.zeros((64, 128), F32)

    def at0(x):
        return r0[x] if 0 <= x < 16 else zero

    def at1(x):
        return r1[x + 1] if -1 <= x < 9 else zero

    for x in range(-1, 9):
        r1[x + 1] = restricted_defect(at0(2 * x - 1), at0(2 * x), at0(2 * x + 1), at0(2 * x + 2), 1, 1)
    for x in range(-1, 5):
        r2[x + 1] = restricted_defect(at1(2 * x - 1), at1(2 * x), at1(2 * x + 1), at1(2 * x + 2), 2, 2)
    lane = index_along((16, 128), 1)
    part = [r2[i, pl.ds(0, 16, 4), :] for i in range(6)]
    odd = lane % 2 == 1
    first = jnp.where(
        lane % 4 < 2, jnp.where(odd, part[1], part[0]), jnp.where(odd, part[3], part[2])
    )
    second = jnp.where(odd, part[5], part[4])
    for ref, face in ((to_left, 0), (to_right, 11)):
        ref[0:16] = first
        ref[16:32] = second
        ref[32:48] = coarse[...]
        for i in range(5):
            ref[48 + 32 * i : 80 + 32 * i] = r0[face + i, 8:40]


def fine_up_body(
    tri_l, tri, tri_r, left, own, right, comb, old, fine, rj, r0, r1, r2, e2, p2, e1, p1, e0, p0, rows, half
):
    for i in range(5):
        r0[i] = left[48 + 32 * i : 80 + 32 * i]
        r0[21 + i] = right[48 + 32 * i : 80 + 32 * i]
    r0[5:21] = own[...]
    lane = index_along((16, 128), 1)
    parts = []
    for ref in (tri_l, tri, tri_r):
        for j in range(3):
            first, second = ref[j, 0:16], ref[j, 16:32]
            even, odd = bit_lane(first, lane, 2, 0), bit_lane(first, lane, 2, 1)
            parts.append(
                [
                    bit_lane(even, lane, 1, 0),
                    bit_lane(even, lane, 1, 1),
                    bit_lane(odd, lane, 1, 0),
                    bit_lane(odd, lane, 1, 1),
                    bit_lane(second, lane, 1, 0),
                    bit_lane(second, lane, 1, 1),
                ]
            )
    for j in range(9):
        for n in range(4):
            value = parts[j][n + 1]
            if n == 0 and j > 0:
                value = value + parts[j - 1][5]
            if n == 3 and j < 8:
                value = value + parts[j + 1][0]
            r2[4 * j + n] = value
    for i, value in enumerate(level2_pressure(r2, e2, 4)):
        for y2 in range(8):
            p2[i, 4 * y2 : 4 * y2 + 4, :] = jnp.broadcast_to(value[y2 + 2 : y2 + 3], (4, 128))
    for k in range(12):
        a = 2 * k + 1
        r1[k] = restricted_defect(r0[a - 1], r0[a], r0[a + 1], r0[a + 2], 1, 1)
        e1[k] = r1[k] * (-4.0 / 9.0) + p2[k // 2]
    for k in range(10):
        p1[k] = smoothed(e1[k], e1[k + 1], e1[k + 2], r1[k + 1], 4.0, 2, 2)
    for j in range(20):
        e0[j] = r0[j + 3] * (-1.0 / 9.0) + p1[j // 2]
    for j in range(18):
        p0[j] = smoothed(e0[j], e0[j + 1], e0[j + 2], r0[j + 4], 1.0, 1, 1)
    for x in range(16):
        here = p0[x + 1]
        fine[0, x] = comb[0, x] - 0.5 * (p0[x + 2, 8:24] - p0[x, 8:24])
        fine[1, x] = comb[1, x] - 0.5 * (nxt(here, 1, 0) - prv(here, 1, 0))[8:24]
        mid = here[8:24]
        fine[2, x] = comb[2, x] - 0.5 * (nxt(mid, 1, 1) - prv(mid, 1, 1))
        fine[3, x] = comb[3, x]
    packed = restricted_packed(fine, rows, half)
    for h in range(2):
        rj[h] = packed[h].reshape(8, 8, 128) - old[h]


def coarse_down_body(before, low, high, after, comb_out, r1, message, state, comb, r2):
    lane = index_along((32, 128), 1)
    for side, ref in enumerate((before, low, high, after)):
        for x in range(4):
            for h in range(2):
                pair = ref[h, x]
                other = shifted(pair, 64, 1)
                state[2 * h, 4 * side + x] = jnp.where(lane < 64, pair, other)
                state[2 * h + 1, 4 * side + x] = jnp.where(lane < 64, other, pair)
    for i in range(1, 15):
        for c in range(3):
            total = state[c, i] - 0.125 * advected(state, 0, i, c)
            if c == 2:
                total = total + 0.5 * state[3, i]
            comb[c, i - 1] = total
            if 4 <= i < 12:
                comb_out[c, i - 4] = total
    for x in range(8):
        comb_out[3, x] = state[3, x + 4] - 0.125 * advected(state, 0, x + 4, 3)
    for k in range(12):
        v = comb[1, k + 1]
        w = comb[2, k + 1]
        div = comb[0, k + 2] - comb[0, k] + nxt(v, 1, 0) - prv(v, 1, 0) + nxt(w, 1, 1) - prv(w, 1, 1)
        r1[k] = 0.25 * div
    for m in range(4):
        a = 2 * m + 2
        r2[m] = restricted_defect(r1[a - 1], r1[a], r1[a + 1], r1[a + 2], 1, 1)
    part = [r2[m, pl.ds(0, 16, 2), :] for m in range(4)]
    lane = index_along((16, 128), 1)
    odd = lane % 2 == 1
    message[...] = jnp.where(
        lane < 64, jnp.where(odd, part[1], part[0]), jnp.where(odd, part[3], part[2])
    )


def coarse_up_core(base, tri_l, tri, tri_r, comb, r1, r2, e2, p2, e1, p1, emit):
    lane = index_along((16, 128), 1)
    for side, ref in enumerate((tri_l, tri, tri_r)):
        for j in range(3):
            block = ref[j, base : base + 16]
            other = shifted(block, 64, 1)
            n = 4 * (3 * side + j)
            for m, pair in enumerate(
                (jnp.where(lane < 64, block, other), jnp.where(lane < 64, other, block))
            ):
                r2[n + 2 * m] = bit_lane(pair, lane, 1, 0)
                r2[n + 2 * m + 1] = bit_lane(pair, lane, 1, 1)
    for i, value in enumerate(level2_pressure(r2, e2, 2)):
        p2[i, pl.ds(0, 16, 2), :] = value
        p2[i, pl.ds(1, 16, 2), :] = value
    for k in range(12):
        e1[k] = r1[k] * (-4.0 / 9.0) + p2[k // 2]
    for k in range(10):
        p1[k] = smoothed(e1[k], e1[k + 1], e1[k + 2], r1[k + 1], 4.0, 1, 1)
    lane = index_along((32, 128), 1)
    for x in range(8):
        here = p1[x + 1]
        u = comb[0, x] - 0.25 * (p1[x + 2] - p1[x])
        v = comb[1, x] - 0.25 * (nxt(here, 1, 0) - prv(here, 1, 0))
        w = comb[2, x] - 0.25 * (nxt(here, 1, 1) - prv(here, 1, 1))
        emit(0, x, jnp.where(lane < 64, u, v))
        emit(1, x, jnp.where(lane < 64, w, comb[3, x]))


UP_SCRATCH = [(36, 16, 128), (8, 16, 128), (6, 32, 128), (12, 32, 128), (10, 32, 128)]


def coarse_up_first_body(tri_l, tri, tri_r, comb, r1, ended, *scratch):
    def emit(h, x, value):
        ended[h, x] = value

    coarse_up_core(32, tri_l, tri, tri_r, comb, r1, *scratch, emit)


def coarse_up_next_body(where, tri_l, tri, tri_r, comb, r1, jump, ended, low, high, *scratch):
    def emit(h, x, value):
        scratch[5][h, x] = value
        ref = low if x < 4 else high
        ref[h, x % 4] = value + jump[h, x]

    coarse_up_core(0, tri_l, tri, tri_r, comb, r1, *scratch[:5], emit)
    ended[...] = scratch[5][:, :, rows_of(where, 0), :]


def coarse_up_last_body(where, tri_l, tri, tri_r, comb, r1, e0, e1, e2, out, *scratch):
    def emit(h, x, value):
        scratch[5][h, x] = value

    coarse_up_core(0, tri_l, tri, tri_r, comb, r1, *scratch[:5], emit)
    t = where[2]
    for h in range(2):
        e3 = scratch[5][h, :, rows_of(where, 0), :]
        value = jnp.where(
            t < 2, jnp.where(t == 0, e0[h], e1[h]), jnp.where(t == 2, e2[h], e3)
        )
        out[2 * h] = value[:, :, :64]
        out[2 * h + 1] = shifted(value, 64, 2)[:, :, :64]


def rows_of(where, step):
    return pl.ds(pl.multiple_of(8 * ((where[1] + 4 - step) % 4), 8), 8)


def join_body(where, a0, a1, a2, a3, low, high):
    for step, ref in enumerate((a0, a1, a2, a3)):
        rows = rows_of(where, step)
        for h in range(2):
            for x in range(4):
                low[h, x, rows, :] = ref[h, x]
                high[h, x, rows, :] = ref[h, x + 4]


def join_jumps_body(where, a0, a1, a2, a3, ended, low, high, second, third, own):
    for step, ref in enumerate((a0, a1, a2, a3)):
        rows = rows_of(where, step)
        for h in range(2):
            for x in range(8):
                first = low if x < 4 else high
                first[h, x % 4, rows, :] = ref[0, h, x] + ended[h, x, rows, :]
                second[h, x, rows, :] = ref[1, h, x]
                third[h, x, rows, :] = ref[2, h, x]
    own[...] = ended[:, :, rows_of(where, 0), :]


def new_start_body(where, fine, initial, l1, h1, l2, h2, l3, h3, out, rows, half, tall):
    t = where[2]

    @pl.when(t == 0)
    def _():
        out[...] = initial[...]

    @pl.when(t > 0)
    def _():
        packed = restricted_packed(fine, rows, half)
        mine = rows_of(where, 0)
        for h in range(2):
            for part, (a, b, c) in enumerate(((l1, l2, l3), (h1, h2, h3))):
                state = jnp.where(
                    t == 1, a[h, :, mine, :], jnp.where(t == 2, b[h, :, mine, :], c[h, :, mine, :])
                )
                change = state.reshape(32, 128) - packed[h][32 * part : 32 * part + 32]
                for side in range(2):
                    comp = 2 * h + side
                    wide = dot(change, z_spread(side)).reshape(4, 8, 128)
                    for x in range(4):
                        tall[comp, 4 * part + x, pl.ds(0, 8, 2), :] = wide[x]
                        tall[comp, 4 * part + x, pl.ds(1, 8, 2), :] = wide[x]
        for comp in range(4):
            for x in range(16):
                out[comp, x] = fine[comp, x] + tall[comp, x // 2]


def moved(value, axis, step):
    count = lax.axis_size(axis)
    return lax.ppermute(value, axis, [(i, (i + step) % count) for i in range(count)])


def both_sides(low_face, high_face, axis, step=1):
    return moved(high_face, axis, step), moved(low_face, axis, -step)


def around(value, axis):
    return [moved(value, axis, step) for step in range(1, 4)]


def nine(message):
    left, right = both_sides(message, message, "sx")
    return nine_of(left, message, right)


def nine_of(left, message, right):
    tri = jnp.stack([left, message, right])
    tri_l, tri_r = both_sides(tri, tri, "sx", 3)
    return [tri_l, tri, tri_r]


def shards(initial_state, start_old, end_old, coarse_old):
    begin, end, old = start_old[0], end_old[0], coarse_old[0]
    sx, sy, t = lax.axis_index("sx"), lax.axis_index("sy"), lax.axis_index("tm")
    where = jnp.stack([sx, sy, t]).astype(jnp.int32)

    def face(cut):
        return jnp.concatenate([begin[cut], end[cut]], axis=0)

    every = slice(None)
    left, right = both_sides(face((every, slice(0, 2))), face((every, slice(14, 16))), "sx")
    opening = call(opening_body, (2, 8, 8, 128), [initial_state], [(4, 8, 16, 128), (4, 8, 8, 128)])
    old_packed = jnp.stack(
        [jnp.concatenate([old[0], old[1]], axis=-1), jnp.concatenate([old[2], old[3]], axis=-1)]
    )

    def y_face(cut):
        inner = face((every, every, cut))
        rows = jnp.concatenate([left[:, :, cut], inner, right[:, :, cut]], axis=1)
        return jnp.concatenate([rows.reshape(160, 2, 128), opening.reshape(64, 2, 128)], axis=0)

    low, high = both_sides(y_face(slice(0, 2)), y_face(slice(14, 16)), "sy")
    opening_across = moved(opening, "sy", 2)
    comb, r0 = call(
        fine_source_body,
        [(4, 16, 16, 128), (16, 16, 128)],
        [begin, end, left, right, low, high],
        [(8, 20, 24, 128), (4, 18, 24, 128)],
    )
    r0_below, r0_across, r0_above = around(r0, "sy")

    def opening_of(got):
        return got[160:].reshape(2, 8, 8, 128)

    c0 = call(
        join_body,
        [(2, 4, 32, 128)] * 2,
        [where, opening, opening_of(low), opening_across, opening_of(high)],
        smem=1,
    )

    def coarse_down(state):
        low, high = state
        before, after = both_sides(low, high, "sx")
        return call(
            coarse_down_body,
            [(4, 8, 32, 128), (12, 32, 128), (16, 128)],
            [before, low, high, after],
            [(4, 16, 32, 128), (3, 14, 32, 128), (4, 32, 128)],
        )

    comb0, first0, message0 = coarse_down(c0)

    to_left, to_right, r0_own = call(
        fine_down_body,
        [(208, 128), (208, 128), (16, 32, 128)],
        [r0, r0_below, r0_across, r0_above, message0],
        [(16, 64, 128), (10, 64, 128), (6, 64, 128)],
    )
    from_left, from_right = both_sides(to_left, to_right, "sx")
    tris = nine_of(from_left[:48], to_left[:48], from_right[:48])
    fine_end, rj = call(
        fine_up_body,
        [(4, 16, 16, 128), (2, 8, 8, 128)],
        tris + [from_left, r0_own, from_right, comb, old_packed],
        [
            (26, 32, 128),
            (12, 32, 128),
            (36, 16, 128),
            (8, 16, 128),
            (6, 32, 128),
            (12, 32, 128),
            (10, 32, 128),
            (20, 32, 128),
            (18, 32, 128),
            (4, 8, 16, 128),
            (4, 8, 8, 128),
        ],
    )

    turned = [rj] + around(rj, "tm")
    ended0 = call(coarse_up_first_body, (2, 8, 32, 128), tris + [comb0, first0], UP_SCRATCH)

    def slice_of(s):
        back = (t - s) % 4
        return jnp.where(
            back < 2,
            jnp.where(back == 0, turned[0], turned[1]),
            jnp.where(back == 2, turned[2], turned[3]),
        )

    jumps = jnp.stack([slice_of(s) for s in range(3)])
    low1, high1, jump1, jump2, own0 = call(
        join_jumps_body,
        [(2, 4, 32, 128)] * 2 + [(2, 8, 32, 128)] * 2 + [(2, 8, 8, 128)],
        [where, jumps] + around(jumps, "sy") + [ended0],
        smem=1,
    )
    c1 = [low1, high1]
    fine_before = moved(fine_end, "tm", 1)

    def coarse_step(state, jump):
        combined, level1, message = coarse_down(state)
        own, low, high = call(
            coarse_up_next_body,
            [(2, 8, 8, 128)] + [(2, 4, 32, 128)] * 2,
            [where] + nine(message) + [combined, level1, jump],
            UP_SCRATCH + [(2, 8, 32, 128)],
            smem=1,
        )
        return own, [low, high]

    own1, c2 = coarse_step(c1, jump1)
    own2, c3 = coarse_step(c2, jump2)
    new_start = call(
        new_start_body,
        (4, 16, 16, 128),
        [where, fine_before, initial_state] + c1 + c2 + c3,
        [(4, 8, 16, 128), (4, 8, 8, 128), (4, 8, 16, 128)],
        smem=1,
    )
    combined, level1, message = coarse_down(c3)
    coarse_end = call(
        coarse_up_last_body,
        (4, 8, 8, 64),
        [where] + nine(message) + [combined, level1, own0, own1, own2],
        UP_SCRATCH + [(2, 8, 32, 128)],
        smem=1,
    )
    return (new_start[None], fine_end[None], coarse_end[None])


def solution(mesh):
    in_specs = (
        P(None, "sx", "sy", None),
        P("tm", None, "sx", "sy", None),
        P("tm", None, "sx", "sy", None),
        P("tm", None, "sx", "sy", None),
    )
    out_specs = (
        P("tm", None, "sx", "sy", None),
        P("tm", None, "sx", "sy", None),
        P("tm", None, "sx", "sy", None),
    )
    return jax.shard_map(shards, mesh=mesh, in_specs=in_specs, out_specs=out_specs, check_vma=False)
```

time: 194 us -> 130 us (0.67)
  Pallas kernels: 63.4 us -> 19.2 us
  blocking collectives: 27.1 us -> 0 us
  starting transfers between devices: 47.3 us -> 57.8 us
  waiting for transfers between devices: 52.2 us -> 49.8 us
    pallas_call x16 -> x15, Pallas kernels: 63.4 us -> 19.2 us  [call(): pl.pallas_call(body, out_shape=[jax.ShapeDtypeStruct(s, F32) for s in sha...]
    all_to_all x2 -> x0, blocking collectives: 27.1 us -> none  [coarse_step(): lax.all_to_all(jnp.broadcast_to(message[None], (16, 2, 128)), 'sx', 0, 0)]
    ppermute x26 -> x39, starting transfers between devices: 31.9 us -> 57.8 us  [moved(): lax.ppermute(value, axis, [(i, (i + step) % count) for i in range(count)])]
    all_to_all x2 -> x0, waiting for transfers between devices: 18.1 us -> none  [the longest x1 12.2 us: shards(): lax.all_to_all(jnp.broadcast_to(message[None], (64, 8, 128)), ('sx', 'sy'...]
    ppermute x26 -> x39, waiting for transfers between devices: 34.1 us -> 49.8 us  [moved(): lax.ppermute(value, axis, [(i, (i + step) % count) for i in range(count)])]
    all_to_all x2 -> x0, starting transfers between devices: 15.4 us -> none  [the longest x1 9.78 us: shards(): lax.all_to_all(jnp.broadcast_to(message[None], (64, 8, 128)), ('sx', 'sy'...]
  transfers between devices with their start and end apart: 28 -> 39, of which waited for: 17 -> 32; matrix products, arithmetic and copies ran while one was open for 1% -> 0% of each run, Pallas kernels for 18% -> 7%
where the time goes in v2:
time: 130 us
  starting transfers between devices  57.8 us (44%)
  waiting for transfers between devices  49.8 us (38%)
  Pallas kernels  19.2 us (15%)
    ppermute x39, starting transfers between devices, moved(): lax.ppermute(value, axis, [(i, (i + step) % count) for i in range(count)])  57.8 us
    ppermute x39, waiting for transfers between devices, moved(): lax.ppermute(value, axis, [(i, (i + step) % count) for i in range(count)])  49.8 us
    pallas_call x15, Pallas kernels, call(): pl.pallas_call(body, out_shape=[jax.ShapeDtypeStruct(s, F32) for s in sha...  19.2 us
  transfers between devices with their start and end apart: 39, of which 32 were waited for; matrix products, arithmetic and copies ran while one was open for 0% of the time, Pallas kernels for 7%

profile of v2, /device:TPU:1, one launch (start us, length us, event | category | flops | bytes accessed | tf_op | source)
XLA Modules:
  0.0 129.5 jit_solution(17825672600012652426)
XLA Ops:
  0.6 1.0 fusion.2
  1.7 3.3 %collective-permute-start.1 = (f32[8,2,16,128]{3,2,1,0:T(8,128)S(1)}, f32[8,2,16,128]{3,2,1,0:T(8,128)S(1)}, u32[]{:S(2)}, u32[]{:S(2)}) collective-permute-start(f32[8,2,16,128]{3,2,1,0:T(8,128)S(1)} %pad_maximum_fusion.6), channel_id=1, source_target_pairs={{0,60},{4,0},{8,4},{12,8},{16,12},{20,16},{24,20},{28,24},{32,28},... | collective-permute-start | bytes 393224 | tf_op jit(solution)/shard_map/ppermute | solution.py:420
  5.5 1.9 %collective-permute-done.1.right = f32[8,2,16,128]{3,2,1,0:T(8,128)S(1)} collective-permute-done((f32[8,2,16,128]{3,2,1,0:T(8,128)S(1)}, f32[8,2,16,128]{3,2,1,0:T(8,128)S(1)}, u32[]{:S(2)}, u32[]{:S(2)}) %collective-permute-start.1) | collective-permute-done | bytes 131104 | tf_op jit(solution)/shard_map/ppermute | solution.py:420
  7.4 2.0 %collective-permute-done.left = f32[8,2,16,128]{3,2,1,0:T(8,128)S(1)} collective-permute-done((f32[8,2,16,128]{3,2,1,0:T(8,128)S(1)}, f32[8,2,16,128]{3,2,1,0:T(8,128)S(1)}, u32[]{:S(2)}, u32[]{:S(2)}) %collective-permute-start) | collective-permute-done | bytes 131104 | tf_op jit(solution)/shard_map/ppermute | solution.py:420
  9.8 1.4 %collective-permute-start.2 = (f32[224,2,128]{2,1,0:T(2,128)S(1)}, f32[224,2,128]{2,1,0:T(2,128)S(1)}, u32[]{:S(2)}, u32[]{:S(2)}) collective-permute-start(f32[224,2,128]{2,1,0:T(2,128)S(1)} %get-tuple-element.87), channel_id=1, source_target_pairs={{0,1},{1,2},{2,3},{3,0},{4,5},{5,6},{6,7},{7,4},{8,9},{9,10},{10,1... | collective-permute-start | bytes 688136 | tf_op jit(solution)/shard_map/ppermute | solution.py:420
  11.2 1.5 %collective-permute-start.3 = (f32[224,2,128]{2,1,0:T(2,128)S(1)}, f32[224,2,128]{2,1,0:T(2,128)S(1)}, u32[]{:S(2)}, u32[]{:S(2)}) collective-permute-start(f32[224,2,128]{2,1,0:T(2,128)S(1)} %get-tuple-element.86), channel_id=1, source_target_pairs={{0,3},{1,0},{2,1},{3,2},{4,7},{5,4},{6,5},{7,6},{8,11},{9,8},{10,9... | collective-permute-start | bytes 688136 | tf_op jit(solution)/shard_map/ppermute | solution.py:420
  12.7 1.6 %collective-permute-start.7 = (f32[2,8,8,128]{3,2,1,0:T(8,128)S(1)}, f32[2,8,8,128]{3,2,1,0:T(8,128)S(1)}, u32[]{:S(2)}, u32[]{:S(2)}) collective-permute-start(f32[2,8,8,128]{3,2,1,0:T(8,128)S(1)} %opening_body.1.a0), channel_id=1, source_target_pairs={{0,2},{1,3},{2,0},{3,1},{4,6},{5,7},{6,4},{7,5},{8,10},{9,11},{10,... | collective-permute-start | bytes 196616 | tf_op jit(solution)/shard_map/ppermute | solution.py:420
  14.3 1.7 %collective-permute-done.2.low = f32[224,2,128]{2,1,0:T(2,128)S(1)} collective-permute-done((f32[224,2,128]{2,1,0:T(2,128)S(1)}, f32[224,2,128]{2,1,0:T(2,128)S(1)}, u32[]{:S(2)}, u32[]{:S(2)}) %collective-permute-start.2) | collective-permute-done | bytes 229408 | tf_op jit(solution)/shard_map/ppermute | solution.py:420
  16.4 1.2 fine_source_body.1
  17.6 1.0 collective-permute-start.4
  18.6 3.3 %collective-permute-start.5 = (f32[16,16,128]{2,1,0:T(8,128)S(1)}, f32[16,16,128]{2,1,0:T(8,128)S(1)}, u32[]{:S(2)}, u32[]{:S(2)}) collective-permute-start(f32[16,16,128]{2,1,0:T(8,128)S(1)} %get-tuple-element.35.own), channel_id=1, source_target_pairs={{0,2},{1,3},{2,0},{3,1},{4,6},{5,7},{6,4},{7,5},{8,10},{9,11},{10,... | collective-permute-start | bytes 393224 | tf_op jit(solution)/shard_map/ppermute | solution.py:420
  22.6 4.3 %collective-permute-start.8 = (f32[2,4,32,128]{3,2,1,0:T(8,128)S(1)}, f32[2,4,32,128]{3,2,1,0:T(8,128)S(1)}, u32[]{:S(2)}, u32[]{:S(2)}) collective-permute-start(f32[2,4,32,128]{3,2,1,0:T(8,128)S(1)} %get-tuple-element.36.high), channel_id=1, source_target_pairs={{0,4},{4,8},{8,12},{12,16},{16,20},{20,24},{24,28},{28,32},{32,36}... | collective-permute-start | bytes 393224 | tf_op jit(solution)/shard_map/ppermute | solution.py:420
  26.9 3.7 %collective-permute-start.9 = (f32[2,4,32,128]{3,2,1,0:T(8,128)S(1)}, f32[2,4,32,128]{3,2,1,0:T(8,128)S(1)}, u32[]{:S(2)}, u32[]{:S(2)}) collective-permute-start(f32[2,4,32,128]{3,2,1,0:T(8,128)S(1)} %get-tuple-element.37.low), channel_id=1, source_target_pairs={{0,60},{4,0},{8,4},{12,8},{16,12},{20,16},{24,20},{28,24},{32,28},... | collective-permute-start | bytes 393224 | tf_op jit(solution)/shard_map/ppermute | solution.py:420
  30.7 0.7 collective-permute-done.8.before
  31.6 0.9 coarse_down_body.4
  32.5 1.3 %fine_down_body.1 = (f32[208,128]{1,0:T(8,128)S(1)}, f32[208,128]{1,0:T(8,128)S(1)}, f32[16,32,128]{2,1,0:T(8,128)S(1)}) custom-call(f32[16,16,128]{2,1,0:T(8,128)S(1)} %get-tuple-element.35.own, f32[16,16,128]{2,1,0:T(8,128)S(1)} %collective-permute-done.4.below, f32[16,16,128]{2,1,0:T(8,128)S(1)} %collective-permute-done.5.across, ...), custom_call_target="tpu_custom_call" | custom-call | tf_op jit(solution)/shard_map/fine_down_body/pallas_call | solution.py:17
  33.9 4.6 %collective-permute-start.11 = (f32[208,128]{1,0:T(8,128)S(1)}, f32[208,128]{1,0:T(8,128)S(1)}, u32[]{:S(2)}, u32[]{:S(2)}) collective-permute-start(f32[208,128]{1,0:T(8,128)S(1)} %get-tuple-element.40), channel_id=1, source_target_pairs={{0,60},{4,0},{8,4},{12,8},{16,12},{20,16},{24,20},{28,24},{32,28},... | collective-permute-start | bytes 319496 | tf_op jit(solution)/shard_map/ppermute | solution.py:420
  38.5 0.9 collective-permute-done.11.right
  39.4 2.8 %collective-permute-done.10.left = f32[208,128]{1,0:T(8,128)S(1)} collective-permute-done((f32[208,128]{1,0:T(8,128)S(1)}, f32[208,128]{1,0:T(8,128)S(1)}, u32[]{:S(2)}, u32[]{:S(2)}) %collective-permute-start.10) | collective-permute-done | bytes 106528 | tf_op jit(solution)/shard_map/ppermute | solution.py:420
  42.3 2.9 %collective-permute-start.13 = (f32[3,48,128]{2,1,0:T(8,128)S(1)}, f32[3,48,128]{2,1,0:T(8,128)S(1)}, u32[]{:S(2)}, u32[]{:S(2)}) collective-permute-start(f32[3,48,128]{2,1,0:T(8,128)S(1)} %pad_maximum_fusion.7.tri), channel_id=1, source_target_pairs={{0,52},{4,56},{8,60},{12,0},{16,4},{20,8},{24,12},{28,16},{32,20},... | collective-permute-start | bytes 221192 | tf_op jit(solution)/shard_map/ppermute | solution.py:420
  45.3 2.0 %collective-permute-done.12.tri_l = f32[3,48,128]{2,1,0:T(8,128)S(1)} collective-permute-done((f32[3,48,128]{2,1,0:T(8,128)S(1)}, f32[3,48,128]{2,1,0:T(8,128)S(1)}, u32[]{:S(2)}, u32[]{:S(2)}) %collective-permute-start.12) | collective-permute-done | bytes 73760 | tf_op jit(solution)/shard_map/ppermute | solution.py:420
  47.3 0.9 collective-permute-done.13.tri_r
  48.2 2.7 %fine_up_body.1 = (f32[4,16,16,128]{3,2,1,0:T(8,128)}, f32[2,8,8,128]{3,2,1,0:T(8,128)S(1)}) custom-call(f32[3,48,128]{2,1,0:T(8,128)S(1)} %collective-permute-done.12.tri_l, f32[3,48,128]{2,1,0:T(8,128)S(1)} %pad_maximum_fusion.7.tri, f32[3,48,128]{2,1,0:T(8,128)S(1)} %collective-permute-done.13.tri_r, f32[208,128]{1,0:T(8,128)S(1)} %collective-permute-done.10.left, ...), custom_call_target="tpu_custom_call" | custom-call | tf_op jit(solution)/shard_map/fine_up_body/pallas_call | solution.py:17
  50.9 1.2 collective-permute-start.15
  52.1 2.5 %collective-permute-start.16 = (f32[2,8,8,128]{3,2,1,0:T(8,128)S(1)}, f32[2,8,8,128]{3,2,1,0:T(8,128)S(1)}, u32[]{:S(2)}, u32[]{:S(2)}) collective-permute-start(f32[2,8,8,128]{3,2,1,0:T(8,128)S(1)} %get-tuple-element.44), channel_id=1, source_target_pairs={{0,128},{64,192},{128,0},{192,64},{1,129},{65,193},{129,1},{193,65... | collective-permute-start | bytes 196616 | tf_op jit(solution)/shard_map/ppermute | solution.py:420
  54.6 1.2 collective-permute-start.17
  55.7 1.2 collective-permute-done.16
  56.9 0.8 collective-permute-done.17
  57.7 1.6 %collective-permute-start.18 = (f32[3,2,8,8,128]{4,3,2,1,0:T(8,128)S(1)}, f32[3,2,8,8,128]{4,3,2,1,0:T(8,128)S(1)}, u32[]{:S(2)}, u32[]{:S(2)}) collective-permute-start(f32[3,2,8,8,128]{4,3,2,1,0:T(8,128)S(1)} %pad_maximum_fusion.2.a0), channel_id=1, source_target_pairs={{0,1},{1,2},{2,3},{3,0},{4,5},{5,6},{6,7},{7,4},{8,9},{9,10},{10,1... | collective-permute-start | bytes 589832 | tf_op jit(solution)/shard_map/ppermute | solution.py:420
  59.4 2.5 %collective-permute-start.20 = (f32[3,2,8,8,128]{4,3,2,1,0:T(8,128)S(1)}, f32[3,2,8,8,128]{4,3,2,1,0:T(8,128)S(1)}, u32[]{:S(2)}, u32[]{:S(2)}) collective-permute-start(f32[3,2,8,8,128]{4,3,2,1,0:T(8,128)S(1)} %pad_maximum_fusion.2.a0), channel_id=1, source_target_pairs={{0,3},{1,0},{2,1},{3,2},{4,7},{5,4},{6,5},{7,6},{8,11},{9,8},{10,9... | collective-permute-start | bytes 589832 | tf_op jit(solution)/shard_map/ppermute | solution.py:420
  61.8 1.3 coarse_up_first_body.1.ended
  63.1 2.5 %collective-permute-done.18.a1 = f32[3,2,8,8,128]{4,3,2,1,0:T(8,128)S(1)} collective-permute-done((f32[3,2,8,8,128]{4,3,2,1,0:T(8,128)S(1)}, f32[3,2,8,8,128]{4,3,2,1,0:T(8,128)S(1)}, u32[]{:S(2)}, u32[]{:S(2)}) %collective-permute-start.18) | collective-permute-done | bytes 196640 | tf_op jit(solution)/shard_map/ppermute | solution.py:420
  66.2 0.7 join_jumps_body.1
  66.9 7.7 %collective-permute-start.21 = (f32[2,4,32,128]{3,2,1,0:T(8,128)S(1)}, f32[2,4,32,128]{3,2,1,0:T(8,128)S(1)}, u32[]{:S(2)}, u32[]{:S(2)}) collective-permute-start(f32[2,4,32,128]{3,2,1,0:T(8,128)S(1)} %get-tuple-element.48.high.h1), channel_id=1, source_target_pairs={{0,4},{4,8},{8,12},{12,16},{16,20},{20,24},{24,28},{28,32},{32,36}... | collective-permute-start | bytes 393224 | tf_op jit(solution)/shard_map/ppermute | solution.py:420
  74.6 1.9 %collective-permute-done.21.before = f32[2,4,32,128]{3,2,1,0:T(8,128)S(1)} collective-permute-done((f32[2,4,32,128]{3,2,1,0:T(8,128)S(1)}, f32[2,4,32,128]{3,2,1,0:T(8,128)S(1)}, u32[]{:S(2)}, u32[]{:S(2)}) %collective-permute-start.21) | collective-permute-done | bytes 131104 | tf_op jit(solution)/shard_map/ppermute | solution.py:420
  76.6 2.7 %collective-permute-done.22.after = f32[2,4,32,128]{3,2,1,0:T(8,128)S(1)} collective-permute-done((f32[2,4,32,128]{3,2,1,0:T(8,128)S(1)}, f32[2,4,32,128]{3,2,1,0:T(8,128)S(1)}, u32[]{:S(2)}, u32[]{:S(2)}) %collective-permute-start.22) | collective-permute-done | bytes 131104 | tf_op jit(solution)/shard_map/ppermute | solution.py:420
  79.3 0.9 coarse_down_body.5
  80.3 0.9 collective-permute-start.24
  81.8 1.5 %collective-permute-done.24 = f32[16,128]{1,0:T(8,128)S(1)} collective-permute-done((f32[16,128]{1,0:T(8,128)S(1)}, f32[16,128]{1,0:T(8,128)S(1)}, u32[]{:S(2)}, u32[]{:S(2)}) %collective-permute-start.24) | collective-permute-done | bytes 8224 | tf_op jit(solution)/shard_map/ppermute | solution.py:420
  83.4 3.0 %collective-permute-start.26 = (f32[3,16,128]{2,1,0:T(8,128)S(1)}, f32[3,16,128]{2,1,0:T(8,128)S(1)}, u32[]{:S(2)}, u32[]{:S(2)}) collective-permute-start(f32[3,16,128]{2,1,0:T(8,128)S(1)} %pad_maximum_fusion.9.tri), channel_id=1, source_target_pairs={{0,52},{4,56},{8,60},{12,0},{16,4},{20,8},{24,12},{28,16},{32,20},... | collective-permute-start | bytes 73736 | tf_op jit(solution)/shard_map/ppermute | solution.py:420
  86.3 1.5 %collective-permute-done.25.tri_l = f32[3,16,128]{2,1,0:T(8,128)S(1)} collective-permute-done((f32[3,16,128]{2,1,0:T(8,128)S(1)}, f32[3,16,128]{2,1,0:T(8,128)S(1)}, u32[]{:S(2)}, u32[]{:S(2)}) %collective-permute-start.25) | collective-permute-done | bytes 24608 | tf_op jit(solution)/shard_map/ppermute | solution.py:420
  87.8 2.3 %collective-permute-done.26.tri_r = f32[3,16,128]{2,1,0:T(8,128)S(1)} collective-permute-done((f32[3,16,128]{2,1,0:T(8,128)S(1)}, f32[3,16,128]{2,1,0:T(8,128)S(1)}, u32[]{:S(2)}, u32[]{:S(2)}) %collective-permute-start.26) | collective-permute-done | bytes 24608 | tf_op jit(solution)/shard_map/ppermute | solution.py:420
  90.1 1.8 %coarse_up_next_body.2 = (f32[2,8,8,128]{3,2,1,0:T(8,128)S(1)}, f32[2,4,32,128]{3,2,1,0:T(8,128)S(1)}, f32[2,4,32,128]{3,2,1,0:T(8,128)S(1)}) custom-call(s32[3]{0:T(128)S(1)} %pad_add_fusion.where, f32[3,16,128]{2,1,0:T(8,128)S(1)} %collective-permute-done.25.tri_l, f32[3,16,128]{2,1,0:T(8,128)S(1)} %pad_maximum_fusion.9.tri, ...), custom_call_target="tpu_custom_call" | custom-call | tf_op jit(solution)/shard_map/coarse_up_next_body/pallas_call | solution.py:17
  92.0 0.9 collective-permute-start.27
  93.2 1.6 %collective-permute-done.27.before = f32[2,4,32,128]{3,2,1,0:T(8,128)S(1)} collective-permute-done((f32[2,4,32,128]{3,2,1,0:T(8,128)S(1)}, f32[2,4,32,128]{3,2,1,0:T(8,128)S(1)}, u32[]{:S(2)}, u32[]{:S(2)}) %collective-permute-start.27) | collective-permute-done | bytes 131104 | tf_op jit(solution)/shard_map/ppermute | solution.py:420
  94.8 2.7 %collective-permute-done.28.after = f32[2,4,32,128]{3,2,1,0:T(8,128)S(1)} collective-permute-done((f32[2,4,32,128]{3,2,1,0:T(8,128)S(1)}, f32[2,4,32,128]{3,2,1,0:T(8,128)S(1)}, u32[]{:S(2)}, u32[]{:S(2)}) %collective-permute-start.28) | collective-permute-done | bytes 131104 | tf_op jit(solution)/shard_map/ppermute | solution.py:420
  97.5 0.9 coarse_down_body.6
  98.5 0.9 collective-permute-start.30
  100.0 1.9 %collective-permute-done.30 = f32[16,128]{1,0:T(8,128)S(1)} collective-permute-done((f32[16,128]{1,0:T(8,128)S(1)}, f32[16,128]{1,0:T(8,128)S(1)}, u32[]{:S(2)}, u32[]{:S(2)}) %collective-permute-start.30) | collective-permute-done | bytes 8224 | tf_op jit(solution)/shard_map/ppermute | solution.py:420
  102.2 2.7 %collective-permute-start.32 = (f32[3,16,128]{2,1,0:T(8,128)S(1)}, f32[3,16,128]{2,1,0:T(8,128)S(1)}, u32[]{:S(2)}, u32[]{:S(2)}) collective-permute-start(f32[3,16,128]{2,1,0:T(8,128)S(1)} %pad_maximum_fusion.10.tri), channel_id=1, source_target_pairs={{0,52},{4,56},{8,60},{12,0},{16,4},{20,8},{24,12},{28,16},{32,20},... | collective-permute-start | bytes 73736 | tf_op jit(solution)/shard_map/ppermute | solution.py:420
  104.8 1.8 %collective-permute-done.31.tri_l = f32[3,16,128]{2,1,0:T(8,128)S(1)} collective-permute-done((f32[3,16,128]{2,1,0:T(8,128)S(1)}, f32[3,16,128]{2,1,0:T(8,128)S(1)}, u32[]{:S(2)}, u32[]{:S(2)}) %collective-permute-start.31) | collective-permute-done | bytes 24608 | tf_op jit(solution)/shard_map/ppermute | solution.py:420
  106.6 2.2 %collective-permute-done.32.tri_r = f32[3,16,128]{2,1,0:T(8,128)S(1)} collective-permute-done((f32[3,16,128]{2,1,0:T(8,128)S(1)}, f32[3,16,128]{2,1,0:T(8,128)S(1)}, u32[]{:S(2)}, u32[]{:S(2)}) %collective-permute-start.32) | collective-permute-done | bytes 24608 | tf_op jit(solution)/shard_map/ppermute | solution.py:420
  108.8 1.8 %coarse_up_next_body.3 = (f32[2,8,8,128]{3,2,1,0:T(8,128)S(1)}, f32[2,4,32,128]{3,2,1,0:T(8,128)S(1)}, f32[2,4,32,128]{3,2,1,0:T(8,128)S(1)}) custom-call(s32[3]{0:T(128)S(1)} %pad_add_fusion.where, f32[3,16,128]{2,1,0:T(8,128)S(1)} %collective-permute-done.31.tri_l, f32[3,16,128]{2,1,0:T(8,128)S(1)} %pad_maximum_fusion.10.tri, ...), custom_call_target="tpu_custom_call" | custom-call | tf_op jit(solution)/shard_map/coarse_up_next_body/pallas_call | solution.py:17
  110.7 0.7 collective-permute-start.33
  111.4 1.9 %collective-permute-done.33.before = f32[2,4,32,128]{3,2,1,0:T(8,128)S(1)} collective-permute-done((f32[2,4,32,128]{3,2,1,0:T(8,128)S(1)}, f32[2,4,32,128]{3,2,1,0:T(8,128)S(1)}, u32[]{:S(2)}, u32[]{:S(2)}) %collective-permute-start.33) | collective-permute-done | bytes 131104 | tf_op jit(solution)/shard_map/ppermute | solution.py:420
  113.3 2.7 %collective-permute-done.34.after = f32[2,4,32,128]{3,2,1,0:T(8,128)S(1)} collective-permute-done((f32[2,4,32,128]{3,2,1,0:T(8,128)S(1)}, f32[2,4,32,128]{3,2,1,0:T(8,128)S(1)}, u32[]{:S(2)}, u32[]{:S(2)}) %collective-permute-start.34) | collective-permute-done | bytes 131104 | tf_op jit(solution)/shard_map/ppermute | solution.py:420
  116.1 0.9 coarse_down_body.7
  117.0 0.8 collective-permute-start.36
  118.4 1.7 %collective-permute-done.36 = f32[16,128]{1,0:T(8,128)S(1)} collective-permute-done((f32[16,128]{1,0:T(8,128)S(1)}, f32[16,128]{1,0:T(8,128)S(1)}, u32[]{:S(2)}, u32[]{:S(2)}) %collective-permute-start.36) | collective-permute-done | bytes 8224 | tf_op jit(solution)/shard_map/ppermute | solution.py:420
  120.1 0.8 collective-permute-start.37
  120.9 2.1 %collective-permute-start.38 = (f32[3,16,128]{2,1,0:T(8,128)S(1)}, f32[3,16,128]{2,1,0:T(8,128)S(1)}, u32[]{:S(2)}, u32[]{:S(2)}) collective-permute-start(f32[3,16,128]{2,1,0:T(8,128)S(1)} %pad_maximum_fusion.11.tri), channel_id=1, source_target_pairs={{0,52},{4,56},{8,60},{12,0},{16,4},{20,8},{24,12},{28,16},{32,20},... | collective-permute-start | bytes 73736 | tf_op jit(solution)/shard_map/ppermute | solution.py:420
  123.1 1.4 %new_start_body.1 = f32[4,16,16,128]{3,2,1,0:T(8,128)} custom-call(s32[3]{0:T(128)S(1)} %pad_add_fusion.where, f32[4,16,16,128]{3,2,1,0:T(8,128)S(1)} %collective-permute-done.14.fine, f32[4,16,16,128]{3,2,1,0:T(8,128)S(1)} %copy-done, f32[2,4,32,128]{3,2,1,0:T(8,128)S(1)} %get-tuple-element.47.low.l1, f32[2,4,32,128]{3,2,1,0:T(8,128)S(1)} %get-tuple-element.48.high.h1, ...), custom_call_target="tpu_custom_call" | custom-call | tf_op jit(solution)/shard_map/new_start_body/pallas_call | solution.py:17
  124.6 2.5 %collective-permute-done.38.tri_r = f32[3,16,128]{2,1,0:T(8,128)S(1)} collective-permute-done((f32[3,16,128]{2,1,0:T(8,128)S(1)}, f32[3,16,128]{2,1,0:T(8,128)S(1)}, u32[]{:S(2)}, u32[]{:S(2)}) %collective-permute-start.38) | collective-permute-done | bytes 24608 | tf_op jit(solution)/shard_map/ppermute | solution.py:420
  127.1 2.5 %coarse_up_last_body.1 = f32[4,8,8,64]{3,2,1,0:T(8,128)} custom-call(s32[3]{0:T(128)S(1)} %pad_add_fusion.where, f32[3,16,128]{2,1,0:T(8,128)S(1)} %collective-permute-done.37.tri_l, f32[3,16,128]{2,1,0:T(8,128)S(1)} %pad_maximum_fusion.11.tri, f32[3,16,128]{2,1,0:T(8,128)S(1)} %collective-permute-done.38.tri_r, ...), custom_call_target="tpu_custom_call" | custom-call | tf_op jit(solution)/shard_map/coarse_up_last_body/pallas_call | solution.py:17
  (63 shorter events, 5.7 us)
Async XLA Ops:
  0.6 4.4 %copy-start = (f32[4,16,16,128]{3,2,1,0:T(8,128)S(1)}, f32[4,16,16,128]{3,2,1,0:T(8,128)}, u32[]{:S(2)}) copy-start(f32[4,16,16,128]{3,2,1,0:T(8,128)} %initial.3) | copy-start | bytes 1572868
  1.7 3.7 %copy-start.1 = (f32[1,4,16,16,128]{4,3,2,1,0:T(8,128)S(1)}, f32[1,4,16,16,128]{4,3,2,1,0:T(8,128)}, u32[]{:S(2)}) copy-start(f32[1,4,16,16,128]{4,3,2,1,0:T(8,128)} %param.5) | copy-start | bytes 1572868
  1.7 3.7 %copy-start.2 = (f32[1,4,16,16,128]{4,3,2,1,0:T(8,128)S(1)}, f32[1,4,16,16,128]{4,3,2,1,0:T(8,128)}, u32[]{:S(2)}) copy-start(f32[1,4,16,16,128]{4,3,2,1,0:T(8,128)} %param.6) | copy-start | bytes 1572868
  1.7 5.7 %collective-permute-start.1 = (f32[8,2,16,128]{3,2,1,0:T(8,128)S(1)}, f32[8,2,16,128]{3,2,1,0:T(8,128)S(1)}, u32[]{:S(2)}, u32[]{:S(2)}) collective-permute-start(f32[8,2,16,128]{3,2,1,0:T(8,128)S(1)} %pad_maximum_fusion.6), channel_id=1, source_target_pairs={{0,60},{4,0},{8,4},{12,8},{16,12},{20,16},{24,20},{28,24},{32,28},... | collective-permute-start | bytes 393224 | tf_op jit(solution)/shard_map/ppermute | solution.py:420
  5.0 4.4 %collective-permute-start = (f32[8,2,16,128]{3,2,1,0:T(8,128)S(1)}, f32[8,2,16,128]{3,2,1,0:T(8,128)S(1)}, u32[]{:S(2)}, u32[]{:S(2)}) collective-permute-start(f32[8,2,16,128]{3,2,1,0:T(8,128)S(1)} %pad_maximum_fusion.5), channel_id=1, source_target_pairs={{0,4},{4,8},{8,12},{12,16},{16,20},{20,24},{24,28},{28,32},{32,36}... | collective-permute-start | bytes 393224 | tf_op jit(solution)/shard_map/ppermute | solution.py:420
  9.8 6.2 %collective-permute-start.2 = (f32[224,2,128]{2,1,0:T(2,128)S(1)}, f32[224,2,128]{2,1,0:T(2,128)S(1)}, u32[]{:S(2)}, u32[]{:S(2)}) collective-permute-start(f32[224,2,128]{2,1,0:T(2,128)S(1)} %get-tuple-element.87), channel_id=1, source_target_pairs={{0,1},{1,2},{2,3},{3,0},{4,5},{5,6},{6,7},{7,4},{8,9},{9,10},{10,1... | collective-permute-start | bytes 688136 | tf_op jit(solution)/shard_map/ppermute | solution.py:420
  11.2 5.2 %collective-permute-start.3 = (f32[224,2,128]{2,1,0:T(2,128)S(1)}, f32[224,2,128]{2,1,0:T(2,128)S(1)}, u32[]{:S(2)}, u32[]{:S(2)}) collective-permute-start(f32[224,2,128]{2,1,0:T(2,128)S(1)} %get-tuple-element.86), channel_id=1, source_target_pairs={{0,3},{1,0},{2,1},{3,2},{4,7},{5,4},{6,5},{7,6},{8,11},{9,8},{10,9... | collective-permute-start | bytes 688136 | tf_op jit(solution)/shard_map/ppermute | solution.py:420
  12.7 9.3 %collective-permute-start.7 = (f32[2,8,8,128]{3,2,1,0:T(8,128)S(1)}, f32[2,8,8,128]{3,2,1,0:T(8,128)S(1)}, u32[]{:S(2)}, u32[]{:S(2)}) collective-permute-start(f32[2,8,8,128]{3,2,1,0:T(8,128)S(1)} %opening_body.1.a0), channel_id=1, source_target_pairs={{0,2},{1,3},{2,0},{3,1},{4,6},{5,7},{6,4},{7,5},{8,10},{9,11},{10,... | collective-permute-start | bytes 196616 | tf_op jit(solution)/shard_map/ppermute | solution.py:420
  17.6 14.9 %collective-permute-start.4 = (f32[16,16,128]{2,1,0:T(8,128)S(1)}, f32[16,16,128]{2,1,0:T(8,128)S(1)}, u32[]{:S(2)}, u32[]{:S(2)}) collective-permute-start(f32[16,16,128]{2,1,0:T(8,128)S(1)} %get-tuple-element.35.own), channel_id=1, source_target_pairs={{0,1},{1,2},{2,3},{3,0},{4,5},{5,6},{6,7},{7,4},{8,9},{9,10},{10,1... | collective-permute-start | bytes 393224 | tf_op jit(solution)/shard_map/ppermute | solution.py:420
  18.6 13.9 %collective-permute-start.5 = (f32[16,16,128]{2,1,0:T(8,128)S(1)}, f32[16,16,128]{2,1,0:T(8,128)S(1)}, u32[]{:S(2)}, u32[]{:S(2)}) collective-permute-start(f32[16,16,128]{2,1,0:T(8,128)S(1)} %get-tuple-element.35.own), channel_id=1, source_target_pairs={{0,2},{1,3},{2,0},{3,1},{4,6},{5,7},{6,4},{7,5},{8,10},{9,11},{10,... | collective-permute-start | bytes 393224 | tf_op jit(solution)/shard_map/ppermute | solution.py:420
  21.9 10.6 %collective-permute-start.6 = (f32[16,16,128]{2,1,0:T(8,128)S(1)}, f32[16,16,128]{2,1,0:T(8,128)S(1)}, u32[]{:S(2)}, u32[]{:S(2)}) collective-permute-start(f32[16,16,128]{2,1,0:T(8,128)S(1)} %get-tuple-element.35.own), channel_id=1, source_target_pairs={{0,3},{1,0},{2,1},{3,2},{4,7},{5,4},{6,5},{7,6},{8,11},{9,8},{10,9... | collective-permute-start | bytes 393224 | tf_op jit(solution)/shard_map/ppermute | solution.py:420
  22.0 8.6 %copy-start.3 = (f32[1,4,8,8,64]{4,3,2,1,0:T(8,128)S(1)}, f32[1,4,8,8,64]{4,3,2,1,0:T(8,128)}, u32[]{:S(2)}) copy-start(f32[1,4,8,8,64]{4,3,2,1,0:T(8,128)} %param.7) | copy-start | bytes 196612
  22.6 8.8 %collective-permute-start.8 = (f32[2,4,32,128]{3,2,1,0:T(8,128)S(1)}, f32[2,4,32,128]{3,2,1,0:T(8,128)S(1)}, u32[]{:S(2)}, u32[]{:S(2)}) collective-permute-start(f32[2,4,32,128]{3,2,1,0:T(8,128)S(1)} %get-tuple-element.36.high), channel_id=1, source_target_pairs={{0,4},{4,8},{8,12},{12,16},{16,20},{20,24},{24,28},{28,32},{32,36}... | collective-permute-start | bytes 393224 | tf_op jit(solution)/shard_map/ppermute | solution.py:420
  26.9 4.7 %collective-permute-start.9 = (f32[2,4,32,128]{3,2,1,0:T(8,128)S(1)}, f32[2,4,32,128]{3,2,1,0:T(8,128)S(1)}, u32[]{:S(2)}, u32[]{:S(2)}) collective-permute-start(f32[2,4,32,128]{3,2,1,0:T(8,128)S(1)} %get-tuple-element.37.low), channel_id=1, source_target_pairs={{0,60},{4,0},{8,4},{12,8},{16,12},{20,16},{24,20},{28,24},{32,28},... | collective-permute-start | bytes 393224 | tf_op jit(solution)/shard_map/ppermute | solution.py:420
  33.9 5.6 %collective-permute-start.11 = (f32[208,128]{1,0:T(8,128)S(1)}, f32[208,128]{1,0:T(8,128)S(1)}, u32[]{:S(2)}, u32[]{:S(2)}) collective-permute-start(f32[208,128]{1,0:T(8,128)S(1)} %get-tuple-element.40), channel_id=1, source_target_pairs={{0,60},{4,0},{8,4},{12,8},{16,12},{20,16},{24,20},{28,24},{32,28},... | collective-permute-start | bytes 319496 | tf_op jit(solution)/shard_map/ppermute | solution.py:420
  38.5 3.8 %collective-permute-start.10 = (f32[208,128]{1,0:T(8,128)S(1)}, f32[208,128]{1,0:T(8,128)S(1)}, u32[]{:S(2)}, u32[]{:S(2)}) collective-permute-start(f32[208,128]{1,0:T(8,128)S(1)} %get-tuple-element.39), channel_id=1, source_target_pairs={{0,4},{4,8},{8,12},{12,16},{16,20},{20,24},{24,28},{28,32},{32,36}... | collective-permute-start | bytes 319496 | tf_op jit(solution)/shard_map/ppermute | solution.py:420
  42.2 5.1 %collective-permute-start.12 = (f32[3,48,128]{2,1,0:T(8,128)S(1)}, f32[3,48,128]{2,1,0:T(8,128)S(1)}, u32[]{:S(2)}, u32[]{:S(2)}) collective-permute-start(f32[3,48,128]{2,1,0:T(8,128)S(1)} %pad_maximum_fusion.7.tri), channel_id=1, source_target_pairs={{0,12},{4,16},{8,20},{12,24},{16,28},{20,32},{24,36},{28,40},{32,4... | collective-permute-start | bytes 221192 | tf_op jit(solution)/shard_map/ppermute | solution.py:420
  42.3 5.9 %collective-permute-start.13 = (f32[3,48,128]{2,1,0:T(8,128)S(1)}, f32[3,48,128]{2,1,0:T(8,128)S(1)}, u32[]{:S(2)}, u32[]{:S(2)}) collective-permute-start(f32[3,48,128]{2,1,0:T(8,128)S(1)} %pad_maximum_fusion.7.tri), channel_id=1, source_target_pairs={{0,52},{4,56},{8,60},{12,0},{16,4},{20,8},{24,12},{28,16},{32,20},... | collective-permute-start | bytes 221192 | tf_op jit(solution)/shard_map/ppermute | solution.py:420
  50.9 4.8 %collective-permute-start.15 = (f32[2,8,8,128]{3,2,1,0:T(8,128)S(1)}, f32[2,8,8,128]{3,2,1,0:T(8,128)S(1)}, u32[]{:S(2)}, u32[]{:S(2)}) collective-permute-start(f32[2,8,8,128]{3,2,1,0:T(8,128)S(1)} %get-tuple-element.44), channel_id=1, source_target_pairs={{0,64},{64,128},{128,192},{192,0},{1,65},{65,129},{129,193},{193,1... | collective-permute-start | bytes 196616 | tf_op jit(solution)/shard_map/ppermute | solution.py:420
  52.1 4.8 %collective-permute-start.16 = (f32[2,8,8,128]{3,2,1,0:T(8,128)S(1)}, f32[2,8,8,128]{3,2,1,0:T(8,128)S(1)}, u32[]{:S(2)}, u32[]{:S(2)}) collective-permute-start(f32[2,8,8,128]{3,2,1,0:T(8,128)S(1)} %get-tuple-element.44), channel_id=1, source_target_pairs={{0,128},{64,192},{128,0},{192,64},{1,129},{65,193},{129,1},{193,65... | collective-permute-start | bytes 196616 | tf_op jit(solution)/shard_map/ppermute | solution.py:420
  54.6 3.1 %collective-permute-start.17 = (f32[2,8,8,128]{3,2,1,0:T(8,128)S(1)}, f32[2,8,8,128]{3,2,1,0:T(8,128)S(1)}, u32[]{:S(2)}, u32[]{:S(2)}) collective-permute-start(f32[2,8,8,128]{3,2,1,0:T(8,128)S(1)} %get-tuple-element.44), channel_id=1, source_target_pairs={{0,192},{64,0},{128,64},{192,128},{1,193},{65,1},{129,65},{193,129... | collective-permute-start | bytes 196616 | tf_op jit(solution)/shard_map/ppermute | solution.py:420
  57.7 7.9 %collective-permute-start.18 = (f32[3,2,8,8,128]{4,3,2,1,0:T(8,128)S(1)}, f32[3,2,8,8,128]{4,3,2,1,0:T(8,128)S(1)}, u32[]{:S(2)}, u32[]{:S(2)}) collective-permute-start(f32[3,2,8,8,128]{4,3,2,1,0:T(8,128)S(1)} %pad_maximum_fusion.2.a0), channel_id=1, source_target_pairs={{0,1},{1,2},{2,3},{3,0},{4,5},{5,6},{6,7},{7,4},{8,9},{9,10},{10,1... | collective-permute-start | bytes 589832 | tf_op jit(solution)/shard_map/ppermute | solution.py:420
  59.4 6.3 %collective-permute-start.19 = (f32[3,2,8,8,128]{4,3,2,1,0:T(8,128)S(1)}, f32[3,2,8,8,128]{4,3,2,1,0:T(8,128)S(1)}, u32[]{:S(2)}, u32[]{:S(2)}) collective-permute-start(f32[3,2,8,8,128]{4,3,2,1,0:T(8,128)S(1)} %pad_maximum_fusion.2.a0), channel_id=1, source_target_pairs={{0,2},{1,3},{2,0},{3,1},{4,6},{5,7},{6,4},{7,5},{8,10},{9,11},{10,... | collective-permute-start | bytes 589832 | tf_op jit(solution)/shard_map/ppermute | solution.py:420
  59.4 6.9 %collective-permute-start.20 = (f32[3,2,8,8,128]{4,3,2,1,0:T(8,128)S(1)}, f32[3,2,8,8,128]{4,3,2,1,0:T(8,128)S(1)}, u32[]{:S(2)}, u32[]{:S(2)}) collective-permute-start(f32[3,2,8,8,128]{4,3,2,1,0:T(8,128)S(1)} %pad_maximum_fusion.2.a0), channel_id=1, source_target_pairs={{0,3},{1,0},{2,1},{3,2},{4,7},{5,4},{6,5},{7,6},{8,11},{9,8},{10,9... | collective-permute-start | bytes 589832 | tf_op jit(solution)/shard_map/ppermute | solution.py:420
  66.9 9.7 %collective-permute-start.21 = (f32[2,4,32,128]{3,2,1,0:T(8,128)S(1)}, f32[2,4,32,128]{3,2,1,0:T(8,128)S(1)}, u32[]{:S(2)}, u32[]{:S(2)}) collective-permute-start(f32[2,4,32,128]{3,2,1,0:T(8,128)S(1)} %get-tuple-element.48.high.h1), channel_id=1, source_target_pairs={{0,4},{4,8},{8,12},{12,16},{16,20},{20,24},{24,28},{28,32},{32,36}... | collective-permute-start | bytes 393224 | tf_op jit(solution)/shard_map/ppermute | solution.py:420
  74.6 4.7 %collective-permute-start.22 = (f32[2,4,32,128]{3,2,1,0:T(8,128)S(1)}, f32[2,4,32,128]{3,2,1,0:T(8,128)S(1)}, u32[]{:S(2)}, u32[]{:S(2)}) collective-permute-start(f32[2,4,32,128]{3,2,1,0:T(8,128)S(1)} %get-tuple-element.47.low.l1), channel_id=1, source_target_pairs={{0,60},{4,0},{8,4},{12,8},{16,12},{20,16},{24,20},{28,24},{32,28},... | collective-permute-start | bytes 393224 | tf_op jit(solution)/shard_map/ppermute | solution.py:420
  80.2 1.6 %collective-permute-start.23 = (f32[16,128]{1,0:T(8,128)S(1)}, f32[16,128]{1,0:T(8,128)S(1)}, u32[]{:S(2)}, u32[]{:S(2)}) collective-permute-start(f32[16,128]{1,0:T(8,128)S(1)} %get-tuple-element.49), channel_id=1, source_target_pairs={{0,4},{4,8},{8,12},{12,16},{16,20},{20,24},{24,28},{28,32},{32,36}... | collective-permute-start | bytes 24584 | tf_op jit(solution)/shard_map/ppermute | solution.py:420
  80.3 3.1 %collective-permute-start.24 = (f32[16,128]{1,0:T(8,128)S(1)}, f32[16,128]{1,0:T(8,128)S(1)}, u32[]{:S(2)}, u32[]{:S(2)}) collective-permute-start(f32[16,128]{1,0:T(8,128)S(1)} %get-tuple-element.49), channel_id=1, source_target_pairs={{0,60},{4,0},{8,4},{12,8},{16,12},{20,16},{24,20},{28,24},{32,28},... | collective-permute-start | bytes 24584 | tf_op jit(solution)/shard_map/ppermute | solution.py:420
  83.4 4.5 %collective-permute-start.25 = (f32[3,16,128]{2,1,0:T(8,128)S(1)}, f32[3,16,128]{2,1,0:T(8,128)S(1)}, u32[]{:S(2)}, u32[]{:S(2)}) collective-permute-start(f32[3,16,128]{2,1,0:T(8,128)S(1)} %pad_maximum_fusion.9.tri), channel_id=1, source_target_pairs={{0,12},{4,16},{8,20},{12,24},{16,28},{20,32},{24,36},{28,40},{32,4... | collective-permute-start | bytes 73736 | tf_op jit(solution)/shard_map/ppermute | solution.py:420
  83.4 6.8 %collective-permute-start.26 = (f32[3,16,128]{2,1,0:T(8,128)S(1)}, f32[3,16,128]{2,1,0:T(8,128)S(1)}, u32[]{:S(2)}, u32[]{:S(2)}) collective-permute-start(f32[3,16,128]{2,1,0:T(8,128)S(1)} %pad_maximum_fusion.9.tri), channel_id=1, source_target_pairs={{0,52},{4,56},{8,60},{12,0},{16,4},{20,8},{24,12},{28,16},{32,20},... | collective-permute-start | bytes 73736 | tf_op jit(solution)/shard_map/ppermute | solution.py:420
  90.1 2.7 %copy-start.4 = (f32[4,16,16,128]{3,2,1,0:T(8,128)S(1)}, f32[4,16,16,128]{3,2,1,0:T(8,128)}, u32[]{:S(2)}) copy-start(f32[4,16,16,128]{3,2,1,0:T(8,128)} %get-tuple-element.43) | copy-start | bytes 1572868
  92.0 2.8 %collective-permute-start.27 = (f32[2,4,32,128]{3,2,1,0:T(8,128)S(1)}, f32[2,4,32,128]{3,2,1,0:T(8,128)S(1)}, u32[]{:S(2)}, u32[]{:S(2)}) collective-permute-start(f32[2,4,32,128]{3,2,1,0:T(8,128)S(1)} %get-tuple-element.54.high.h2), channel_id=1, source_target_pairs={{0,4},{4,8},{8,12},{12,16},{16,20},{20,24},{24,28},{28,32},{32,36}... | collective-permute-start | bytes 393224 | tf_op jit(solution)/shard_map/ppermute | solution.py:420
  92.9 4.7 %collective-permute-start.28 = (f32[2,4,32,128]{3,2,1,0:T(8,128)S(1)}, f32[2,4,32,128]{3,2,1,0:T(8,128)S(1)}, u32[]{:S(2)}, u32[]{:S(2)}) collective-permute-start(f32[2,4,32,128]{3,2,1,0:T(8,128)S(1)} %get-tuple-element.53.low.l2), channel_id=1, source_target_pairs={{0,60},{4,0},{8,4},{12,8},{16,12},{20,16},{24,20},{28,24},{32,28},... | collective-permute-start | bytes 393224 | tf_op jit(solution)/shard_map/ppermute | solution.py:420
  92.9 30.2 %collective-permute-start.14 = (f32[4,16,16,128]{3,2,1,0:T(8,128)S(1)}, f32[4,16,16,128]{3,2,1,0:T(8,128)S(1)}, u32[]{:S(2)}, u32[]{:S(2)}) collective-permute-start(f32[4,16,16,128]{3,2,1,0:T(8,128)S(1)} %copy-done.4), channel_id=1, source_target_pairs={{0,64},{64,128},{128,192},{192,0},{1,65},{65,129},{129,193},{193,1... | collective-permute-start | bytes 1572872 | tf_op jit(solution)/shard_map/ppermute | solution.py:420
  98.5 1.6 %collective-permute-start.29 = (f32[16,128]{1,0:T(8,128)S(1)}, f32[16,128]{1,0:T(8,128)S(1)}, u32[]{:S(2)}, u32[]{:S(2)}) collective-permute-start(f32[16,128]{1,0:T(8,128)S(1)} %get-tuple-element.55), channel_id=1, source_target_pairs={{0,4},{4,8},{8,12},{12,16},{16,20},{20,24},{24,28},{28,32},{32,36}... | collective-permute-start | bytes 24584 | tf_op jit(solution)/shard_map/ppermute | solution.py:420
  98.5 3.4 %collective-permute-start.30 = (f32[16,128]{1,0:T(8,128)S(1)}, f32[16,128]{1,0:T(8,128)S(1)}, u32[]{:S(2)}, u32[]{:S(2)}) collective-permute-start(f32[16,128]{1,0:T(8,128)S(1)} %get-tuple-element.55), channel_id=1, source_target_pairs={{0,60},{4,0},{8,4},{12,8},{16,12},{20,16},{24,20},{28,24},{32,28},... | collective-permute-start | bytes 24584 | tf_op jit(solution)/shard_map/ppermute | solution.py:420
  101.9 4.8 %collective-permute-start.31 = (f32[3,16,128]{2,1,0:T(8,128)S(1)}, f32[3,16,128]{2,1,0:T(8,128)S(1)}, u32[]{:S(2)}, u32[]{:S(2)}) collective-permute-start(f32[3,16,128]{2,1,0:T(8,128)S(1)} %pad_maximum_fusion.10.tri), channel_id=1, source_target_pairs={{0,12},{4,16},{8,20},{12,24},{16,28},{20,32},{24,36},{28,40},{32,4... | collective-permute-start | bytes 73736 | tf_op jit(solution)/shard_map/ppermute | solution.py:420
  102.2 6.7 %collective-permute-start.32 = (f32[3,16,128]{2,1,0:T(8,128)S(1)}, f32[3,16,128]{2,1,0:T(8,128)S(1)}, u32[]{:S(2)}, u32[]{:S(2)}) collective-permute-start(f32[3,16,128]{2,1,0:T(8,128)S(1)} %pad_maximum_fusion.10.tri), channel_id=1, source_target_pairs={{0,52},{4,56},{8,60},{12,0},{16,4},{20,8},{24,12},{28,16},{32,20},... | collective-permute-start | bytes 73736 | tf_op jit(solution)/shard_map/ppermute | solution.py:420
  110.7 2.6 %collective-permute-start.33 = (f32[2,4,32,128]{3,2,1,0:T(8,128)S(1)}, f32[2,4,32,128]{3,2,1,0:T(8,128)S(1)}, u32[]{:S(2)}, u32[]{:S(2)}) collective-permute-start(f32[2,4,32,128]{3,2,1,0:T(8,128)S(1)} %get-tuple-element.60.h3.high), channel_id=1, source_target_pairs={{0,4},{4,8},{8,12},{12,16},{16,20},{20,24},{24,28},{28,32},{32,36}... | collective-permute-start | bytes 393224 | tf_op jit(solution)/shard_map/ppermute | solution.py:420
  111.4 4.7 %collective-permute-start.34 = (f32[2,4,32,128]{3,2,1,0:T(8,128)S(1)}, f32[2,4,32,128]{3,2,1,0:T(8,128)S(1)}, u32[]{:S(2)}, u32[]{:S(2)}) collective-permute-start(f32[2,4,32,128]{3,2,1,0:T(8,128)S(1)} %get-tuple-element.59.l3.low), channel_id=1, source_target_pairs={{0,60},{4,0},{8,4},{12,8},{16,12},{20,16},{24,20},{28,24},{32,28},... | collective-permute-start | bytes 393224 | tf_op jit(solution)/shard_map/ppermute | solution.py:420
  117.0 1.4 %collective-permute-start.35 = (f32[16,128]{1,0:T(8,128)S(1)}, f32[16,128]{1,0:T(8,128)S(1)}, u32[]{:S(2)}, u32[]{:S(2)}) collective-permute-start(f32[16,128]{1,0:T(8,128)S(1)} %get-tuple-element.61), channel_id=1, source_target_pairs={{0,4},{4,8},{8,12},{12,16},{16,20},{20,24},{24,28},{28,32},{32,36}... | collective-permute-start | bytes 24584 | tf_op jit(solution)/shard_map/ppermute | solution.py:420
  117.0 3.1 %collective-permute-start.36 = (f32[16,128]{1,0:T(8,128)S(1)}, f32[16,128]{1,0:T(8,128)S(1)}, u32[]{:S(2)}, u32[]{:S(2)}) collective-permute-start(f32[16,128]{1,0:T(8,128)S(1)} %get-tuple-element.61), channel_id=1, source_target_pairs={{0,60},{4,0},{8,4},{12,8},{16,12},{20,16},{24,20},{28,24},{32,28},... | collective-permute-start | bytes 24584 | tf_op jit(solution)/shard_map/ppermute | solution.py:420
  120.1 4.5 %collective-permute-start.37 = (f32[3,16,128]{2,1,0:T(8,128)S(1)}, f32[3,16,128]{2,1,0:T(8,128)S(1)}, u32[]{:S(2)}, u32[]{:S(2)}) collective-permute-start(f32[3,16,128]{2,1,0:T(8,128)S(1)} %pad_maximum_fusion.11.tri), channel_id=1, source_target_pairs={{0,12},{4,16},{8,20},{12,24},{16,28},{20,32},{24,36},{28,40},{32,4... | collective-permute-start | bytes 73736 | tf_op jit(solution)/shard_map/ppermute | solution.py:420
  120.9 6.2 %collective-permute-start.38 = (f32[3,16,128]{2,1,0:T(8,128)S(1)}, f32[3,16,128]{2,1,0:T(8,128)S(1)}, u32[]{:S(2)}, u32[]{:S(2)}) collective-permute-start(f32[3,16,128]{2,1,0:T(8,128)S(1)} %pad_maximum_fusion.11.tri), channel_id=1, source_target_pairs={{0,52},{4,56},{8,60},{12,0},{16,4},{20,8},{24,12},{28,16},{32,20},... | collective-permute-start | bytes 73736 | tf_op jit(solution)/shard_map/ppermute | solution.py:420

commit v3 on v2

v3 whole, which is shorter than its diff:
```python
import jax
import jax.numpy as jnp
from jax import lax
from jax.experimental import pallas as pl
from jax.experimental.pallas import tpu as pltpu
from jax.sharding import PartitionSpec as P

F32 = jnp.float32
HIGH = lax.Precision.HIGHEST


def call(body, outs, args, scratch=(), smem=0, limit=24, far=False):
    vmem = pl.BlockSpec(memory_space=pltpu.VMEM)
    scalar = pl.BlockSpec(memory_space=pltpu.SMEM)
    single = not isinstance(outs, list)
    shapes = [outs] if single else outs
    got = pl.pallas_call(
        body,
        out_shape=[jax.ShapeDtypeStruct(s, F32) for s in shapes],
        in_specs=[scalar] * smem
        + [pl.BlockSpec(memory_space=pl.ANY) if far else vmem] * (len(args) - smem),
        out_specs=[vmem] * len(shapes),
        scratch_shapes=[pltpu.VMEM(s, F32) for s in scratch]
        + ([pltpu.SemaphoreType.DMA((3, 4))] if far else []),
        compiler_params=pltpu.CompilerParams(vmem_limit_bytes=limit * 2**20),
        name=body.__name__,
    )(*args)
    return got[0] if single else got


def shifted(value, amount, axis):
    return pltpu.roll(value, amount % value.shape[axis], axis)


def nxt(value, step, axis):
    return shifted(value, -step, axis)


def prv(value, step, axis):
    return shifted(value, step, axis)


def index_along(shape, axis):
    return lax.broadcasted_iota(jnp.int32, shape, axis)


def pair_sum(value, step, axis):
    upper = (index_along(value.shape, axis) // step) % 2 == 1
    return value + jnp.where(upper, prv(value, step, axis), nxt(value, step, axis))


def ring_sum(value, step_y, step_z):
    return (
        nxt(value, step_y, 0)
        + prv(value, step_y, 0)
        + nxt(value, step_z, 1)
        + prv(value, step_z, 1)
    )


def restricted_defect(before, first, second, after, step_y, step_z):
    both = first + second
    total = both * (1.0 / 3.0) + (before + both + after + ring_sum(both, step_y, step_z)) * (1.0 / 9.0)
    return pair_sum(pair_sum(total, step_y, 0), step_z, 1) * 0.125


def smoothed(before, here, after, source, spacing_sq, step_y, step_z):
    around = before + after + ring_sum(here, step_y, step_z)
    return here * (1.0 / 3.0) + (around - spacing_sq * source) * (1.0 / 9.0)


def deep_pressure(r3, step_y, step_z):
    r4 = [
        restricted_defect(r3[2 * w], r3[2 * w + 1], r3[2 * w + 2], r3[2 * w + 3], step_y, step_z)
        for w in range(7)
    ]
    low_y, low_z = 2 * step_y, 2 * step_z
    p4 = [r * (-256.0 / 9.0) for r in r4]
    for sweep in range(2):
        inner = range(1 + sweep, 6 - sweep)
        fresh = {w: smoothed(p4[w - 1], p4[w], p4[w + 1], r4[w], 256.0, low_y, low_z) for w in inner}
        p4 = [fresh.get(w) for w in range(7)]
    e3 = {q: r3[q] * (-64.0 / 9.0) + p4[(q - 7) // 2 + 3] for q in range(5, 11)}
    return [
        smoothed(e3[q - 1], e3[q], e3[q + 1], r3[q], 64.0, step_y, step_z) for q in range(6, 10)
    ]


def advected(ref, i, comp):
    here = ref[comp, i]
    grad_x = ref[comp, i + 1] - ref[comp, i - 1]
    grad_y = nxt(here, 1, 0) - prv(here, 1, 0)
    grad_z = nxt(here, 1, 1) - prv(here, 1, 1)
    return ref[0, i] * grad_x + ref[1, i] * grad_y + ref[2, i] * grad_z


def z_pick(high):
    k = index_along((128, 128), 0)
    j = index_along((128, 128), 1)
    return jnp.where(k // 2 == j - 64 * high, 1.0, 0.0).astype(F32)


def z_spread(high):
    k = index_along((128, 128), 0)
    j = index_along((128, 128), 1)
    return jnp.where(k == j // 2 + 64 * high, 1.0, 0.0).astype(F32)


def dot(a, b):
    return lax.dot_general(a, b, (((1,), (0,)), ((), ())), precision=HIGH, preferred_element_type=F32)


def packed_pairs(half, rows):
    low, high = z_pick(0), z_pick(1)
    packed = []
    for h in range(2):
        value = dot(half[2 * h].reshape(rows, 128), low)
        if 2 * h + 1 < half.shape[0]:
            value = value + dot(half[2 * h + 1].reshape(rows, 128), high)
        packed.append(0.125 * value)
    return packed


def restricted_packed(fine, rows, half):
    for comp in range(4):
        for big in range(8):
            rows[comp, big] = fine[comp, 2 * big] + fine[comp, 2 * big + 1]
    for comp in range(4):
        for big in range(8):
            half[comp, big] = rows[comp, big, pl.ds(0, 8, 2), :] + rows[comp, big, pl.ds(1, 8, 2), :]
    return packed_pairs(half, 64)


def pack_body(
    initial_far, begin_far, end_far, x_low, x_high, y_low, y_high, opening,
    rows, half, initial, begin, end, arrived
):
    copies = [
        pltpu.make_async_copy(far.at[c], near.at[c], arrived.at[n, c])
        for n, (far, near) in enumerate(
            ((begin_far, begin), (end_far, end), (initial_far, initial))
        )
        for c in range(4)
    ]
    for copy in copies:
        copy.start()
    for copy in copies[:8]:
        copy.wait()
    for f in range(8):
        ref = begin if f < 4 else end
        x_low[f] = ref[f % 4, 0]
        x_high[f] = ref[f % 4, 15]
        for x in range(16):
            y_low[f, x : x + 1, :] = ref[f % 4, x, 0:1, :]
            y_high[f, x : x + 1, :] = ref[f % 4, x, 15:16, :]
    for copy in copies[8:]:
        copy.wait()
    packed = restricted_packed(initial, rows, half)
    for h in range(2):
        for x in range(4):
            block = packed[h][16 * x : 16 * x + 16]
            opening[4 * h + x] = block
            y_low[8 + 4 * h + x] = block
            y_high[8 + 4 * h + x] = block


def join_body(below, own, above, across, low, high):
    for b, (ref, first) in enumerate(((below, 8), (own, 0), (above, 8), (across, 0))):
        for h in range(2):
            for x in range(8):
                side = low if x < 4 else high
                side[h, x % 4, 8 * b : 8 * b + 8, :] = ref[
                    first + 4 * h + x // 2, 8 * (x % 2) : 8 * (x % 2) + 8
                ]


def level2_pressure(r2, first, e2, step_z):
    r3 = [
        restricted_defect(
            r2[first + 2 * q + 1], r2[first + 2 * q + 2], r2[first + 2 * q + 3], r2[first + 2 * q + 4], 1, step_z
        )
        for q in range(16)
    ]
    p3 = deep_pressure(r3, 2, 2 * step_z)
    for i in range(8):
        e2[i] = r2[first + 14 + i] * (-16.0 / 9.0) + p3[i // 2]
    return [
        smoothed(e2[i], e2[i + 1], e2[i + 2], r2[first + 15 + i], 16.0, 1, step_z) for i in range(6)
    ]


def ordered(where, got, rows, base, size, blocks):
    own, partner, near, far, swapped = got
    k = where[1]
    blocks[4 + k, 0:size] = own[base : base + size]
    blocks[5 - k, 0:size] = partner[base : base + size]
    for j in range(2):
        low = rows * j + base
        turn = j * (2 * k - 1)
        blocks[3 + 3 * k + turn, 0:size] = near[low : low + size]
        blocks[1 + 7 * k + turn, 0:size] = far[low : low + size]
        blocks[6 - 3 * k - turn, 0:size] = swapped[low : low + size]
        blocks[8 - 7 * k - turn, 0:size] = swapped[2 * rows + low : 2 * rows + low + size]


def bit_lane(value, lane, step, bit):
    same = (lane // step) % 2 == bit
    return jnp.where(same, value, nxt(value, step, 1) if bit else prv(value, step, 1))


def fine_source_body(begin, end, left, right, low, high, old, comb, out, rows, half):
    row = index_along((16, 128), 0)
    first, last = row == 0, row == 15

    def at(f, x):
        if x < 0:
            return left[f]
        if x > 15:
            return right[f]
        return (begin if f < 4 else end)[f % 4, x]

    def carried(f, x):
        base = f - f % 4
        here = at(f, x)
        grad_x = at(f, x + 1) - at(f, x - 1)
        above = jnp.where(last, high[f, x : x + 1, :], nxt(here, 1, 0))
        below = jnp.where(first, low[f, x : x + 1, :], prv(here, 1, 0))
        grad_z = nxt(here, 1, 1) - prv(here, 1, 1)
        return at(base, x) * grad_x + at(base + 1, x) * (above - below) + at(base + 2, x) * grad_z

    for x in range(16):
        for c in range(4):
            total = begin[c, x] - 0.125 * (carried(c, x) + carried(c + 4, x))
            if c == 2:
                total = total + 0.25 * (begin[3, x] + end[3, x])
            comb[c, x] = total
    out[0] = 0.5 * comb[0, 0]
    out[17] = -0.5 * comb[0, 15]
    for x in range(16):
        v = comb[1, x]
        w = comb[2, x]
        div = jnp.where(last, 0.0, nxt(v, 1, 0)) - jnp.where(first, 0.0, prv(v, 1, 0))
        div = div + nxt(w, 1, 1) - prv(w, 1, 1)
        if x < 15:
            div = div + comb[0, x + 1]
        if x > 0:
            div = div - comb[0, x - 1]
        out[x + 1] = 0.5 * div
        out[18, x : x + 1, :] = 0.5 * v[0:1]
        out[19, x : x + 1, :] = -0.5 * v[15:16]
    packed = restricted_packed(comb, rows, half)
    for h in range(2):
        for x in range(4):
            out[20 + 4 * h + x, 0:8] = packed[h][16 * x : 16 * x + 8] - old[h, 2 * x]
            out[20 + 4 * h + x, 8:16] = packed[h][16 * x + 8 : 16 * x + 16] - old[h, 2 * x + 1]


def fine_down_body(
    where, below, own, above, across, coarse,
    message, inner, outer, r0, r1, r2
):
    blocks = (below, own, above, across)
    for b, ref in enumerate(blocks):
        r0[:, 16 * b : 16 * b + 16] = ref[0:18]
    message[32:48] = coarse[...]
    for b in range(4):
        upper, lower = blocks[(b + 1) % 4], blocks[(b + 3) % 4]
        for x in range(16):
            r0[x + 1, 16 * b + 15 : 16 * b + 16] += upper[18, x : x + 1, :]
            r0[x + 1, 16 * b : 16 * b + 1] += lower[19, x : x + 1, :]
    zero = jnp.zeros((64, 128), F32)

    def at0(x):
        return r0[x + 1] if -1 <= x < 17 else zero

    def at1(x):
        return r1[x + 1] if -1 <= x < 9 else zero

    for x in range(-1, 9):
        r1[x + 1] = restricted_defect(at0(2 * x - 1), at0(2 * x), at0(2 * x + 1), at0(2 * x + 2), 1, 1)
    for x in range(-1, 5):
        r2[x + 1] = restricted_defect(at1(2 * x - 1), at1(2 * x), at1(2 * x + 1), at1(2 * x + 2), 2, 2)
    lane = index_along((16, 128), 1)
    part = [r2[i, pl.ds(0, 16, 4), :] for i in range(6)]
    odd = lane % 2 == 1
    first = jnp.where(
        lane % 4 < 2, jnp.where(odd, part[1], part[0]), jnp.where(odd, part[3], part[2])
    )
    second = jnp.where(odd, part[5], part[4])
    message[0:16] = first
    message[16:32] = second
    k = where[1]
    for i in range(6):
        inner[64 * i : 64 * i + 64] = r0[12 - 12 * k + i]
        outer[64 * i : 64 * i + 64] = r0[12 * k + i]


def fine_up_body(
    where, own, partner, near, far, swapped, face_in, face_out, mine, comb, below, own_share, above, across_jump, fine, jump,
    r0, r1, r2, e2, p2, e1, p1, e0, p0, rows, half, blocks
):
    k = where[1]
    ordered(where, (own, partner, near, far, swapped), 48, 0, 32, blocks)
    r0[5:21] = mine[1:17]
    for i in range(6):
        inside = face_in[64 * i : 64 * i + 64]
        outside = face_out[64 * i : 64 * i + 64]
        left = jnp.where(k == 0, outside, inside)
        right = jnp.where(k == 0, inside, outside)
        if i < 5:
            r0[i] = left
        else:
            r0[5] += left
        if i > 0:
            r0[20 + i] = right
        else:
            r0[20] += right
    r0[4] += mine[0]
    r0[21] += mine[17]
    lane = index_along((16, 128), 1)
    parts = []
    for j in range(10):
        first, second = blocks[j, 0:16], blocks[j, 16:32]
        even, odd = bit_lane(first, lane, 2, 0), bit_lane(first, lane, 2, 1)
        parts.append(
            [
                bit_lane(even, lane, 1, 0),
                bit_lane(even, lane, 1, 1),
                bit_lane(odd, lane, 1, 0),
                bit_lane(odd, lane, 1, 1),
                bit_lane(second, lane, 1, 0),
                bit_lane(second, lane, 1, 1),
            ]
        )
    for j in range(10):
        for n in range(4):
            value = parts[j][n + 1]
            if n == 0 and j > 0:
                value = value + parts[j - 1][5]
            if n == 3 and j < 9:
                value = value + parts[j + 1][0]
            r2[4 * j + n] = value
    for i, value in enumerate(level2_pressure(r2, 4 * k, e2, 4)):
        for y2 in range(16):
            p2[i, 4 * y2 : 4 * y2 + 4, :] = jnp.broadcast_to(value[y2 : y2 + 1], (4, 128))
    for k in range(12):
        a = 2 * k + 1
        r1[k] = restricted_defect(r0[a - 1], r0[a], r0[a + 1], r0[a + 2], 1, 1)
        e1[k] = r1[k] * (-4.0 / 9.0) + p2[k // 2]
    for k in range(10):
        p1[k] = smoothed(e1[k], e1[k + 1], e1[k + 2], r1[k + 1], 4.0, 2, 2)
    for j in range(20):
        e0[j] = r0[j + 3] * (-1.0 / 9.0) + p1[j // 2]
    for j in range(18):
        p0[j] = smoothed(e0[j], e0[j + 1], e0[j + 2], r0[j + 4], 1.0, 1, 1)
    for big in range(8):
        a = 2 * big + 1
        pair = p0[a] + p0[a + 1]
        rows[0, big] = p0[a + 1] + p0[a + 2] - p0[a - 1] - p0[a]
        rows[1, big] = nxt(pair, 1, 0) - prv(pair, 1, 0)
        rows[2, big] = nxt(pair, 1, 1) - prv(pair, 1, 1)
    for c in range(3):
        for big in range(8):
            half[c, big] = rows[c, big, pl.ds(0, 32, 2), :] + rows[c, big, pl.ds(1, 32, 2), :]
    packed = packed_pairs(half, 256)
    for h in range(2):
        slope = 0.5 * packed[h].reshape(8, 32, 128)
        for b, (ref, first) in enumerate(((below, 20), (own_share, 20), (above, 20), (across_jump, 0))):
            for x in range(8):
                jump[h, x, 8 * b : 8 * b + 8] = (
                    ref[first + 4 * h + x // 2, 8 * (x % 2) : 8 * (x % 2) + 8]
                    - slope[x, 8 * b : 8 * b + 8]
                )
    for x in range(16):
        here = p0[x + 1, 8:40]
        fine[0, x] = comb[0, x] - 0.5 * (p0[x + 2, 16:32] - p0[x, 16:32])
        fine[1, x] = comb[1, x] - 0.5 * (nxt(here, 1, 0) - prv(here, 1, 0))[8:24]
        mid = here[8:24]
        fine[2, x] = comb[2, x] - 0.5 * (nxt(mid, 1, 1) - prv(mid, 1, 1))
        fine[3, x] = comb[3, x]


def coarse_down_body(before, low, high, after, comb_out, r1, message, state, comb, r2):
    lane = index_along((32, 128), 1)
    for side, ref in enumerate((before, low, high, after)):
        for x in range(4):
            for h in range(2):
                pair = ref[h, x]
                other = shifted(pair, 64, 1)
                state[2 * h, 4 * side + x] = jnp.where(lane < 64, pair, other)
                state[2 * h + 1, 4 * side + x] = jnp.where(lane < 64, other, pair)
    message[...] = coarse_down_core(comb_out, r1, state, comb, r2)


def coarse_down_core(comb_out, r1, state, comb, r2):
    for i in range(1, 15):
        for c in range(3):
            total = state[c, i] - 0.125 * advected(state, i, c)
            if c == 2:
                total = total + 0.5 * state[3, i]
            comb[c, i - 1] = total
            if 4 <= i < 12:
                comb_out[c, i - 4] = total
    for x in range(8):
        comb_out[3, x] = state[3, x + 4] - 0.125 * advected(state, x + 4, 3)
    for k in range(12):
        v = comb[1, k + 1]
        w = comb[2, k + 1]
        div = comb[0, k + 2] - comb[0, k] + nxt(v, 1, 0) - prv(v, 1, 0) + nxt(w, 1, 1) - prv(w, 1, 1)
        r1[k] = 0.25 * div
    for m in range(4):
        a = 2 * m + 2
        r2[m] = restricted_defect(r1[a - 1], r1[a], r1[a + 1], r1[a + 2], 1, 1)
    part = [r2[m, pl.ds(0, 16, 2), :] for m in range(4)]
    lane = index_along((16, 128), 1)
    odd = lane % 2 == 1
    return jnp.where(
        lane < 64, jnp.where(odd, part[1], part[0]), jnp.where(odd, part[3], part[2])
    )


def coarse_up_core(where, rows, base, got, comb, r1, blocks, r2, e2, p2, e1, p1, emit):
    ordered(where, got, rows, base, 16, blocks)
    lane = index_along((16, 128), 1)
    for j in range(10):
        block = blocks[j]
        other = shifted(block, 64, 1)
        for m, pair in enumerate(
            (jnp.where(lane < 64, block, other), jnp.where(lane < 64, other, block))
        ):
            r2[4 * j + 2 * m] = bit_lane(pair, lane, 1, 0)
            r2[4 * j + 2 * m + 1] = bit_lane(pair, lane, 1, 1)
    for i, value in enumerate(level2_pressure(r2, 4 * where[1], e2, 2)):
        p2[i, pl.ds(0, 16, 2), :] = value
        p2[i, pl.ds(1, 16, 2), :] = value
    for k in range(12):
        e1[k] = r1[k] * (-4.0 / 9.0) + p2[k // 2]
    for k in range(10):
        p1[k] = smoothed(e1[k], e1[k + 1], e1[k + 2], r1[k + 1], 4.0, 1, 1)
    lane = index_along((32, 128), 1)
    for x in range(8):
        here = p1[x + 1]
        u = comb[0, x] - 0.25 * (p1[x + 2] - p1[x])
        v = comb[1, x] - 0.25 * (nxt(here, 1, 0) - prv(here, 1, 0))
        w = comb[2, x] - 0.25 * (nxt(here, 1, 1) - prv(here, 1, 1))
        emit(0, x, jnp.where(lane < 64, u, v))
        emit(1, x, jnp.where(lane < 64, w, comb[3, x]))


UP_SCRATCH = [(10, 16, 128), (40, 16, 128), (8, 16, 128), (6, 32, 128), (12, 32, 128), (10, 32, 128)]


def coarse_up_next_body(
    rows, base, where, a, b, c, d, e, comb, r1, jump, ended, own, low, high, *scratch
):
    def emit(h, x, value):
        after = value + jump[h, x]
        ref = low if x < 4 else high
        ref[h, x % 4] = after
        ended[h, x] = value[8:16]
        own[h, x] = after[8:16]

    coarse_up_core(where, rows, base, (a, b, c, d, e), comb, r1, *scratch, emit)


def coarse_up_first_body(*refs):
    coarse_up_next_body(48, 32, *refs)


def coarse_up_middle_body(*refs):
    coarse_up_next_body(16, 0, *refs)


def coarse_up_last_body(where, a, b, c, d, e, comb, r1, ended, *scratch):
    def emit(h, x, value):
        ended[h, x] = value[8:16]

    coarse_up_core(where, 16, 0, (a, b, c, d, e), comb, r1, *scratch, emit)


def new_start_body(where, fine, initial, state, out, rows, half, tall):
    t = where[0]

    @pl.when(t == 0)
    def _():
        out[...] = initial[...]

    @pl.when(t > 0)
    def _():
        packed = restricted_packed(fine, rows, half)
        for h in range(2):
            change = state[h].reshape(64, 128) - packed[h]
            for side in range(2):
                comp = 2 * h + side
                wide = dot(change, z_spread(side)).reshape(8, 8, 128)
                for x in range(8):
                    tall[comp, x, pl.ds(0, 8, 2), :] = wide[x]
                    tall[comp, x, pl.ds(1, 8, 2), :] = wide[x]
        for comp in range(4):
            for x in range(16):
                out[comp, x] = fine[comp, x] + tall[comp, x // 2]


def coarse_end_body(where, e0, e1, e2, e3, out):
    t = where[0]
    for h in range(2):
        low = jnp.where(t == 0, e0[h], e1[h])
        high = jnp.where(t == 2, e2[h], e3[h])
        value = jnp.where(t < 2, low, high)
        out[2 * h] = value[:, :, :64]
        out[2 * h + 1] = shifted(value, 64, 2)[:, :, :64]


def moved(value, axis, step):
    count = lax.axis_size(axis)
    return lax.ppermute(value, axis, [(i, (i + step) % count) for i in range(count)])


def both_sides(low_face, high_face, axis, step=1):
    return moved(high_face, axis, step), moved(low_face, axis, -step)


def around(value, axis):
    return [moved(value, axis, step) for step in range(1, 4)]


def swapped_cores(value):
    return lax.ppermute(value, "sx", [(i, i ^ 1) for i in range(lax.axis_size("sx"))])


def from_chips(value, chips):
    count = lax.axis_size("sx")
    far = 2 * chips - 1
    return lax.ppermute(
        value, "sx", [(i, (i + (far if i % 2 else -far)) % count) for i in range(count)]
    )


def five_chips(message):
    partner = swapped_cores(message)
    both = jnp.concatenate([message, partner], axis=0)
    near, far = from_chips(both, 1), from_chips(both, 2)
    return [message, partner, near, far, swapped_cores(jnp.concatenate([near, far], axis=0))]


def sent(value, source, target):
    return lax.ppermute(value, "tm", [(source, target)])


def shards(initial_state, start_old, end_old, coarse_old):
    begin, end, old = start_old[0], end_old[0], coarse_old[0]
    where = jnp.stack([lax.axis_index("tm"), lax.axis_index("sx") % 2]).astype(jnp.int32)

    x_low, x_high, y_low, y_high, opening = call(
        pack_body,
        [(8, 16, 128)] * 2 + [(16, 16, 128)] * 2 + [(8, 16, 128)],
        [initial_state, begin, end],
        [(4, 8, 16, 128), (4, 8, 8, 128)] + [(4, 16, 16, 128)] * 3,
        limit=56,
        far=True,
    )
    old_packed = jnp.stack(
        [jnp.concatenate([old[0], old[1]], axis=-1), jnp.concatenate([old[2], old[3]], axis=-1)]
    )
    left, right = both_sides(x_low, x_high, "sx")
    low, high = both_sides(y_low, y_high, "sy")
    opening_across = moved(opening, "sy", 2)
    comb, share = call(
        fine_source_body,
        [(4, 16, 16, 128), (28, 16, 128)],
        [begin, end, left, right, low, high, old_packed],
        [(4, 8, 16, 128), (4, 8, 8, 128)],
    )
    c0 = call(join_body, [(2, 4, 32, 128)] * 2, [low, opening, high, opening_across])
    share, c0 = lax.optimization_barrier((share, c0))
    below, above = both_sides(share, share, "sy")
    across = moved(share[:20], "sy", 2)

    def coarse_down(state):
        low, high = state
        before, after = both_sides(low, high, "sx")
        return call(
            coarse_down_body,
            [(4, 8, 32, 128), (12, 32, 128), (16, 128)],
            [before, low, high, after],
            [(4, 16, 32, 128), (3, 14, 32, 128), (4, 32, 128)],
        )

    comb0, first0, message0 = coarse_down(c0)
    message, inner, outer, r0 = call(
        fine_down_body,
        [(48, 128), (384, 128), (384, 128), (18, 64, 128)],
        [where, below, share, above, across, message0],
        [(10, 64, 128), (6, 64, 128)],
        smem=1,
    )
    across_jump = moved(share[20:], "sy", 2)
    partner = swapped_cores(jnp.concatenate([message, inner], axis=0))
    both = jnp.concatenate([message, partner[:48]], axis=0)
    near, far = from_chips(jnp.concatenate([both, outer], axis=0), 1), from_chips(both, 2)
    near, far, across_jump = lax.optimization_barrier((near, far, across_jump))
    crossed = swapped_cores(jnp.concatenate([near[:96], far], axis=0))
    got = [message, partner, near, far, crossed]
    fine_end, jump0 = call(
        fine_up_body,
        [(4, 16, 16, 128), (2, 8, 32, 128)],
        [where] + got + [partner[48:], near[96:], r0, comb, below, share, above, across_jump],
        [
            (26, 64, 128),
            (12, 64, 128),
            (40, 16, 128),
            (8, 16, 128),
            (6, 64, 128),
            (12, 64, 128),
            (10, 64, 128),
            (20, 64, 128),
            (18, 64, 128),
            (3, 8, 64, 128),
            (3, 8, 32, 128),
            (10, 32, 128),
        ],
        smem=1,
    )

    def coarse_up(body, got, combined, level1, jump):
        ended, own, low, high = call(
            body,
            [(2, 8, 8, 128)] * 2 + [(2, 4, 32, 128)] * 2,
            [where] + got + [combined, level1, jump],
            UP_SCRATCH,
            smem=1,
        )
        return ended, own, [low, high]

    ended0, own1, c1 = coarse_up(coarse_up_first_body, got, comb0, first0, jump0)
    jump1 = lax.ppermute(jump0, "tm", [(1, 0), (2, 1)])
    fine_before = moved(fine_end, "tm", 1)

    combined, level1, message = coarse_down(c1)
    got, jump1 = lax.optimization_barrier((five_chips(message), jump1))
    ended1, own2, c2 = coarse_up(coarse_up_middle_body, got, combined, level1, jump1)

    combined, level1, message = coarse_down(c2)
    jump2 = sent(jump1, 1, 0)
    hand1 = sent(jnp.concatenate([own1, ended1], axis=0), 0, 1)
    got, hand1, jump2, fine_before = lax.optimization_barrier(
        (five_chips(message), hand1, jump2, fine_before)
    )
    ended2, own3, c3 = coarse_up(coarse_up_middle_body, got, combined, level1, jump2)

    combined, level1, message = coarse_down(c3)
    hand2 = sent(jnp.concatenate([own2, ended2], axis=0), 0, 2)
    hand3 = sent(own3, 0, 3)
    got, hand2, hand3 = lax.optimization_barrier((five_chips(message), hand2, hand3))
    ended3 = call(
        coarse_up_last_body,
        (2, 8, 8, 128),
        [where] + got + [combined, level1],
        UP_SCRATCH,
        smem=1,
    )
    new_start = call(
        new_start_body,
        (4, 16, 16, 128),
        [where, fine_before, initial_state, hand1[:2] + hand2[:2] + hand3],
        [(4, 8, 16, 128), (4, 8, 8, 128), (4, 8, 16, 128)],
        smem=1,
    )
    coarse_end = call(
        coarse_end_body,
        (4, 8, 8, 64),
        [where, ended0, hand1[2:], hand2[2:], sent(ended3, 0, 3)],
        smem=1,
    )
    return (new_start[None], fine_end[None], coarse_end[None])


def solution(mesh):
    in_specs = (
        P(None, "sx", "sy", None),
        P("tm", None, "sx", "sy", None),
        P("tm", None, "sx", "sy", None),
        P("tm", None, "sx", "sy", None),
    )
    out_specs = (
        P("tm", None, "sx", "sy", None),
        P("tm", None, "sx", "sy", None),
        P("tm", None, "sx", "sy", None),
    )
    return jax.shard_map(shards, mesh=mesh, in_specs=in_specs, out_specs=out_specs, check_vma=False)
```

time: 130 us -> 117 us (0.900)
  waiting for transfers between devices: 49.8 us -> 27.8 us
  starting transfers between devices: 57.8 us -> 62.7 us
  Pallas kernels: 19.2 us -> 24.1 us
    ppermute x0 -> x22, starting transfers between devices: none -> 37.9 us  [the longest x8 14.6 us: from_chips(): lax.ppermute(value, 'sx', [(i, (i + (far if i % 2 else -far)) % count) fo...]
    ppermute x39 -> x18, waiting for transfers between devices: 49.8 us -> 14.2 us  [moved(): lax.ppermute(value, axis, [(i, (i + step) % count) for i in range(count)])]
    ppermute x39 -> x18, starting transfers between devices: 57.8 us -> 24.8 us  [moved(): lax.ppermute(value, axis, [(i, (i + step) % count) for i in range(count)])]
    ppermute x0 -> x22, waiting for transfers between devices: none -> 13.6 us  [the longest x8 5.67 us: swapped_cores(): lax.ppermute(value, 'sx', [(i, i ^ 1) for i in range(lax.axis_size('sx'))])]
    pallas_call x15, Pallas kernels: 19.2 us -> 24.1 us  [call(): pl.pallas_call(body, out_shape=[jax.ShapeDtypeStruct(s, F32) for s in sha...]
  transfers between devices with their start and end apart: 39 -> 40, of which waited for: 32 -> 19; matrix products, arithmetic and copies ran while one was open for 0% -> 0% of each run, Pallas kernels for 7% -> 4%
where the time goes in v3:
time: 117 us; the launch traced here: 116 us
  starting transfers between devices  62.7 us (54%)
  waiting for transfers between devices  27.8 us (24%)
  Pallas kernels  24.1 us (21%)
    ppermute x18, starting transfers between devices, moved(): lax.ppermute(value, axis, [(i, (i + step) % count) for i in range(count)])  24.8 us
    pallas_call x15, Pallas kernels, call(): pl.pallas_call(body, out_shape=[jax.ShapeDtypeStruct(s, F32) for s in sha...  24.1 us
    ppermute x8, starting transfers between devices, from_chips(): lax.ppermute(value, 'sx', [(i, (i + (far if i % 2 else -far)) % count) fo...  14.6 us
    ppermute x18, waiting for transfers between devices, moved(): lax.ppermute(value, axis, [(i, (i + step) % count) for i in range(count)])  14.2 us
    ppermute x8, starting transfers between devices, swapped_cores(): lax.ppermute(value, 'sx', [(i, i ^ 1) for i in range(lax.axis_size('sx'))])  11.5 us
    ppermute x5, starting transfers between devices, sent(): return lax.ppermute(value, 'tm', [(source, target)])  10.5 us
    ppermute x8, waiting for transfers between devices, swapped_cores(): lax.ppermute(value, 'sx', [(i, i ^ 1) for i in range(lax.axis_size('sx'))])  5.67 us
    ppermute x5, waiting for transfers between devices, sent(): return lax.ppermute(value, 'tm', [(source, target)])  4.44 us
  transfers between devices with their start and end apart: 40, of which 19 were waited for; matrix products, arithmetic and copies ran while one was open for 0% of the time, Pallas kernels for 4%

profile of v3, /device:TPU:1, one launch (start us, length us, event | category | flops | bytes accessed | tf_op | source)
XLA Modules:
  0.0 116.0 jit_solution(165246698555266985)
XLA Ops:
  0.7 2.7 %pack_body.1 = (f32[8,16,128]{2,1,0:T(8,128)}, f32[8,16,128]{2,1,0:T(8,128)}, f32[16,16,128]{2,1,0:T(8,128)}, f32[16,16,128]{2,1,0:T(8,128)}, f32[8,16,128]{2,1,0:T(8,128)}) custom-call(f32[4,16,16,128]{3,2,1,0:T(8,128)} %initial.1, f32[4,16,16,128]{3,2,1,0:T(8,128)} %bitcast.19, f32[4,16,16,128]{3,2,1,0:T(8,128)} %bitcast.21), custom_call_target="tpu_custom_call" | custom-call | tf_op jit(solution)/shard_map/pack_body/pallas_call | solution.py:17
  3.3 3.0 %collective-permute-start = (f32[8,16,128]{2,1,0:T(8,128)}, f32[8,16,128]{2,1,0:T(8,128)S(1)}, u32[]{:S(2)}, u32[]{:S(2)}) collective-permute-start(f32[8,16,128]{2,1,0:T(8,128)} %get-tuple-element.69), channel_id=1, source_target_pairs={{0,4},{4,8},{8,12},{12,16},{16,20},{20,24},{24,28},{28,32},{32,36}... | collective-permute-start | bytes 196616 | tf_op jit(solution)/shard_map/ppermute | solution.py:516
  6.6 2.7 %collective-permute-start.4 = (f32[8,16,128]{2,1,0:T(8,128)}, f32[8,16,128]{2,1,0:T(8,128)S(1)}, u32[]{:S(2)}, u32[]{:S(2)}) collective-permute-start(f32[8,16,128]{2,1,0:T(8,128)} %get-tuple-element.74.own), channel_id=1, source_target_pairs={{0,2},{1,3},{2,0},{3,1},{4,6},{5,7},{6,4},{7,5},{8,10},{9,11},{10,... | collective-permute-start | bytes 196616 | tf_op jit(solution)/shard_map/ppermute | solution.py:516
  9.3 0.4 collective-permute-start.2
  9.7 2.3 %collective-permute-start.3 = (f32[16,16,128]{2,1,0:T(8,128)}, f32[16,16,128]{2,1,0:T(8,128)S(1)}, u32[]{:S(2)}, u32[]{:S(2)}) collective-permute-start(f32[16,16,128]{2,1,0:T(8,128)} %get-tuple-element.72), channel_id=1, source_target_pairs={{0,3},{1,0},{2,1},{3,2},{4,7},{5,4},{6,5},{7,6},{8,11},{9,8},{10,9... | collective-permute-start | bytes 393224 | tf_op jit(solution)/shard_map/ppermute | solution.py:516
  12.1 2.4 %collective-permute-done.2.low.below = f32[16,16,128]{2,1,0:T(8,128)S(1)} collective-permute-done((f32[16,16,128]{2,1,0:T(8,128)}, f32[16,16,128]{2,1,0:T(8,128)S(1)}, u32[]{:S(2)}, u32[]{:S(2)}) %collective-permute-start.2) | collective-permute-done | bytes 131104 | tf_op jit(solution)/shard_map/ppermute | solution.py:516
  14.6 1.0 fine_source_body.1
  15.6 2.8 %collective-permute-start.6 = (f32[28,16,128]{2,1,0:T(8,128)S(1)}, f32[28,16,128]{2,1,0:T(8,128)S(1)}, u32[]{:S(2)}, u32[]{:S(2)}) collective-permute-start(f32[28,16,128]{2,1,0:T(8,128)S(1)} %get-tuple-element.77.own.own_share), channel_id=1, source_target_pairs={{0,3},{1,0},{2,1},{3,2},{4,7},{5,4},{6,5},{7,6},{8,11},{9,8},{10,9... | collective-permute-start | bytes 688136 | tf_op jit(solution)/shard_map/ppermute | solution.py:516
  18.3 1.4 %collective-permute-start.7 = (f32[20,16,128]{2,1,0:T(8,128)S(1)}, f32[20,16,128]{2,1,0:T(8,128)S(1)}, u32[]{:S(2)}, u32[]{:S(2)}) collective-permute-start(f32[20,16,128]{2,1,0:T(8,128)S(1)} %slice.50), channel_id=1, source_target_pairs={{0,2},{1,3},{2,0},{3,1},{4,6},{5,7},{6,4},{7,5},{8,10},{9,11},{10,... | collective-permute-start | bytes 491528 | tf_op jit(solution)/shard_map/ppermute | solution.py:516
  19.7 4.2 %collective-permute-start.8 = (f32[2,4,32,128]{3,2,1,0:T(8,128)S(1)}, f32[2,4,32,128]{3,2,1,0:T(8,128)S(1)}, u32[]{:S(2)}, u32[]{:S(2)}) collective-permute-start(f32[2,4,32,128]{3,2,1,0:T(8,128)S(1)} %get-tuple-element.78.high), channel_id=1, source_target_pairs={{0,4},{4,8},{8,12},{12,16},{16,20},{20,24},{24,28},{28,32},{32,36}... | collective-permute-start | bytes 393224 | tf_op jit(solution)/shard_map/ppermute | solution.py:516
  23.9 1.9 %collective-permute-start.9 = (f32[2,4,32,128]{3,2,1,0:T(8,128)S(1)}, f32[2,4,32,128]{3,2,1,0:T(8,128)S(1)}, u32[]{:S(2)}, u32[]{:S(2)}) collective-permute-start(f32[2,4,32,128]{3,2,1,0:T(8,128)S(1)} %get-tuple-element.79.low), channel_id=1, source_target_pairs={{0,60},{4,0},{8,4},{12,8},{16,12},{20,16},{24,20},{28,24},{32,28},... | collective-permute-start | bytes 393224 | tf_op jit(solution)/shard_map/ppermute | solution.py:516
  25.9 0.8 collective-permute-done.8.before
  26.6 1.9 %collective-permute-done.9.after = f32[2,4,32,128]{3,2,1,0:T(8,128)S(1)} collective-permute-done((f32[2,4,32,128]{3,2,1,0:T(8,128)S(1)}, f32[2,4,32,128]{3,2,1,0:T(8,128)S(1)}, u32[]{:S(2)}, u32[]{:S(2)}) %collective-permute-start.9) | collective-permute-done | bytes 131104 | tf_op jit(solution)/shard_map/ppermute | solution.py:516
  28.6 0.9 coarse_down_body.4
  29.5 2.0 %fine_down_body.1 = (f32[48,128]{1,0:T(8,128)S(1)}, f32[384,128]{1,0:T(8,128)S(1)}, f32[384,128]{1,0:T(8,128)S(1)}, f32[18,64,128]{2,1,0:T(8,128)S(1)}) custom-call(s32[2]{0:T(128)S(1)} %pad_add_fusion.where.refs_0_, f32[28,16,128]{2,1,0:T(8,128)S(1)} %collective-permute-done.5.below, f32[28,16,128]{2,1,0:T(8,128)S(1)} %get-tuple-element.77.own.own_share, ...), custom_call_target="tpu_custom_call" | custom-call | tf_op jit(solution)/shard_map/fine_down_body/pallas_call | solution.py:17
  31.5 3.7 %collective-permute-start.10 = (f32[432,128]{1,0:T(8,128)S(1)}, f32[432,128]{1,0:T(8,128)S(1)}, u32[]{:S(2)}, u32[]{:S(2)}) collective-permute-start(f32[432,128]{1,0:T(8,128)S(1)} %pad_maximum_fusion.1), channel_id=1, source_target_pairs={{0,4},{4,0},{8,12},{12,8},{16,20},{20,16},{24,28},{28,24},{32,36},... | collective-permute-start | bytes 663560 | tf_op jit(solution)/shard_map/ppermute | solution.py:528
  35.3 1.1 collective-permute-done.10.partner.refs_2_
  36.7 0.8 collective-permute-start.13
  37.5 1.9 %collective-permute-start.12 = (f32[96,128]{1,0:T(8,128)S(1)}, f32[96,128]{1,0:T(8,128)S(1)}, u32[]{:S(2)}, u32[]{:S(2)}) collective-permute-start(f32[96,128]{1,0:T(8,128)S(1)} %pad_maximum_fusion.6), channel_id=1, source_target_pairs={{0,52},{4,16},{8,60},{12,24},{16,4},{20,32},{24,12},{28,40},{32,20... | collective-permute-start | bytes 147464 | tf_op jit(solution)/shard_map/ppermute | solution.py:534
  39.5 1.9 %collective-permute-done.13.across_jump = f32[8,16,128]{2,1,0:T(8,128)S(1)} collective-permute-done((f32[8,16,128]{2,1,0:T(8,128)S(1)}, f32[8,16,128]{2,1,0:T(8,128)S(1)}, u32[]{:S(2)}, u32[]{:S(2)}) %collective-permute-start.13) | collective-permute-done | bytes 65568 | tf_op jit(solution)/shard_map/ppermute | solution.py:516
  41.4 1.4 %collective-permute-done.12.far.refs_4_ = f32[96,128]{1,0:T(8,128)S(1)} collective-permute-done((f32[96,128]{1,0:T(8,128)S(1)}, f32[96,128]{1,0:T(8,128)S(1)}, u32[]{:S(2)}, u32[]{:S(2)}) %collective-permute-start.12) | collective-permute-done | bytes 49184 | tf_op jit(solution)/shard_map/ppermute | solution.py:534
  42.9 4.0 %collective-permute-start.14 = (f32[192,128]{1,0:T(8,128)S(1)}, f32[192,128]{1,0:T(8,128)S(1)}, u32[]{:S(2)}, u32[]{:S(2)}) collective-permute-start(f32[192,128]{1,0:T(8,128)S(1)} %pad_maximum_fusion.4), channel_id=1, source_target_pairs={{0,4},{4,0},{8,12},{12,8},{16,20},{20,16},{24,28},{28,24},{32,36},... | collective-permute-start | bytes 294920 | tf_op jit(solution)/shard_map/ppermute | solution.py:528
  47.0 0.9 collective-permute-done.14.swapped.refs_5_
  47.9 5.2 %fine_up_body.1 = (f32[4,16,16,128]{3,2,1,0:T(8,128)}, f32[2,8,32,128]{3,2,1,0:T(8,128)S(1)}) custom-call(s32[2]{0:T(128)S(1)} %pad_add_fusion.where.refs_0_, f32[48,128]{1,0:T(8,128)S(1)} %get-tuple-element.81.own.refs_1_, f32[432,128]{1,0:T(8,128)S(1)} %collective-permute-done.10.partner.refs_2_, f32[480,128]{1,0:T(8,128)S(1)} %collective-permute-done.11.near.refs_3_, ...), custom_call_target="tpu_custom_call" | custom-call | tf_op jit(solution)/shard_map/fine_up_body/pallas_call | solution.py:17
  53.1 1.8 %coarse_up_first_body.1 = (f32[2,8,8,128]{3,2,1,0:T(8,128)S(1)}, f32[2,8,8,128]{3,2,1,0:T(8,128)S(1)}, f32[2,4,32,128]{3,2,1,0:T(8,128)S(1)}, f32[2,4,32,128]{3,2,1,0:T(8,128)S(1)}) custom-call(s32[2]{0:T(128)S(1)} %pad_add_fusion.where.refs_0_, f32[48,128]{1,0:T(8,128)S(1)} %get-tuple-element.81.own.refs_1_, ...), custom_call_target="tpu_custom_call" | custom-call | tf_op jit(solution)/shard_map/coarse_up_first_body/pallas_call | solution.py:17
  54.9 0.4 collective-permute-start.15
  55.4 1.3 %collective-permute-start.21 = (f32[2,8,32,128]{3,2,1,0:T(8,128)S(1)}, f32[2,8,32,128]{3,2,1,0:T(8,128)S(1)}, u32[]{:S(2)}, u32[]{:S(2)}) collective-permute-start(f32[2,8,32,128]{3,2,1,0:T(8,128)S(1)} %get-tuple-element.91.refs_8_), channel_id=1, source_target_pairs={{64,0},{128,64},{65,1},{129,65},{66,2},{130,66},{67,3},{131,67},{6... | collective-permute-start | bytes 786440 | tf_op jit(solution)/shard_map/ppermute | solution.py:636
  56.7 0.5 collective-permute-done.15.before
  57.2 2.7 %collective-permute-done.16.after = f32[2,4,32,128]{3,2,1,0:T(8,128)S(1)} collective-permute-done((f32[2,4,32,128]{3,2,1,0:T(8,128)S(1)}, f32[2,4,32,128]{3,2,1,0:T(8,128)S(1)}, u32[]{:S(2)}, u32[]{:S(2)}) %collective-permute-start.16) | collective-permute-done | bytes 131104 | tf_op jit(solution)/shard_map/ppermute | solution.py:516
  59.9 0.9 coarse_down_body.5
  60.9 1.0 collective-permute-start.17
  61.9 0.8 collective-permute-done.17.refs_2_
  62.7 2.1 %collective-permute-start.19 = (f32[32,128]{1,0:T(8,128)S(1)}, f32[32,128]{1,0:T(8,128)S(1)}, u32[]{:S(2)}, u32[]{:S(2)}) collective-permute-start(f32[32,128]{1,0:T(8,128)S(1)} %constant_dynamic-update-slice_fusion), channel_id=1, source_target_pairs={{0,52},{4,16},{8,60},{12,24},{16,4},{20,32},{24,12},{28,40},{32,20... | collective-permute-start | bytes 49160 | tf_op jit(solution)/shard_map/ppermute | solution.py:534
  64.8 2.3 %collective-permute-start.18 = (f32[32,128]{1,0:T(8,128)S(1)}, f32[32,128]{1,0:T(8,128)S(1)}, u32[]{:S(2)}, u32[]{:S(2)}) collective-permute-start(f32[32,128]{1,0:T(8,128)S(1)} %constant_dynamic-update-slice_fusion), channel_id=1, source_target_pairs={{0,60},{4,8},{8,4},{12,16},{16,12},{20,24},{24,20},{28,32},{32,28}... | collective-permute-start | bytes 49160 | tf_op jit(solution)/shard_map/ppermute | solution.py:534
  67.1 1.9 %collective-permute-done.18.refs_3_ = f32[32,128]{1,0:T(8,128)S(1)} collective-permute-done((f32[32,128]{1,0:T(8,128)S(1)}, f32[32,128]{1,0:T(8,128)S(1)}, u32[]{:S(2)}, u32[]{:S(2)}) %collective-permute-start.18) | collective-permute-done | bytes 16416 | tf_op jit(solution)/shard_map/ppermute | solution.py:534
  69.0 0.8 collective-permute-start.20
  69.8 0.9 collective-permute-done.20.refs_5_
  70.6 1.8 %coarse_up_middle_body.2 = (f32[2,8,8,128]{3,2,1,0:T(8,128)S(1)}, f32[2,8,8,128]{3,2,1,0:T(8,128)S(1)}, f32[2,4,32,128]{3,2,1,0:T(8,128)S(1)}, f32[2,4,32,128]{3,2,1,0:T(8,128)S(1)}) custom-call(s32[2]{0:T(128)S(1)} %pad_add_fusion.where.refs_0_, f32[16,128]{1,0:T(8,128)S(1)} %get-tuple-element.95.refs_1_, f32[16,128]{1,0:T(8,128)S(1)} %collective-permute-done.17.refs_2_, ...), custom_call_target="tpu_custom_call" | custom-call | tf_op jit(solution)/shard_map/coarse_up_middle_body/pallas_call | solution.py:17
  72.4 2.0 %collective-permute-start.22 = (f32[2,4,32,128]{3,2,1,0:T(8,128)S(1)}, f32[2,4,32,128]{3,2,1,0:T(8,128)S(1)}, u32[]{:S(2)}, u32[]{:S(2)}) collective-permute-start(f32[2,4,32,128]{3,2,1,0:T(8,128)S(1)} %get-tuple-element.103.high), channel_id=1, source_target_pairs={{0,4},{4,8},{8,12},{12,16},{16,20},{20,24},{24,28},{28,32},{32,36}... | collective-permute-start | bytes 393224 | tf_op jit(solution)/shard_map/ppermute | solution.py:516
  74.4 1.2 %collective-permute-start.30 = (f32[4,16,16,128]{3,2,1,0:T(8,128)S(1)}, f32[4,16,16,128]{3,2,1,0:T(8,128)S(1)}, u32[]{:S(2)}, u32[]{:S(2)}) collective-permute-start(f32[4,16,16,128]{3,2,1,0:T(8,128)S(1)} %copy-done.5), channel_id=1, source_target_pairs={{0,64},{64,128},{128,192},{192,0},{1,65},{65,129},{129,193},{193,1... | collective-permute-start | bytes 1572872 | tf_op jit(solution)/shard_map/ppermute | solution.py:516
  75.6 1.3 %collective-permute-start.29 = (f32[2,8,32,128]{3,2,1,0:T(8,128)S(1)}, f32[2,8,32,128]{3,2,1,0:T(8,128)S(1)}, u32[]{:S(2)}, u32[]{:S(2)}) collective-permute-start(f32[2,8,32,128]{3,2,1,0:T(8,128)S(1)} %collective-permute-done.21.refs_8_), channel_id=1, source_target_pairs={{64,0},{65,1},{66,2},{67,3},{68,4},{69,5},{70,6},{71,7},{72,8},{73... | collective-permute-start | bytes 786440 | tf_op jit(solution)/shard_map/ppermute | solution.py:547
  76.9 1.9 %collective-permute-done.23.after = f32[2,4,32,128]{3,2,1,0:T(8,128)S(1)} collective-permute-done((f32[2,4,32,128]{3,2,1,0:T(8,128)S(1)}, f32[2,4,32,128]{3,2,1,0:T(8,128)S(1)}, u32[]{:S(2)}, u32[]{:S(2)}) %collective-permute-start.23) | collective-permute-done | bytes 131104 | tf_op jit(solution)/shard_map/ppermute | solution.py:516
  78.8 0.9 coarse_down_body.6
  79.9 1.1 collective-permute-done.24.refs_2_
  81.0 2.4 %collective-permute-start.26 = (f32[32,128]{1,0:T(8,128)S(1)}, f32[32,128]{1,0:T(8,128)S(1)}, u32[]{:S(2)}, u32[]{:S(2)}) collective-permute-start(f32[32,128]{1,0:T(8,128)S(1)} %constant_dynamic-update-slice_fusion.2), channel_id=1, source_target_pairs={{0,52},{4,16},{8,60},{12,24},{16,4},{20,32},{24,12},{28,40},{32,20... | collective-permute-start | bytes 49160 | tf_op jit(solution)/shard_map/ppermute | solution.py:534
  83.4 1.2 %collective-permute-start.25 = (f32[32,128]{1,0:T(8,128)S(1)}, f32[32,128]{1,0:T(8,128)S(1)}, u32[]{:S(2)}, u32[]{:S(2)}) collective-permute-start(f32[32,128]{1,0:T(8,128)S(1)} %constant_dynamic-update-slice_fusion.2), channel_id=1, source_target_pairs={{0,60},{4,8},{8,4},{12,16},{16,12},{20,24},{24,20},{28,32},{32,28}... | collective-permute-start | bytes 49160 | tf_op jit(solution)/shard_map/ppermute | solution.py:534
  84.6 3.1 %collective-permute-start.28 = (f32[4,8,8,128]{3,2,1,0:T(8,128)S(1)}, f32[4,8,8,128]{3,2,1,0:T(8,128)S(1)}, u32[]{:S(2)}, u32[]{:S(2)}) collective-permute-start(f32[4,8,8,128]{3,2,1,0:T(8,128)S(1)} %pad_maximum_fusion.2), channel_id=1, source_target_pairs={{0,64},{1,65},{2,66},{3,67},{4,68},{5,69},{6,70},{7,71},{8,72},{9,... | collective-permute-start | bytes 393224 | tf_op jit(solution)/shard_map/ppermute | solution.py:547
  87.8 0.9 collective-permute-start.27
  88.7 1.4 %collective-permute-done.28 = f32[4,8,8,128]{3,2,1,0:T(8,128)S(1)} collective-permute-done((f32[4,8,8,128]{3,2,1,0:T(8,128)S(1)}, f32[4,8,8,128]{3,2,1,0:T(8,128)S(1)}, u32[]{:S(2)}, u32[]{:S(2)}) %collective-permute-start.28) | collective-permute-done | bytes 131104 | tf_op jit(solution)/shard_map/ppermute | solution.py:547
  90.1 1.8 %coarse_up_middle_body.3 = (f32[2,8,8,128]{3,2,1,0:T(8,128)S(1)}, f32[2,8,8,128]{3,2,1,0:T(8,128)S(1)}, f32[2,4,32,128]{3,2,1,0:T(8,128)S(1)}, f32[2,4,32,128]{3,2,1,0:T(8,128)S(1)}) custom-call(s32[2]{0:T(128)S(1)} %pad_add_fusion.where.refs_0_, f32[16,128]{1,0:T(8,128)S(1)} %get-tuple-element.111.refs_1_, f32[16,128]{1,0:T(8,128)S(1)} %collective-permute-done.24.refs_2_, ...), custom_call_target="tpu_custom_call" | custom-call | tf_op jit(solution)/shard_map/coarse_up_middle_body/pallas_call | solution.py:17
  91.8 1.5 %collective-permute-start.31 = (f32[2,4,32,128]{3,2,1,0:T(8,128)S(1)}, f32[2,4,32,128]{3,2,1,0:T(8,128)S(1)}, u32[]{:S(2)}, u32[]{:S(2)}) collective-permute-start(f32[2,4,32,128]{3,2,1,0:T(8,128)S(1)} %get-tuple-element.119.high), channel_id=1, source_target_pairs={{0,4},{4,8},{8,12},{12,16},{16,20},{20,24},{24,28},{28,32},{32,36}... | collective-permute-start | bytes 393224 | tf_op jit(solution)/shard_map/ppermute | solution.py:516
  93.3 2.6 %collective-permute-start.38 = (f32[2,8,8,128]{3,2,1,0:T(8,128)S(1)}, f32[2,8,8,128]{3,2,1,0:T(8,128)S(1)}, u32[]{:S(2)}, u32[]{:S(2)}) collective-permute-start(f32[2,8,8,128]{3,2,1,0:T(8,128)S(1)} %get-tuple-element.124), channel_id=1, source_target_pairs={{0,192},{1,193},{2,194},{3,195},{4,196},{5,197},{6,198},{7,199},{8... | collective-permute-start | bytes 196616 | tf_op jit(solution)/shard_map/ppermute | solution.py:547
  95.9 2.1 %collective-permute-done.32.after = f32[2,4,32,128]{3,2,1,0:T(8,128)S(1)} collective-permute-done((f32[2,4,32,128]{3,2,1,0:T(8,128)S(1)}, f32[2,4,32,128]{3,2,1,0:T(8,128)S(1)}, u32[]{:S(2)}, u32[]{:S(2)}) %collective-permute-start.32) | collective-permute-done | bytes 131104 | tf_op jit(solution)/shard_map/ppermute | solution.py:516
  98.0 0.9 coarse_down_body.7
  98.9 0.9 collective-permute-start.33
  99.8 0.8 collective-permute-done.33.b
  100.7 2.0 %collective-permute-start.35 = (f32[32,128]{1,0:T(8,128)S(1)}, f32[32,128]{1,0:T(8,128)S(1)}, u32[]{:S(2)}, u32[]{:S(2)}) collective-permute-start(f32[32,128]{1,0:T(8,128)S(1)} %constant_dynamic-update-slice_fusion.4), channel_id=1, source_target_pairs={{0,52},{4,16},{8,60},{12,24},{16,4},{20,32},{24,12},{28,40},{32,20... | collective-permute-start | bytes 49160 | tf_op jit(solution)/shard_map/ppermute | solution.py:534
  102.7 2.4 %collective-permute-start.34 = (f32[32,128]{1,0:T(8,128)S(1)}, f32[32,128]{1,0:T(8,128)S(1)}, u32[]{:S(2)}, u32[]{:S(2)}) collective-permute-start(f32[32,128]{1,0:T(8,128)S(1)} %constant_dynamic-update-slice_fusion.4), channel_id=1, source_target_pairs={{0,60},{4,8},{8,4},{12,16},{16,12},{20,24},{24,20},{28,32},{32,28}... | collective-permute-start | bytes 49160 | tf_op jit(solution)/shard_map/ppermute | solution.py:534
  105.0 2.2 %collective-permute-start.37 = (f32[4,8,8,128]{3,2,1,0:T(8,128)S(1)}, f32[4,8,8,128]{3,2,1,0:T(8,128)S(1)}, u32[]{:S(2)}, u32[]{:S(2)}) collective-permute-start(f32[4,8,8,128]{3,2,1,0:T(8,128)S(1)} %pad_maximum_fusion.3), channel_id=1, source_target_pairs={{0,128},{1,129},{2,130},{3,131},{4,132},{5,133},{6,134},{7,135},{8... | collective-permute-start | bytes 393224 | tf_op jit(solution)/shard_map/ppermute | solution.py:547
  107.4 3.0 %collective-permute-done.37 = f32[4,8,8,128]{3,2,1,0:T(8,128)S(1)} collective-permute-done((f32[4,8,8,128]{3,2,1,0:T(8,128)S(1)}, f32[4,8,8,128]{3,2,1,0:T(8,128)S(1)}, u32[]{:S(2)}, u32[]{:S(2)}) %collective-permute-start.37) | collective-permute-done | bytes 131104 | tf_op jit(solution)/shard_map/ppermute | solution.py:547
  110.4 1.6 %coarse_up_last_body.1 = f32[2,8,8,128]{3,2,1,0:T(8,128)S(1)} custom-call(s32[2]{0:T(128)S(1)} %pad_add_fusion.where.refs_0_, f32[16,128]{1,0:T(8,128)S(1)} %get-tuple-element.128.a, f32[16,128]{1,0:T(8,128)S(1)} %collective-permute-done.33.b, f32[32,128]{1,0:T(8,128)S(1)} %collective-permute-done.34.c, f32[32,128]{1,0:T(8,128)S(1)} %collective-permute-done.35.d, ...), custom_call_target="tpu_custom_call" | custom-call | tf_op jit(solution)/shard_map/coarse_up_last_body/pallas_call | solution.py:17
  112.0 1.3 %collective-permute-start.39 = (f32[2,8,8,128]{3,2,1,0:T(8,128)S(1)}, f32[2,8,8,128]{3,2,1,0:T(8,128)S(1)}, u32[]{:S(2)}, u32[]{:S(2)}) collective-permute-start(f32[2,8,8,128]{3,2,1,0:T(8,128)S(1)} %coarse_up_last_body.1), channel_id=1, source_target_pairs={{0,192},{1,193},{2,194},{3,195},{4,196},{5,197},{6,198},{7,199},{8... | collective-permute-start | bytes 196616 | tf_op jit(solution)/shard_map/ppermute | solution.py:547
  113.4 1.4 %new_start_body.1 = f32[4,16,16,128]{3,2,1,0:T(8,128)} custom-call(s32[2]{0:T(128)S(1)} %pad_add_fusion.where.refs_0_, f32[4,16,16,128]{3,2,1,0:T(8,128)S(1)} %collective-permute-done.30.fine, f32[4,16,16,128]{3,2,1,0:T(8,128)S(1)} %copy-done.2, f32[2,8,8,128]{3,2,1,0:T(8,128)S(1)} %get-tuple-element.136.state), custom_call_target="tpu_custom_call" | custom-call | tf_op jit(solution)/shard_map/new_start_body/pallas_call | solution.py:17
  114.8 1.3 %coarse_end_body.1 = f32[4,8,8,64]{3,2,1,0:T(8,128)} custom-call(s32[2]{0:T(128)S(1)} %pad_add_fusion.where.refs_0_, f32[2,8,8,128]{3,2,1,0:T(8,128)S(1)} %get-tuple-element.127.e0, f32[2,8,8,128]{3,2,1,0:T(8,128)S(1)} %get-tuple-element.137.e1, f32[2,8,8,128]{3,2,1,0:T(8,128)S(1)} %get-tuple-element.135.e2, f32[2,8,8,128]{3,2,1,0:T(8,128)S(1)} %collective-permute-done.39.e3), custom_call_target="tpu_custom_call" | custom-call | tf_op jit(solution)/shard_map/coarse_end_body/pallas_call | solution.py:17
  (69 shorter events, 1.5 us)
Async XLA Ops:
  0.6 11.4 %copy-start.4 = (f32[1,4,8,8,64]{4,3,2,1,0:T(8,128)S(1)}, f32[1,4,8,8,64]{4,3,2,1,0:T(8,128)}, u32[]{:S(2)}) copy-start(f32[1,4,8,8,64]{4,3,2,1,0:T(8,128)} %param.7) | copy-start | bytes 196612
  0.6 14.0 %copy-start.1 = (f32[1,4,16,16,128]{4,3,2,1,0:T(8,128)S(1)}, f32[1,4,16,16,128]{4,3,2,1,0:T(8,128)}, u32[]{:S(2)}) copy-start(f32[1,4,16,16,128]{4,3,2,1,0:T(8,128)} %param.6) | copy-start | bytes 1572868
  3.3 11.3 %copy-start = (f32[1,4,16,16,128]{4,3,2,1,0:T(8,128)S(1)}, f32[1,4,16,16,128]{4,3,2,1,0:T(8,128)}, u32[]{:S(2)}) copy-start(f32[1,4,16,16,128]{4,3,2,1,0:T(8,128)} %param.5) | copy-start | bytes 1572868
  3.3 11.2 %collective-permute-start = (f32[8,16,128]{2,1,0:T(8,128)}, f32[8,16,128]{2,1,0:T(8,128)S(1)}, u32[]{:S(2)}, u32[]{:S(2)}) collective-permute-start(f32[8,16,128]{2,1,0:T(8,128)} %get-tuple-element.69), channel_id=1, source_target_pairs={{0,4},{4,8},{8,12},{12,16},{16,20},{20,24},{24,28},{28,32},{32,36}... | collective-permute-start | bytes 196616 | tf_op jit(solution)/shard_map/ppermute | solution.py:516
  6.4 8.2 %collective-permute-start.1 = (f32[8,16,128]{2,1,0:T(8,128)}, f32[8,16,128]{2,1,0:T(8,128)S(1)}, u32[]{:S(2)}, u32[]{:S(2)}) collective-permute-start(f32[8,16,128]{2,1,0:T(8,128)} %get-tuple-element.70), channel_id=1, source_target_pairs={{0,60},{4,0},{8,4},{12,8},{16,12},{20,16},{24,20},{28,24},{32,28},... | collective-permute-start | bytes 196616 | tf_op jit(solution)/shard_map/ppermute | solution.py:516
  6.6 5.5 %collective-permute-start.4 = (f32[8,16,128]{2,1,0:T(8,128)}, f32[8,16,128]{2,1,0:T(8,128)S(1)}, u32[]{:S(2)}, u32[]{:S(2)}) collective-permute-start(f32[8,16,128]{2,1,0:T(8,128)} %get-tuple-element.74.own), channel_id=1, source_target_pairs={{0,2},{1,3},{2,0},{3,1},{4,6},{5,7},{6,4},{7,5},{8,10},{9,11},{10,... | collective-permute-start | bytes 196616 | tf_op jit(solution)/shard_map/ppermute | solution.py:516
  9.3 5.2 %collective-permute-start.2 = (f32[16,16,128]{2,1,0:T(8,128)}, f32[16,16,128]{2,1,0:T(8,128)S(1)}, u32[]{:S(2)}, u32[]{:S(2)}) collective-permute-start(f32[16,16,128]{2,1,0:T(8,128)} %get-tuple-element.71), channel_id=1, source_target_pairs={{0,1},{1,2},{2,3},{3,0},{4,5},{5,6},{6,7},{7,4},{8,9},{9,10},{10,1... | collective-permute-start | bytes 393224 | tf_op jit(solution)/shard_map/ppermute | solution.py:516
  9.7 4.8 %collective-permute-start.3 = (f32[16,16,128]{2,1,0:T(8,128)}, f32[16,16,128]{2,1,0:T(8,128)S(1)}, u32[]{:S(2)}, u32[]{:S(2)}) collective-permute-start(f32[16,16,128]{2,1,0:T(8,128)} %get-tuple-element.72), channel_id=1, source_target_pairs={{0,3},{1,0},{2,1},{3,2},{4,7},{5,4},{6,5},{7,6},{8,11},{9,8},{10,9... | collective-permute-start | bytes 393224 | tf_op jit(solution)/shard_map/ppermute | solution.py:516
  12.1 2.5 %copy-start.3 = (f32[8,16,128]{2,1,0:T(8,128)S(1)}, f32[8,16,128]{2,1,0:T(8,128)}, u32[]{:S(2)}) copy-start(f32[8,16,128]{2,1,0:T(8,128)} %get-tuple-element.74.own) | copy-start | bytes 196612
  15.6 13.9 %collective-permute-start.6 = (f32[28,16,128]{2,1,0:T(8,128)S(1)}, f32[28,16,128]{2,1,0:T(8,128)S(1)}, u32[]{:S(2)}, u32[]{:S(2)}) collective-permute-start(f32[28,16,128]{2,1,0:T(8,128)S(1)} %get-tuple-element.77.own.own_share), channel_id=1, source_target_pairs={{0,3},{1,0},{2,1},{3,2},{4,7},{5,4},{6,5},{7,6},{8,11},{9,8},{10,9... | collective-permute-start | bytes 688136 | tf_op jit(solution)/shard_map/ppermute | solution.py:516
  18.3 11.2 %collective-permute-start.5 = (f32[28,16,128]{2,1,0:T(8,128)S(1)}, f32[28,16,128]{2,1,0:T(8,128)S(1)}, u32[]{:S(2)}, u32[]{:S(2)}) collective-permute-start(f32[28,16,128]{2,1,0:T(8,128)S(1)} %get-tuple-element.77.own.own_share), channel_id=1, source_target_pairs={{0,1},{1,2},{2,3},{3,0},{4,5},{5,6},{6,7},{7,4},{8,9},{9,10},{10,1... | collective-permute-start | bytes 688136 | tf_op jit(solution)/shard_map/ppermute | solution.py:516
  18.3 11.1 %collective-permute-start.7 = (f32[20,16,128]{2,1,0:T(8,128)S(1)}, f32[20,16,128]{2,1,0:T(8,128)S(1)}, u32[]{:S(2)}, u32[]{:S(2)}) collective-permute-start(f32[20,16,128]{2,1,0:T(8,128)S(1)} %slice.50), channel_id=1, source_target_pairs={{0,2},{1,3},{2,0},{3,1},{4,6},{5,7},{6,4},{7,5},{8,10},{9,11},{10,... | collective-permute-start | bytes 491528 | tf_op jit(solution)/shard_map/ppermute | solution.py:516
  19.7 6.9 %collective-permute-start.8 = (f32[2,4,32,128]{3,2,1,0:T(8,128)S(1)}, f32[2,4,32,128]{3,2,1,0:T(8,128)S(1)}, u32[]{:S(2)}, u32[]{:S(2)}) collective-permute-start(f32[2,4,32,128]{3,2,1,0:T(8,128)S(1)} %get-tuple-element.78.high), channel_id=1, source_target_pairs={{0,4},{4,8},{8,12},{12,16},{16,20},{20,24},{24,28},{28,32},{32,36}... | collective-permute-start | bytes 393224 | tf_op jit(solution)/shard_map/ppermute | solution.py:516
  23.9 4.7 %collective-permute-start.9 = (f32[2,4,32,128]{3,2,1,0:T(8,128)S(1)}, f32[2,4,32,128]{3,2,1,0:T(8,128)S(1)}, u32[]{:S(2)}, u32[]{:S(2)}) collective-permute-start(f32[2,4,32,128]{3,2,1,0:T(8,128)S(1)} %get-tuple-element.79.low), channel_id=1, source_target_pairs={{0,60},{4,0},{8,4},{12,8},{16,12},{20,16},{24,20},{28,24},{32,28},... | collective-permute-start | bytes 393224 | tf_op jit(solution)/shard_map/ppermute | solution.py:516
  31.5 4.8 %collective-permute-start.10 = (f32[432,128]{1,0:T(8,128)S(1)}, f32[432,128]{1,0:T(8,128)S(1)}, u32[]{:S(2)}, u32[]{:S(2)}) collective-permute-start(f32[432,128]{1,0:T(8,128)S(1)} %pad_maximum_fusion.1), channel_id=1, source_target_pairs={{0,4},{4,0},{8,12},{12,8},{16,20},{20,16},{24,28},{28,24},{32,36},... | collective-permute-start | bytes 663560 | tf_op jit(solution)/shard_map/ppermute | solution.py:528
  36.4 6.5 %collective-permute-start.11 = (f32[480,128]{1,0:T(8,128)S(1)}, f32[480,128]{1,0:T(8,128)S(1)}, u32[]{:S(2)}, u32[]{:S(2)}) collective-permute-start(f32[480,128]{1,0:T(8,128)S(1)} %pad_maximum_fusion), channel_id=1, source_target_pairs={{0,60},{4,8},{8,4},{12,16},{16,12},{20,24},{24,20},{28,32},{32,28}... | collective-permute-start | bytes 737288 | tf_op jit(solution)/shard_map/ppermute | solution.py:534
  36.7 4.6 %collective-permute-start.13 = (f32[8,16,128]{2,1,0:T(8,128)S(1)}, f32[8,16,128]{2,1,0:T(8,128)S(1)}, u32[]{:S(2)}, u32[]{:S(2)}) collective-permute-start(f32[8,16,128]{2,1,0:T(8,128)S(1)} %slice.52), channel_id=1, source_target_pairs={{0,2},{1,3},{2,0},{3,1},{4,6},{5,7},{6,4},{7,5},{8,10},{9,11},{10,... | collective-permute-start | bytes 196616 | tf_op jit(solution)/shard_map/ppermute | solution.py:516
  37.5 5.3 %collective-permute-start.12 = (f32[96,128]{1,0:T(8,128)S(1)}, f32[96,128]{1,0:T(8,128)S(1)}, u32[]{:S(2)}, u32[]{:S(2)}) collective-permute-start(f32[96,128]{1,0:T(8,128)S(1)} %pad_maximum_fusion.6), channel_id=1, source_target_pairs={{0,52},{4,16},{8,60},{12,24},{16,4},{20,32},{24,12},{28,40},{32,20... | collective-permute-start | bytes 147464 | tf_op jit(solution)/shard_map/ppermute | solution.py:534
  42.9 4.9 %collective-permute-start.14 = (f32[192,128]{1,0:T(8,128)S(1)}, f32[192,128]{1,0:T(8,128)S(1)}, u32[]{:S(2)}, u32[]{:S(2)}) collective-permute-start(f32[192,128]{1,0:T(8,128)S(1)} %pad_maximum_fusion.4), channel_id=1, source_target_pairs={{0,4},{4,0},{8,12},{12,8},{16,20},{20,16},{24,28},{28,24},{32,36},... | collective-permute-start | bytes 294920 | tf_op jit(solution)/shard_map/ppermute | solution.py:528
  54.9 2.3 %collective-permute-start.15 = (f32[2,4,32,128]{3,2,1,0:T(8,128)S(1)}, f32[2,4,32,128]{3,2,1,0:T(8,128)S(1)}, u32[]{:S(2)}, u32[]{:S(2)}) collective-permute-start(f32[2,4,32,128]{3,2,1,0:T(8,128)S(1)} %get-tuple-element.92.high), channel_id=1, source_target_pairs={{0,4},{4,8},{8,12},{12,16},{16,20},{20,24},{24,28},{28,32},{32,36}... | collective-permute-start | bytes 393224 | tf_op jit(solution)/shard_map/ppermute | solution.py:516
  55.3 4.7 %collective-permute-start.16 = (f32[2,4,32,128]{3,2,1,0:T(8,128)S(1)}, f32[2,4,32,128]{3,2,1,0:T(8,128)S(1)}, u32[]{:S(2)}, u32[]{:S(2)}) collective-permute-start(f32[2,4,32,128]{3,2,1,0:T(8,128)S(1)} %get-tuple-element.93.low), channel_id=1, source_target_pairs={{0,60},{4,0},{8,4},{12,8},{16,12},{20,16},{24,20},{28,24},{32,28},... | collective-permute-start | bytes 393224 | tf_op jit(solution)/shard_map/ppermute | solution.py:516
  55.4 15.2 %collective-permute-start.21 = (f32[2,8,32,128]{3,2,1,0:T(8,128)S(1)}, f32[2,8,32,128]{3,2,1,0:T(8,128)S(1)}, u32[]{:S(2)}, u32[]{:S(2)}) collective-permute-start(f32[2,8,32,128]{3,2,1,0:T(8,128)S(1)} %get-tuple-element.91.refs_8_), channel_id=1, source_target_pairs={{64,0},{128,64},{65,1},{129,65},{66,2},{130,66},{67,3},{131,67},{6... | collective-permute-start | bytes 786440 | tf_op jit(solution)/shard_map/ppermute | solution.py:636
  60.9 1.9 %collective-permute-start.17 = (f32[16,128]{1,0:T(8,128)S(1)}, f32[16,128]{1,0:T(8,128)S(1)}, u32[]{:S(2)}, u32[]{:S(2)}) collective-permute-start(f32[16,128]{1,0:T(8,128)S(1)} %get-tuple-element.95.refs_1_), channel_id=1, source_target_pairs={{0,4},{4,0},{8,12},{12,8},{16,20},{20,16},{24,28},{28,24},{32,36},... | collective-permute-start | bytes 24584 | tf_op jit(solution)/shard_map/ppermute | solution.py:528
  62.7 4.4 %collective-permute-start.19 = (f32[32,128]{1,0:T(8,128)S(1)}, f32[32,128]{1,0:T(8,128)S(1)}, u32[]{:S(2)}, u32[]{:S(2)}) collective-permute-start(f32[32,128]{1,0:T(8,128)S(1)} %constant_dynamic-update-slice_fusion), channel_id=1, source_target_pairs={{0,52},{4,16},{8,60},{12,24},{16,4},{20,32},{24,12},{28,40},{32,20... | collective-permute-start | bytes 49160 | tf_op jit(solution)/shard_map/ppermute | solution.py:534
  64.8 4.2 %collective-permute-start.18 = (f32[32,128]{1,0:T(8,128)S(1)}, f32[32,128]{1,0:T(8,128)S(1)}, u32[]{:S(2)}, u32[]{:S(2)}) collective-permute-start(f32[32,128]{1,0:T(8,128)S(1)} %constant_dynamic-update-slice_fusion), channel_id=1, source_target_pairs={{0,60},{4,8},{8,4},{12,16},{16,12},{20,24},{24,20},{28,32},{32,28}... | collective-permute-start | bytes 49160 | tf_op jit(solution)/shard_map/ppermute | solution.py:534
  69.0 1.7 %collective-permute-start.20 = (f32[64,128]{1,0:T(8,128)S(1)}, f32[64,128]{1,0:T(8,128)S(1)}, u32[]{:S(2)}, u32[]{:S(2)}) collective-permute-start(f32[64,128]{1,0:T(8,128)S(1)} %pad_maximum_fusion.7), channel_id=1, source_target_pairs={{0,4},{4,0},{8,12},{12,8},{16,20},{20,16},{24,28},{28,24},{32,36},... | collective-permute-start | bytes 98312 | tf_op jit(solution)/shard_map/ppermute | solution.py:528
  70.6 3.8 %copy-start.5 = (f32[4,16,16,128]{3,2,1,0:T(8,128)S(1)}, f32[4,16,16,128]{3,2,1,0:T(8,128)}, u32[]{:S(2)}) copy-start(f32[4,16,16,128]{3,2,1,0:T(8,128)} %get-tuple-element.108) | copy-start | bytes 1572868
  72.4 4.5 %collective-permute-start.22 = (f32[2,4,32,128]{3,2,1,0:T(8,128)S(1)}, f32[2,4,32,128]{3,2,1,0:T(8,128)S(1)}, u32[]{:S(2)}, u32[]{:S(2)}) collective-permute-start(f32[2,4,32,128]{3,2,1,0:T(8,128)S(1)} %get-tuple-element.103.high), channel_id=1, source_target_pairs={{0,4},{4,8},{8,12},{12,16},{16,20},{20,24},{24,28},{28,32},{32,36}... | collective-permute-start | bytes 393224 | tf_op jit(solution)/shard_map/ppermute | solution.py:516
  74.4 4.4 %collective-permute-start.23 = (f32[2,4,32,128]{3,2,1,0:T(8,128)S(1)}, f32[2,4,32,128]{3,2,1,0:T(8,128)S(1)}, u32[]{:S(2)}, u32[]{:S(2)}) collective-permute-start(f32[2,4,32,128]{3,2,1,0:T(8,128)S(1)} %get-tuple-element.104.low), channel_id=1, source_target_pairs={{0,60},{4,0},{8,4},{12,8},{16,12},{20,16},{24,20},{28,24},{32,28},... | collective-permute-start | bytes 393224 | tf_op jit(solution)/shard_map/ppermute | solution.py:516
  74.4 15.6 %collective-permute-start.30 = (f32[4,16,16,128]{3,2,1,0:T(8,128)S(1)}, f32[4,16,16,128]{3,2,1,0:T(8,128)S(1)}, u32[]{:S(2)}, u32[]{:S(2)}) collective-permute-start(f32[4,16,16,128]{3,2,1,0:T(8,128)S(1)} %copy-done.5), channel_id=1, source_target_pairs={{0,64},{64,128},{128,192},{192,0},{1,65},{65,129},{129,193},{193,1... | collective-permute-start | bytes 1572872 | tf_op jit(solution)/shard_map/ppermute | solution.py:516
  75.6 14.4 %collective-permute-start.29 = (f32[2,8,32,128]{3,2,1,0:T(8,128)S(1)}, f32[2,8,32,128]{3,2,1,0:T(8,128)S(1)}, u32[]{:S(2)}, u32[]{:S(2)}) collective-permute-start(f32[2,8,32,128]{3,2,1,0:T(8,128)S(1)} %collective-permute-done.21.refs_8_), channel_id=1, source_target_pairs={{64,0},{65,1},{66,2},{67,3},{68,4},{69,5},{70,6},{71,7},{72,8},{73... | collective-permute-start | bytes 786440 | tf_op jit(solution)/shard_map/ppermute | solution.py:547
  79.7 1.3 %collective-permute-start.24 = (f32[16,128]{1,0:T(8,128)S(1)}, f32[16,128]{1,0:T(8,128)S(1)}, u32[]{:S(2)}, u32[]{:S(2)}) collective-permute-start(f32[16,128]{1,0:T(8,128)S(1)} %get-tuple-element.111.refs_1_), channel_id=1, source_target_pairs={{0,4},{4,0},{8,12},{12,8},{16,20},{20,16},{24,28},{28,24},{32,36},... | collective-permute-start | bytes 24584 | tf_op jit(solution)/shard_map/ppermute | solution.py:528
  81.0 6.7 %collective-permute-start.26 = (f32[32,128]{1,0:T(8,128)S(1)}, f32[32,128]{1,0:T(8,128)S(1)}, u32[]{:S(2)}, u32[]{:S(2)}) collective-permute-start(f32[32,128]{1,0:T(8,128)S(1)} %constant_dynamic-update-slice_fusion.2), channel_id=1, source_target_pairs={{0,52},{4,16},{8,60},{12,24},{16,4},{20,32},{24,12},{28,40},{32,20... | collective-permute-start | bytes 49160 | tf_op jit(solution)/shard_map/ppermute | solution.py:534
  83.4 4.3 %collective-permute-start.25 = (f32[32,128]{1,0:T(8,128)S(1)}, f32[32,128]{1,0:T(8,128)S(1)}, u32[]{:S(2)}, u32[]{:S(2)}) collective-permute-start(f32[32,128]{1,0:T(8,128)S(1)} %constant_dynamic-update-slice_fusion.2), channel_id=1, source_target_pairs={{0,60},{4,8},{8,4},{12,16},{16,12},{20,24},{24,20},{28,32},{32,28}... | collective-permute-start | bytes 49160 | tf_op jit(solution)/shard_map/ppermute | solution.py:534
  84.6 5.4 %collective-permute-start.28 = (f32[4,8,8,128]{3,2,1,0:T(8,128)S(1)}, f32[4,8,8,128]{3,2,1,0:T(8,128)S(1)}, u32[]{:S(2)}, u32[]{:S(2)}) collective-permute-start(f32[4,8,8,128]{3,2,1,0:T(8,128)S(1)} %pad_maximum_fusion.2), channel_id=1, source_target_pairs={{0,64},{1,65},{2,66},{3,67},{4,68},{5,69},{6,70},{7,71},{8,72},{9,... | collective-permute-start | bytes 393224 | tf_op jit(solution)/shard_map/ppermute | solution.py:547
  87.8 2.3 %collective-permute-start.27 = (f32[64,128]{1,0:T(8,128)S(1)}, f32[64,128]{1,0:T(8,128)S(1)}, u32[]{:S(2)}, u32[]{:S(2)}) collective-permute-start(f32[64,128]{1,0:T(8,128)S(1)} %pad_maximum_fusion.8), channel_id=1, source_target_pairs={{0,4},{4,0},{8,12},{12,8},{16,20},{20,16},{24,28},{28,24},{32,36},... | collective-permute-start | bytes 98312 | tf_op jit(solution)/shard_map/ppermute | solution.py:528
  91.8 4.1 %collective-permute-start.31 = (f32[2,4,32,128]{3,2,1,0:T(8,128)S(1)}, f32[2,4,32,128]{3,2,1,0:T(8,128)S(1)}, u32[]{:S(2)}, u32[]{:S(2)}) collective-permute-start(f32[2,4,32,128]{3,2,1,0:T(8,128)S(1)} %get-tuple-element.119.high), channel_id=1, source_target_pairs={{0,4},{4,8},{8,12},{12,16},{16,20},{20,24},{24,28},{28,32},{32,36}... | collective-permute-start | bytes 393224 | tf_op jit(solution)/shard_map/ppermute | solution.py:516
  93.3 4.7 %collective-permute-start.32 = (f32[2,4,32,128]{3,2,1,0:T(8,128)S(1)}, f32[2,4,32,128]{3,2,1,0:T(8,128)S(1)}, u32[]{:S(2)}, u32[]{:S(2)}) collective-permute-start(f32[2,4,32,128]{3,2,1,0:T(8,128)S(1)} %get-tuple-element.120.low), channel_id=1, source_target_pairs={{0,60},{4,0},{8,4},{12,8},{16,12},{20,16},{24,20},{28,24},{32,28},... | collective-permute-start | bytes 393224 | tf_op jit(solution)/shard_map/ppermute | solution.py:516
  93.3 14.1 %collective-permute-start.38 = (f32[2,8,8,128]{3,2,1,0:T(8,128)S(1)}, f32[2,8,8,128]{3,2,1,0:T(8,128)S(1)}, u32[]{:S(2)}, u32[]{:S(2)}) collective-permute-start(f32[2,8,8,128]{3,2,1,0:T(8,128)S(1)} %get-tuple-element.124), channel_id=1, source_target_pairs={{0,192},{1,193},{2,194},{3,195},{4,196},{5,197},{6,198},{7,199},{8... | collective-permute-start | bytes 196616 | tf_op jit(solution)/shard_map/ppermute | solution.py:547
  98.9 1.8 %collective-permute-start.33 = (f32[16,128]{1,0:T(8,128)S(1)}, f32[16,128]{1,0:T(8,128)S(1)}, u32[]{:S(2)}, u32[]{:S(2)}) collective-permute-start(f32[16,128]{1,0:T(8,128)S(1)} %get-tuple-element.128.a), channel_id=1, source_target_pairs={{0,4},{4,0},{8,12},{12,8},{16,20},{20,16},{24,28},{28,24},{32,36},... | collective-permute-start | bytes 24584 | tf_op jit(solution)/shard_map/ppermute | solution.py:528
  100.7 6.6 %collective-permute-start.35 = (f32[32,128]{1,0:T(8,128)S(1)}, f32[32,128]{1,0:T(8,128)S(1)}, u32[]{:S(2)}, u32[]{:S(2)}) collective-permute-start(f32[32,128]{1,0:T(8,128)S(1)} %constant_dynamic-update-slice_fusion.4), channel_id=1, source_target_pairs={{0,52},{4,16},{8,60},{12,24},{16,4},{20,32},{24,12},{28,40},{32,20... | collective-permute-start | bytes 49160 | tf_op jit(solution)/shard_map/ppermute | solution.py:534
  102.7 4.6 %collective-permute-start.34 = (f32[32,128]{1,0:T(8,128)S(1)}, f32[32,128]{1,0:T(8,128)S(1)}, u32[]{:S(2)}, u32[]{:S(2)}) collective-permute-start(f32[32,128]{1,0:T(8,128)S(1)} %constant_dynamic-update-slice_fusion.4), channel_id=1, source_target_pairs={{0,60},{4,8},{8,4},{12,16},{16,12},{20,24},{24,20},{28,32},{32,28}... | collective-permute-start | bytes 49160 | tf_op jit(solution)/shard_map/ppermute | solution.py:534
  105.0 5.4 %collective-permute-start.37 = (f32[4,8,8,128]{3,2,1,0:T(8,128)S(1)}, f32[4,8,8,128]{3,2,1,0:T(8,128)S(1)}, u32[]{:S(2)}, u32[]{:S(2)}) collective-permute-start(f32[4,8,8,128]{3,2,1,0:T(8,128)S(1)} %pad_maximum_fusion.3), channel_id=1, source_target_pairs={{0,128},{1,129},{2,130},{3,131},{4,132},{5,133},{6,134},{7,135},{8... | collective-permute-start | bytes 393224 | tf_op jit(solution)/shard_map/ppermute | solution.py:547
  107.3 3.2 %collective-permute-start.36 = (f32[64,128]{1,0:T(8,128)S(1)}, f32[64,128]{1,0:T(8,128)S(1)}, u32[]{:S(2)}, u32[]{:S(2)}) collective-permute-start(f32[64,128]{1,0:T(8,128)S(1)} %pad_maximum_fusion.9), channel_id=1, source_target_pairs={{0,4},{4,0},{8,12},{12,8},{16,20},{20,16},{24,28},{28,24},{32,36},... | collective-permute-start | bytes 98312 | tf_op jit(solution)/shard_map/ppermute | solution.py:528
  110.4 2.9 %copy-start.2 = (f32[4,16,16,128]{3,2,1,0:T(8,128)S(1)}, f32[4,16,16,128]{3,2,1,0:T(8,128)}, u32[]{:S(2)}) copy-start(f32[4,16,16,128]{3,2,1,0:T(8,128)} %initial.1) | copy-start | bytes 1572868
  112.0 2.7 %collective-permute-start.39 = (f32[2,8,8,128]{3,2,1,0:T(8,128)S(1)}, f32[2,8,8,128]{3,2,1,0:T(8,128)S(1)}, u32[]{:S(2)}, u32[]{:S(2)}) collective-permute-start(f32[2,8,8,128]{3,2,1,0:T(8,128)S(1)} %coarse_up_last_body.1), channel_id=1, source_target_pairs={{0,192},{1,193},{2,194},{3,195},{4,196},{5,197},{6,198},{7,199},{8... | collective-permute-start | bytes 196616 | tf_op jit(solution)/shard_map/ppermute | solution.py:547

commit v4 on v3

--- a/solution.py
+++ b/solution.py
@@ -158,20 +158,22 @@
     packed = restricted_packed(initial, rows, half)
     for h in range(2):
         for x in range(4):
-            block = packed[h][16 * x : 16 * x + 16]
-            opening[4 * h + x] = block
-            y_low[8 + 4 * h + x] = block
-            y_high[8 + 4 * h + x] = block
-
-
-def join_body(below, own, above, across, low, high):
-    for b, (ref, first) in enumerate(((below, 8), (own, 0), (above, 8), (across, 0))):
-        for h in range(2):
-            for x in range(8):
-                side = low if x < 4 else high
-                side[h, x % 4, 8 * b : 8 * b + 8, :] = ref[
-                    first + 4 * h + x // 2, 8 * (x % 2) : 8 * (x % 2) + 8
-                ]
+            opening[4 * h + x] = packed[h][16 * x : 16 * x + 16]
+        x_low[8, 8 * h : 8 * h + 8] = packed[h][0:8]
+        x_high[8, 8 * h : 8 * h + 8] = packed[h][56:64]
+        for x in range(8):
+            y_low[8, 8 * h + x : 8 * h + x + 1] = packed[h][8 * x : 8 * x + 1]
+            y_high[8, 8 * h + x : 8 * h + x + 1] = packed[h][8 * x + 7 : 8 * x + 8]
+
+
+def halves(pair):
+    lane = index_along(pair.shape, 1)
+    other = shifted(pair, 64, 1)
+    return jnp.where(lane < 64, pair, other), jnp.where(lane < 64, other, pair)
+
+
+def paired(low, high):
+    return jnp.where(index_along(low.shape, 1) < 64, low, high)
 
 
 def level2_pressure(r2, first, e2, step_z):
@@ -208,7 +210,9 @@
     return jnp.where(same, value, nxt(value, step, 1) if bit else prv(value, step, 1))
 
 
-def fine_source_body(begin, end, left, right, low, high, old, comb, out, rows, half):
+def fine_source_body(
+    where, begin, end, left, right, low, high, old, opening, comb, out, comb0, rows, half, rim
+):
     row = index_along((16, 128), 0)
     first, last = row == 0, row == 15
 
@@ -248,21 +252,90 @@
         out[x + 1] = 0.5 * div
         out[18, x : x + 1, :] = 0.5 * v[0:1]
         out[19, x : x + 1, :] = -0.5 * v[15:16]
+    coarse_source(opening, left, right, low, high, comb0, out, rim)
     packed = restricted_packed(comb, rows, half)
     for h in range(2):
         for x in range(4):
-            out[20 + 4 * h + x, 0:8] = packed[h][16 * x : 16 * x + 8] - old[h, 2 * x]
-            out[20 + 4 * h + x, 8:16] = packed[h][16 * x + 8 : 16 * x + 16] - old[h, 2 * x + 1]
+            for n in range(2):
+                part = packed[h][16 * x + 8 * n : 16 * x + 8 * n + 8] - old[h, 2 * x + n]
+                part = part + jnp.where(where[0] == 0, comb0[h, 2 * x + n], 0.0)
+                out[23 + 4 * h + x, 8 * n : 8 * n + 8] = part
+
+
+def coarse_source(opening, left, right, low, high, comb0, out, rim):
+    row = index_along((8, 128), 0)
+
+    def inside(x):
+        rows = 8 * (x % 2)
+        return [
+            *halves(opening[x // 2, rows : rows + 8]),
+            *halves(opening[4 + x // 2, rows : rows + 8]),
+        ]
+
+    def outside(ref):
+        return [*halves(ref[8, 0:8]), *halves(ref[8, 8:16])]
+
+    plane = {x: inside(x) for x in range(8)}
+    plane[-1], plane[8] = outside(left), outside(right)
+    under, over = outside(low), outside(high)
+    comb = []
+    for x in range(8):
+        u, v, w, b = plane[x]
+        fresh = []
+        for c in range(4):
+            here = plane[x][c]
+            above = jnp.where(row == 7, over[c][x : x + 1], nxt(here, 1, 0))
+            below = jnp.where(row == 0, under[c][x : x + 1], prv(here, 1, 0))
+            moving = u * (plane[x + 1][c] - plane[x - 1][c]) + v * (above - below)
+            moving = moving + w * (nxt(here, 1, 1) - prv(here, 1, 1))
+            fresh.append(here - 0.125 * moving + (0.5 * b if c == 2 else 0.0))
+        comb.append(fresh)
+        comb0[0, x] = paired(fresh[0], fresh[1])
+        comb0[1, x] = paired(fresh[2], fresh[3])
+    source = [0.25 * comb[0][0]]
+    for x in range(8):
+        u, v, w, b = comb[x]
+        div = jnp.where(row == 7, 0.0, nxt(v, 1, 0)) - jnp.where(row == 0, 0.0, prv(v, 1, 0))
+        div = div + nxt(w, 1, 1) - prv(w, 1, 1)
+        if x < 7:
+            div = div + comb[x + 1][0]
+        if x > 0:
+            div = div - comb[x - 1][0]
+        source.append(0.25 * div)
+        rim[0, x : x + 1, :] = 0.25 * v[0:1]
+        rim[1, x : x + 1, :] = -0.25 * v[7:8]
+    source.append(-0.25 * comb[7][0])
+    source += [rim[0], rim[1]]
+    for i in range(6):
+        out[20 + i // 2, 8 * (i % 2) : 8 * (i % 2) + 8] = paired(source[2 * i], source[2 * i + 1])
 
 
 def fine_down_body(
-    where, below, own, above, across, coarse,
-    message, inner, outer, r0, r1, r2
+    where, below, own, above, across,
+    message, inner, outer, r0, coarse_r1, r1, r2, rim, coarse_r2
 ):
     blocks = (below, own, above, across)
     for b, ref in enumerate(blocks):
         r0[:, 16 * b : 16 * b + 16] = ref[0:18]
-    message[32:48] = coarse[...]
+    for b, ref in enumerate(blocks):
+        for i in range(6):
+            pair = halves(ref[20 + i // 2, 8 * (i % 2) : 8 * (i % 2) + 8])
+            for n in range(2):
+                if i < 5:
+                    coarse_r1[2 * i + n, 8 * b : 8 * b + 8] = pair[n]
+                else:
+                    rim[b, n] = pair[n]
+    for b in range(4):
+        for x in range(8):
+            coarse_r1[x + 1, 8 * b + 7 : 8 * b + 8] += rim[(b + 1) % 4, 0, x : x + 1, :]
+            coarse_r1[x + 1, 8 * b : 8 * b + 1] += rim[(b + 3) % 4, 1, x : x + 1, :]
+    nothing = jnp.zeros((32, 128), F32)
+
+    def at(x):
+        return coarse_r1[x + 1] if -1 <= x < 9 else nothing
+
+    for x in range(-1, 5):
+        coarse_r2[x + 1] = restricted_defect(at(2 * x - 1), at(2 * x), at(2 * x + 1), at(2 * x + 2), 1, 1)
     for b in range(4):
         upper, lower = blocks[(b + 1) % 4], blocks[(b + 3) % 4]
         for x in range(16):
@@ -289,10 +362,27 @@
     second = jnp.where(odd, part[5], part[4])
     message[0:16] = first
     message[16:32] = second
+    part = [coarse_r2[i, pl.ds(0, 16, 2), :] for i in range(6)]
+    message[32:48] = paired(jnp.where(odd, part[1], part[0]), jnp.where(odd, part[3], part[2]))
+    message[48:64] = jnp.where(odd, part[5], part[4])
     k = where[1]
+    for i in range(3):
+        inner[384 + 32 * i : 416 + 32 * i] = coarse_r1[7 - 7 * k + i]
+        outer[384 + 32 * i : 416 + 32 * i] = coarse_r1[7 * k + i]
     for i in range(6):
         inner[64 * i : 64 * i + 64] = r0[12 - 12 * k + i]
         outer[64 * i : 64 * i + 64] = r0[12 * k + i]
+
+
+def sum_parts(parts, r2):
+    for j in range(10):
+        for n in range(4):
+            value = parts[j][n + 1]
+            if n == 0 and j > 0:
+                value = value + parts[j - 1][5]
+            if n == 3 and j < 9:
+                value = value + parts[j + 1][0]
+            r2[4 * j + n] = value
 
 
 def fine_up_body(
@@ -300,7 +390,7 @@
     r0, r1, r2, e2, p2, e1, p1, e0, p0, rows, half, blocks
 ):
     k = where[1]
-    ordered(where, (own, partner, near, far, swapped), 48, 0, 32, blocks)
+    ordered(where, (own, partner, near, far, swapped), 64, 0, 32, blocks)
     r0[5:21] = mine[1:17]
     for i in range(6):
         inside = face_in[64 * i : 64 * i + 64]
@@ -332,14 +422,7 @@
                 bit_lane(second, lane, 1, 1),
             ]
         )
-    for j in range(10):
-        for n in range(4):
-            value = parts[j][n + 1]
-            if n == 0 and j > 0:
-                value = value + parts[j - 1][5]
-            if n == 3 and j < 9:
-                value = value + parts[j + 1][0]
-            r2[4 * j + n] = value
+    sum_parts(parts, r2)
     for i, value in enumerate(level2_pressure(r2, 4 * k, e2, 4)):
         for y2 in range(16):
             p2[i, 4 * y2 : 4 * y2 + 4, :] = jnp.broadcast_to(value[y2 : y2 + 1], (4, 128))
@@ -365,7 +448,7 @@
     packed = packed_pairs(half, 256)
     for h in range(2):
         slope = 0.5 * packed[h].reshape(8, 32, 128)
-        for b, (ref, first) in enumerate(((below, 20), (own_share, 20), (above, 20), (across_jump, 0))):
+        for b, (ref, first) in enumerate(((below, 23), (own_share, 23), (above, 23), (across_jump, 0))):
             for x in range(8):
                 jump[h, x, 8 * b : 8 * b + 8] = (
                     ref[first + 4 * h + x // 2, 8 * (x % 2) : 8 * (x % 2) + 8]
@@ -419,17 +502,21 @@
     )
 
 
-def coarse_up_core(where, rows, base, got, comb, r1, blocks, r2, e2, p2, e1, p1, emit):
-    ordered(where, got, rows, base, 16, blocks)
+def coarse_up_core(where, got, comb, r1, blocks, r2, e2, p2, e1, p1, emit):
+    ordered(where, got, 16, 0, 16, blocks)
     lane = index_along((16, 128), 1)
     for j in range(10):
-        block = blocks[j]
-        other = shifted(block, 64, 1)
-        for m, pair in enumerate(
-            (jnp.where(lane < 64, block, other), jnp.where(lane < 64, other, block))
-        ):
+        for m, pair in enumerate(halves(blocks[j])):
             r2[4 * j + 2 * m] = bit_lane(pair, lane, 1, 0)
             r2[4 * j + 2 * m + 1] = bit_lane(pair, lane, 1, 1)
+    level1_pressure(where, r1, r2, e2, p2, e1, p1)
+    for x in range(8):
+        u, v, w = slopes(p1, x)
+        emit(0, x, paired(comb[0, x] - u, comb[1, x] - v))
+        emit(1, x, paired(comb[2, x] - w, comb[3, x]))
+
+
+def level1_pressure(where, r1, r2, e2, p2, e1, p1):
     for i, value in enumerate(level2_pressure(r2, 4 * where[1], e2, 2)):
         p2[i, pl.ds(0, 16, 2), :] = value
         p2[i, pl.ds(1, 16, 2), :] = value
@@ -437,22 +524,63 @@
         e1[k] = r1[k] * (-4.0 / 9.0) + p2[k // 2]
     for k in range(10):
         p1[k] = smoothed(e1[k], e1[k + 1], e1[k + 2], r1[k + 1], 4.0, 1, 1)
-    lane = index_along((32, 128), 1)
+
+
+def slopes(p1, x):
+    here = p1[x + 1]
+    return (
+        0.25 * (p1[x + 2] - p1[x]),
+        0.25 * (nxt(here, 1, 0) - prv(here, 1, 0)),
+        0.25 * (nxt(here, 1, 1) - prv(here, 1, 1)),
+    )
+
+
+UP_SCRATCH = [(10, 16, 128), (40, 16, 128), (8, 16, 128), (6, 32, 128), (12, 32, 128), (10, 32, 128)]
+
+
+def coarse_up_first_body(
+    where, own, partner, near, far, swapped, face_in, face_out, mine, comb0, jump,
+    ended, after, low, high, blocks, r2, e2, p2, e1, p1, r1
+):
+    k = where[1]
+    ordered(where, (own, partner, near, far, swapped), 64, 32, 32, blocks)
+    lane = index_along((16, 128), 1)
+    parts = []
+    for j in range(10):
+        second = blocks[j, 16:32]
+        shares = []
+        for pair in halves(blocks[j, 0:16]):
+            shares += [bit_lane(pair, lane, 1, 0), bit_lane(pair, lane, 1, 1)]
+        parts.append(shares + [bit_lane(second, lane, 1, 0), bit_lane(second, lane, 1, 1)])
+    sum_parts(parts, r2)
+    r1[2:10] = mine[1:9]
+    for i in range(3):
+        inside = face_in[384 + 32 * i : 416 + 32 * i]
+        outside = face_out[384 + 32 * i : 416 + 32 * i]
+        left = jnp.where(k == 0, outside, inside)
+        right = jnp.where(k == 0, inside, outside)
+        if i < 2:
+            r1[i] = left
+        else:
+            r1[2] += left
+        if i > 0:
+            r1[9 + i] = right
+        else:
+            r1[9] += right
+    r1[1] += mine[0]
+    r1[10] += mine[9]
+    level1_pressure(where, r1, r2, e2, p2, e1, p1)
     for x in range(8):
-        here = p1[x + 1]
-        u = comb[0, x] - 0.25 * (p1[x + 2] - p1[x])
-        v = comb[1, x] - 0.25 * (nxt(here, 1, 0) - prv(here, 1, 0))
-        w = comb[2, x] - 0.25 * (nxt(here, 1, 1) - prv(here, 1, 1))
-        emit(0, x, jnp.where(lane < 64, u, v))
-        emit(1, x, jnp.where(lane < 64, w, comb[3, x]))
-
-
-UP_SCRATCH = [(10, 16, 128), (40, 16, 128), (8, 16, 128), (6, 32, 128), (12, 32, 128), (10, 32, 128)]
-
-
-def coarse_up_next_body(
-    rows, base, where, a, b, c, d, e, comb, r1, jump, ended, own, low, high, *scratch
-):
+        u, v, w = slopes(p1, x)
+        for h, change in enumerate((paired(u, v), paired(w, jnp.zeros_like(w)))):
+            value = jump[h, x] - change
+            ref = low if x < 4 else high
+            ref[h, x % 4] = value
+            after[h, x] = value[8:16]
+            ended[h, x] = comb0[h, x] - change[8:16]
+
+
+def coarse_up_middle_body(where, a, b, c, d, e, comb, r1, jump, ended, own, low, high, *scratch):
     def emit(h, x, value):
         after = value + jump[h, x]
         ref = low if x < 4 else high
@@ -460,22 +588,14 @@
         ended[h, x] = value[8:16]
         own[h, x] = after[8:16]
 
-    coarse_up_core(where, rows, base, (a, b, c, d, e), comb, r1, *scratch, emit)
-
-
-def coarse_up_first_body(*refs):
-    coarse_up_next_body(48, 32, *refs)
-
-
-def coarse_up_middle_body(*refs):
-    coarse_up_next_body(16, 0, *refs)
+    coarse_up_core(where, (a, b, c, d, e), comb, r1, *scratch, emit)
 
 
 def coarse_up_last_body(where, a, b, c, d, e, comb, r1, ended, *scratch):
     def emit(h, x, value):
         ended[h, x] = value[8:16]
 
-    coarse_up_core(where, 16, 0, (a, b, c, d, e), comb, r1, *scratch, emit)
+    coarse_up_core(where, (a, b, c, d, e), comb, r1, *scratch, emit)
 
 
 def new_start_body(where, fine, initial, state, out, rows, half, tall):
@@ -553,7 +673,7 @@
 
     x_low, x_high, y_low, y_high, opening = call(
         pack_body,
-        [(8, 16, 128)] * 2 + [(16, 16, 128)] * 2 + [(8, 16, 128)],
+        [(9, 16, 128)] * 4 + [(8, 16, 128)],
         [initial_state, begin, end],
         [(4, 8, 16, 128), (4, 8, 8, 128)] + [(4, 16, 16, 128)] * 3,
         limit=56,
@@ -564,17 +684,15 @@
     )
     left, right = both_sides(x_low, x_high, "sx")
     low, high = both_sides(y_low, y_high, "sy")
-    opening_across = moved(opening, "sy", 2)
-    comb, share = call(
+    comb, share, comb0 = call(
         fine_source_body,
-        [(4, 16, 16, 128), (28, 16, 128)],
-        [begin, end, left, right, low, high, old_packed],
-        [(4, 8, 16, 128), (4, 8, 8, 128)],
-    )
-    c0 = call(join_body, [(2, 4, 32, 128)] * 2, [low, opening, high, opening_across])
-    share, c0 = lax.optimization_barrier((share, c0))
+        [(4, 16, 16, 128), (31, 16, 128), (2, 8, 8, 128)],
+        [where, begin, end, left, right, low, high, old_packed, opening],
+        [(4, 8, 16, 128), (4, 8, 8, 128), (2, 8, 128)],
+        smem=1,
+    )
     below, above = both_sides(share, share, "sy")
-    across = moved(share[:20], "sy", 2)
+    across = moved(share[:23], "sy", 2)
 
     def coarse_down(state):
         low, high = state
@@ -586,25 +704,24 @@
             [(4, 16, 32, 128), (3, 14, 32, 128), (4, 32, 128)],
         )
 
-    comb0, first0, message0 = coarse_down(c0)
-    message, inner, outer, r0 = call(
+    message, inner, outer, r0, first0 = call(
         fine_down_body,
-        [(48, 128), (384, 128), (384, 128), (18, 64, 128)],
-        [where, below, share, above, across, message0],
-        [(10, 64, 128), (6, 64, 128)],
+        [(64, 128), (480, 128), (480, 128), (18, 64, 128), (10, 32, 128)],
+        [where, below, share, above, across],
+        [(10, 64, 128), (6, 64, 128), (4, 2, 8, 128), (6, 32, 128)],
         smem=1,
     )
-    across_jump = moved(share[20:], "sy", 2)
+    across_jump = moved(share[23:], "sy", 2)
     partner = swapped_cores(jnp.concatenate([message, inner], axis=0))
-    both = jnp.concatenate([message, partner[:48]], axis=0)
+    both = jnp.concatenate([message, partner[:64]], axis=0)
     near, far = from_chips(jnp.concatenate([both, outer], axis=0), 1), from_chips(both, 2)
     near, far, across_jump = lax.optimization_barrier((near, far, across_jump))
-    crossed = swapped_cores(jnp.concatenate([near[:96], far], axis=0))
+    crossed = swapped_cores(jnp.concatenate([near[:128], far], axis=0))
     got = [message, partner, near, far, crossed]
     fine_end, jump0 = call(
         fine_up_body,
         [(4, 16, 16, 128), (2, 8, 32, 128)],
-        [where] + got + [partner[48:], near[96:], r0, comb, below, share, above, across_jump],
+        [where] + got + [partner[64:], near[128:], r0, comb, below, share, above, across_jump],
         [
             (26, 64, 128),
             (12, 64, 128),
@@ -622,23 +739,27 @@
         smem=1,
     )
 
-    def coarse_up(body, got, combined, level1, jump):
+    def coarse_up(body, args, scratch):
         ended, own, low, high = call(
             body,
             [(2, 8, 8, 128)] * 2 + [(2, 4, 32, 128)] * 2,
-            [where] + got + [combined, level1, jump],
-            UP_SCRATCH,
+            [where] + args,
+            scratch,
             smem=1,
         )
         return ended, own, [low, high]
 
-    ended0, own1, c1 = coarse_up(coarse_up_first_body, got, comb0, first0, jump0)
+    ended0, own1, c1 = coarse_up(
+        coarse_up_first_body,
+        got + [partner[64:], near[128:], first0, comb0, jump0],
+        [(10, 32, 128)] + UP_SCRATCH[1:] + [(12, 32, 128)],
+    )
     jump1 = lax.ppermute(jump0, "tm", [(1, 0), (2, 1)])
     fine_before = moved(fine_end, "tm", 1)
 
     combined, level1, message = coarse_down(c1)
     got, jump1 = lax.optimization_barrier((five_chips(message), jump1))
-    ended1, own2, c2 = coarse_up(coarse_up_middle_body, got, combined, level1, jump1)
+    ended1, own2, c2 = coarse_up(coarse_up_middle_body, got + [combined, level1, jump1], UP_SCRATCH)
 
     combined, level1, message = coarse_down(c2)
     jump2 = sent(jump1, 1, 0)
@@ -646,7 +767,7 @@
     got, hand1, jump2, fine_before = lax.optimization_barrier(
         (five_chips(message), hand1, jump2, fine_before)
     )
-    ended2, own3, c3 = coarse_up(coarse_up_middle_body, got, combined, level1, jump2)
+    ended2, own3, c3 = coarse_up(coarse_up_middle_body, got + [combined, level1, jump2], UP_SCRATCH)
 
     combined, level1, message = coarse_down(c3)
     hand2 = sent(jnp.concatenate([own2, ended2], axis=0), 0, 2)

time: 117 us -> 115 us (0.983)
  starting transfers between devices: 62.7 us -> 55.2 us
  waiting for transfers between devices: 27.8 us -> 33.8 us
    ppermute x18 -> x15, starting transfers between devices: 24.8 us -> 15.1 us  [moved(): lax.ppermute(value, axis, [(i, (i + step) % count) for i in range(count)])]
    ppermute x18 -> x15, waiting for transfers between devices: 14.2 us -> 18.7 us  [moved(): lax.ppermute(value, axis, [(i, (i + step) % count) for i in range(count)])]
    ppermute x8, starting transfers between devices: 11.5 us -> 13.3 us  [swapped_cores(): lax.ppermute(value, 'sx', [(i, i ^ 1) for i in range(lax.axis_size('sx'))])]
    pallas_call x15 -> x13, Pallas kernels: 24.1 us -> 24.4 us  [call(): pl.pallas_call(body, out_shape=[jax.ShapeDtypeStruct(s, F32) for s in sha...]
  transfers between devices with their start and end apart: 40 -> 37, of which waited for: 19 -> 21; matrix products, arithmetic and copies ran while one was open for 0% -> 0% of each run, Pallas kernels for 4% -> 4%
where the time goes in v4:
time: 115 us
  starting transfers between devices  55.2 us (48%)
  waiting for transfers between devices  33.8 us (29%)
  Pallas kernels  24.4 us (21%)
    pallas_call x13, Pallas kernels, call(): pl.pallas_call(body, out_shape=[jax.ShapeDtypeStruct(s, F32) for s in sha...  24.4 us
    ppermute x15, waiting for transfers between devices, moved(): lax.ppermute(value, axis, [(i, (i + step) % count) for i in range(count)])  18.7 us
    ppermute x8, starting transfers between devices, from_chips(): lax.ppermute(value, 'sx', [(i, (i + (far if i % 2 else -far)) % count) fo...  15.4 us
    ppermute x15, starting transfers between devices, moved(): lax.ppermute(value, axis, [(i, (i + step) % count) for i in range(count)])  15.1 us
    ppermute x8, starting transfers between devices, swapped_cores(): lax.ppermute(value, 'sx', [(i, i ^ 1) for i in range(lax.axis_size('sx'))])  13.3 us
    ppermute x5, starting transfers between devices, sent(): return lax.ppermute(value, 'tm', [(source, target)])  10.1 us
    ppermute x8, waiting for transfers between devices, swapped_cores(): lax.ppermute(value, 'sx', [(i, i ^ 1) for i in range(lax.axis_size('sx'))])  5.6 us
    ppermute x5, waiting for transfers between devices, sent(): return lax.ppermute(value, 'tm', [(source, target)])  5.41 us
  transfers between devices with their start and end apart: 37, of which 21 were waited for; matrix products, arithmetic and copies ran while one was open for 0% of the time, Pallas kernels for 4%

profile of v4, /device:TPU:1, one launch (start us, length us, event | category | flops | bytes accessed | tf_op | source)
XLA Modules:
  0.0 114.8 jit_solution(4538296491028496704)
XLA Ops:
  0.7 2.7 %pack_body.1 = (f32[9,16,128]{2,1,0:T(8,128)}, f32[9,16,128]{2,1,0:T(8,128)}, f32[9,16,128]{2,1,0:T(8,128)}, f32[9,16,128]{2,1,0:T(8,128)}, f32[8,16,128]{2,1,0:T(8,128)}) custom-call(f32[4,16,16,128]{3,2,1,0:T(8,128)} %initial.1, f32[4,16,16,128]{3,2,1,0:T(8,128)} %bitcast.19, f32[4,16,16,128]{3,2,1,0:T(8,128)} %bitcast.21), custom_call_target="tpu_custom_call" | custom-call | tf_op jit(solution)/shard_map/pack_body/pallas_call | solution.py:17
  3.3 3.0 %collective-permute-start = (f32[9,16,128]{2,1,0:T(8,128)}, f32[9,16,128]{2,1,0:T(8,128)S(1)}, u32[]{:S(2)}, u32[]{:S(2)}) collective-permute-start(f32[9,16,128]{2,1,0:T(8,128)} %get-tuple-element.63), channel_id=1, source_target_pairs={{0,4},{4,8},{8,12},{12,16},{16,20},{20,24},{24,28},{28,32},{32,36}... | collective-permute-start | bytes 221192 | tf_op jit(solution)/shard_map/ppermute | solution.py:636
  6.6 1.1 collective-permute-start.2
  7.7 1.6 %collective-permute-start.3 = (f32[9,16,128]{2,1,0:T(8,128)}, f32[9,16,128]{2,1,0:T(8,128)S(1)}, u32[]{:S(2)}, u32[]{:S(2)}) collective-permute-start(f32[9,16,128]{2,1,0:T(8,128)} %get-tuple-element.66), channel_id=1, source_target_pairs={{0,3},{1,0},{2,1},{3,2},{4,7},{5,4},{6,5},{7,6},{8,11},{9,8},{10,9... | collective-permute-start | bytes 221192 | tf_op jit(solution)/shard_map/ppermute | solution.py:636
  9.5 0.9 collective-permute-done.1.right
  10.4 1.2 %collective-permute-done.2.low = f32[9,16,128]{2,1,0:T(8,128)S(1)} collective-permute-done((f32[9,16,128]{2,1,0:T(8,128)}, f32[9,16,128]{2,1,0:T(8,128)S(1)}, u32[]{:S(2)}, u32[]{:S(2)}) %collective-permute-start.2) | collective-permute-done | bytes 73760 | tf_op jit(solution)/shard_map/ppermute | solution.py:636
  11.6 1.6 %fine_source_body.1 = (f32[4,16,16,128]{3,2,1,0:T(8,128)S(1)}, f32[31,16,128]{2,1,0:T(8,128)S(1)}, f32[2,8,8,128]{3,2,1,0:T(8,128)S(1)}) custom-call(s32[2]{0:T(128)S(1)} %pad_add_fusion.where, f32[4,16,16,128]{3,2,1,0:T(8,128)S(1)} %bitcast.20, f32[4,16,16,128]{3,2,1,0:T(8,128)S(1)} %bitcast.22, f32[9,16,128]{2,1,0:T(8,128)S(1)} %collective-permute-done.left, ...), custom_call_target="tpu_custom_call" | custom-call | tf_op jit(solution)/shard_map/fine_source_body/pallas_call | solution.py:17
  13.1 2.7 %collective-permute-start.5 = (f32[31,16,128]{2,1,0:T(8,128)S(1)}, f32[31,16,128]{2,1,0:T(8,128)S(1)}, u32[]{:S(2)}, u32[]{:S(2)}) collective-permute-start(f32[31,16,128]{2,1,0:T(8,128)S(1)} %get-tuple-element.68.own.own_share), channel_id=1, source_target_pairs={{0,3},{1,0},{2,1},{3,2},{4,7},{5,4},{6,5},{7,6},{8,11},{9,8},{10,9... | collective-permute-start | bytes 761864 | tf_op jit(solution)/shard_map/ppermute | solution.py:636
  15.9 1.4 %collective-permute-start.6 = (f32[23,16,128]{2,1,0:T(8,128)S(1)}, f32[23,16,128]{2,1,0:T(8,128)S(1)}, u32[]{:S(2)}, u32[]{:S(2)}) collective-permute-start(f32[23,16,128]{2,1,0:T(8,128)S(1)} %slice.52), channel_id=1, source_target_pairs={{0,2},{1,3},{2,0},{3,1},{4,6},{5,7},{6,4},{7,5},{8,10},{9,11},{10,... | collective-permute-start | bytes 565256 | tf_op jit(solution)/shard_map/ppermute | solution.py:636
  17.3 5.7 %collective-permute-done.6.across = f32[23,16,128]{2,1,0:T(8,128)S(1)} collective-permute-done((f32[23,16,128]{2,1,0:T(8,128)S(1)}, f32[23,16,128]{2,1,0:T(8,128)S(1)}, u32[]{:S(2)}, u32[]{:S(2)}) %collective-permute-start.6) | collective-permute-done | bytes 188448 | tf_op jit(solution)/shard_map/ppermute | solution.py:636
  23.0 1.3 %collective-permute-done.4.below = f32[31,16,128]{2,1,0:T(8,128)S(1)} collective-permute-done((f32[31,16,128]{2,1,0:T(8,128)S(1)}, f32[31,16,128]{2,1,0:T(8,128)S(1)}, u32[]{:S(2)}, u32[]{:S(2)}) %collective-permute-start.4) | collective-permute-done | bytes 253984 | tf_op jit(solution)/shard_map/ppermute | solution.py:636
  24.2 2.4 %fine_down_body.1 = (f32[64,128]{1,0:T(8,128)S(1)}, f32[480,128]{1,0:T(8,128)S(1)}, f32[480,128]{1,0:T(8,128)S(1)}, f32[18,64,128]{2,1,0:T(8,128)S(1)}, f32[10,32,128]{2,1,0:T(8,128)S(1)}) custom-call(s32[2]{0:T(128)S(1)} %pad_add_fusion.where, f32[31,16,128]{2,1,0:T(8,128)S(1)} %collective-permute-done.4.below, ...), custom_call_target="tpu_custom_call" | custom-call | tf_op jit(solution)/shard_map/fine_down_body/pallas_call | solution.py:17
  26.7 6.2 %collective-permute-start.7 = (f32[544,128]{1,0:T(8,128)S(1)}, f32[544,128]{1,0:T(8,128)S(1)}, u32[]{:S(2)}, u32[]{:S(2)}) collective-permute-start(f32[544,128]{1,0:T(8,128)S(1)} %pad_maximum_fusion.1), channel_id=1, source_target_pairs={{0,4},{4,0},{8,12},{12,8},{16,20},{20,16},{24,28},{28,24},{32,36},... | collective-permute-start | bytes 835592 | tf_op jit(solution)/shard_map/ppermute | solution.py:648
  32.9 1.2 %collective-permute-done.7.partner = f32[544,128]{1,0:T(8,128)S(1)} collective-permute-done((f32[544,128]{1,0:T(8,128)S(1)}, f32[544,128]{1,0:T(8,128)S(1)}, u32[]{:S(2)}, u32[]{:S(2)}) %collective-permute-start.7) | collective-permute-done | bytes 278560 | tf_op jit(solution)/shard_map/ppermute | solution.py:648
  34.1 0.8 collective-permute-start.8
  34.9 0.3 collective-permute-start.10
  35.2 1.7 %collective-permute-start.9 = (f32[128,128]{1,0:T(8,128)S(1)}, f32[128,128]{1,0:T(8,128)S(1)}, u32[]{:S(2)}, u32[]{:S(2)}) collective-permute-start(f32[128,128]{1,0:T(8,128)S(1)} %pad_maximum_fusion.6), channel_id=1, source_target_pairs={{0,52},{4,16},{8,60},{12,24},{16,4},{20,32},{24,12},{28,40},{32,20... | collective-permute-start | bytes 196616 | tf_op jit(solution)/shard_map/ppermute | solution.py:654
  37.0 2.6 %collective-permute-done.10.across_jump = f32[8,16,128]{2,1,0:T(8,128)S(1)} collective-permute-done((f32[8,16,128]{2,1,0:T(8,128)S(1)}, f32[8,16,128]{2,1,0:T(8,128)S(1)}, u32[]{:S(2)}, u32[]{:S(2)}) %collective-permute-start.10) | collective-permute-done | bytes 65568 | tf_op jit(solution)/shard_map/ppermute | solution.py:636
  39.5 2.2 %collective-permute-done.9.far = f32[128,128]{1,0:T(8,128)S(1)} collective-permute-done((f32[128,128]{1,0:T(8,128)S(1)}, f32[128,128]{1,0:T(8,128)S(1)}, u32[]{:S(2)}, u32[]{:S(2)}) %collective-permute-start.9) | collective-permute-done | bytes 65568 | tf_op jit(solution)/shard_map/ppermute | solution.py:654
  41.7 2.8 %collective-permute-start.11 = (f32[256,128]{1,0:T(8,128)S(1)}, f32[256,128]{1,0:T(8,128)S(1)}, u32[]{:S(2)}, u32[]{:S(2)}) collective-permute-start(f32[256,128]{1,0:T(8,128)S(1)} %pad_maximum_fusion.2), channel_id=1, source_target_pairs={{0,4},{4,0},{8,12},{12,8},{16,20},{20,16},{24,28},{28,24},{32,36},... | collective-permute-start | bytes 393224 | tf_op jit(solution)/shard_map/ppermute | solution.py:648
  44.6 0.9 collective-permute-done.11.swapped
  45.5 5.3 %fine_up_body.1 = (f32[4,16,16,128]{3,2,1,0:T(8,128)}, f32[2,8,32,128]{3,2,1,0:T(8,128)S(1)}) custom-call(s32[2]{0:T(128)S(1)} %pad_add_fusion.where, f32[64,128]{1,0:T(8,128)S(1)} %get-tuple-element.69.own, f32[544,128]{1,0:T(8,128)S(1)} %collective-permute-done.7.partner, f32[608,128]{1,0:T(8,128)S(1)} %collective-permute-done.8.near, ...), custom_call_target="tpu_custom_call" | custom-call | tf_op jit(solution)/shard_map/fine_up_body/pallas_call | solution.py:17
  50.8 2.0 %coarse_up_first_body.1 = (f32[2,8,8,128]{3,2,1,0:T(8,128)S(1)}, f32[2,8,8,128]{3,2,1,0:T(8,128)S(1)}, f32[2,4,32,128]{3,2,1,0:T(8,128)S(1)}, f32[2,4,32,128]{3,2,1,0:T(8,128)S(1)}) custom-call(s32[2]{0:T(128)S(1)} %pad_add_fusion.where, f32[64,128]{1,0:T(8,128)S(1)} %get-tuple-element.69.own, f32[544,128]{1,0:T(8,128)S(1)} %collective-permute-done.7.partner, ...), custom_call_target="tpu_custom_call" | custom-call | tf_op jit(solution)/shard_map/coarse_up_first_body/pallas_call | solution.py:17
  52.7 1.2 %collective-permute-start.12 = (f32[2,4,32,128]{3,2,1,0:T(8,128)S(1)}, f32[2,4,32,128]{3,2,1,0:T(8,128)S(1)}, u32[]{:S(2)}, u32[]{:S(2)}) collective-permute-start(f32[2,4,32,128]{3,2,1,0:T(8,128)S(1)} %get-tuple-element.80.high), channel_id=1, source_target_pairs={{0,4},{4,8},{8,12},{12,16},{16,20},{20,24},{24,28},{28,32},{32,36}... | collective-permute-start | bytes 393224 | tf_op jit(solution)/shard_map/ppermute | solution.py:636
  53.9 1.3 %collective-permute-start.18 = (f32[2,8,32,128]{3,2,1,0:T(8,128)S(1)}, f32[2,8,32,128]{3,2,1,0:T(8,128)S(1)}, u32[]{:S(2)}, u32[]{:S(2)}) collective-permute-start(f32[2,8,32,128]{3,2,1,0:T(8,128)S(1)} %get-tuple-element.79.jump), channel_id=1, source_target_pairs={{64,0},{128,64},{65,1},{129,65},{66,2},{130,66},{67,3},{131,67},{6... | collective-permute-start | bytes 786440 | tf_op jit(solution)/shard_map/ppermute | solution.py:757
  55.2 0.7 collective-permute-done.12.before
  55.8 2.4 %collective-permute-done.13.after = f32[2,4,32,128]{3,2,1,0:T(8,128)S(1)} collective-permute-done((f32[2,4,32,128]{3,2,1,0:T(8,128)S(1)}, f32[2,4,32,128]{3,2,1,0:T(8,128)S(1)}, u32[]{:S(2)}, u32[]{:S(2)}) %collective-permute-start.13) | collective-permute-done | bytes 131104 | tf_op jit(solution)/shard_map/ppermute | solution.py:636
  58.3 0.9 coarse_down_body.3
  59.2 0.5 collective-permute-start.14
  59.7 0.8 collective-permute-done.14.b
  60.5 3.1 %collective-permute-start.16 = (f32[32,128]{1,0:T(8,128)S(1)}, f32[32,128]{1,0:T(8,128)S(1)}, u32[]{:S(2)}, u32[]{:S(2)}) collective-permute-start(f32[32,128]{1,0:T(8,128)S(1)} %constant_dynamic-update-slice_fusion), channel_id=1, source_target_pairs={{0,52},{4,16},{8,60},{12,24},{16,4},{20,32},{24,12},{28,40},{32,20... | collective-permute-start | bytes 49160 | tf_op jit(solution)/shard_map/ppermute | solution.py:654
  63.6 1.3 %collective-permute-start.15 = (f32[32,128]{1,0:T(8,128)S(1)}, f32[32,128]{1,0:T(8,128)S(1)}, u32[]{:S(2)}, u32[]{:S(2)}) collective-permute-start(f32[32,128]{1,0:T(8,128)S(1)} %constant_dynamic-update-slice_fusion), channel_id=1, source_target_pairs={{0,60},{4,8},{8,4},{12,16},{16,12},{20,24},{24,20},{28,32},{32,28}... | collective-permute-start | bytes 49160 | tf_op jit(solution)/shard_map/ppermute | solution.py:654
  64.9 0.5 collective-permute-done.16.d
  65.4 1.4 %collective-permute-done.15.c = f32[32,128]{1,0:T(8,128)S(1)} collective-permute-done((f32[32,128]{1,0:T(8,128)S(1)}, f32[32,128]{1,0:T(8,128)S(1)}, u32[]{:S(2)}, u32[]{:S(2)}) %collective-permute-start.15) | collective-permute-done | bytes 16416 | tf_op jit(solution)/shard_map/ppermute | solution.py:654
  66.8 1.8 %collective-permute-start.17 = (f32[64,128]{1,0:T(8,128)S(1)}, f32[64,128]{1,0:T(8,128)S(1)}, u32[]{:S(2)}, u32[]{:S(2)}) collective-permute-start(f32[64,128]{1,0:T(8,128)S(1)} %pad_maximum_fusion.7), channel_id=1, source_target_pairs={{0,4},{4,0},{8,12},{12,8},{16,20},{20,16},{24,28},{28,24},{32,36},... | collective-permute-start | bytes 98312 | tf_op jit(solution)/shard_map/ppermute | solution.py:648
  68.6 0.9 collective-permute-done.17.e
  69.5 1.8 %coarse_up_middle_body.2 = (f32[2,8,8,128]{3,2,1,0:T(8,128)S(1)}, f32[2,8,8,128]{3,2,1,0:T(8,128)S(1)}, f32[2,4,32,128]{3,2,1,0:T(8,128)S(1)}, f32[2,4,32,128]{3,2,1,0:T(8,128)S(1)}) custom-call(s32[2]{0:T(128)S(1)} %pad_add_fusion.where, f32[16,128]{1,0:T(8,128)S(1)} %get-tuple-element.83.a, f32[16,128]{1,0:T(8,128)S(1)} %collective-permute-done.14.b, ...), custom_call_target="tpu_custom_call" | custom-call | tf_op jit(solution)/shard_map/coarse_up_middle_body/pallas_call | solution.py:17
  71.3 1.5 %collective-permute-start.19 = (f32[2,4,32,128]{3,2,1,0:T(8,128)S(1)}, f32[2,4,32,128]{3,2,1,0:T(8,128)S(1)}, u32[]{:S(2)}, u32[]{:S(2)}) collective-permute-start(f32[2,4,32,128]{3,2,1,0:T(8,128)S(1)} %get-tuple-element.91.high), channel_id=1, source_target_pairs={{0,4},{4,8},{8,12},{12,16},{16,20},{20,24},{24,28},{28,32},{32,36}... | collective-permute-start | bytes 393224 | tf_op jit(solution)/shard_map/ppermute | solution.py:636
  72.8 1.2 %collective-permute-start.27 = (f32[4,16,16,128]{3,2,1,0:T(8,128)S(1)}, f32[4,16,16,128]{3,2,1,0:T(8,128)S(1)}, u32[]{:S(2)}, u32[]{:S(2)}) collective-permute-start(f32[4,16,16,128]{3,2,1,0:T(8,128)S(1)} %copy-done.5), channel_id=1, source_target_pairs={{0,64},{64,128},{128,192},{192,0},{1,65},{65,129},{129,193},{193,1... | collective-permute-start | bytes 1572872 | tf_op jit(solution)/shard_map/ppermute | solution.py:636
  74.0 1.3 %collective-permute-start.26 = (f32[2,8,32,128]{3,2,1,0:T(8,128)S(1)}, f32[2,8,32,128]{3,2,1,0:T(8,128)S(1)}, u32[]{:S(2)}, u32[]{:S(2)}) collective-permute-start(f32[2,8,32,128]{3,2,1,0:T(8,128)S(1)} %collective-permute-done.18.jump), channel_id=1, source_target_pairs={{64,0},{65,1},{66,2},{67,3},{68,4},{69,5},{70,6},{71,7},{72,8},{73... | collective-permute-start | bytes 786440 | tf_op jit(solution)/shard_map/ppermute | solution.py:667
  75.3 1.9 %collective-permute-done.20.after = f32[2,4,32,128]{3,2,1,0:T(8,128)S(1)} collective-permute-done((f32[2,4,32,128]{3,2,1,0:T(8,128)S(1)}, f32[2,4,32,128]{3,2,1,0:T(8,128)S(1)}, u32[]{:S(2)}, u32[]{:S(2)}) %collective-permute-start.20) | collective-permute-done | bytes 131104 | tf_op jit(solution)/shard_map/ppermute | solution.py:636
  77.2 0.9 coarse_down_body.4
  78.1 0.3 collective-permute-start.21
  78.4 1.0 collective-permute-done.21.b
  79.3 2.4 %collective-permute-start.23 = (f32[32,128]{1,0:T(8,128)S(1)}, f32[32,128]{1,0:T(8,128)S(1)}, u32[]{:S(2)}, u32[]{:S(2)}) collective-permute-start(f32[32,128]{1,0:T(8,128)S(1)} %constant_dynamic-update-slice_fusion.2), channel_id=1, source_target_pairs={{0,52},{4,16},{8,60},{12,24},{16,4},{20,32},{24,12},{28,40},{32,20... | collective-permute-start | bytes 49160 | tf_op jit(solution)/shard_map/ppermute | solution.py:654
  81.8 1.7 %collective-permute-start.22 = (f32[32,128]{1,0:T(8,128)S(1)}, f32[32,128]{1,0:T(8,128)S(1)}, u32[]{:S(2)}, u32[]{:S(2)}) collective-permute-start(f32[32,128]{1,0:T(8,128)S(1)} %constant_dynamic-update-slice_fusion.2), channel_id=1, source_target_pairs={{0,60},{4,8},{8,4},{12,16},{16,12},{20,24},{24,20},{28,32},{32,28}... | collective-permute-start | bytes 49160 | tf_op jit(solution)/shard_map/ppermute | solution.py:654
  83.4 3.1 %collective-permute-start.25 = (f32[4,8,8,128]{3,2,1,0:T(8,128)S(1)}, f32[4,8,8,128]{3,2,1,0:T(8,128)S(1)}, u32[]{:S(2)}, u32[]{:S(2)}) collective-permute-start(f32[4,8,8,128]{3,2,1,0:T(8,128)S(1)} %pad_maximum_fusion.3), channel_id=1, source_target_pairs={{0,64},{1,65},{2,66},{3,67},{4,68},{5,69},{6,70},{7,71},{8,72},{9,... | collective-permute-start | bytes 393224 | tf_op jit(solution)/shard_map/ppermute | solution.py:667
  86.6 0.4 collective-permute-start.24
  87.0 2.4 %collective-permute-done.25 = f32[4,8,8,128]{3,2,1,0:T(8,128)S(1)} collective-permute-done((f32[4,8,8,128]{3,2,1,0:T(8,128)S(1)}, f32[4,8,8,128]{3,2,1,0:T(8,128)S(1)}, u32[]{:S(2)}, u32[]{:S(2)}) %collective-permute-start.25) | collective-permute-done | bytes 131104 | tf_op jit(solution)/shard_map/ppermute | solution.py:667
  89.4 1.8 %coarse_up_middle_body.3 = (f32[2,8,8,128]{3,2,1,0:T(8,128)S(1)}, f32[2,8,8,128]{3,2,1,0:T(8,128)S(1)}, f32[2,4,32,128]{3,2,1,0:T(8,128)S(1)}, f32[2,4,32,128]{3,2,1,0:T(8,128)S(1)}) custom-call(s32[2]{0:T(128)S(1)} %pad_add_fusion.where, f32[16,128]{1,0:T(8,128)S(1)} %get-tuple-element.99.a, f32[16,128]{1,0:T(8,128)S(1)} %collective-permute-done.21.b, ...), custom_call_target="tpu_custom_call" | custom-call | tf_op jit(solution)/shard_map/coarse_up_middle_body/pallas_call | solution.py:17
  91.2 0.6 collective-permute-start.28
  92.1 2.3 %collective-permute-start.35 = (f32[2,8,8,128]{3,2,1,0:T(8,128)S(1)}, f32[2,8,8,128]{3,2,1,0:T(8,128)S(1)}, u32[]{:S(2)}, u32[]{:S(2)}) collective-permute-start(f32[2,8,8,128]{3,2,1,0:T(8,128)S(1)} %get-tuple-element.112), channel_id=1, source_target_pairs={{0,192},{1,193},{2,194},{3,195},{4,196},{5,197},{6,198},{7,199},{8... | collective-permute-start | bytes 196616 | tf_op jit(solution)/shard_map/ppermute | solution.py:667
  94.4 2.2 %collective-permute-done.29.after = f32[2,4,32,128]{3,2,1,0:T(8,128)S(1)} collective-permute-done((f32[2,4,32,128]{3,2,1,0:T(8,128)S(1)}, f32[2,4,32,128]{3,2,1,0:T(8,128)S(1)}, u32[]{:S(2)}, u32[]{:S(2)}) %collective-permute-start.29) | collective-permute-done | bytes 131104 | tf_op jit(solution)/shard_map/ppermute | solution.py:636
  96.5 0.9 coarse_down_body.5
  97.4 1.2 %collective-permute-start.30 = (f32[16,128]{1,0:T(8,128)S(1)}, f32[16,128]{1,0:T(8,128)S(1)}, u32[]{:S(2)}, u32[]{:S(2)}) collective-permute-start(f32[16,128]{1,0:T(8,128)S(1)} %get-tuple-element.116.a), channel_id=1, source_target_pairs={{0,4},{4,0},{8,12},{12,8},{16,20},{20,16},{24,28},{28,24},{32,36},... | collective-permute-start | bytes 24584 | tf_op jit(solution)/shard_map/ppermute | solution.py:648
  98.7 0.8 collective-permute-done.30.b
  99.5 1.5 %collective-permute-start.32 = (f32[32,128]{1,0:T(8,128)S(1)}, f32[32,128]{1,0:T(8,128)S(1)}, u32[]{:S(2)}, u32[]{:S(2)}) collective-permute-start(f32[32,128]{1,0:T(8,128)S(1)} %constant_dynamic-update-slice_fusion.4), channel_id=1, source_target_pairs={{0,52},{4,16},{8,60},{12,24},{16,4},{20,32},{24,12},{28,40},{32,20... | collective-permute-start | bytes 49160 | tf_op jit(solution)/shard_map/ppermute | solution.py:654
  101.0 2.9 %collective-permute-start.31 = (f32[32,128]{1,0:T(8,128)S(1)}, f32[32,128]{1,0:T(8,128)S(1)}, u32[]{:S(2)}, u32[]{:S(2)}) collective-permute-start(f32[32,128]{1,0:T(8,128)S(1)} %constant_dynamic-update-slice_fusion.4), channel_id=1, source_target_pairs={{0,60},{4,8},{8,4},{12,16},{16,12},{20,24},{24,20},{28,32},{32,28}... | collective-permute-start | bytes 49160 | tf_op jit(solution)/shard_map/ppermute | solution.py:654
  103.9 2.2 %collective-permute-start.34 = (f32[4,8,8,128]{3,2,1,0:T(8,128)S(1)}, f32[4,8,8,128]{3,2,1,0:T(8,128)S(1)}, u32[]{:S(2)}, u32[]{:S(2)}) collective-permute-start(f32[4,8,8,128]{3,2,1,0:T(8,128)S(1)} %pad_maximum_fusion.4), channel_id=1, source_target_pairs={{0,128},{1,129},{2,130},{3,131},{4,132},{5,133},{6,134},{7,135},{8... | collective-permute-start | bytes 393224 | tf_op jit(solution)/shard_map/ppermute | solution.py:667
  106.2 2.8 %collective-permute-done.34 = f32[4,8,8,128]{3,2,1,0:T(8,128)S(1)} collective-permute-done((f32[4,8,8,128]{3,2,1,0:T(8,128)S(1)}, f32[4,8,8,128]{3,2,1,0:T(8,128)S(1)}, u32[]{:S(2)}, u32[]{:S(2)}) %collective-permute-start.34) | collective-permute-done | bytes 131104 | tf_op jit(solution)/shard_map/ppermute | solution.py:667
  109.0 1.6 %coarse_up_last_body.1 = f32[2,8,8,128]{3,2,1,0:T(8,128)S(1)} custom-call(s32[2]{0:T(128)S(1)} %pad_add_fusion.where, f32[16,128]{1,0:T(8,128)S(1)} %get-tuple-element.116.a, f32[16,128]{1,0:T(8,128)S(1)} %collective-permute-done.30.b, f32[32,128]{1,0:T(8,128)S(1)} %collective-permute-done.31.c, f32[32,128]{1,0:T(8,128)S(1)} %collective-permute-done.32.d, ...), custom_call_target="tpu_custom_call" | custom-call | tf_op jit(solution)/shard_map/coarse_up_last_body/pallas_call | solution.py:17
  110.6 1.3 %collective-permute-start.36 = (f32[2,8,8,128]{3,2,1,0:T(8,128)S(1)}, f32[2,8,8,128]{3,2,1,0:T(8,128)S(1)}, u32[]{:S(2)}, u32[]{:S(2)}) collective-permute-start(f32[2,8,8,128]{3,2,1,0:T(8,128)S(1)} %coarse_up_last_body.1), channel_id=1, source_target_pairs={{0,192},{1,193},{2,194},{3,195},{4,196},{5,197},{6,198},{7,199},{8... | collective-permute-start | bytes 196616 | tf_op jit(solution)/shard_map/ppermute | solution.py:667
  111.9 1.4 %new_start_body.1 = f32[4,16,16,128]{3,2,1,0:T(8,128)} custom-call(s32[2]{0:T(128)S(1)} %pad_add_fusion.where, f32[4,16,16,128]{3,2,1,0:T(8,128)S(1)} %collective-permute-done.27.fine, f32[4,16,16,128]{3,2,1,0:T(8,128)S(1)} %copy-done.2, f32[2,8,8,128]{3,2,1,0:T(8,128)S(1)} %get-tuple-element.124.state), custom_call_target="tpu_custom_call" | custom-call | tf_op jit(solution)/shard_map/new_start_body/pallas_call | solution.py:17
  113.5 1.3 %coarse_end_body.1 = f32[4,8,8,64]{3,2,1,0:T(8,128)} custom-call(s32[2]{0:T(128)S(1)} %pad_add_fusion.where, f32[2,8,8,128]{3,2,1,0:T(8,128)S(1)} %get-tuple-element.115.e0, f32[2,8,8,128]{3,2,1,0:T(8,128)S(1)} %get-tuple-element.125.e1, f32[2,8,8,128]{3,2,1,0:T(8,128)S(1)} %get-tuple-element.123.e2, f32[2,8,8,128]{3,2,1,0:T(8,128)S(1)} %collective-permute-done.36.e3), custom_call_target="tpu_custom_call" | custom-call | tf_op jit(solution)/shard_map/coarse_end_body/pallas_call | solution.py:17
  (61 shorter events, 1.2 us)
Async XLA Ops:
  0.6 8.7 %copy-start.4 = (f32[1,4,8,8,64]{4,3,2,1,0:T(8,128)S(1)}, f32[1,4,8,8,64]{4,3,2,1,0:T(8,128)}, u32[]{:S(2)}) copy-start(f32[1,4,8,8,64]{4,3,2,1,0:T(8,128)} %param.7) | copy-start | bytes 196612
  0.6 10.9 %copy-start.1 = (f32[1,4,16,16,128]{4,3,2,1,0:T(8,128)S(1)}, f32[1,4,16,16,128]{4,3,2,1,0:T(8,128)}, u32[]{:S(2)}) copy-start(f32[1,4,16,16,128]{4,3,2,1,0:T(8,128)} %param.6) | copy-start | bytes 1572868
  3.3 8.2 %copy-start = (f32[1,4,16,16,128]{4,3,2,1,0:T(8,128)S(1)}, f32[1,4,16,16,128]{4,3,2,1,0:T(8,128)}, u32[]{:S(2)}) copy-start(f32[1,4,16,16,128]{4,3,2,1,0:T(8,128)} %param.5) | copy-start | bytes 1572868
  3.3 6.2 %collective-permute-start = (f32[9,16,128]{2,1,0:T(8,128)}, f32[9,16,128]{2,1,0:T(8,128)S(1)}, u32[]{:S(2)}, u32[]{:S(2)}) collective-permute-start(f32[9,16,128]{2,1,0:T(8,128)} %get-tuple-element.63), channel_id=1, source_target_pairs={{0,4},{4,8},{8,12},{12,16},{16,20},{20,24},{24,28},{28,32},{32,36}... | collective-permute-start | bytes 221192 | tf_op jit(solution)/shard_map/ppermute | solution.py:636
  6.4 4.0 %collective-permute-start.1 = (f32[9,16,128]{2,1,0:T(8,128)}, f32[9,16,128]{2,1,0:T(8,128)S(1)}, u32[]{:S(2)}, u32[]{:S(2)}) collective-permute-start(f32[9,16,128]{2,1,0:T(8,128)} %get-tuple-element.64), channel_id=1, source_target_pairs={{0,60},{4,0},{8,4},{12,8},{16,12},{20,16},{24,20},{28,24},{32,28},... | collective-permute-start | bytes 221192 | tf_op jit(solution)/shard_map/ppermute | solution.py:636
  6.6 4.9 %collective-permute-start.2 = (f32[9,16,128]{2,1,0:T(8,128)}, f32[9,16,128]{2,1,0:T(8,128)S(1)}, u32[]{:S(2)}, u32[]{:S(2)}) collective-permute-start(f32[9,16,128]{2,1,0:T(8,128)} %get-tuple-element.65), channel_id=1, source_target_pairs={{0,1},{1,2},{2,3},{3,0},{4,5},{5,6},{6,7},{7,4},{8,9},{9,10},{10,1... | collective-permute-start | bytes 221192 | tf_op jit(solution)/shard_map/ppermute | solution.py:636
  7.7 3.9 %collective-permute-start.3 = (f32[9,16,128]{2,1,0:T(8,128)}, f32[9,16,128]{2,1,0:T(8,128)S(1)}, u32[]{:S(2)}, u32[]{:S(2)}) collective-permute-start(f32[9,16,128]{2,1,0:T(8,128)} %get-tuple-element.66), channel_id=1, source_target_pairs={{0,3},{1,0},{2,1},{3,2},{4,7},{5,4},{6,5},{7,6},{8,11},{9,8},{10,9... | collective-permute-start | bytes 221192 | tf_op jit(solution)/shard_map/ppermute | solution.py:636
  9.4 2.1 %copy-start.3 = (f32[8,16,128]{2,1,0:T(8,128)S(1)}, f32[8,16,128]{2,1,0:T(8,128)}, u32[]{:S(2)}) copy-start(f32[8,16,128]{2,1,0:T(8,128)} %get-tuple-element.67.opening) | copy-start | bytes 196612
  13.1 9.8 %collective-permute-start.5 = (f32[31,16,128]{2,1,0:T(8,128)S(1)}, f32[31,16,128]{2,1,0:T(8,128)S(1)}, u32[]{:S(2)}, u32[]{:S(2)}) collective-permute-start(f32[31,16,128]{2,1,0:T(8,128)S(1)} %get-tuple-element.68.own.own_share), channel_id=1, source_target_pairs={{0,3},{1,0},{2,1},{3,2},{4,7},{5,4},{6,5},{7,6},{8,11},{9,8},{10,9... | collective-permute-start | bytes 761864 | tf_op jit(solution)/shard_map/ppermute | solution.py:636
  15.9 8.4 %collective-permute-start.4 = (f32[31,16,128]{2,1,0:T(8,128)S(1)}, f32[31,16,128]{2,1,0:T(8,128)S(1)}, u32[]{:S(2)}, u32[]{:S(2)}) collective-permute-start(f32[31,16,128]{2,1,0:T(8,128)S(1)} %get-tuple-element.68.own.own_share), channel_id=1, source_target_pairs={{0,1},{1,2},{2,3},{3,0},{4,5},{5,6},{6,7},{7,4},{8,9},{9,10},{10,1... | collective-permute-start | bytes 761864 | tf_op jit(solution)/shard_map/ppermute | solution.py:636
  15.9 7.0 %collective-permute-start.6 = (f32[23,16,128]{2,1,0:T(8,128)S(1)}, f32[23,16,128]{2,1,0:T(8,128)S(1)}, u32[]{:S(2)}, u32[]{:S(2)}) collective-permute-start(f32[23,16,128]{2,1,0:T(8,128)S(1)} %slice.52), channel_id=1, source_target_pairs={{0,2},{1,3},{2,0},{3,1},{4,6},{5,7},{6,4},{7,5},{8,10},{9,11},{10,... | collective-permute-start | bytes 565256 | tf_op jit(solution)/shard_map/ppermute | solution.py:636
  26.7 7.4 %collective-permute-start.7 = (f32[544,128]{1,0:T(8,128)S(1)}, f32[544,128]{1,0:T(8,128)S(1)}, u32[]{:S(2)}, u32[]{:S(2)}) collective-permute-start(f32[544,128]{1,0:T(8,128)S(1)} %pad_maximum_fusion.1), channel_id=1, source_target_pairs={{0,4},{4,0},{8,12},{12,8},{16,20},{20,16},{24,28},{28,24},{32,36},... | collective-permute-start | bytes 835592 | tf_op jit(solution)/shard_map/ppermute | solution.py:648
  34.1 7.6 %collective-permute-start.8 = (f32[608,128]{1,0:T(8,128)S(1)}, f32[608,128]{1,0:T(8,128)S(1)}, u32[]{:S(2)}, u32[]{:S(2)}) collective-permute-start(f32[608,128]{1,0:T(8,128)S(1)} %pad_maximum_fusion), channel_id=1, source_target_pairs={{0,60},{4,8},{8,4},{12,16},{16,12},{20,24},{24,20},{28,32},{32,28}... | collective-permute-start | bytes 933896 | tf_op jit(solution)/shard_map/ppermute | solution.py:654
  34.9 4.6 %collective-permute-start.10 = (f32[8,16,128]{2,1,0:T(8,128)S(1)}, f32[8,16,128]{2,1,0:T(8,128)S(1)}, u32[]{:S(2)}, u32[]{:S(2)}) collective-permute-start(f32[8,16,128]{2,1,0:T(8,128)S(1)} %slice.54), channel_id=1, source_target_pairs={{0,2},{1,3},{2,0},{3,1},{4,6},{5,7},{6,4},{7,5},{8,10},{9,11},{10,... | collective-permute-start | bytes 196616 | tf_op jit(solution)/shard_map/ppermute | solution.py:636
  35.2 6.5 %collective-permute-start.9 = (f32[128,128]{1,0:T(8,128)S(1)}, f32[128,128]{1,0:T(8,128)S(1)}, u32[]{:S(2)}, u32[]{:S(2)}) collective-permute-start(f32[128,128]{1,0:T(8,128)S(1)} %pad_maximum_fusion.6), channel_id=1, source_target_pairs={{0,52},{4,16},{8,60},{12,24},{16,4},{20,32},{24,12},{28,40},{32,20... | collective-permute-start | bytes 196616 | tf_op jit(solution)/shard_map/ppermute | solution.py:654
  41.7 3.8 %collective-permute-start.11 = (f32[256,128]{1,0:T(8,128)S(1)}, f32[256,128]{1,0:T(8,128)S(1)}, u32[]{:S(2)}, u32[]{:S(2)}) collective-permute-start(f32[256,128]{1,0:T(8,128)S(1)} %pad_maximum_fusion.2), channel_id=1, source_target_pairs={{0,4},{4,0},{8,12},{12,8},{16,20},{20,16},{24,28},{28,24},{32,36},... | collective-permute-start | bytes 393224 | tf_op jit(solution)/shard_map/ppermute | solution.py:648
  52.7 3.1 %collective-permute-start.12 = (f32[2,4,32,128]{3,2,1,0:T(8,128)S(1)}, f32[2,4,32,128]{3,2,1,0:T(8,128)S(1)}, u32[]{:S(2)}, u32[]{:S(2)}) collective-permute-start(f32[2,4,32,128]{3,2,1,0:T(8,128)S(1)} %get-tuple-element.80.high), channel_id=1, source_target_pairs={{0,4},{4,8},{8,12},{12,16},{16,20},{20,24},{24,28},{28,32},{32,36}... | collective-permute-start | bytes 393224 | tf_op jit(solution)/shard_map/ppermute | solution.py:636
  53.9 4.4 %collective-permute-start.13 = (f32[2,4,32,128]{3,2,1,0:T(8,128)S(1)}, f32[2,4,32,128]{3,2,1,0:T(8,128)S(1)}, u32[]{:S(2)}, u32[]{:S(2)}) collective-permute-start(f32[2,4,32,128]{3,2,1,0:T(8,128)S(1)} %get-tuple-element.81.low), channel_id=1, source_target_pairs={{0,60},{4,0},{8,4},{12,8},{16,12},{20,16},{24,20},{28,24},{32,28},... | collective-permute-start | bytes 393224 | tf_op jit(solution)/shard_map/ppermute | solution.py:636
  53.9 15.6 %collective-permute-start.18 = (f32[2,8,32,128]{3,2,1,0:T(8,128)S(1)}, f32[2,8,32,128]{3,2,1,0:T(8,128)S(1)}, u32[]{:S(2)}, u32[]{:S(2)}) collective-permute-start(f32[2,8,32,128]{3,2,1,0:T(8,128)S(1)} %get-tuple-element.79.jump), channel_id=1, source_target_pairs={{64,0},{128,64},{65,1},{129,65},{66,2},{130,66},{67,3},{131,67},{6... | collective-permute-start | bytes 786440 | tf_op jit(solution)/shard_map/ppermute | solution.py:757
  59.2 1.3 %collective-permute-start.14 = (f32[16,128]{1,0:T(8,128)S(1)}, f32[16,128]{1,0:T(8,128)S(1)}, u32[]{:S(2)}, u32[]{:S(2)}) collective-permute-start(f32[16,128]{1,0:T(8,128)S(1)} %get-tuple-element.83.a), channel_id=1, source_target_pairs={{0,4},{4,0},{8,12},{12,8},{16,20},{20,16},{24,28},{28,24},{32,36},... | collective-permute-start | bytes 24584 | tf_op jit(solution)/shard_map/ppermute | solution.py:648
  60.5 4.8 %collective-permute-start.16 = (f32[32,128]{1,0:T(8,128)S(1)}, f32[32,128]{1,0:T(8,128)S(1)}, u32[]{:S(2)}, u32[]{:S(2)}) collective-permute-start(f32[32,128]{1,0:T(8,128)S(1)} %constant_dynamic-update-slice_fusion), channel_id=1, source_target_pairs={{0,52},{4,16},{8,60},{12,24},{16,4},{20,32},{24,12},{28,40},{32,20... | collective-permute-start | bytes 49160 | tf_op jit(solution)/shard_map/ppermute | solution.py:654
  63.6 3.2 %collective-permute-start.15 = (f32[32,128]{1,0:T(8,128)S(1)}, f32[32,128]{1,0:T(8,128)S(1)}, u32[]{:S(2)}, u32[]{:S(2)}) collective-permute-start(f32[32,128]{1,0:T(8,128)S(1)} %constant_dynamic-update-slice_fusion), channel_id=1, source_target_pairs={{0,60},{4,8},{8,4},{12,16},{16,12},{20,24},{24,20},{28,32},{32,28}... | collective-permute-start | bytes 49160 | tf_op jit(solution)/shard_map/ppermute | solution.py:654
  66.8 2.7 %collective-permute-start.17 = (f32[64,128]{1,0:T(8,128)S(1)}, f32[64,128]{1,0:T(8,128)S(1)}, u32[]{:S(2)}, u32[]{:S(2)}) collective-permute-start(f32[64,128]{1,0:T(8,128)S(1)} %pad_maximum_fusion.7), channel_id=1, source_target_pairs={{0,4},{4,0},{8,12},{12,8},{16,20},{20,16},{24,28},{28,24},{32,36},... | collective-permute-start | bytes 98312 | tf_op jit(solution)/shard_map/ppermute | solution.py:648
  69.5 3.3 %copy-start.5 = (f32[4,16,16,128]{3,2,1,0:T(8,128)S(1)}, f32[4,16,16,128]{3,2,1,0:T(8,128)}, u32[]{:S(2)}) copy-start(f32[4,16,16,128]{3,2,1,0:T(8,128)} %get-tuple-element.96) | copy-start | bytes 1572868
  71.3 4.0 %collective-permute-start.19 = (f32[2,4,32,128]{3,2,1,0:T(8,128)S(1)}, f32[2,4,32,128]{3,2,1,0:T(8,128)S(1)}, u32[]{:S(2)}, u32[]{:S(2)}) collective-permute-start(f32[2,4,32,128]{3,2,1,0:T(8,128)S(1)} %get-tuple-element.91.high), channel_id=1, source_target_pairs={{0,4},{4,8},{8,12},{12,16},{16,20},{20,24},{24,28},{28,32},{32,36}... | collective-permute-start | bytes 393224 | tf_op jit(solution)/shard_map/ppermute | solution.py:636
  72.8 4.4 %collective-permute-start.20 = (f32[2,4,32,128]{3,2,1,0:T(8,128)S(1)}, f32[2,4,32,128]{3,2,1,0:T(8,128)S(1)}, u32[]{:S(2)}, u32[]{:S(2)}) collective-permute-start(f32[2,4,32,128]{3,2,1,0:T(8,128)S(1)} %get-tuple-element.92.low), channel_id=1, source_target_pairs={{0,60},{4,0},{8,4},{12,8},{16,12},{20,16},{24,20},{28,24},{32,28},... | collective-permute-start | bytes 393224 | tf_op jit(solution)/shard_map/ppermute | solution.py:636
  72.8 16.7 %collective-permute-start.27 = (f32[4,16,16,128]{3,2,1,0:T(8,128)S(1)}, f32[4,16,16,128]{3,2,1,0:T(8,128)S(1)}, u32[]{:S(2)}, u32[]{:S(2)}) collective-permute-start(f32[4,16,16,128]{3,2,1,0:T(8,128)S(1)} %copy-done.5), channel_id=1, source_target_pairs={{0,64},{64,128},{128,192},{192,0},{1,65},{65,129},{129,193},{193,1... | collective-permute-start | bytes 1572872 | tf_op jit(solution)/shard_map/ppermute | solution.py:636
  74.0 15.5 %collective-permute-start.26 = (f32[2,8,32,128]{3,2,1,0:T(8,128)S(1)}, f32[2,8,32,128]{3,2,1,0:T(8,128)S(1)}, u32[]{:S(2)}, u32[]{:S(2)}) collective-permute-start(f32[2,8,32,128]{3,2,1,0:T(8,128)S(1)} %collective-permute-done.18.jump), channel_id=1, source_target_pairs={{64,0},{65,1},{66,2},{67,3},{68,4},{69,5},{70,6},{71,7},{72,8},{73... | collective-permute-start | bytes 786440 | tf_op jit(solution)/shard_map/ppermute | solution.py:667
  78.1 1.3 %collective-permute-start.21 = (f32[16,128]{1,0:T(8,128)S(1)}, f32[16,128]{1,0:T(8,128)S(1)}, u32[]{:S(2)}, u32[]{:S(2)}) collective-permute-start(f32[16,128]{1,0:T(8,128)S(1)} %get-tuple-element.99.a), channel_id=1, source_target_pairs={{0,4},{4,0},{8,12},{12,8},{16,20},{20,16},{24,28},{28,24},{32,36},... | collective-permute-start | bytes 24584 | tf_op jit(solution)/shard_map/ppermute | solution.py:648
  79.3 7.2 %collective-permute-start.23 = (f32[32,128]{1,0:T(8,128)S(1)}, f32[32,128]{1,0:T(8,128)S(1)}, u32[]{:S(2)}, u32[]{:S(2)}) collective-permute-start(f32[32,128]{1,0:T(8,128)S(1)} %constant_dynamic-update-slice_fusion.2), channel_id=1, source_target_pairs={{0,52},{4,16},{8,60},{12,24},{16,4},{20,32},{24,12},{28,40},{32,20... | collective-permute-start | bytes 49160 | tf_op jit(solution)/shard_map/ppermute | solution.py:654
  81.8 4.8 %collective-permute-start.22 = (f32[32,128]{1,0:T(8,128)S(1)}, f32[32,128]{1,0:T(8,128)S(1)}, u32[]{:S(2)}, u32[]{:S(2)}) collective-permute-start(f32[32,128]{1,0:T(8,128)S(1)} %constant_dynamic-update-slice_fusion.2), channel_id=1, source_target_pairs={{0,60},{4,8},{8,4},{12,16},{16,12},{20,24},{24,20},{28,32},{32,28}... | collective-permute-start | bytes 49160 | tf_op jit(solution)/shard_map/ppermute | solution.py:654
  83.4 6.0 %collective-permute-start.25 = (f32[4,8,8,128]{3,2,1,0:T(8,128)S(1)}, f32[4,8,8,128]{3,2,1,0:T(8,128)S(1)}, u32[]{:S(2)}, u32[]{:S(2)}) collective-permute-start(f32[4,8,8,128]{3,2,1,0:T(8,128)S(1)} %pad_maximum_fusion.3), channel_id=1, source_target_pairs={{0,64},{1,65},{2,66},{3,67},{4,68},{5,69},{6,70},{7,71},{8,72},{9,... | collective-permute-start | bytes 393224 | tf_op jit(solution)/shard_map/ppermute | solution.py:667
  86.6 2.8 %collective-permute-start.24 = (f32[64,128]{1,0:T(8,128)S(1)}, f32[64,128]{1,0:T(8,128)S(1)}, u32[]{:S(2)}, u32[]{:S(2)}) collective-permute-start(f32[64,128]{1,0:T(8,128)S(1)} %pad_maximum_fusion.8), channel_id=1, source_target_pairs={{0,4},{4,0},{8,12},{12,8},{16,20},{20,16},{24,28},{28,24},{32,36},... | collective-permute-start | bytes 98312 | tf_op jit(solution)/shard_map/ppermute | solution.py:648
  91.2 3.1 %collective-permute-start.28 = (f32[2,4,32,128]{3,2,1,0:T(8,128)S(1)}, f32[2,4,32,128]{3,2,1,0:T(8,128)S(1)}, u32[]{:S(2)}, u32[]{:S(2)}) collective-permute-start(f32[2,4,32,128]{3,2,1,0:T(8,128)S(1)} %get-tuple-element.107.high), channel_id=1, source_target_pairs={{0,4},{4,8},{8,12},{12,16},{16,20},{20,24},{24,28},{28,32},{32,36}... | collective-permute-start | bytes 393224 | tf_op jit(solution)/shard_map/ppermute | solution.py:636
  91.8 4.7 %collective-permute-start.29 = (f32[2,4,32,128]{3,2,1,0:T(8,128)S(1)}, f32[2,4,32,128]{3,2,1,0:T(8,128)S(1)}, u32[]{:S(2)}, u32[]{:S(2)}) collective-permute-start(f32[2,4,32,128]{3,2,1,0:T(8,128)S(1)} %get-tuple-element.108.low), channel_id=1, source_target_pairs={{0,60},{4,0},{8,4},{12,8},{16,12},{20,16},{24,20},{28,24},{32,28},... | collective-permute-start | bytes 393224 | tf_op jit(solution)/shard_map/ppermute | solution.py:636
  92.1 14.1 %collective-permute-start.35 = (f32[2,8,8,128]{3,2,1,0:T(8,128)S(1)}, f32[2,8,8,128]{3,2,1,0:T(8,128)S(1)}, u32[]{:S(2)}, u32[]{:S(2)}) collective-permute-start(f32[2,8,8,128]{3,2,1,0:T(8,128)S(1)} %get-tuple-element.112), channel_id=1, source_target_pairs={{0,192},{1,193},{2,194},{3,195},{4,196},{5,197},{6,198},{7,199},{8... | collective-permute-start | bytes 196616 | tf_op jit(solution)/shard_map/ppermute | solution.py:667
  97.4 2.1 %collective-permute-start.30 = (f32[16,128]{1,0:T(8,128)S(1)}, f32[16,128]{1,0:T(8,128)S(1)}, u32[]{:S(2)}, u32[]{:S(2)}) collective-permute-start(f32[16,128]{1,0:T(8,128)S(1)} %get-tuple-element.116.a), channel_id=1, source_target_pairs={{0,4},{4,0},{8,12},{12,8},{16,20},{20,16},{24,28},{28,24},{32,36},... | collective-permute-start | bytes 24584 | tf_op jit(solution)/shard_map/ppermute | solution.py:648
  99.5 6.6 %collective-permute-start.32 = (f32[32,128]{1,0:T(8,128)S(1)}, f32[32,128]{1,0:T(8,128)S(1)}, u32[]{:S(2)}, u32[]{:S(2)}) collective-permute-start(f32[32,128]{1,0:T(8,128)S(1)} %constant_dynamic-update-slice_fusion.4), channel_id=1, source_target_pairs={{0,52},{4,16},{8,60},{12,24},{16,4},{20,32},{24,12},{28,40},{32,20... | collective-permute-start | bytes 49160 | tf_op jit(solution)/shard_map/ppermute | solution.py:654
  101.0 5.1 %collective-permute-start.31 = (f32[32,128]{1,0:T(8,128)S(1)}, f32[32,128]{1,0:T(8,128)S(1)}, u32[]{:S(2)}, u32[]{:S(2)}) collective-permute-start(f32[32,128]{1,0:T(8,128)S(1)} %constant_dynamic-update-slice_fusion.4), channel_id=1, source_target_pairs={{0,60},{4,8},{8,4},{12,16},{16,12},{20,24},{24,20},{28,32},{32,28}... | collective-permute-start | bytes 49160 | tf_op jit(solution)/shard_map/ppermute | solution.py:654
  103.9 5.1 %collective-permute-start.34 = (f32[4,8,8,128]{3,2,1,0:T(8,128)S(1)}, f32[4,8,8,128]{3,2,1,0:T(8,128)S(1)}, u32[]{:S(2)}, u32[]{:S(2)}) collective-permute-start(f32[4,8,8,128]{3,2,1,0:T(8,128)S(1)} %pad_maximum_fusion.4), channel_id=1, source_target_pairs={{0,128},{1,129},{2,130},{3,131},{4,132},{5,133},{6,134},{7,135},{8... | collective-permute-start | bytes 393224 | tf_op jit(solution)/shard_map/ppermute | solution.py:667
  106.1 2.9 %collective-permute-start.33 = (f32[64,128]{1,0:T(8,128)S(1)}, f32[64,128]{1,0:T(8,128)S(1)}, u32[]{:S(2)}, u32[]{:S(2)}) collective-permute-start(f32[64,128]{1,0:T(8,128)S(1)} %pad_maximum_fusion.9), channel_id=1, source_target_pairs={{0,4},{4,0},{8,12},{12,8},{16,20},{20,16},{24,28},{28,24},{32,36},... | collective-permute-start | bytes 98312 | tf_op jit(solution)/shard_map/ppermute | solution.py:648
  109.0 2.9 %copy-start.2 = (f32[4,16,16,128]{3,2,1,0:T(8,128)S(1)}, f32[4,16,16,128]{3,2,1,0:T(8,128)}, u32[]{:S(2)}) copy-start(f32[4,16,16,128]{3,2,1,0:T(8,128)} %initial.1) | copy-start | bytes 1572868
  110.6 2.9 %collective-permute-start.36 = (f32[2,8,8,128]{3,2,1,0:T(8,128)S(1)}, f32[2,8,8,128]{3,2,1,0:T(8,128)S(1)}, u32[]{:S(2)}, u32[]{:S(2)}) collective-permute-start(f32[2,8,8,128]{3,2,1,0:T(8,128)S(1)} %coarse_up_last_body.1), channel_id=1, source_target_pairs={{0,192},{1,193},{2,194},{3,195},{4,196},{5,197},{6,198},{7,199},{8... | collective-permute-start | bytes 196616 | tf_op jit(solution)/shard_map/ppermute | solution.py:667

commit v5 on v4

--- a/solution.py
+++ b/solution.py
@@ -386,7 +386,7 @@
 
 
 def fine_up_body(
-    where, own, partner, near, far, swapped, face_in, face_out, mine, comb, below, own_share, above, across_jump, fine, jump,
+    where, own, partner, near, far, swapped, face_in, face_out, mine, below, own_share, above, across_jump, pressure, jump,
     r0, r1, r2, e2, p2, e1, p1, e0, p0, rows, half, blocks
 ):
     k = where[1]
@@ -454,21 +454,28 @@
                     ref[first + 4 * h + x // 2, 8 * (x % 2) : 8 * (x % 2) + 8]
                     - slope[x, 8 * b : 8 * b + 8]
                 )
+    pressure[...] = p0[:, 8:40]
+
+
+def fine_end_body(pressure, comb, fine):
     for x in range(16):
-        here = p0[x + 1, 8:40]
-        fine[0, x] = comb[0, x] - 0.5 * (p0[x + 2, 16:32] - p0[x, 16:32])
+        here = pressure[x + 1]
+        mid = here[8:24]
+        fine[0, x] = comb[0, x] - 0.5 * (pressure[x + 2, 8:24] - pressure[x, 8:24])
         fine[1, x] = comb[1, x] - 0.5 * (nxt(here, 1, 0) - prv(here, 1, 0))[8:24]
-        mid = here[8:24]
         fine[2, x] = comb[2, x] - 0.5 * (nxt(mid, 1, 1) - prv(mid, 1, 1))
         fine[3, x] = comb[3, x]
 
 
-def coarse_down_body(before, low, high, after, comb_out, r1, message, state, comb, r2):
+def coarse_down_body(where, inner, low, high, outer, comb_out, r1, message, state, comb, r2):
     lane = index_along((32, 128), 1)
-    for side, ref in enumerate((before, low, high, after)):
+    k = where[1]
+    for side, ref in enumerate((outer, low, high, inner)):
         for x in range(4):
             for h in range(2):
                 pair = ref[h, x]
+                if side in (0, 3):
+                    pair = jnp.where(k == 0, pair, (inner if side == 0 else outer)[h, x])
                 other = shifted(pair, 64, 1)
                 state[2 * h, 4 * side + x] = jnp.where(lane < 64, pair, other)
                 state[2 * h + 1, 4 * side + x] = jnp.where(lane < 64, other, pair)
@@ -656,6 +663,12 @@
     )
 
 
+def turned_sides(low_face, high_face):
+    first = lax.axis_index("sx") % 2 == 0
+    inner = swapped_cores(jnp.where(first, high_face, low_face))
+    return inner, from_chips(jnp.where(first, low_face, high_face), 1)
+
+
 def five_chips(message):
     partner = swapped_cores(message)
     both = jnp.concatenate([message, partner], axis=0)
@@ -696,12 +709,13 @@
 
     def coarse_down(state):
         low, high = state
-        before, after = both_sides(low, high, "sx")
+        inner, outer = turned_sides(low, high)
         return call(
             coarse_down_body,
             [(4, 8, 32, 128), (12, 32, 128), (16, 128)],
-            [before, low, high, after],
+            [where, inner, low, high, outer],
             [(4, 16, 32, 128), (3, 14, 32, 128), (4, 32, 128)],
+            smem=1,
         )
 
     message, inner, outer, r0, first0 = call(
@@ -714,14 +728,14 @@
     across_jump = moved(share[23:], "sy", 2)
     partner = swapped_cores(jnp.concatenate([message, inner], axis=0))
     both = jnp.concatenate([message, partner[:64]], axis=0)
-    near, far = from_chips(jnp.concatenate([both, outer], axis=0), 1), from_chips(both, 2)
-    near, far, across_jump = lax.optimization_barrier((near, far, across_jump))
-    crossed = swapped_cores(jnp.concatenate([near[:128], far], axis=0))
+    near, far, beyond = from_chips(both, 1), from_chips(both, 2), from_chips(outer, 1)
+    near, far, beyond, across_jump = lax.optimization_barrier((near, far, beyond, across_jump))
+    crossed = swapped_cores(jnp.concatenate([near, far], axis=0))
     got = [message, partner, near, far, crossed]
-    fine_end, jump0 = call(
+    pressure, jump0 = call(
         fine_up_body,
-        [(4, 16, 16, 128), (2, 8, 32, 128)],
-        [where] + got + [partner[64:], near[128:], r0, comb, below, share, above, across_jump],
+        [(18, 32, 128), (2, 8, 32, 128)],
+        [where] + got + [partner[64:], beyond, r0, below, share, above, across_jump],
         [
             (26, 64, 128),
             (12, 64, 128),
@@ -751,14 +765,21 @@
 
     ended0, own1, c1 = coarse_up(
         coarse_up_first_body,
-        got + [partner[64:], near[128:], first0, comb0, jump0],
+        got + [partner[64:], beyond, first0, comb0, jump0],
         [(10, 32, 128)] + UP_SCRATCH[1:] + [(12, 32, 128)],
     )
     jump1 = lax.ppermute(jump0, "tm", [(1, 0), (2, 1)])
+    combined, level1, message = coarse_down(c1)
+    partner = swapped_cores(message)
+    both, pressure = lax.optimization_barrier(
+        (jnp.concatenate([message, partner], axis=0), pressure)
+    )
+    near, far = from_chips(both, 1), from_chips(both, 2)
+    fine_end = call(fine_end_body, (4, 16, 16, 128), [pressure, comb])
+    near, far, fine_end = lax.optimization_barrier((near, far, fine_end))
     fine_before = moved(fine_end, "tm", 1)
-
-    combined, level1, message = coarse_down(c1)
-    got, jump1 = lax.optimization_barrier((five_chips(message), jump1))
+    got = [message, partner, near, far, swapped_cores(jnp.concatenate([near, far], axis=0))]
+    got, jump1 = lax.optimization_barrier((got, jump1))
     ended1, own2, c2 = coarse_up(coarse_up_middle_body, got + [combined, level1, jump1], UP_SCRATCH)
 
     combined, level1, message = coarse_down(c2)

time: 115 us -> 113 us (0.983)
  waiting for transfers between devices: 33.8 us -> 28 us
  Pallas kernels: 24.4 us -> 26.3 us
  starting transfers between devices: 55.2 us -> 56.6 us
    ppermute x15 -> x9, waiting for transfers between devices: 18.7 us -> 9.02 us  [moved(): lax.ppermute(value, axis, [(i, (i + step) % count) for i in range(count)])]
    ppermute x8 -> x12, waiting for transfers between devices: 4.07 us -> 9.79 us  [from_chips(): lax.ppermute(value, 'sx', [(i, (i + (far if i % 2 else -far)) % count) fo...]
    ppermute x8 -> x11, starting transfers between devices: 13.3 us -> 18.9 us  [swapped_cores(): lax.ppermute(value, 'sx', [(i, i ^ 1) for i in range(lax.axis_size('sx'))])]
    ppermute x15 -> x9, starting transfers between devices: 15.1 us -> 11.9 us  [moved(): lax.ppermute(value, axis, [(i, (i + step) % count) for i in range(count)])]
    ppermute x5, waiting for transfers between devices: 5.41 us -> 3.2 us  [sent(): return lax.ppermute(value, 'tm', [(source, target)])]
    ppermute x1, waiting for transfers between devices: 0.01 us -> 2.05 us  [shards(): jump1 = lax.ppermute(jump0, 'tm', [(1, 0), (2, 1)])]
    pallas_call x13 -> x14, Pallas kernels: 24.4 us -> 26.3 us  [call(): pl.pallas_call(body, out_shape=[jax.ShapeDtypeStruct(s, F32) for s in sha...]
    ppermute x8 -> x12, starting transfers between devices: 15.4 us -> 13.5 us  [from_chips(): lax.ppermute(value, 'sx', [(i, (i + (far if i % 2 else -far)) % count) fo...]
  transfers between devices with their start and end apart: 37 -> 38, of which waited for: 21 -> 21; matrix products, arithmetic and copies ran while one was open for 0% -> 0% of each run, Pallas kernels for 4% -> 5%
where the time goes in v5:
time: 113 us; the launch traced here: 112 us
  starting transfers between devices  56.6 us (50%)
  waiting for transfers between devices  28 us (25%)
  Pallas kernels  26.3 us (23%)
    pallas_call x14, Pallas kernels, call(): pl.pallas_call(body, out_shape=[jax.ShapeDtypeStruct(s, F32) for s in sha...  26.3 us
    ppermute x11, starting transfers between devices, swapped_cores(): lax.ppermute(value, 'sx', [(i, i ^ 1) for i in range(lax.axis_size('sx'))])  18.9 us
    ppermute x12, starting transfers between devices, from_chips(): lax.ppermute(value, 'sx', [(i, (i + (far if i % 2 else -far)) % count) fo...  13.5 us
    ppermute x9, starting transfers between devices, moved(): lax.ppermute(value, axis, [(i, (i + step) % count) for i in range(count)])  11.9 us
    ppermute x5, starting transfers between devices, sent(): return lax.ppermute(value, 'tm', [(source, target)])  11 us
    ppermute x12, waiting for transfers between devices, from_chips(): lax.ppermute(value, 'sx', [(i, (i + (far if i % 2 else -far)) % count) fo...  9.79 us
    ppermute x9, waiting for transfers between devices, moved(): lax.ppermute(value, axis, [(i, (i + step) % count) for i in range(count)])  9.02 us
    ppermute x11, waiting for transfers between devices, swapped_cores(): lax.ppermute(value, 'sx', [(i, i ^ 1) for i in range(lax.axis_size('sx'))])  3.91 us
  transfers between devices with their start and end apart: 38, of which 21 were waited for; matrix products, arithmetic and copies ran while one was open for 0% of the time, Pallas kernels for 5%

profile of v5, /device:TPU:1, one launch (start us, length us, event | category | flops | bytes accessed | tf_op | source)
XLA Modules:
  0.0 112.3 jit_solution(16970590271716782723)
XLA Ops:
  0.7 2.7 %pack_body.1 = (f32[9,16,128]{2,1,0:T(8,128)}, f32[9,16,128]{2,1,0:T(8,128)}, f32[9,16,128]{2,1,0:T(8,128)}, f32[9,16,128]{2,1,0:T(8,128)}, f32[8,16,128]{2,1,0:T(8,128)}) custom-call(f32[4,16,16,128]{3,2,1,0:T(8,128)} %initial.1, f32[4,16,16,128]{3,2,1,0:T(8,128)} %bitcast.19, f32[4,16,16,128]{3,2,1,0:T(8,128)} %bitcast.21), custom_call_target="tpu_custom_call" | custom-call | tf_op jit(solution)/shard_map/pack_body/pallas_call | solution.py:17
  3.3 3.0 %collective-permute-start = (f32[9,16,128]{2,1,0:T(8,128)}, f32[9,16,128]{2,1,0:T(8,128)S(1)}, u32[]{:S(2)}, u32[]{:S(2)}) collective-permute-start(f32[9,16,128]{2,1,0:T(8,128)} %get-tuple-element.69), channel_id=1, source_target_pairs={{0,4},{4,8},{8,12},{12,16},{16,20},{20,24},{24,28},{28,32},{32,36}... | collective-permute-start | bytes 221192 | tf_op jit(solution)/shard_map/ppermute | solution.py:643
  6.6 1.1 collective-permute-start.2
  7.7 1.6 %collective-permute-start.3 = (f32[9,16,128]{2,1,0:T(8,128)}, f32[9,16,128]{2,1,0:T(8,128)S(1)}, u32[]{:S(2)}, u32[]{:S(2)}) collective-permute-start(f32[9,16,128]{2,1,0:T(8,128)} %get-tuple-element.72), channel_id=1, source_target_pairs={{0,3},{1,0},{2,1},{3,2},{4,7},{5,4},{6,5},{7,6},{8,11},{9,8},{10,9... | collective-permute-start | bytes 221192 | tf_op jit(solution)/shard_map/ppermute | solution.py:643
  9.5 0.9 collective-permute-done.1.right
  10.4 1.2 %collective-permute-done.2.low = f32[9,16,128]{2,1,0:T(8,128)S(1)} collective-permute-done((f32[9,16,128]{2,1,0:T(8,128)}, f32[9,16,128]{2,1,0:T(8,128)S(1)}, u32[]{:S(2)}, u32[]{:S(2)}) %collective-permute-start.2) | collective-permute-done | bytes 73760 | tf_op jit(solution)/shard_map/ppermute | solution.py:643
  11.6 1.6 %fine_source_body.1 = (f32[4,16,16,128]{3,2,1,0:T(8,128)S(1)}, f32[31,16,128]{2,1,0:T(8,128)S(1)}, f32[2,8,8,128]{3,2,1,0:T(8,128)S(1)}) custom-call(s32[2]{0:T(128)S(1)} %pad_add_fusion.where, f32[4,16,16,128]{3,2,1,0:T(8,128)S(1)} %bitcast.20, f32[4,16,16,128]{3,2,1,0:T(8,128)S(1)} %bitcast.22, f32[9,16,128]{2,1,0:T(8,128)S(1)} %collective-permute-done.left, ...), custom_call_target="tpu_custom_call" | custom-call | tf_op jit(solution)/shard_map/fine_source_body/pallas_call | solution.py:17
  13.2 2.7 %collective-permute-start.5 = (f32[31,16,128]{2,1,0:T(8,128)S(1)}, f32[31,16,128]{2,1,0:T(8,128)S(1)}, u32[]{:S(2)}, u32[]{:S(2)}) collective-permute-start(f32[31,16,128]{2,1,0:T(8,128)S(1)} %get-tuple-element.74.own.own_share), channel_id=1, source_target_pairs={{0,3},{1,0},{2,1},{3,2},{4,7},{5,4},{6,5},{7,6},{8,11},{9,8},{10,9... | collective-permute-start | bytes 761864 | tf_op jit(solution)/shard_map/ppermute | solution.py:643
  16.0 1.4 %collective-permute-start.6 = (f32[23,16,128]{2,1,0:T(8,128)S(1)}, f32[23,16,128]{2,1,0:T(8,128)S(1)}, u32[]{:S(2)}, u32[]{:S(2)}) collective-permute-start(f32[23,16,128]{2,1,0:T(8,128)S(1)} %slice.45), channel_id=1, source_target_pairs={{0,2},{1,3},{2,0},{3,1},{4,6},{5,7},{6,4},{7,5},{8,10},{9,11},{10,... | collective-permute-start | bytes 565256 | tf_op jit(solution)/shard_map/ppermute | solution.py:643
  17.3 5.7 %collective-permute-done.6.across = f32[23,16,128]{2,1,0:T(8,128)S(1)} collective-permute-done((f32[23,16,128]{2,1,0:T(8,128)S(1)}, f32[23,16,128]{2,1,0:T(8,128)S(1)}, u32[]{:S(2)}, u32[]{:S(2)}) %collective-permute-start.6) | collective-permute-done | bytes 188448 | tf_op jit(solution)/shard_map/ppermute | solution.py:643
  23.0 1.3 %collective-permute-done.4.below = f32[31,16,128]{2,1,0:T(8,128)S(1)} collective-permute-done((f32[31,16,128]{2,1,0:T(8,128)S(1)}, f32[31,16,128]{2,1,0:T(8,128)S(1)}, u32[]{:S(2)}, u32[]{:S(2)}) %collective-permute-start.4) | collective-permute-done | bytes 253984 | tf_op jit(solution)/shard_map/ppermute | solution.py:643
  24.3 2.4 %fine_down_body.1 = (f32[64,128]{1,0:T(8,128)S(1)}, f32[480,128]{1,0:T(8,128)S(1)}, f32[480,128]{1,0:T(8,128)S(1)}, f32[18,64,128]{2,1,0:T(8,128)S(1)}, f32[10,32,128]{2,1,0:T(8,128)S(1)}) custom-call(s32[2]{0:T(128)S(1)} %pad_add_fusion.where, f32[31,16,128]{2,1,0:T(8,128)S(1)} %collective-permute-done.4.below, ...), custom_call_target="tpu_custom_call" | custom-call | tf_op jit(solution)/shard_map/fine_down_body/pallas_call | solution.py:17
  26.7 6.2 %collective-permute-start.7 = (f32[544,128]{1,0:T(8,128)S(1)}, f32[544,128]{1,0:T(8,128)S(1)}, u32[]{:S(2)}, u32[]{:S(2)}) collective-permute-start(f32[544,128]{1,0:T(8,128)S(1)} %pad_maximum_fusion), channel_id=1, source_target_pairs={{0,4},{4,0},{8,12},{12,8},{16,20},{20,16},{24,28},{28,24},{32,36},... | collective-permute-start | bytes 835592 | tf_op jit(solution)/shard_map/ppermute | solution.py:655
  33.0 0.5 collective-permute-start.10
  34.2 2.2 %collective-permute-start.9 = (f32[128,128]{1,0:T(8,128)S(1)}, f32[128,128]{1,0:T(8,128)S(1)}, u32[]{:S(2)}, u32[]{:S(2)}) collective-permute-start(f32[128,128]{1,0:T(8,128)S(1)} %pad_maximum_fusion.5), channel_id=1, source_target_pairs={{0,52},{4,16},{8,60},{12,24},{16,4},{20,32},{24,12},{28,40},{32,20... | collective-permute-start | bytes 196616 | tf_op jit(solution)/shard_map/ppermute | solution.py:661
  36.3 2.3 %collective-permute-start.8 = (f32[128,128]{1,0:T(8,128)S(1)}, f32[128,128]{1,0:T(8,128)S(1)}, u32[]{:S(2)}, u32[]{:S(2)}) collective-permute-start(f32[128,128]{1,0:T(8,128)S(1)} %pad_maximum_fusion.5), channel_id=1, source_target_pairs={{0,60},{4,8},{8,4},{12,16},{16,12},{20,24},{24,20},{28,32},{32,28}... | collective-permute-start | bytes 196616 | tf_op jit(solution)/shard_map/ppermute | solution.py:661
  38.9 0.9 collective-permute-done.9.far
  39.7 1.8 %collective-permute-done.8.near = f32[128,128]{1,0:T(8,128)S(1)} collective-permute-done((f32[128,128]{1,0:T(8,128)S(1)}, f32[128,128]{1,0:T(8,128)S(1)}, u32[]{:S(2)}, u32[]{:S(2)}) %collective-permute-start.8) | collective-permute-done | bytes 65568 | tf_op jit(solution)/shard_map/ppermute | solution.py:661
  41.6 2.5 %collective-permute-start.12 = (f32[256,128]{1,0:T(8,128)S(1)}, f32[256,128]{1,0:T(8,128)S(1)}, u32[]{:S(2)}, u32[]{:S(2)}) collective-permute-start(f32[256,128]{1,0:T(8,128)S(1)} %pad_maximum_fusion.1), channel_id=1, source_target_pairs={{0,4},{4,0},{8,12},{12,8},{16,20},{20,16},{24,28},{28,24},{32,36},... | collective-permute-start | bytes 393224 | tf_op jit(solution)/shard_map/ppermute | solution.py:655
  44.1 1.0 collective-permute-done.12.swapped
  45.1 4.5 %fine_up_body.1 = (f32[18,32,128]{2,1,0:T(8,128)S(1)}, f32[2,8,32,128]{3,2,1,0:T(8,128)S(1)}) custom-call(s32[2]{0:T(128)S(1)} %pad_add_fusion.where, f32[64,128]{1,0:T(8,128)S(1)} %get-tuple-element.75.own, f32[544,128]{1,0:T(8,128)S(1)} %collective-permute-done.7.partner, f32[128,128]{1,0:T(8,128)S(1)} %collective-permute-done.8.near, ...), custom_call_target="tpu_custom_call" | custom-call | tf_op jit(solution)/shard_map/fine_up_body/pallas_call | solution.py:17
  49.6 2.0 %coarse_up_first_body.1 = (f32[2,8,8,128]{3,2,1,0:T(8,128)S(1)}, f32[2,8,8,128]{3,2,1,0:T(8,128)S(1)}, f32[2,4,32,128]{3,2,1,0:T(8,128)S(1)}, f32[2,4,32,128]{3,2,1,0:T(8,128)S(1)}) custom-call(s32[2]{0:T(128)S(1)} %pad_add_fusion.where, f32[64,128]{1,0:T(8,128)S(1)} %get-tuple-element.75.own, f32[544,128]{1,0:T(8,128)S(1)} %collective-permute-done.7.partner, ...), custom_call_target="tpu_custom_call" | custom-call | tf_op jit(solution)/shard_map/coarse_up_first_body/pallas_call | solution.py:17
  51.8 1.7 %collective-permute-start.13 = (f32[2,4,32,128]{3,2,1,0:T(8,128)S(1)}, f32[2,4,32,128]{3,2,1,0:T(8,128)S(1)}, u32[]{:S(2)}, u32[]{:S(2)}) collective-permute-start(f32[2,4,32,128]{3,2,1,0:T(8,128)S(1)} %get-tuple-element.140), channel_id=1, source_target_pairs={{0,4},{4,0},{8,12},{12,8},{16,20},{20,16},{24,28},{28,24},{32,36},... | collective-permute-start | bytes 393224 | tf_op jit(solution)/shard_map/ppermute | solution.py:655
  53.5 2.9 %collective-permute-done.14.outer = f32[2,4,32,128]{3,2,1,0:T(8,128)S(1)} collective-permute-done((f32[2,4,32,128]{3,2,1,0:T(8,128)S(1)}, f32[2,4,32,128]{3,2,1,0:T(8,128)S(1)}, u32[]{:S(2)}, u32[]{:S(2)}) %collective-permute-start.14) | collective-permute-done | bytes 131104 | tf_op jit(solution)/shard_map/ppermute | solution.py:661
  56.4 1.5 %coarse_down_body.3 = (f32[4,8,32,128]{3,2,1,0:T(8,128)S(1)}, f32[12,32,128]{2,1,0:T(8,128)S(1)}, f32[16,128]{1,0:T(8,128)S(1)}) custom-call(s32[2]{0:T(128)S(1)} %pad_add_fusion.where, f32[2,4,32,128]{3,2,1,0:T(8,128)S(1)} %collective-permute-done.13.inner, f32[2,4,32,128]{3,2,1,0:T(8,128)S(1)} %get-tuple-element.87.low, ...), custom_call_target="tpu_custom_call" | custom-call | tf_op jit(solution)/shard_map/coarse_down_body/pallas_call | solution.py:17
  57.8 1.4 %collective-permute-start.15 = (f32[16,128]{1,0:T(8,128)S(1)}, f32[16,128]{1,0:T(8,128)S(1)}, u32[]{:S(2)}, u32[]{:S(2)}) collective-permute-start(f32[16,128]{1,0:T(8,128)S(1)} %get-tuple-element.95.a), channel_id=1, source_target_pairs={{0,4},{4,0},{8,12},{12,8},{16,20},{20,16},{24,28},{28,24},{32,36},... | collective-permute-start | bytes 24584 | tf_op jit(solution)/shard_map/ppermute | solution.py:655
  59.2 1.3 %collective-permute-start.19 = (f32[2,8,32,128]{3,2,1,0:T(8,128)S(1)}, f32[2,8,32,128]{3,2,1,0:T(8,128)S(1)}, u32[]{:S(2)}, u32[]{:S(2)}) collective-permute-start(f32[2,8,32,128]{3,2,1,0:T(8,128)S(1)} %get-tuple-element.85.jump), channel_id=1, source_target_pairs={{64,0},{128,64},{65,1},{129,65},{66,2},{130,66},{67,3},{131,67},{6... | collective-permute-start | bytes 786440 | tf_op jit(solution)/shard_map/ppermute | solution.py:771
  60.5 1.7 %collective-permute-start.17 = (f32[32,128]{1,0:T(8,128)S(1)}, f32[32,128]{1,0:T(8,128)S(1)}, u32[]{:S(2)}, u32[]{:S(2)}) collective-permute-start(f32[32,128]{1,0:T(8,128)S(1)} %pad_maximum_fusion.9), channel_id=1, source_target_pairs={{0,52},{4,16},{8,60},{12,24},{16,4},{20,32},{24,12},{28,40},{32,20... | collective-permute-start | bytes 49160 | tf_op jit(solution)/shard_map/ppermute | solution.py:661
  62.2 0.9 collective-permute-start.16
  63.1 0.9 fine_end_body.1
  64.0 0.9 collective-permute-done.17.d
  65.0 0.7 collective-permute-done.16.c
  65.6 0.5 collective-permute-start.18
  66.1 0.9 collective-permute-done.18.e
  66.9 2.1 %collective-permute-done.19.jump = f32[2,8,32,128]{3,2,1,0:T(8,128)S(1)} collective-permute-done((f32[2,8,32,128]{3,2,1,0:T(8,128)S(1)}, f32[2,8,32,128]{3,2,1,0:T(8,128)S(1)}, u32[]{:S(2)}, u32[]{:S(2)}) %collective-permute-start.19) | collective-permute-done | bytes 262176 | tf_op jit(solution)/shard_map/ppermute | solution.py:771
  69.0 1.8 %coarse_up_middle_body.2 = (f32[2,8,8,128]{3,2,1,0:T(8,128)S(1)}, f32[2,8,8,128]{3,2,1,0:T(8,128)S(1)}, f32[2,4,32,128]{3,2,1,0:T(8,128)S(1)}, f32[2,4,32,128]{3,2,1,0:T(8,128)S(1)}) custom-call(s32[2]{0:T(128)S(1)} %pad_add_fusion.where, f32[16,128]{1,0:T(8,128)S(1)} %get-tuple-element.95.a, f32[16,128]{1,0:T(8,128)S(1)} %collective-permute-done.15.b, ...), custom_call_target="tpu_custom_call" | custom-call | tf_op jit(solution)/shard_map/coarse_up_middle_body/pallas_call | solution.py:17
  70.8 0.5 collective-permute-start.21
  71.8 1.6 %collective-permute-start.28 = (f32[4,16,16,128]{3,2,1,0:T(8,128)S(1)}, f32[4,16,16,128]{3,2,1,0:T(8,128)S(1)}, u32[]{:S(2)}, u32[]{:S(2)}) collective-permute-start(f32[4,16,16,128]{3,2,1,0:T(8,128)S(1)} %copy-done.4), channel_id=1, source_target_pairs={{0,64},{64,128},{128,192},{192,0},{1,65},{65,129},{129,193},{193,1... | collective-permute-start | bytes 1572872 | tf_op jit(solution)/shard_map/ppermute | solution.py:643
  73.4 1.3 %collective-permute-start.27 = (f32[2,8,32,128]{3,2,1,0:T(8,128)S(1)}, f32[2,8,32,128]{3,2,1,0:T(8,128)S(1)}, u32[]{:S(2)}, u32[]{:S(2)}) collective-permute-start(f32[2,8,32,128]{3,2,1,0:T(8,128)S(1)} %collective-permute-done.19.jump), channel_id=1, source_target_pairs={{64,0},{65,1},{66,2},{67,3},{68,4},{69,5},{70,6},{71,7},{72,8},{73... | collective-permute-start | bytes 786440 | tf_op jit(solution)/shard_map/ppermute | solution.py:680
  74.7 0.9 collective-permute-done.21.outer
  75.6 1.5 %coarse_down_body.4 = (f32[4,8,32,128]{3,2,1,0:T(8,128)S(1)}, f32[12,32,128]{2,1,0:T(8,128)S(1)}, f32[16,128]{1,0:T(8,128)S(1)}) custom-call(s32[2]{0:T(128)S(1)} %pad_add_fusion.where, f32[2,4,32,128]{3,2,1,0:T(8,128)S(1)} %collective-permute-done.20.inner, f32[2,4,32,128]{3,2,1,0:T(8,128)S(1)} %get-tuple-element.104.low, ...), custom_call_target="tpu_custom_call" | custom-call | tf_op jit(solution)/shard_map/coarse_down_body/pallas_call | solution.py:17
  77.1 1.8 %collective-permute-start.22 = (f32[16,128]{1,0:T(8,128)S(1)}, f32[16,128]{1,0:T(8,128)S(1)}, u32[]{:S(2)}, u32[]{:S(2)}) collective-permute-start(f32[16,128]{1,0:T(8,128)S(1)} %get-tuple-element.111.a), channel_id=1, source_target_pairs={{0,4},{4,0},{8,12},{12,8},{16,20},{20,16},{24,28},{28,24},{32,36},... | collective-permute-start | bytes 24584 | tf_op jit(solution)/shard_map/ppermute | solution.py:655
  78.9 0.8 collective-permute-done.22.b
  79.7 1.2 %collective-permute-start.24 = (f32[32,128]{1,0:T(8,128)S(1)}, f32[32,128]{1,0:T(8,128)S(1)}, u32[]{:S(2)}, u32[]{:S(2)}) collective-permute-start(f32[32,128]{1,0:T(8,128)S(1)} %constant_dynamic-update-slice_fusion), channel_id=1, source_target_pairs={{0,52},{4,16},{8,60},{12,24},{16,4},{20,32},{24,12},{28,40},{32,20... | collective-permute-start | bytes 49160 | tf_op jit(solution)/shard_map/ppermute | solution.py:661
  80.9 0.5 collective-permute-start.23
  81.4 4.3 %collective-permute-start.26 = (f32[4,8,8,128]{3,2,1,0:T(8,128)S(1)}, f32[4,8,8,128]{3,2,1,0:T(8,128)S(1)}, u32[]{:S(2)}, u32[]{:S(2)}) collective-permute-start(f32[4,8,8,128]{3,2,1,0:T(8,128)S(1)} %pad_maximum_fusion.2), channel_id=1, source_target_pairs={{0,64},{1,65},{2,66},{3,67},{4,68},{5,69},{6,70},{7,71},{8,72},{9,... | collective-permute-start | bytes 393224 | tf_op jit(solution)/shard_map/ppermute | solution.py:680
  85.8 0.8 collective-permute-start.25
  86.6 1.5 %collective-permute-done.26 = f32[4,8,8,128]{3,2,1,0:T(8,128)S(1)} collective-permute-done((f32[4,8,8,128]{3,2,1,0:T(8,128)S(1)}, f32[4,8,8,128]{3,2,1,0:T(8,128)S(1)}, u32[]{:S(2)}, u32[]{:S(2)}) %collective-permute-start.26) | collective-permute-done | bytes 131104 | tf_op jit(solution)/shard_map/ppermute | solution.py:680
  88.1 1.8 %coarse_up_middle_body.3 = (f32[2,8,8,128]{3,2,1,0:T(8,128)S(1)}, f32[2,8,8,128]{3,2,1,0:T(8,128)S(1)}, f32[2,4,32,128]{3,2,1,0:T(8,128)S(1)}, f32[2,4,32,128]{3,2,1,0:T(8,128)S(1)}) custom-call(s32[2]{0:T(128)S(1)} %pad_add_fusion.where, f32[16,128]{1,0:T(8,128)S(1)} %get-tuple-element.111.a, f32[16,128]{1,0:T(8,128)S(1)} %collective-permute-done.22.b, ...), custom_call_target="tpu_custom_call" | custom-call | tf_op jit(solution)/shard_map/coarse_up_middle_body/pallas_call | solution.py:17
  89.9 2.1 %collective-permute-start.30 = (f32[2,4,32,128]{3,2,1,0:T(8,128)S(1)}, f32[2,4,32,128]{3,2,1,0:T(8,128)S(1)}, u32[]{:S(2)}, u32[]{:S(2)}) collective-permute-start(f32[2,4,32,128]{3,2,1,0:T(8,128)S(1)} %get-tuple-element.135), channel_id=1, source_target_pairs={{0,60},{4,8},{8,4},{12,16},{16,12},{20,24},{24,20},{28,32},{32,28}... | collective-permute-start | bytes 393224 | tf_op jit(solution)/shard_map/ppermute | solution.py:661
  92.0 1.3 %collective-permute-start.36 = (f32[2,8,8,128]{3,2,1,0:T(8,128)S(1)}, f32[2,8,8,128]{3,2,1,0:T(8,128)S(1)}, u32[]{:S(2)}, u32[]{:S(2)}) collective-permute-start(f32[2,8,8,128]{3,2,1,0:T(8,128)S(1)} %get-tuple-element.124), channel_id=1, source_target_pairs={{0,192},{1,193},{2,194},{3,195},{4,196},{5,197},{6,198},{7,199},{8... | collective-permute-start | bytes 196616 | tf_op jit(solution)/shard_map/ppermute | solution.py:680
  93.3 1.4 %collective-permute-done.30.outer = f32[2,4,32,128]{3,2,1,0:T(8,128)S(1)} collective-permute-done((f32[2,4,32,128]{3,2,1,0:T(8,128)S(1)}, f32[2,4,32,128]{3,2,1,0:T(8,128)S(1)}, u32[]{:S(2)}, u32[]{:S(2)}) %collective-permute-start.30) | collective-permute-done | bytes 131104 | tf_op jit(solution)/shard_map/ppermute | solution.py:661
  94.7 1.5 %coarse_down_body.5 = (f32[4,8,32,128]{3,2,1,0:T(8,128)S(1)}, f32[12,32,128]{2,1,0:T(8,128)S(1)}, f32[16,128]{1,0:T(8,128)S(1)}) custom-call(s32[2]{0:T(128)S(1)} %pad_add_fusion.where, f32[2,4,32,128]{3,2,1,0:T(8,128)S(1)} %collective-permute-done.29.inner, f32[2,4,32,128]{3,2,1,0:T(8,128)S(1)} %get-tuple-element.120.low, ...), custom_call_target="tpu_custom_call" | custom-call | tf_op jit(solution)/shard_map/coarse_down_body/pallas_call | solution.py:17
  96.1 2.4 %collective-permute-start.31 = (f32[16,128]{1,0:T(8,128)S(1)}, f32[16,128]{1,0:T(8,128)S(1)}, u32[]{:S(2)}, u32[]{:S(2)}) collective-permute-start(f32[16,128]{1,0:T(8,128)S(1)} %get-tuple-element.128.a), channel_id=1, source_target_pairs={{0,4},{4,0},{8,12},{12,8},{16,20},{20,16},{24,28},{28,24},{32,36},... | collective-permute-start | bytes 24584 | tf_op jit(solution)/shard_map/ppermute | solution.py:655
  98.5 0.8 collective-permute-done.31.b
  99.3 0.8 collective-permute-start.33
  100.1 0.7 collective-permute-start.32
  100.8 2.9 %collective-permute-start.35 = (f32[4,8,8,128]{3,2,1,0:T(8,128)S(1)}, f32[4,8,8,128]{3,2,1,0:T(8,128)S(1)}, u32[]{:S(2)}, u32[]{:S(2)}) collective-permute-start(f32[4,8,8,128]{3,2,1,0:T(8,128)S(1)} %pad_maximum_fusion.3), channel_id=1, source_target_pairs={{0,128},{1,129},{2,130},{3,131},{4,132},{5,133},{6,134},{7,135},{8... | collective-permute-start | bytes 393224 | tf_op jit(solution)/shard_map/ppermute | solution.py:680
  103.7 1.3 %collective-permute-start.34 = (f32[64,128]{1,0:T(8,128)S(1)}, f32[64,128]{1,0:T(8,128)S(1)}, u32[]{:S(2)}, u32[]{:S(2)}) collective-permute-start(f32[64,128]{1,0:T(8,128)S(1)} %pad_maximum_fusion.8), channel_id=1, source_target_pairs={{0,4},{4,0},{8,12},{12,8},{16,20},{20,16},{24,28},{28,24},{32,36},... | collective-permute-start | bytes 98312 | tf_op jit(solution)/shard_map/ppermute | solution.py:655
  105.0 1.7 %collective-permute-done.35 = f32[4,8,8,128]{3,2,1,0:T(8,128)S(1)} collective-permute-done((f32[4,8,8,128]{3,2,1,0:T(8,128)S(1)}, f32[4,8,8,128]{3,2,1,0:T(8,128)S(1)}, u32[]{:S(2)}, u32[]{:S(2)}) %collective-permute-start.35) | collective-permute-done | bytes 131104 | tf_op jit(solution)/shard_map/ppermute | solution.py:680
  106.7 1.6 %coarse_up_last_body.1 = f32[2,8,8,128]{3,2,1,0:T(8,128)S(1)} custom-call(s32[2]{0:T(128)S(1)} %pad_add_fusion.where, f32[16,128]{1,0:T(8,128)S(1)} %get-tuple-element.128.a, f32[16,128]{1,0:T(8,128)S(1)} %collective-permute-done.31.b, f32[32,128]{1,0:T(8,128)S(1)} %collective-permute-done.32.c, f32[32,128]{1,0:T(8,128)S(1)} %collective-permute-done.33.d, ...), custom_call_target="tpu_custom_call" | custom-call | tf_op jit(solution)/shard_map/coarse_up_last_body/pallas_call | solution.py:17
  108.3 1.3 %collective-permute-start.37 = (f32[2,8,8,128]{3,2,1,0:T(8,128)S(1)}, f32[2,8,8,128]{3,2,1,0:T(8,128)S(1)}, u32[]{:S(2)}, u32[]{:S(2)}) collective-permute-start(f32[2,8,8,128]{3,2,1,0:T(8,128)S(1)} %coarse_up_last_body.1), channel_id=1, source_target_pairs={{0,192},{1,193},{2,194},{3,195},{4,196},{5,197},{6,198},{7,199},{8... | collective-permute-start | bytes 196616 | tf_op jit(solution)/shard_map/ppermute | solution.py:680
  109.6 1.4 %new_start_body.1 = f32[4,16,16,128]{3,2,1,0:T(8,128)} custom-call(s32[2]{0:T(128)S(1)} %pad_add_fusion.where, f32[4,16,16,128]{3,2,1,0:T(8,128)S(1)} %collective-permute-done.28.fine, f32[4,16,16,128]{3,2,1,0:T(8,128)S(1)} %copy-done.2, f32[2,8,8,128]{3,2,1,0:T(8,128)S(1)} %get-tuple-element.142.state), custom_call_target="tpu_custom_call" | custom-call | tf_op jit(solution)/shard_map/new_start_body/pallas_call | solution.py:17
  111.0 1.3 %coarse_end_body.1 = f32[4,8,8,64]{3,2,1,0:T(8,128)} custom-call(s32[2]{0:T(128)S(1)} %pad_add_fusion.where, f32[2,8,8,128]{3,2,1,0:T(8,128)S(1)} %get-tuple-element.127.e0, f32[2,8,8,128]{3,2,1,0:T(8,128)S(1)} %get-tuple-element.143.e1, f32[2,8,8,128]{3,2,1,0:T(8,128)S(1)} %get-tuple-element.141.e2, f32[2,8,8,128]{3,2,1,0:T(8,128)S(1)} %collective-permute-done.37.e3), custom_call_target="tpu_custom_call" | custom-call | tf_op jit(solution)/shard_map/coarse_end_body/pallas_call | solution.py:17
  (63 shorter events, 2.4 us)
Async XLA Ops:
  0.6 8.7 %copy-start.5 = (f32[1,4,8,8,64]{4,3,2,1,0:T(8,128)S(1)}, f32[1,4,8,8,64]{4,3,2,1,0:T(8,128)}, u32[]{:S(2)}) copy-start(f32[1,4,8,8,64]{4,3,2,1,0:T(8,128)} %param.7) | copy-start | bytes 196612
  0.6 10.9 %copy-start.1 = (f32[1,4,16,16,128]{4,3,2,1,0:T(8,128)S(1)}, f32[1,4,16,16,128]{4,3,2,1,0:T(8,128)}, u32[]{:S(2)}) copy-start(f32[1,4,16,16,128]{4,3,2,1,0:T(8,128)} %param.6) | copy-start | bytes 1572868
  3.3 8.2 %copy-start = (f32[1,4,16,16,128]{4,3,2,1,0:T(8,128)S(1)}, f32[1,4,16,16,128]{4,3,2,1,0:T(8,128)}, u32[]{:S(2)}) copy-start(f32[1,4,16,16,128]{4,3,2,1,0:T(8,128)} %param.5) | copy-start | bytes 1572868
  3.3 6.2 %collective-permute-start = (f32[9,16,128]{2,1,0:T(8,128)}, f32[9,16,128]{2,1,0:T(8,128)S(1)}, u32[]{:S(2)}, u32[]{:S(2)}) collective-permute-start(f32[9,16,128]{2,1,0:T(8,128)} %get-tuple-element.69), channel_id=1, source_target_pairs={{0,4},{4,8},{8,12},{12,16},{16,20},{20,24},{24,28},{28,32},{32,36}... | collective-permute-start | bytes 221192 | tf_op jit(solution)/shard_map/ppermute | solution.py:643
  6.4 4.0 %collective-permute-start.1 = (f32[9,16,128]{2,1,0:T(8,128)}, f32[9,16,128]{2,1,0:T(8,128)S(1)}, u32[]{:S(2)}, u32[]{:S(2)}) collective-permute-start(f32[9,16,128]{2,1,0:T(8,128)} %get-tuple-element.70), channel_id=1, source_target_pairs={{0,60},{4,0},{8,4},{12,8},{16,12},{20,16},{24,20},{28,24},{32,28},... | collective-permute-start | bytes 221192 | tf_op jit(solution)/shard_map/ppermute | solution.py:643
  6.6 4.9 %collective-permute-start.2 = (f32[9,16,128]{2,1,0:T(8,128)}, f32[9,16,128]{2,1,0:T(8,128)S(1)}, u32[]{:S(2)}, u32[]{:S(2)}) collective-permute-start(f32[9,16,128]{2,1,0:T(8,128)} %get-tuple-element.71), channel_id=1, source_target_pairs={{0,1},{1,2},{2,3},{3,0},{4,5},{5,6},{6,7},{7,4},{8,9},{9,10},{10,1... | collective-permute-start | bytes 221192 | tf_op jit(solution)/shard_map/ppermute | solution.py:643
  7.7 3.9 %collective-permute-start.3 = (f32[9,16,128]{2,1,0:T(8,128)}, f32[9,16,128]{2,1,0:T(8,128)S(1)}, u32[]{:S(2)}, u32[]{:S(2)}) collective-permute-start(f32[9,16,128]{2,1,0:T(8,128)} %get-tuple-element.72), channel_id=1, source_target_pairs={{0,3},{1,0},{2,1},{3,2},{4,7},{5,4},{6,5},{7,6},{8,11},{9,8},{10,9... | collective-permute-start | bytes 221192 | tf_op jit(solution)/shard_map/ppermute | solution.py:643
  9.4 2.1 %copy-start.3 = (f32[8,16,128]{2,1,0:T(8,128)S(1)}, f32[8,16,128]{2,1,0:T(8,128)}, u32[]{:S(2)}) copy-start(f32[8,16,128]{2,1,0:T(8,128)} %get-tuple-element.73.opening) | copy-start | bytes 196612
  13.2 9.8 %collective-permute-start.5 = (f32[31,16,128]{2,1,0:T(8,128)S(1)}, f32[31,16,128]{2,1,0:T(8,128)S(1)}, u32[]{:S(2)}, u32[]{:S(2)}) collective-permute-start(f32[31,16,128]{2,1,0:T(8,128)S(1)} %get-tuple-element.74.own.own_share), channel_id=1, source_target_pairs={{0,3},{1,0},{2,1},{3,2},{4,7},{5,4},{6,5},{7,6},{8,11},{9,8},{10,9... | collective-permute-start | bytes 761864 | tf_op jit(solution)/shard_map/ppermute | solution.py:643
  15.9 8.4 %collective-permute-start.4 = (f32[31,16,128]{2,1,0:T(8,128)S(1)}, f32[31,16,128]{2,1,0:T(8,128)S(1)}, u32[]{:S(2)}, u32[]{:S(2)}) collective-permute-start(f32[31,16,128]{2,1,0:T(8,128)S(1)} %get-tuple-element.74.own.own_share), channel_id=1, source_target_pairs={{0,1},{1,2},{2,3},{3,0},{4,5},{5,6},{6,7},{7,4},{8,9},{9,10},{10,1... | collective-permute-start | bytes 761864 | tf_op jit(solution)/shard_map/ppermute | solution.py:643
  16.0 7.0 %collective-permute-start.6 = (f32[23,16,128]{2,1,0:T(8,128)S(1)}, f32[23,16,128]{2,1,0:T(8,128)S(1)}, u32[]{:S(2)}, u32[]{:S(2)}) collective-permute-start(f32[23,16,128]{2,1,0:T(8,128)S(1)} %slice.45), channel_id=1, source_target_pairs={{0,2},{1,3},{2,0},{3,1},{4,6},{5,7},{6,4},{7,5},{8,10},{9,11},{10,... | collective-permute-start | bytes 565256 | tf_op jit(solution)/shard_map/ppermute | solution.py:643
  26.7 7.4 %collective-permute-start.7 = (f32[544,128]{1,0:T(8,128)S(1)}, f32[544,128]{1,0:T(8,128)S(1)}, u32[]{:S(2)}, u32[]{:S(2)}) collective-permute-start(f32[544,128]{1,0:T(8,128)S(1)} %pad_maximum_fusion), channel_id=1, source_target_pairs={{0,4},{4,0},{8,12},{12,8},{16,20},{20,16},{24,28},{28,24},{32,36},... | collective-permute-start | bytes 835592 | tf_op jit(solution)/shard_map/ppermute | solution.py:655
  33.0 5.9 %collective-permute-start.10 = (f32[480,128]{1,0:T(8,128)S(1)}, f32[480,128]{1,0:T(8,128)S(1)}, u32[]{:S(2)}, u32[]{:S(2)}) collective-permute-start(f32[480,128]{1,0:T(8,128)S(1)} %get-tuple-element.77), channel_id=1, source_target_pairs={{0,60},{4,8},{8,4},{12,16},{16,12},{20,24},{24,20},{28,32},{32,28}... | collective-permute-start | bytes 737288 | tf_op jit(solution)/shard_map/ppermute | solution.py:661
  33.4 5.2 %collective-permute-start.11 = (f32[8,16,128]{2,1,0:T(8,128)S(1)}, f32[8,16,128]{2,1,0:T(8,128)S(1)}, u32[]{:S(2)}, u32[]{:S(2)}) collective-permute-start(f32[8,16,128]{2,1,0:T(8,128)S(1)} %slice.47), channel_id=1, source_target_pairs={{0,2},{1,3},{2,0},{3,1},{4,6},{5,7},{6,4},{7,5},{8,10},{9,11},{10,... | collective-permute-start | bytes 196616 | tf_op jit(solution)/shard_map/ppermute | solution.py:643
  34.2 5.6 %collective-permute-start.9 = (f32[128,128]{1,0:T(8,128)S(1)}, f32[128,128]{1,0:T(8,128)S(1)}, u32[]{:S(2)}, u32[]{:S(2)}) collective-permute-start(f32[128,128]{1,0:T(8,128)S(1)} %pad_maximum_fusion.5), channel_id=1, source_target_pairs={{0,52},{4,16},{8,60},{12,24},{16,4},{20,32},{24,12},{28,40},{32,20... | collective-permute-start | bytes 196616 | tf_op jit(solution)/shard_map/ppermute | solution.py:661
  36.3 5.2 %collective-permute-start.8 = (f32[128,128]{1,0:T(8,128)S(1)}, f32[128,128]{1,0:T(8,128)S(1)}, u32[]{:S(2)}, u32[]{:S(2)}) collective-permute-start(f32[128,128]{1,0:T(8,128)S(1)} %pad_maximum_fusion.5), channel_id=1, source_target_pairs={{0,60},{4,8},{8,4},{12,16},{16,12},{20,24},{24,20},{28,32},{32,28}... | collective-permute-start | bytes 196616 | tf_op jit(solution)/shard_map/ppermute | solution.py:661
  41.6 3.5 %collective-permute-start.12 = (f32[256,128]{1,0:T(8,128)S(1)}, f32[256,128]{1,0:T(8,128)S(1)}, u32[]{:S(2)}, u32[]{:S(2)}) collective-permute-start(f32[256,128]{1,0:T(8,128)S(1)} %pad_maximum_fusion.1), channel_id=1, source_target_pairs={{0,4},{4,0},{8,12},{12,8},{16,20},{20,16},{24,28},{28,24},{32,36},... | collective-permute-start | bytes 393224 | tf_op jit(solution)/shard_map/ppermute | solution.py:655
  51.6 4.8 %collective-permute-start.14 = (f32[2,4,32,128]{3,2,1,0:T(8,128)S(1)}, f32[2,4,32,128]{3,2,1,0:T(8,128)S(1)}, u32[]{:S(2)}, u32[]{:S(2)}) collective-permute-start(f32[2,4,32,128]{3,2,1,0:T(8,128)S(1)} %get-tuple-element.139), channel_id=1, source_target_pairs={{0,60},{4,8},{8,4},{12,16},{16,12},{20,24},{24,20},{28,32},{32,28}... | collective-permute-start | bytes 393224 | tf_op jit(solution)/shard_map/ppermute | solution.py:661
  51.8 4.6 %collective-permute-start.13 = (f32[2,4,32,128]{3,2,1,0:T(8,128)S(1)}, f32[2,4,32,128]{3,2,1,0:T(8,128)S(1)}, u32[]{:S(2)}, u32[]{:S(2)}) collective-permute-start(f32[2,4,32,128]{3,2,1,0:T(8,128)S(1)} %get-tuple-element.140), channel_id=1, source_target_pairs={{0,4},{4,0},{8,12},{12,8},{16,20},{20,16},{24,28},{28,24},{32,36},... | collective-permute-start | bytes 393224 | tf_op jit(solution)/shard_map/ppermute | solution.py:655
  57.8 2.7 %collective-permute-start.15 = (f32[16,128]{1,0:T(8,128)S(1)}, f32[16,128]{1,0:T(8,128)S(1)}, u32[]{:S(2)}, u32[]{:S(2)}) collective-permute-start(f32[16,128]{1,0:T(8,128)S(1)} %get-tuple-element.95.a), channel_id=1, source_target_pairs={{0,4},{4,0},{8,12},{12,8},{16,20},{20,16},{24,28},{28,24},{32,36},... | collective-permute-start | bytes 24584 | tf_op jit(solution)/shard_map/ppermute | solution.py:655
  59.2 9.8 %collective-permute-start.19 = (f32[2,8,32,128]{3,2,1,0:T(8,128)S(1)}, f32[2,8,32,128]{3,2,1,0:T(8,128)S(1)}, u32[]{:S(2)}, u32[]{:S(2)}) collective-permute-start(f32[2,8,32,128]{3,2,1,0:T(8,128)S(1)} %get-tuple-element.85.jump), channel_id=1, source_target_pairs={{64,0},{128,64},{65,1},{129,65},{66,2},{130,66},{67,3},{131,67},{6... | collective-permute-start | bytes 786440 | tf_op jit(solution)/shard_map/ppermute | solution.py:771
  60.5 4.4 %collective-permute-start.17 = (f32[32,128]{1,0:T(8,128)S(1)}, f32[32,128]{1,0:T(8,128)S(1)}, u32[]{:S(2)}, u32[]{:S(2)}) collective-permute-start(f32[32,128]{1,0:T(8,128)S(1)} %pad_maximum_fusion.9), channel_id=1, source_target_pairs={{0,52},{4,16},{8,60},{12,24},{16,4},{20,32},{24,12},{28,40},{32,20... | collective-permute-start | bytes 49160 | tf_op jit(solution)/shard_map/ppermute | solution.py:661
  62.2 3.5 %collective-permute-start.16 = (f32[32,128]{1,0:T(8,128)S(1)}, f32[32,128]{1,0:T(8,128)S(1)}, u32[]{:S(2)}, u32[]{:S(2)}) collective-permute-start(f32[32,128]{1,0:T(8,128)S(1)} %pad_maximum_fusion.9), channel_id=1, source_target_pairs={{0,60},{4,8},{8,4},{12,16},{16,12},{20,24},{24,20},{28,32},{32,28}... | collective-permute-start | bytes 49160 | tf_op jit(solution)/shard_map/ppermute | solution.py:661
  65.6 1.3 %collective-permute-start.18 = (f32[64,128]{1,0:T(8,128)S(1)}, f32[64,128]{1,0:T(8,128)S(1)}, u32[]{:S(2)}, u32[]{:S(2)}) collective-permute-start(f32[64,128]{1,0:T(8,128)S(1)} %pad_maximum_fusion.6), channel_id=1, source_target_pairs={{0,4},{4,0},{8,12},{12,8},{16,20},{20,16},{24,28},{28,24},{32,36},... | collective-permute-start | bytes 98312 | tf_op jit(solution)/shard_map/ppermute | solution.py:655
  70.8 1.0 copy-start.4
  70.8 4.8 %collective-permute-start.21 = (f32[2,4,32,128]{3,2,1,0:T(8,128)S(1)}, f32[2,4,32,128]{3,2,1,0:T(8,128)S(1)}, u32[]{:S(2)}, u32[]{:S(2)}) collective-permute-start(f32[2,4,32,128]{3,2,1,0:T(8,128)S(1)} %get-tuple-element.137), channel_id=1, source_target_pairs={{0,60},{4,8},{8,4},{12,16},{16,12},{20,24},{24,20},{28,32},{32,28}... | collective-permute-start | bytes 393224 | tf_op jit(solution)/shard_map/ppermute | solution.py:661
  71.4 4.2 %collective-permute-start.20 = (f32[2,4,32,128]{3,2,1,0:T(8,128)S(1)}, f32[2,4,32,128]{3,2,1,0:T(8,128)S(1)}, u32[]{:S(2)}, u32[]{:S(2)}) collective-permute-start(f32[2,4,32,128]{3,2,1,0:T(8,128)S(1)} %get-tuple-element.138), channel_id=1, source_target_pairs={{0,4},{4,0},{8,12},{12,8},{16,20},{20,16},{24,28},{28,24},{32,36},... | collective-permute-start | bytes 393224 | tf_op jit(solution)/shard_map/ppermute | solution.py:655
  71.8 16.3 %collective-permute-start.28 = (f32[4,16,16,128]{3,2,1,0:T(8,128)S(1)}, f32[4,16,16,128]{3,2,1,0:T(8,128)S(1)}, u32[]{:S(2)}, u32[]{:S(2)}) collective-permute-start(f32[4,16,16,128]{3,2,1,0:T(8,128)S(1)} %copy-done.4), channel_id=1, source_target_pairs={{0,64},{64,128},{128,192},{192,0},{1,65},{65,129},{129,193},{193,1... | collective-permute-start | bytes 1572872 | tf_op jit(solution)/shard_map/ppermute | solution.py:643
  73.4 14.7 %collective-permute-start.27 = (f32[2,8,32,128]{3,2,1,0:T(8,128)S(1)}, f32[2,8,32,128]{3,2,1,0:T(8,128)S(1)}, u32[]{:S(2)}, u32[]{:S(2)}) collective-permute-start(f32[2,8,32,128]{3,2,1,0:T(8,128)S(1)} %collective-permute-done.19.jump), channel_id=1, source_target_pairs={{64,0},{65,1},{66,2},{67,3},{68,4},{69,5},{70,6},{71,7},{72,8},{73... | collective-permute-start | bytes 786440 | tf_op jit(solution)/shard_map/ppermute | solution.py:680
  77.1 2.6 %collective-permute-start.22 = (f32[16,128]{1,0:T(8,128)S(1)}, f32[16,128]{1,0:T(8,128)S(1)}, u32[]{:S(2)}, u32[]{:S(2)}) collective-permute-start(f32[16,128]{1,0:T(8,128)S(1)} %get-tuple-element.111.a), channel_id=1, source_target_pairs={{0,4},{4,0},{8,12},{12,8},{16,20},{20,16},{24,28},{28,24},{32,36},... | collective-permute-start | bytes 24584 | tf_op jit(solution)/shard_map/ppermute | solution.py:655
  79.7 6.0 %collective-permute-start.24 = (f32[32,128]{1,0:T(8,128)S(1)}, f32[32,128]{1,0:T(8,128)S(1)}, u32[]{:S(2)}, u32[]{:S(2)}) collective-permute-start(f32[32,128]{1,0:T(8,128)S(1)} %constant_dynamic-update-slice_fusion), channel_id=1, source_target_pairs={{0,52},{4,16},{8,60},{12,24},{16,4},{20,32},{24,12},{28,40},{32,20... | collective-permute-start | bytes 49160 | tf_op jit(solution)/shard_map/ppermute | solution.py:661
  80.9 4.8 %collective-permute-start.23 = (f32[32,128]{1,0:T(8,128)S(1)}, f32[32,128]{1,0:T(8,128)S(1)}, u32[]{:S(2)}, u32[]{:S(2)}) collective-permute-start(f32[32,128]{1,0:T(8,128)S(1)} %constant_dynamic-update-slice_fusion), channel_id=1, source_target_pairs={{0,60},{4,8},{8,4},{12,16},{16,12},{20,24},{24,20},{28,32},{32,28}... | collective-permute-start | bytes 49160 | tf_op jit(solution)/shard_map/ppermute | solution.py:661
  81.4 6.7 %collective-permute-start.26 = (f32[4,8,8,128]{3,2,1,0:T(8,128)S(1)}, f32[4,8,8,128]{3,2,1,0:T(8,128)S(1)}, u32[]{:S(2)}, u32[]{:S(2)}) collective-permute-start(f32[4,8,8,128]{3,2,1,0:T(8,128)S(1)} %pad_maximum_fusion.2), channel_id=1, source_target_pairs={{0,64},{1,65},{2,66},{3,67},{4,68},{5,69},{6,70},{7,71},{8,72},{9,... | collective-permute-start | bytes 393224 | tf_op jit(solution)/shard_map/ppermute | solution.py:680
  85.8 2.3 %collective-permute-start.25 = (f32[64,128]{1,0:T(8,128)S(1)}, f32[64,128]{1,0:T(8,128)S(1)}, u32[]{:S(2)}, u32[]{:S(2)}) collective-permute-start(f32[64,128]{1,0:T(8,128)S(1)} %pad_maximum_fusion.7), channel_id=1, source_target_pairs={{0,4},{4,0},{8,12},{12,8},{16,20},{20,16},{24,28},{28,24},{32,36},... | collective-permute-start | bytes 98312 | tf_op jit(solution)/shard_map/ppermute | solution.py:655
  89.9 4.7 %collective-permute-start.30 = (f32[2,4,32,128]{3,2,1,0:T(8,128)S(1)}, f32[2,4,32,128]{3,2,1,0:T(8,128)S(1)}, u32[]{:S(2)}, u32[]{:S(2)}) collective-permute-start(f32[2,4,32,128]{3,2,1,0:T(8,128)S(1)} %get-tuple-element.135), channel_id=1, source_target_pairs={{0,60},{4,8},{8,4},{12,16},{16,12},{20,24},{24,20},{28,32},{32,28}... | collective-permute-start | bytes 393224 | tf_op jit(solution)/shard_map/ppermute | solution.py:661
  92.0 2.7 %collective-permute-start.29 = (f32[2,4,32,128]{3,2,1,0:T(8,128)S(1)}, f32[2,4,32,128]{3,2,1,0:T(8,128)S(1)}, u32[]{:S(2)}, u32[]{:S(2)}) collective-permute-start(f32[2,4,32,128]{3,2,1,0:T(8,128)S(1)} %get-tuple-element.136), channel_id=1, source_target_pairs={{0,4},{4,0},{8,12},{12,8},{16,20},{20,16},{24,28},{28,24},{32,36},... | collective-permute-start | bytes 393224 | tf_op jit(solution)/shard_map/ppermute | solution.py:655
  92.0 13.0 %collective-permute-start.36 = (f32[2,8,8,128]{3,2,1,0:T(8,128)S(1)}, f32[2,8,8,128]{3,2,1,0:T(8,128)S(1)}, u32[]{:S(2)}, u32[]{:S(2)}) collective-permute-start(f32[2,8,8,128]{3,2,1,0:T(8,128)S(1)} %get-tuple-element.124), channel_id=1, source_target_pairs={{0,192},{1,193},{2,194},{3,195},{4,196},{5,197},{6,198},{7,199},{8... | collective-permute-start | bytes 196616 | tf_op jit(solution)/shard_map/ppermute | solution.py:680
  96.1 3.2 %collective-permute-start.31 = (f32[16,128]{1,0:T(8,128)S(1)}, f32[16,128]{1,0:T(8,128)S(1)}, u32[]{:S(2)}, u32[]{:S(2)}) collective-permute-start(f32[16,128]{1,0:T(8,128)S(1)} %get-tuple-element.128.a), channel_id=1, source_target_pairs={{0,4},{4,0},{8,12},{12,8},{16,20},{20,16},{24,28},{28,24},{32,36},... | collective-permute-start | bytes 24584 | tf_op jit(solution)/shard_map/ppermute | solution.py:655
  99.3 4.4 %collective-permute-start.33 = (f32[32,128]{1,0:T(8,128)S(1)}, f32[32,128]{1,0:T(8,128)S(1)}, u32[]{:S(2)}, u32[]{:S(2)}) collective-permute-start(f32[32,128]{1,0:T(8,128)S(1)} %constant_dynamic-update-slice_fusion.2), channel_id=1, source_target_pairs={{0,52},{4,16},{8,60},{12,24},{16,4},{20,32},{24,12},{28,40},{32,20... | collective-permute-start | bytes 49160 | tf_op jit(solution)/shard_map/ppermute | solution.py:661
  100.1 3.6 %collective-permute-start.32 = (f32[32,128]{1,0:T(8,128)S(1)}, f32[32,128]{1,0:T(8,128)S(1)}, u32[]{:S(2)}, u32[]{:S(2)}) collective-permute-start(f32[32,128]{1,0:T(8,128)S(1)} %constant_dynamic-update-slice_fusion.2), channel_id=1, source_target_pairs={{0,60},{4,8},{8,4},{12,16},{16,12},{20,24},{24,20},{28,32},{32,28}... | collective-permute-start | bytes 49160 | tf_op jit(solution)/shard_map/ppermute | solution.py:661
  100.8 5.9 %collective-permute-start.35 = (f32[4,8,8,128]{3,2,1,0:T(8,128)S(1)}, f32[4,8,8,128]{3,2,1,0:T(8,128)S(1)}, u32[]{:S(2)}, u32[]{:S(2)}) collective-permute-start(f32[4,8,8,128]{3,2,1,0:T(8,128)S(1)} %pad_maximum_fusion.3), channel_id=1, source_target_pairs={{0,128},{1,129},{2,130},{3,131},{4,132},{5,133},{6,134},{7,135},{8... | collective-permute-start | bytes 393224 | tf_op jit(solution)/shard_map/ppermute | solution.py:680
  103.7 3.0 %collective-permute-start.34 = (f32[64,128]{1,0:T(8,128)S(1)}, f32[64,128]{1,0:T(8,128)S(1)}, u32[]{:S(2)}, u32[]{:S(2)}) collective-permute-start(f32[64,128]{1,0:T(8,128)S(1)} %pad_maximum_fusion.8), channel_id=1, source_target_pairs={{0,4},{4,0},{8,12},{12,8},{16,20},{20,16},{24,28},{28,24},{32,36},... | collective-permute-start | bytes 98312 | tf_op jit(solution)/shard_map/ppermute | solution.py:655
  106.7 2.9 %copy-start.2 = (f32[4,16,16,128]{3,2,1,0:T(8,128)S(1)}, f32[4,16,16,128]{3,2,1,0:T(8,128)}, u32[]{:S(2)}) copy-start(f32[4,16,16,128]{3,2,1,0:T(8,128)} %initial.1) | copy-start | bytes 1572868
  108.3 2.7 %collective-permute-start.37 = (f32[2,8,8,128]{3,2,1,0:T(8,128)S(1)}, f32[2,8,8,128]{3,2,1,0:T(8,128)S(1)}, u32[]{:S(2)}, u32[]{:S(2)}) collective-permute-start(f32[2,8,8,128]{3,2,1,0:T(8,128)S(1)} %coarse_up_last_body.1), channel_id=1, source_target_pairs={{0,192},{1,193},{2,194},{3,195},{4,196},{5,197},{6,198},{7,199},{8... | collective-permute-start | bytes 196616 | tf_op jit(solution)/shard_map/ppermute | solution.py:680

commit v6 on v5

--- a/solution.py
+++ b/solution.py
@@ -785,15 +785,15 @@
     combined, level1, message = coarse_down(c2)
     jump2 = sent(jump1, 1, 0)
     hand1 = sent(jnp.concatenate([own1, ended1], axis=0), 0, 1)
-    got, hand1, jump2, fine_before = lax.optimization_barrier(
-        (five_chips(message), hand1, jump2, fine_before)
-    )
+    got, jump2, fine_before = lax.optimization_barrier((five_chips(message), jump2, fine_before))
     ended2, own3, c3 = coarse_up(coarse_up_middle_body, got + [combined, level1, jump2], UP_SCRATCH)
 
     combined, level1, message = coarse_down(c3)
     hand2 = sent(jnp.concatenate([own2, ended2], axis=0), 0, 2)
     hand3 = sent(own3, 0, 3)
-    got, hand2, hand3 = lax.optimization_barrier((five_chips(message), hand2, hand3))
+    got, hand1, hand2, hand3 = lax.optimization_barrier(
+        (five_chips(message), hand1, hand2, hand3)
+    )
     ended3 = call(
         coarse_up_last_body,
         (2, 8, 8, 128),

time: 113 us -> 113 us (level)
    ppermute x12, starting transfers between devices: 13.5 us -> 15.6 us  [from_chips(): lax.ppermute(value, 'sx', [(i, (i + (far if i % 2 else -far)) % count) fo...]
    ppermute x11, starting transfers between devices: 18.9 us -> 16.8 us  [swapped_cores(): lax.ppermute(value, 'sx', [(i, i ^ 1) for i in range(lax.axis_size('sx'))])]
    ppermute x12, waiting for transfers between devices: 9.79 us -> 11.5 us  [from_chips(): lax.ppermute(value, 'sx', [(i, (i + (far if i % 2 else -far)) % count) fo...]
    ppermute x1, waiting for transfers between devices: 2.05 us -> 0.54 us  [shards(): jump1 = lax.ppermute(jump0, 'tm', [(1, 0), (2, 1)])]
  transfers between devices with their start and end apart: 38 -> 38, of which waited for: 21 -> 21; matrix products, arithmetic and copies ran while one was open for 0% -> 0% of each run, Pallas kernels for 5% -> 6%
where the time goes in v6:
time: 113 us; the launch traced here: 112 us
  starting transfers between devices  56.7 us (50%)
  waiting for transfers between devices  28 us (25%)
  Pallas kernels  26.3 us (23%)
    pallas_call x14, Pallas kernels, call(): pl.pallas_call(body, out_shape=[jax.ShapeDtypeStruct(s, F32) for s in sha...  26.3 us
    ppermute x11, starting transfers between devices, swapped_cores(): lax.ppermute(value, 'sx', [(i, i ^ 1) for i in range(lax.axis_size('sx'))])  16.8 us
    ppermute x12, starting transfers between devices, from_chips(): lax.ppermute(value, 'sx', [(i, (i + (far if i % 2 else -far)) % count) fo...  15.6 us
    ppermute x9, starting transfers between devices, moved(): lax.ppermute(value, axis, [(i, (i + step) % count) for i in range(count)])  12.7 us
    ppermute x12, waiting for transfers between devices, from_chips(): lax.ppermute(value, 'sx', [(i, (i + (far if i % 2 else -far)) % count) fo...  11.5 us
    ppermute x5, starting transfers between devices, sent(): return lax.ppermute(value, 'tm', [(source, target)])  10.2 us
    ppermute x9, waiting for transfers between devices, moved(): lax.ppermute(value, axis, [(i, (i + step) % count) for i in range(count)])  9.02 us
    ppermute x11, waiting for transfers between devices, swapped_cores(): lax.ppermute(value, 'sx', [(i, i ^ 1) for i in range(lax.axis_size('sx'))])  3.97 us
  transfers between devices with their start and end apart: 38, of which 21 were waited for; matrix products, arithmetic and copies ran while one was open for 0% of the time, Pallas kernels for 6%

profile of v6, /device:TPU:1, one launch (start us, length us, event | category | flops | bytes accessed | tf_op | source)
XLA Modules:
  0.0 112.3 jit_solution(302338215027016707)
XLA Ops:
  0.7 2.7 %pack_body.1 = (f32[9,16,128]{2,1,0:T(8,128)}, f32[9,16,128]{2,1,0:T(8,128)}, f32[9,16,128]{2,1,0:T(8,128)}, f32[9,16,128]{2,1,0:T(8,128)}, f32[8,16,128]{2,1,0:T(8,128)}) custom-call(f32[4,16,16,128]{3,2,1,0:T(8,128)} %initial.1, f32[4,16,16,128]{3,2,1,0:T(8,128)} %bitcast.19, f32[4,16,16,128]{3,2,1,0:T(8,128)} %bitcast.21), custom_call_target="tpu_custom_call" | custom-call | tf_op jit(solution)/shard_map/pack_body/pallas_call | solution.py:17
  3.3 3.0 %collective-permute-start = (f32[9,16,128]{2,1,0:T(8,128)}, f32[9,16,128]{2,1,0:T(8,128)S(1)}, u32[]{:S(2)}, u32[]{:S(2)}) collective-permute-start(f32[9,16,128]{2,1,0:T(8,128)} %get-tuple-element.69), channel_id=1, source_target_pairs={{0,4},{4,8},{8,12},{12,16},{16,20},{20,24},{24,28},{28,32},{32,36}... | collective-permute-start | bytes 221192 | tf_op jit(solution)/shard_map/ppermute | solution.py:643
  6.6 1.1 collective-permute-start.2
  7.7 1.6 %collective-permute-start.3 = (f32[9,16,128]{2,1,0:T(8,128)}, f32[9,16,128]{2,1,0:T(8,128)S(1)}, u32[]{:S(2)}, u32[]{:S(2)}) collective-permute-start(f32[9,16,128]{2,1,0:T(8,128)} %get-tuple-element.72), channel_id=1, source_target_pairs={{0,3},{1,0},{2,1},{3,2},{4,7},{5,4},{6,5},{7,6},{8,11},{9,8},{10,9... | collective-permute-start | bytes 221192 | tf_op jit(solution)/shard_map/ppermute | solution.py:643
  9.5 0.9 collective-permute-done.1.right
  10.4 1.2 %collective-permute-done.2.low = f32[9,16,128]{2,1,0:T(8,128)S(1)} collective-permute-done((f32[9,16,128]{2,1,0:T(8,128)}, f32[9,16,128]{2,1,0:T(8,128)S(1)}, u32[]{:S(2)}, u32[]{:S(2)}) %collective-permute-start.2) | collective-permute-done | bytes 73760 | tf_op jit(solution)/shard_map/ppermute | solution.py:643
  11.6 1.6 %fine_source_body.1 = (f32[4,16,16,128]{3,2,1,0:T(8,128)S(1)}, f32[31,16,128]{2,1,0:T(8,128)S(1)}, f32[2,8,8,128]{3,2,1,0:T(8,128)S(1)}) custom-call(s32[2]{0:T(128)S(1)} %pad_add_fusion.where, f32[4,16,16,128]{3,2,1,0:T(8,128)S(1)} %bitcast.20, f32[4,16,16,128]{3,2,1,0:T(8,128)S(1)} %bitcast.22, f32[9,16,128]{2,1,0:T(8,128)S(1)} %collective-permute-done.left, ...), custom_call_target="tpu_custom_call" | custom-call | tf_op jit(solution)/shard_map/fine_source_body/pallas_call | solution.py:17
  13.2 2.7 %collective-permute-start.5 = (f32[31,16,128]{2,1,0:T(8,128)S(1)}, f32[31,16,128]{2,1,0:T(8,128)S(1)}, u32[]{:S(2)}, u32[]{:S(2)}) collective-permute-start(f32[31,16,128]{2,1,0:T(8,128)S(1)} %get-tuple-element.74.own.own_share), channel_id=1, source_target_pairs={{0,3},{1,0},{2,1},{3,2},{4,7},{5,4},{6,5},{7,6},{8,11},{9,8},{10,9... | collective-permute-start | bytes 761864 | tf_op jit(solution)/shard_map/ppermute | solution.py:643
  16.0 1.4 %collective-permute-start.6 = (f32[23,16,128]{2,1,0:T(8,128)S(1)}, f32[23,16,128]{2,1,0:T(8,128)S(1)}, u32[]{:S(2)}, u32[]{:S(2)}) collective-permute-start(f32[23,16,128]{2,1,0:T(8,128)S(1)} %slice.45), channel_id=1, source_target_pairs={{0,2},{1,3},{2,0},{3,1},{4,6},{5,7},{6,4},{7,5},{8,10},{9,11},{10,... | collective-permute-start | bytes 565256 | tf_op jit(solution)/shard_map/ppermute | solution.py:643
  17.3 5.7 %collective-permute-done.6.across = f32[23,16,128]{2,1,0:T(8,128)S(1)} collective-permute-done((f32[23,16,128]{2,1,0:T(8,128)S(1)}, f32[23,16,128]{2,1,0:T(8,128)S(1)}, u32[]{:S(2)}, u32[]{:S(2)}) %collective-permute-start.6) | collective-permute-done | bytes 188448 | tf_op jit(solution)/shard_map/ppermute | solution.py:643
  23.0 1.3 %collective-permute-done.4.below = f32[31,16,128]{2,1,0:T(8,128)S(1)} collective-permute-done((f32[31,16,128]{2,1,0:T(8,128)S(1)}, f32[31,16,128]{2,1,0:T(8,128)S(1)}, u32[]{:S(2)}, u32[]{:S(2)}) %collective-permute-start.4) | collective-permute-done | bytes 253984 | tf_op jit(solution)/shard_map/ppermute | solution.py:643
  24.3 2.4 %fine_down_body.1 = (f32[64,128]{1,0:T(8,128)S(1)}, f32[480,128]{1,0:T(8,128)S(1)}, f32[480,128]{1,0:T(8,128)S(1)}, f32[18,64,128]{2,1,0:T(8,128)S(1)}, f32[10,32,128]{2,1,0:T(8,128)S(1)}) custom-call(s32[2]{0:T(128)S(1)} %pad_add_fusion.where, f32[31,16,128]{2,1,0:T(8,128)S(1)} %collective-permute-done.4.below, ...), custom_call_target="tpu_custom_call" | custom-call | tf_op jit(solution)/shard_map/fine_down_body/pallas_call | solution.py:17
  26.7 6.2 %collective-permute-start.7 = (f32[544,128]{1,0:T(8,128)S(1)}, f32[544,128]{1,0:T(8,128)S(1)}, u32[]{:S(2)}, u32[]{:S(2)}) collective-permute-start(f32[544,128]{1,0:T(8,128)S(1)} %pad_maximum_fusion), channel_id=1, source_target_pairs={{0,4},{4,0},{8,12},{12,8},{16,20},{20,16},{24,28},{28,24},{32,36},... | collective-permute-start | bytes 835592 | tf_op jit(solution)/shard_map/ppermute | solution.py:655
  32.9 0.5 collective-permute-start.10
  33.7 0.4 collective-permute-done.7.partner
  34.1 2.2 %collective-permute-start.9 = (f32[128,128]{1,0:T(8,128)S(1)}, f32[128,128]{1,0:T(8,128)S(1)}, u32[]{:S(2)}, u32[]{:S(2)}) collective-permute-start(f32[128,128]{1,0:T(8,128)S(1)} %pad_maximum_fusion.5), channel_id=1, source_target_pairs={{0,52},{4,16},{8,60},{12,24},{16,4},{20,32},{24,12},{28,40},{32,20... | collective-permute-start | bytes 196616 | tf_op jit(solution)/shard_map/ppermute | solution.py:661
  36.3 2.3 %collective-permute-start.8 = (f32[128,128]{1,0:T(8,128)S(1)}, f32[128,128]{1,0:T(8,128)S(1)}, u32[]{:S(2)}, u32[]{:S(2)}) collective-permute-start(f32[128,128]{1,0:T(8,128)S(1)} %pad_maximum_fusion.5), channel_id=1, source_target_pairs={{0,60},{4,8},{8,4},{12,16},{16,12},{20,24},{24,20},{28,32},{32,28}... | collective-permute-start | bytes 196616 | tf_op jit(solution)/shard_map/ppermute | solution.py:661
  38.9 0.9 collective-permute-done.9.far
  39.7 1.8 %collective-permute-done.8.near = f32[128,128]{1,0:T(8,128)S(1)} collective-permute-done((f32[128,128]{1,0:T(8,128)S(1)}, f32[128,128]{1,0:T(8,128)S(1)}, u32[]{:S(2)}, u32[]{:S(2)}) %collective-permute-start.8) | collective-permute-done | bytes 65568 | tf_op jit(solution)/shard_map/ppermute | solution.py:661
  41.6 2.5 %collective-permute-start.12 = (f32[256,128]{1,0:T(8,128)S(1)}, f32[256,128]{1,0:T(8,128)S(1)}, u32[]{:S(2)}, u32[]{:S(2)}) collective-permute-start(f32[256,128]{1,0:T(8,128)S(1)} %pad_maximum_fusion.1), channel_id=1, source_target_pairs={{0,4},{4,0},{8,12},{12,8},{16,20},{20,16},{24,28},{28,24},{32,36},... | collective-permute-start | bytes 393224 | tf_op jit(solution)/shard_map/ppermute | solution.py:655
  44.1 1.0 collective-permute-done.12.swapped
  45.0 4.5 %fine_up_body.1 = (f32[18,32,128]{2,1,0:T(8,128)S(1)}, f32[2,8,32,128]{3,2,1,0:T(8,128)S(1)}) custom-call(s32[2]{0:T(128)S(1)} %pad_add_fusion.where, f32[64,128]{1,0:T(8,128)S(1)} %get-tuple-element.75.own, f32[544,128]{1,0:T(8,128)S(1)} %collective-permute-done.7.partner, f32[128,128]{1,0:T(8,128)S(1)} %collective-permute-done.8.near, ...), custom_call_target="tpu_custom_call" | custom-call | tf_op jit(solution)/shard_map/fine_up_body/pallas_call | solution.py:17
  49.6 2.0 %coarse_up_first_body.1 = (f32[2,8,8,128]{3,2,1,0:T(8,128)S(1)}, f32[2,8,8,128]{3,2,1,0:T(8,128)S(1)}, f32[2,4,32,128]{3,2,1,0:T(8,128)S(1)}, f32[2,4,32,128]{3,2,1,0:T(8,128)S(1)}) custom-call(s32[2]{0:T(128)S(1)} %pad_add_fusion.where, f32[64,128]{1,0:T(8,128)S(1)} %get-tuple-element.75.own, f32[544,128]{1,0:T(8,128)S(1)} %collective-permute-done.7.partner, ...), custom_call_target="tpu_custom_call" | custom-call | tf_op jit(solution)/shard_map/coarse_up_first_body/pallas_call | solution.py:17
  51.8 1.7 %collective-permute-start.13 = (f32[2,4,32,128]{3,2,1,0:T(8,128)S(1)}, f32[2,4,32,128]{3,2,1,0:T(8,128)S(1)}, u32[]{:S(2)}, u32[]{:S(2)}) collective-permute-start(f32[2,4,32,128]{3,2,1,0:T(8,128)S(1)} %get-tuple-element.140), channel_id=1, source_target_pairs={{0,4},{4,0},{8,12},{12,8},{16,20},{20,16},{24,28},{28,24},{32,36},... | collective-permute-start | bytes 393224 | tf_op jit(solution)/shard_map/ppermute | solution.py:655
  53.4 2.9 %collective-permute-done.14.outer = f32[2,4,32,128]{3,2,1,0:T(8,128)S(1)} collective-permute-done((f32[2,4,32,128]{3,2,1,0:T(8,128)S(1)}, f32[2,4,32,128]{3,2,1,0:T(8,128)S(1)}, u32[]{:S(2)}, u32[]{:S(2)}) %collective-permute-start.14) | collective-permute-done | bytes 131104 | tf_op jit(solution)/shard_map/ppermute | solution.py:661
  56.4 1.5 %coarse_down_body.3 = (f32[4,8,32,128]{3,2,1,0:T(8,128)S(1)}, f32[12,32,128]{2,1,0:T(8,128)S(1)}, f32[16,128]{1,0:T(8,128)S(1)}) custom-call(s32[2]{0:T(128)S(1)} %pad_add_fusion.where, f32[2,4,32,128]{3,2,1,0:T(8,128)S(1)} %collective-permute-done.13.inner, f32[2,4,32,128]{3,2,1,0:T(8,128)S(1)} %get-tuple-element.87.low, ...), custom_call_target="tpu_custom_call" | custom-call | tf_op jit(solution)/shard_map/coarse_down_body/pallas_call | solution.py:17
  57.8 1.4 %collective-permute-start.15 = (f32[16,128]{1,0:T(8,128)S(1)}, f32[16,128]{1,0:T(8,128)S(1)}, u32[]{:S(2)}, u32[]{:S(2)}) collective-permute-start(f32[16,128]{1,0:T(8,128)S(1)} %get-tuple-element.95.a), channel_id=1, source_target_pairs={{0,4},{4,0},{8,12},{12,8},{16,20},{20,16},{24,28},{28,24},{32,36},... | collective-permute-start | bytes 24584 | tf_op jit(solution)/shard_map/ppermute | solution.py:655
  59.2 1.3 %collective-permute-start.19 = (f32[2,8,32,128]{3,2,1,0:T(8,128)S(1)}, f32[2,8,32,128]{3,2,1,0:T(8,128)S(1)}, u32[]{:S(2)}, u32[]{:S(2)}) collective-permute-start(f32[2,8,32,128]{3,2,1,0:T(8,128)S(1)} %get-tuple-element.85.jump), channel_id=1, source_target_pairs={{64,0},{128,64},{65,1},{129,65},{66,2},{130,66},{67,3},{131,67},{6... | collective-permute-start | bytes 786440 | tf_op jit(solution)/shard_map/ppermute | solution.py:771
  60.5 1.7 %collective-permute-start.17 = (f32[32,128]{1,0:T(8,128)S(1)}, f32[32,128]{1,0:T(8,128)S(1)}, u32[]{:S(2)}, u32[]{:S(2)}) collective-permute-start(f32[32,128]{1,0:T(8,128)S(1)} %pad_maximum_fusion.9), channel_id=1, source_target_pairs={{0,52},{4,16},{8,60},{12,24},{16,4},{20,32},{24,12},{28,40},{32,20... | collective-permute-start | bytes 49160 | tf_op jit(solution)/shard_map/ppermute | solution.py:661
  62.1 0.9 collective-permute-start.16
  63.1 0.9 fine_end_body.1
  64.0 0.9 collective-permute-done.17.d
  64.9 0.7 collective-permute-done.16.c
  65.6 0.5 collective-permute-start.18
  66.1 2.4 %collective-permute-start.27 = (f32[4,16,16,128]{3,2,1,0:T(8,128)}, f32[4,16,16,128]{3,2,1,0:T(8,128)S(1)}, u32[]{:S(2)}, u32[]{:S(2)}) collective-permute-start(f32[4,16,16,128]{3,2,1,0:T(8,128)} %fine_end_body.1), channel_id=1, source_target_pairs={{0,64},{64,128},{128,192},{192,0},{1,65},{65,129},{129,193},{193,1... | collective-permute-start | bytes 1572872 | tf_op jit(solution)/shard_map/ppermute | solution.py:643
  68.4 0.5 collective-permute-done.19.jump
  69.0 1.8 %coarse_up_middle_body.2 = (f32[2,8,8,128]{3,2,1,0:T(8,128)S(1)}, f32[2,8,8,128]{3,2,1,0:T(8,128)S(1)}, f32[2,4,32,128]{3,2,1,0:T(8,128)S(1)}, f32[2,4,32,128]{3,2,1,0:T(8,128)S(1)}) custom-call(s32[2]{0:T(128)S(1)} %pad_add_fusion.where, f32[16,128]{1,0:T(8,128)S(1)} %get-tuple-element.95.a, f32[16,128]{1,0:T(8,128)S(1)} %collective-permute-done.15.b, ...), custom_call_target="tpu_custom_call" | custom-call | tf_op jit(solution)/shard_map/coarse_up_middle_body/pallas_call | solution.py:17
  70.8 2.0 %collective-permute-start.21 = (f32[2,4,32,128]{3,2,1,0:T(8,128)S(1)}, f32[2,4,32,128]{3,2,1,0:T(8,128)S(1)}, u32[]{:S(2)}, u32[]{:S(2)}) collective-permute-start(f32[2,4,32,128]{3,2,1,0:T(8,128)S(1)} %get-tuple-element.137), channel_id=1, source_target_pairs={{0,60},{4,8},{8,4},{12,16},{16,12},{20,24},{24,20},{28,32},{32,28}... | collective-permute-start | bytes 393224 | tf_op jit(solution)/shard_map/ppermute | solution.py:661
  72.7 1.3 %collective-permute-start.26 = (f32[2,8,32,128]{3,2,1,0:T(8,128)S(1)}, f32[2,8,32,128]{3,2,1,0:T(8,128)S(1)}, u32[]{:S(2)}, u32[]{:S(2)}) collective-permute-start(f32[2,8,32,128]{3,2,1,0:T(8,128)S(1)} %collective-permute-done.19.jump), channel_id=1, source_target_pairs={{64,0},{65,1},{66,2},{67,3},{68,4},{69,5},{70,6},{71,7},{72,8},{73... | collective-permute-start | bytes 786440 | tf_op jit(solution)/shard_map/ppermute | solution.py:680
  74.0 1.7 %collective-permute-done.21.outer = f32[2,4,32,128]{3,2,1,0:T(8,128)S(1)} collective-permute-done((f32[2,4,32,128]{3,2,1,0:T(8,128)S(1)}, f32[2,4,32,128]{3,2,1,0:T(8,128)S(1)}, u32[]{:S(2)}, u32[]{:S(2)}) %collective-permute-start.21) | collective-permute-done | bytes 131104 | tf_op jit(solution)/shard_map/ppermute | solution.py:661
  75.7 1.5 %coarse_down_body.4 = (f32[4,8,32,128]{3,2,1,0:T(8,128)S(1)}, f32[12,32,128]{2,1,0:T(8,128)S(1)}, f32[16,128]{1,0:T(8,128)S(1)}) custom-call(s32[2]{0:T(128)S(1)} %pad_add_fusion.where, f32[2,4,32,128]{3,2,1,0:T(8,128)S(1)} %collective-permute-done.20.inner, f32[2,4,32,128]{3,2,1,0:T(8,128)S(1)} %get-tuple-element.104.low, ...), custom_call_target="tpu_custom_call" | custom-call | tf_op jit(solution)/shard_map/coarse_down_body/pallas_call | solution.py:17
  77.2 1.7 %collective-permute-start.22 = (f32[16,128]{1,0:T(8,128)S(1)}, f32[16,128]{1,0:T(8,128)S(1)}, u32[]{:S(2)}, u32[]{:S(2)}) collective-permute-start(f32[16,128]{1,0:T(8,128)S(1)} %get-tuple-element.108.a), channel_id=1, source_target_pairs={{0,4},{4,0},{8,12},{12,8},{16,20},{20,16},{24,28},{28,24},{32,36},... | collective-permute-start | bytes 24584 | tf_op jit(solution)/shard_map/ppermute | solution.py:655
  78.8 0.8 collective-permute-done.22.b
  79.7 1.0 collective-permute-start.24
  80.7 1.2 %collective-permute-start.23 = (f32[32,128]{1,0:T(8,128)S(1)}, f32[32,128]{1,0:T(8,128)S(1)}, u32[]{:S(2)}, u32[]{:S(2)}) collective-permute-start(f32[32,128]{1,0:T(8,128)S(1)} %constant_dynamic-update-slice_fusion), channel_id=1, source_target_pairs={{0,60},{4,8},{8,4},{12,16},{16,12},{20,24},{24,20},{28,32},{32,28}... | collective-permute-start | bytes 49160 | tf_op jit(solution)/shard_map/ppermute | solution.py:661
  81.9 1.9 %collective-permute-done.24.d = f32[32,128]{1,0:T(8,128)S(1)} collective-permute-done((f32[32,128]{1,0:T(8,128)S(1)}, f32[32,128]{1,0:T(8,128)S(1)}, u32[]{:S(2)}, u32[]{:S(2)}) %collective-permute-start.24) | collective-permute-done | bytes 16416 | tf_op jit(solution)/shard_map/ppermute | solution.py:661
  83.7 0.5 collective-permute-done.23.c
  84.2 1.1 collective-permute-start.25
  85.3 0.9 collective-permute-done.25.e
  86.2 1.8 %coarse_up_middle_body.3 = (f32[2,8,8,128]{3,2,1,0:T(8,128)S(1)}, f32[2,8,8,128]{3,2,1,0:T(8,128)S(1)}, f32[2,4,32,128]{3,2,1,0:T(8,128)S(1)}, f32[2,4,32,128]{3,2,1,0:T(8,128)S(1)}) custom-call(s32[2]{0:T(128)S(1)} %pad_add_fusion.where, f32[16,128]{1,0:T(8,128)S(1)} %get-tuple-element.108.a, f32[16,128]{1,0:T(8,128)S(1)} %collective-permute-done.22.b, ...), custom_call_target="tpu_custom_call" | custom-call | tf_op jit(solution)/shard_map/coarse_up_middle_body/pallas_call | solution.py:17
  88.0 0.8 collective-permute-start.29
  88.7 1.4 %collective-permute-start.28 = (f32[2,4,32,128]{3,2,1,0:T(8,128)S(1)}, f32[2,4,32,128]{3,2,1,0:T(8,128)S(1)}, u32[]{:S(2)}, u32[]{:S(2)}) collective-permute-start(f32[2,4,32,128]{3,2,1,0:T(8,128)S(1)} %get-tuple-element.136), channel_id=1, source_target_pairs={{0,4},{4,0},{8,12},{12,8},{16,20},{20,16},{24,28},{28,24},{32,36},... | collective-permute-start | bytes 393224 | tf_op jit(solution)/shard_map/ppermute | solution.py:655
  90.2 2.8 %collective-permute-start.34 = (f32[4,8,8,128]{3,2,1,0:T(8,128)S(1)}, f32[4,8,8,128]{3,2,1,0:T(8,128)S(1)}, u32[]{:S(2)}, u32[]{:S(2)}) collective-permute-start(f32[4,8,8,128]{3,2,1,0:T(8,128)S(1)} %pad_maximum_fusion.2), channel_id=1, source_target_pairs={{0,64},{1,65},{2,66},{3,67},{4,68},{5,69},{6,70},{7,71},{8,72},{9,... | collective-permute-start | bytes 393224 | tf_op jit(solution)/shard_map/ppermute | solution.py:680
  93.0 1.3 %collective-permute-start.36 = (f32[2,8,8,128]{3,2,1,0:T(8,128)S(1)}, f32[2,8,8,128]{3,2,1,0:T(8,128)S(1)}, u32[]{:S(2)}, u32[]{:S(2)}) collective-permute-start(f32[2,8,8,128]{3,2,1,0:T(8,128)S(1)} %get-tuple-element.123), channel_id=1, source_target_pairs={{0,192},{1,193},{2,194},{3,195},{4,196},{5,197},{6,198},{7,199},{8... | collective-permute-start | bytes 196616 | tf_op jit(solution)/shard_map/ppermute | solution.py:680
  94.3 1.5 %coarse_down_body.5 = (f32[4,8,32,128]{3,2,1,0:T(8,128)S(1)}, f32[12,32,128]{2,1,0:T(8,128)S(1)}, f32[16,128]{1,0:T(8,128)S(1)}) custom-call(s32[2]{0:T(128)S(1)} %pad_add_fusion.where, f32[2,4,32,128]{3,2,1,0:T(8,128)S(1)} %collective-permute-done.28.inner, f32[2,4,32,128]{3,2,1,0:T(8,128)S(1)} %get-tuple-element.117.low, ...), custom_call_target="tpu_custom_call" | custom-call | tf_op jit(solution)/shard_map/coarse_down_body/pallas_call | solution.py:17
  96.2 0.9 collective-permute-done.30.b
  97.1 1.6 %collective-permute-start.32 = (f32[32,128]{1,0:T(8,128)S(1)}, f32[32,128]{1,0:T(8,128)S(1)}, u32[]{:S(2)}, u32[]{:S(2)}) collective-permute-start(f32[32,128]{1,0:T(8,128)S(1)} %constant_dynamic-update-slice_fusion.2), channel_id=1, source_target_pairs={{0,52},{4,16},{8,60},{12,24},{16,4},{20,32},{24,12},{28,40},{32,20... | collective-permute-start | bytes 49160 | tf_op jit(solution)/shard_map/ppermute | solution.py:661
  98.6 1.5 %collective-permute-start.31 = (f32[32,128]{1,0:T(8,128)S(1)}, f32[32,128]{1,0:T(8,128)S(1)}, u32[]{:S(2)}, u32[]{:S(2)}) collective-permute-start(f32[32,128]{1,0:T(8,128)S(1)} %constant_dynamic-update-slice_fusion.2), channel_id=1, source_target_pairs={{0,60},{4,8},{8,4},{12,16},{16,12},{20,24},{24,20},{28,32},{32,28}... | collective-permute-start | bytes 49160 | tf_op jit(solution)/shard_map/ppermute | solution.py:661
  100.1 3.5 %collective-permute-start.35 = (f32[4,8,8,128]{3,2,1,0:T(8,128)S(1)}, f32[4,8,8,128]{3,2,1,0:T(8,128)S(1)}, u32[]{:S(2)}, u32[]{:S(2)}) collective-permute-start(f32[4,8,8,128]{3,2,1,0:T(8,128)S(1)} %pad_maximum_fusion.3), channel_id=1, source_target_pairs={{0,128},{1,129},{2,130},{3,131},{4,132},{5,133},{6,134},{7,135},{8... | collective-permute-start | bytes 393224 | tf_op jit(solution)/shard_map/ppermute | solution.py:680
  103.8 2.6 %collective-permute-done.35 = f32[4,8,8,128]{3,2,1,0:T(8,128)S(1)} collective-permute-done((f32[4,8,8,128]{3,2,1,0:T(8,128)S(1)}, f32[4,8,8,128]{3,2,1,0:T(8,128)S(1)}, u32[]{:S(2)}, u32[]{:S(2)}) %collective-permute-start.35) | collective-permute-done | bytes 131104 | tf_op jit(solution)/shard_map/ppermute | solution.py:680
  106.4 1.6 %coarse_up_last_body.1 = f32[2,8,8,128]{3,2,1,0:T(8,128)S(1)} custom-call(s32[2]{0:T(128)S(1)} %pad_add_fusion.where, f32[16,128]{1,0:T(8,128)S(1)} %get-tuple-element.128.a, f32[16,128]{1,0:T(8,128)S(1)} %collective-permute-done.30.b, f32[32,128]{1,0:T(8,128)S(1)} %collective-permute-done.31.c, f32[32,128]{1,0:T(8,128)S(1)} %collective-permute-done.32.d, ...), custom_call_target="tpu_custom_call" | custom-call | tf_op jit(solution)/shard_map/coarse_up_last_body/pallas_call | solution.py:17
  108.0 1.3 %collective-permute-start.37 = (f32[2,8,8,128]{3,2,1,0:T(8,128)S(1)}, f32[2,8,8,128]{3,2,1,0:T(8,128)S(1)}, u32[]{:S(2)}, u32[]{:S(2)}) collective-permute-start(f32[2,8,8,128]{3,2,1,0:T(8,128)S(1)} %coarse_up_last_body.1), channel_id=1, source_target_pairs={{0,192},{1,193},{2,194},{3,195},{4,196},{5,197},{6,198},{7,199},{8... | collective-permute-start | bytes 196616 | tf_op jit(solution)/shard_map/ppermute | solution.py:680
  109.3 1.4 %new_start_body.1 = f32[4,16,16,128]{3,2,1,0:T(8,128)} custom-call(s32[2]{0:T(128)S(1)} %pad_add_fusion.where, f32[4,16,16,128]{3,2,1,0:T(8,128)S(1)} %collective-permute-done.27.fine, f32[4,16,16,128]{3,2,1,0:T(8,128)S(1)} %copy-done.2, f32[2,8,8,128]{3,2,1,0:T(8,128)S(1)} %get-tuple-element.142.state), custom_call_target="tpu_custom_call" | custom-call | tf_op jit(solution)/shard_map/new_start_body/pallas_call | solution.py:17
  111.1 1.3 %coarse_end_body.1 = f32[4,8,8,64]{3,2,1,0:T(8,128)} custom-call(s32[2]{0:T(128)S(1)} %pad_add_fusion.where, f32[2,8,8,128]{3,2,1,0:T(8,128)S(1)} %get-tuple-element.127.e0, f32[2,8,8,128]{3,2,1,0:T(8,128)S(1)} %get-tuple-element.143.e1, f32[2,8,8,128]{3,2,1,0:T(8,128)S(1)} %get-tuple-element.141.e2, f32[2,8,8,128]{3,2,1,0:T(8,128)S(1)} %collective-permute-done.37.e3), custom_call_target="tpu_custom_call" | custom-call | tf_op jit(solution)/shard_map/coarse_end_body/pallas_call | solution.py:17
  (61 shorter events, 2.3 us)
Async XLA Ops:
  0.6 8.7 %copy-start.4 = (f32[1,4,8,8,64]{4,3,2,1,0:T(8,128)S(1)}, f32[1,4,8,8,64]{4,3,2,1,0:T(8,128)}, u32[]{:S(2)}) copy-start(f32[1,4,8,8,64]{4,3,2,1,0:T(8,128)} %param.7) | copy-start | bytes 196612
  0.6 10.9 %copy-start.1 = (f32[1,4,16,16,128]{4,3,2,1,0:T(8,128)S(1)}, f32[1,4,16,16,128]{4,3,2,1,0:T(8,128)}, u32[]{:S(2)}) copy-start(f32[1,4,16,16,128]{4,3,2,1,0:T(8,128)} %param.6) | copy-start | bytes 1572868
  3.3 8.2 %copy-start = (f32[1,4,16,16,128]{4,3,2,1,0:T(8,128)S(1)}, f32[1,4,16,16,128]{4,3,2,1,0:T(8,128)}, u32[]{:S(2)}) copy-start(f32[1,4,16,16,128]{4,3,2,1,0:T(8,128)} %param.5) | copy-start | bytes 1572868
  3.3 6.2 %collective-permute-start = (f32[9,16,128]{2,1,0:T(8,128)}, f32[9,16,128]{2,1,0:T(8,128)S(1)}, u32[]{:S(2)}, u32[]{:S(2)}) collective-permute-start(f32[9,16,128]{2,1,0:T(8,128)} %get-tuple-element.69), channel_id=1, source_target_pairs={{0,4},{4,8},{8,12},{12,16},{16,20},{20,24},{24,28},{28,32},{32,36}... | collective-permute-start | bytes 221192 | tf_op jit(solution)/shard_map/ppermute | solution.py:643
  6.4 4.0 %collective-permute-start.1 = (f32[9,16,128]{2,1,0:T(8,128)}, f32[9,16,128]{2,1,0:T(8,128)S(1)}, u32[]{:S(2)}, u32[]{:S(2)}) collective-permute-start(f32[9,16,128]{2,1,0:T(8,128)} %get-tuple-element.70), channel_id=1, source_target_pairs={{0,60},{4,0},{8,4},{12,8},{16,12},{20,16},{24,20},{28,24},{32,28},... | collective-permute-start | bytes 221192 | tf_op jit(solution)/shard_map/ppermute | solution.py:643
  6.6 4.9 %collective-permute-start.2 = (f32[9,16,128]{2,1,0:T(8,128)}, f32[9,16,128]{2,1,0:T(8,128)S(1)}, u32[]{:S(2)}, u32[]{:S(2)}) collective-permute-start(f32[9,16,128]{2,1,0:T(8,128)} %get-tuple-element.71), channel_id=1, source_target_pairs={{0,1},{1,2},{2,3},{3,0},{4,5},{5,6},{6,7},{7,4},{8,9},{9,10},{10,1... | collective-permute-start | bytes 221192 | tf_op jit(solution)/shard_map/ppermute | solution.py:643
  7.7 3.9 %collective-permute-start.3 = (f32[9,16,128]{2,1,0:T(8,128)}, f32[9,16,128]{2,1,0:T(8,128)S(1)}, u32[]{:S(2)}, u32[]{:S(2)}) collective-permute-start(f32[9,16,128]{2,1,0:T(8,128)} %get-tuple-element.72), channel_id=1, source_target_pairs={{0,3},{1,0},{2,1},{3,2},{4,7},{5,4},{6,5},{7,6},{8,11},{9,8},{10,9... | collective-permute-start | bytes 221192 | tf_op jit(solution)/shard_map/ppermute | solution.py:643
  9.4 2.1 %copy-start.3 = (f32[8,16,128]{2,1,0:T(8,128)S(1)}, f32[8,16,128]{2,1,0:T(8,128)}, u32[]{:S(2)}) copy-start(f32[8,16,128]{2,1,0:T(8,128)} %get-tuple-element.73.opening) | copy-start | bytes 196612
  13.2 9.8 %collective-permute-start.5 = (f32[31,16,128]{2,1,0:T(8,128)S(1)}, f32[31,16,128]{2,1,0:T(8,128)S(1)}, u32[]{:S(2)}, u32[]{:S(2)}) collective-permute-start(f32[31,16,128]{2,1,0:T(8,128)S(1)} %get-tuple-element.74.own.own_share), channel_id=1, source_target_pairs={{0,3},{1,0},{2,1},{3,2},{4,7},{5,4},{6,5},{7,6},{8,11},{9,8},{10,9... | collective-permute-start | bytes 761864 | tf_op jit(solution)/shard_map/ppermute | solution.py:643
  15.9 8.4 %collective-permute-start.4 = (f32[31,16,128]{2,1,0:T(8,128)S(1)}, f32[31,16,128]{2,1,0:T(8,128)S(1)}, u32[]{:S(2)}, u32[]{:S(2)}) collective-permute-start(f32[31,16,128]{2,1,0:T(8,128)S(1)} %get-tuple-element.74.own.own_share), channel_id=1, source_target_pairs={{0,1},{1,2},{2,3},{3,0},{4,5},{5,6},{6,7},{7,4},{8,9},{9,10},{10,1... | collective-permute-start | bytes 761864 | tf_op jit(solution)/shard_map/ppermute | solution.py:643
  16.0 7.0 %collective-permute-start.6 = (f32[23,16,128]{2,1,0:T(8,128)S(1)}, f32[23,16,128]{2,1,0:T(8,128)S(1)}, u32[]{:S(2)}, u32[]{:S(2)}) collective-permute-start(f32[23,16,128]{2,1,0:T(8,128)S(1)} %slice.45), channel_id=1, source_target_pairs={{0,2},{1,3},{2,0},{3,1},{4,6},{5,7},{6,4},{7,5},{8,10},{9,11},{10,... | collective-permute-start | bytes 565256 | tf_op jit(solution)/shard_map/ppermute | solution.py:643
  26.7 7.4 %collective-permute-start.7 = (f32[544,128]{1,0:T(8,128)S(1)}, f32[544,128]{1,0:T(8,128)S(1)}, u32[]{:S(2)}, u32[]{:S(2)}) collective-permute-start(f32[544,128]{1,0:T(8,128)S(1)} %pad_maximum_fusion), channel_id=1, source_target_pairs={{0,4},{4,0},{8,12},{12,8},{16,20},{20,16},{24,28},{28,24},{32,36},... | collective-permute-start | bytes 835592 | tf_op jit(solution)/shard_map/ppermute | solution.py:655
  32.9 5.9 %collective-permute-start.10 = (f32[480,128]{1,0:T(8,128)S(1)}, f32[480,128]{1,0:T(8,128)S(1)}, u32[]{:S(2)}, u32[]{:S(2)}) collective-permute-start(f32[480,128]{1,0:T(8,128)S(1)} %get-tuple-element.77), channel_id=1, source_target_pairs={{0,60},{4,8},{8,4},{12,16},{16,12},{20,24},{24,20},{28,32},{32,28}... | collective-permute-start | bytes 737288 | tf_op jit(solution)/shard_map/ppermute | solution.py:661
  33.4 5.2 %collective-permute-start.11 = (f32[8,16,128]{2,1,0:T(8,128)S(1)}, f32[8,16,128]{2,1,0:T(8,128)S(1)}, u32[]{:S(2)}, u32[]{:S(2)}) collective-permute-start(f32[8,16,128]{2,1,0:T(8,128)S(1)} %slice.47), channel_id=1, source_target_pairs={{0,2},{1,3},{2,0},{3,1},{4,6},{5,7},{6,4},{7,5},{8,10},{9,11},{10,... | collective-permute-start | bytes 196616 | tf_op jit(solution)/shard_map/ppermute | solution.py:643
  34.1 5.6 %collective-permute-start.9 = (f32[128,128]{1,0:T(8,128)S(1)}, f32[128,128]{1,0:T(8,128)S(1)}, u32[]{:S(2)}, u32[]{:S(2)}) collective-permute-start(f32[128,128]{1,0:T(8,128)S(1)} %pad_maximum_fusion.5), channel_id=1, source_target_pairs={{0,52},{4,16},{8,60},{12,24},{16,4},{20,32},{24,12},{28,40},{32,20... | collective-permute-start | bytes 196616 | tf_op jit(solution)/shard_map/ppermute | solution.py:661
  36.3 5.2 %collective-permute-start.8 = (f32[128,128]{1,0:T(8,128)S(1)}, f32[128,128]{1,0:T(8,128)S(1)}, u32[]{:S(2)}, u32[]{:S(2)}) collective-permute-start(f32[128,128]{1,0:T(8,128)S(1)} %pad_maximum_fusion.5), channel_id=1, source_target_pairs={{0,60},{4,8},{8,4},{12,16},{16,12},{20,24},{24,20},{28,32},{32,28}... | collective-permute-start | bytes 196616 | tf_op jit(solution)/shard_map/ppermute | solution.py:661
  41.6 3.5 %collective-permute-start.12 = (f32[256,128]{1,0:T(8,128)S(1)}, f32[256,128]{1,0:T(8,128)S(1)}, u32[]{:S(2)}, u32[]{:S(2)}) collective-permute-start(f32[256,128]{1,0:T(8,128)S(1)} %pad_maximum_fusion.1), channel_id=1, source_target_pairs={{0,4},{4,0},{8,12},{12,8},{16,20},{20,16},{24,28},{28,24},{32,36},... | collective-permute-start | bytes 393224 | tf_op jit(solution)/shard_map/ppermute | solution.py:655
  51.6 4.8 %collective-permute-start.14 = (f32[2,4,32,128]{3,2,1,0:T(8,128)S(1)}, f32[2,4,32,128]{3,2,1,0:T(8,128)S(1)}, u32[]{:S(2)}, u32[]{:S(2)}) collective-permute-start(f32[2,4,32,128]{3,2,1,0:T(8,128)S(1)} %get-tuple-element.139), channel_id=1, source_target_pairs={{0,60},{4,8},{8,4},{12,16},{16,12},{20,24},{24,20},{28,32},{32,28}... | collective-permute-start | bytes 393224 | tf_op jit(solution)/shard_map/ppermute | solution.py:661
  51.8 4.6 %collective-permute-start.13 = (f32[2,4,32,128]{3,2,1,0:T(8,128)S(1)}, f32[2,4,32,128]{3,2,1,0:T(8,128)S(1)}, u32[]{:S(2)}, u32[]{:S(2)}) collective-permute-start(f32[2,4,32,128]{3,2,1,0:T(8,128)S(1)} %get-tuple-element.140), channel_id=1, source_target_pairs={{0,4},{4,0},{8,12},{12,8},{16,20},{20,16},{24,28},{28,24},{32,36},... | collective-permute-start | bytes 393224 | tf_op jit(solution)/shard_map/ppermute | solution.py:655
  57.8 2.7 %collective-permute-start.15 = (f32[16,128]{1,0:T(8,128)S(1)}, f32[16,128]{1,0:T(8,128)S(1)}, u32[]{:S(2)}, u32[]{:S(2)}) collective-permute-start(f32[16,128]{1,0:T(8,128)S(1)} %get-tuple-element.95.a), channel_id=1, source_target_pairs={{0,4},{4,0},{8,12},{12,8},{16,20},{20,16},{24,28},{28,24},{32,36},... | collective-permute-start | bytes 24584 | tf_op jit(solution)/shard_map/ppermute | solution.py:655
  59.2 9.8 %collective-permute-start.19 = (f32[2,8,32,128]{3,2,1,0:T(8,128)S(1)}, f32[2,8,32,128]{3,2,1,0:T(8,128)S(1)}, u32[]{:S(2)}, u32[]{:S(2)}) collective-permute-start(f32[2,8,32,128]{3,2,1,0:T(8,128)S(1)} %get-tuple-element.85.jump), channel_id=1, source_target_pairs={{64,0},{128,64},{65,1},{129,65},{66,2},{130,66},{67,3},{131,67},{6... | collective-permute-start | bytes 786440 | tf_op jit(solution)/shard_map/ppermute | solution.py:771
  60.5 4.4 %collective-permute-start.17 = (f32[32,128]{1,0:T(8,128)S(1)}, f32[32,128]{1,0:T(8,128)S(1)}, u32[]{:S(2)}, u32[]{:S(2)}) collective-permute-start(f32[32,128]{1,0:T(8,128)S(1)} %pad_maximum_fusion.9), channel_id=1, source_target_pairs={{0,52},{4,16},{8,60},{12,24},{16,4},{20,32},{24,12},{28,40},{32,20... | collective-permute-start | bytes 49160 | tf_op jit(solution)/shard_map/ppermute | solution.py:661
  62.1 3.5 %collective-permute-start.16 = (f32[32,128]{1,0:T(8,128)S(1)}, f32[32,128]{1,0:T(8,128)S(1)}, u32[]{:S(2)}, u32[]{:S(2)}) collective-permute-start(f32[32,128]{1,0:T(8,128)S(1)} %pad_maximum_fusion.9), channel_id=1, source_target_pairs={{0,60},{4,8},{8,4},{12,16},{16,12},{20,24},{24,20},{28,32},{32,28}... | collective-permute-start | bytes 49160 | tf_op jit(solution)/shard_map/ppermute | solution.py:661
  65.6 2.8 %collective-permute-start.18 = (f32[64,128]{1,0:T(8,128)S(1)}, f32[64,128]{1,0:T(8,128)S(1)}, u32[]{:S(2)}, u32[]{:S(2)}) collective-permute-start(f32[64,128]{1,0:T(8,128)S(1)} %pad_maximum_fusion.6), channel_id=1, source_target_pairs={{0,4},{4,0},{8,12},{12,8},{16,20},{20,16},{24,28},{28,24},{32,36},... | collective-permute-start | bytes 98312 | tf_op jit(solution)/shard_map/ppermute | solution.py:655
  66.1 20.1 %collective-permute-start.27 = (f32[4,16,16,128]{3,2,1,0:T(8,128)}, f32[4,16,16,128]{3,2,1,0:T(8,128)S(1)}, u32[]{:S(2)}, u32[]{:S(2)}) collective-permute-start(f32[4,16,16,128]{3,2,1,0:T(8,128)} %fine_end_body.1), channel_id=1, source_target_pairs={{0,64},{64,128},{128,192},{192,0},{1,65},{65,129},{129,193},{193,1... | collective-permute-start | bytes 1572872 | tf_op jit(solution)/shard_map/ppermute | solution.py:643
  70.8 4.9 %collective-permute-start.21 = (f32[2,4,32,128]{3,2,1,0:T(8,128)S(1)}, f32[2,4,32,128]{3,2,1,0:T(8,128)S(1)}, u32[]{:S(2)}, u32[]{:S(2)}) collective-permute-start(f32[2,4,32,128]{3,2,1,0:T(8,128)S(1)} %get-tuple-element.137), channel_id=1, source_target_pairs={{0,60},{4,8},{8,4},{12,16},{16,12},{20,24},{24,20},{28,32},{32,28}... | collective-permute-start | bytes 393224 | tf_op jit(solution)/shard_map/ppermute | solution.py:661
  72.7 3.0 %collective-permute-start.20 = (f32[2,4,32,128]{3,2,1,0:T(8,128)S(1)}, f32[2,4,32,128]{3,2,1,0:T(8,128)S(1)}, u32[]{:S(2)}, u32[]{:S(2)}) collective-permute-start(f32[2,4,32,128]{3,2,1,0:T(8,128)S(1)} %get-tuple-element.138), channel_id=1, source_target_pairs={{0,4},{4,0},{8,12},{12,8},{16,20},{20,16},{24,28},{28,24},{32,36},... | collective-permute-start | bytes 393224 | tf_op jit(solution)/shard_map/ppermute | solution.py:655
  72.7 13.4 %collective-permute-start.26 = (f32[2,8,32,128]{3,2,1,0:T(8,128)S(1)}, f32[2,8,32,128]{3,2,1,0:T(8,128)S(1)}, u32[]{:S(2)}, u32[]{:S(2)}) collective-permute-start(f32[2,8,32,128]{3,2,1,0:T(8,128)S(1)} %collective-permute-done.19.jump), channel_id=1, source_target_pairs={{64,0},{65,1},{66,2},{67,3},{68,4},{69,5},{70,6},{71,7},{72,8},{73... | collective-permute-start | bytes 786440 | tf_op jit(solution)/shard_map/ppermute | solution.py:680
  77.2 2.5 %collective-permute-start.22 = (f32[16,128]{1,0:T(8,128)S(1)}, f32[16,128]{1,0:T(8,128)S(1)}, u32[]{:S(2)}, u32[]{:S(2)}) collective-permute-start(f32[16,128]{1,0:T(8,128)S(1)} %get-tuple-element.108.a), channel_id=1, source_target_pairs={{0,4},{4,0},{8,12},{12,8},{16,20},{20,16},{24,28},{28,24},{32,36},... | collective-permute-start | bytes 24584 | tf_op jit(solution)/shard_map/ppermute | solution.py:655
  79.7 4.1 %collective-permute-start.24 = (f32[32,128]{1,0:T(8,128)S(1)}, f32[32,128]{1,0:T(8,128)S(1)}, u32[]{:S(2)}, u32[]{:S(2)}) collective-permute-start(f32[32,128]{1,0:T(8,128)S(1)} %constant_dynamic-update-slice_fusion), channel_id=1, source_target_pairs={{0,52},{4,16},{8,60},{12,24},{16,4},{20,32},{24,12},{28,40},{32,20... | collective-permute-start | bytes 49160 | tf_op jit(solution)/shard_map/ppermute | solution.py:661
  80.7 3.5 %collective-permute-start.23 = (f32[32,128]{1,0:T(8,128)S(1)}, f32[32,128]{1,0:T(8,128)S(1)}, u32[]{:S(2)}, u32[]{:S(2)}) collective-permute-start(f32[32,128]{1,0:T(8,128)S(1)} %constant_dynamic-update-slice_fusion), channel_id=1, source_target_pairs={{0,60},{4,8},{8,4},{12,16},{16,12},{20,24},{24,20},{28,32},{32,28}... | collective-permute-start | bytes 49160 | tf_op jit(solution)/shard_map/ppermute | solution.py:661
  84.2 1.9 %collective-permute-start.25 = (f32[64,128]{1,0:T(8,128)S(1)}, f32[64,128]{1,0:T(8,128)S(1)}, u32[]{:S(2)}, u32[]{:S(2)}) collective-permute-start(f32[64,128]{1,0:T(8,128)S(1)} %pad_maximum_fusion.7), channel_id=1, source_target_pairs={{0,4},{4,0},{8,12},{12,8},{16,20},{20,16},{24,28},{28,24},{32,36},... | collective-permute-start | bytes 98312 | tf_op jit(solution)/shard_map/ppermute | solution.py:655
  88.0 6.3 %collective-permute-start.29 = (f32[2,4,32,128]{3,2,1,0:T(8,128)S(1)}, f32[2,4,32,128]{3,2,1,0:T(8,128)S(1)}, u32[]{:S(2)}, u32[]{:S(2)}) collective-permute-start(f32[2,4,32,128]{3,2,1,0:T(8,128)S(1)} %get-tuple-element.135), channel_id=1, source_target_pairs={{0,60},{4,8},{8,4},{12,16},{16,12},{20,24},{24,20},{28,32},{32,28}... | collective-permute-start | bytes 393224 | tf_op jit(solution)/shard_map/ppermute | solution.py:661
  88.7 5.6 %collective-permute-start.28 = (f32[2,4,32,128]{3,2,1,0:T(8,128)S(1)}, f32[2,4,32,128]{3,2,1,0:T(8,128)S(1)}, u32[]{:S(2)}, u32[]{:S(2)}) collective-permute-start(f32[2,4,32,128]{3,2,1,0:T(8,128)S(1)} %get-tuple-element.136), channel_id=1, source_target_pairs={{0,4},{4,0},{8,12},{12,8},{16,20},{20,16},{24,28},{28,24},{32,36},... | collective-permute-start | bytes 393224 | tf_op jit(solution)/shard_map/ppermute | solution.py:655
  90.2 13.6 %collective-permute-start.34 = (f32[4,8,8,128]{3,2,1,0:T(8,128)S(1)}, f32[4,8,8,128]{3,2,1,0:T(8,128)S(1)}, u32[]{:S(2)}, u32[]{:S(2)}) collective-permute-start(f32[4,8,8,128]{3,2,1,0:T(8,128)S(1)} %pad_maximum_fusion.2), channel_id=1, source_target_pairs={{0,64},{1,65},{2,66},{3,67},{4,68},{5,69},{6,70},{7,71},{8,72},{9,... | collective-permute-start | bytes 393224 | tf_op jit(solution)/shard_map/ppermute | solution.py:680
  93.0 10.7 %collective-permute-start.36 = (f32[2,8,8,128]{3,2,1,0:T(8,128)S(1)}, f32[2,8,8,128]{3,2,1,0:T(8,128)S(1)}, u32[]{:S(2)}, u32[]{:S(2)}) collective-permute-start(f32[2,8,8,128]{3,2,1,0:T(8,128)S(1)} %get-tuple-element.123), channel_id=1, source_target_pairs={{0,192},{1,193},{2,194},{3,195},{4,196},{5,197},{6,198},{7,199},{8... | collective-permute-start | bytes 196616 | tf_op jit(solution)/shard_map/ppermute | solution.py:680
  95.8 1.3 %collective-permute-start.30 = (f32[16,128]{1,0:T(8,128)S(1)}, f32[16,128]{1,0:T(8,128)S(1)}, u32[]{:S(2)}, u32[]{:S(2)}) collective-permute-start(f32[16,128]{1,0:T(8,128)S(1)} %get-tuple-element.128.a), channel_id=1, source_target_pairs={{0,4},{4,0},{8,12},{12,8},{16,20},{20,16},{24,28},{28,24},{32,36},... | collective-permute-start | bytes 24584 | tf_op jit(solution)/shard_map/ppermute | solution.py:655
  97.1 6.6 %collective-permute-start.32 = (f32[32,128]{1,0:T(8,128)S(1)}, f32[32,128]{1,0:T(8,128)S(1)}, u32[]{:S(2)}, u32[]{:S(2)}) collective-permute-start(f32[32,128]{1,0:T(8,128)S(1)} %constant_dynamic-update-slice_fusion.2), channel_id=1, source_target_pairs={{0,52},{4,16},{8,60},{12,24},{16,4},{20,32},{24,12},{28,40},{32,20... | collective-permute-start | bytes 49160 | tf_op jit(solution)/shard_map/ppermute | solution.py:661
  98.6 5.0 %collective-permute-start.31 = (f32[32,128]{1,0:T(8,128)S(1)}, f32[32,128]{1,0:T(8,128)S(1)}, u32[]{:S(2)}, u32[]{:S(2)}) collective-permute-start(f32[32,128]{1,0:T(8,128)S(1)} %constant_dynamic-update-slice_fusion.2), channel_id=1, source_target_pairs={{0,60},{4,8},{8,4},{12,16},{16,12},{20,24},{24,20},{28,32},{32,28}... | collective-permute-start | bytes 49160 | tf_op jit(solution)/shard_map/ppermute | solution.py:661
  100.1 6.3 %collective-permute-start.35 = (f32[4,8,8,128]{3,2,1,0:T(8,128)S(1)}, f32[4,8,8,128]{3,2,1,0:T(8,128)S(1)}, u32[]{:S(2)}, u32[]{:S(2)}) collective-permute-start(f32[4,8,8,128]{3,2,1,0:T(8,128)S(1)} %pad_maximum_fusion.3), channel_id=1, source_target_pairs={{0,128},{1,129},{2,130},{3,131},{4,132},{5,133},{6,134},{7,135},{8... | collective-permute-start | bytes 393224 | tf_op jit(solution)/shard_map/ppermute | solution.py:680
  103.6 2.7 %collective-permute-start.33 = (f32[64,128]{1,0:T(8,128)S(1)}, f32[64,128]{1,0:T(8,128)S(1)}, u32[]{:S(2)}, u32[]{:S(2)}) collective-permute-start(f32[64,128]{1,0:T(8,128)S(1)} %pad_maximum_fusion.8), channel_id=1, source_target_pairs={{0,4},{4,0},{8,12},{12,8},{16,20},{20,16},{24,28},{28,24},{32,36},... | collective-permute-start | bytes 98312 | tf_op jit(solution)/shard_map/ppermute | solution.py:655
  106.4 2.9 %copy-start.2 = (f32[4,16,16,128]{3,2,1,0:T(8,128)S(1)}, f32[4,16,16,128]{3,2,1,0:T(8,128)}, u32[]{:S(2)}) copy-start(f32[4,16,16,128]{3,2,1,0:T(8,128)} %initial.1) | copy-start | bytes 1572868
  108.0 3.1 %collective-permute-start.37 = (f32[2,8,8,128]{3,2,1,0:T(8,128)S(1)}, f32[2,8,8,128]{3,2,1,0:T(8,128)S(1)}, u32[]{:S(2)}, u32[]{:S(2)}) collective-permute-start(f32[2,8,8,128]{3,2,1,0:T(8,128)S(1)} %coarse_up_last_body.1), channel_id=1, source_target_pairs={{0,192},{1,193},{2,194},{3,195},{4,196},{5,197},{6,198},{7,199},{8... | collective-permute-start | bytes 196616 | tf_op jit(solution)/shard_map/ppermute | solution.py:680
